TPU v7x, 32 devices: a whole 2x2x4 slice. The times are simulated.
32 devices in a mesh: grp: 2 (over y), wide: 4 (over z), narrow: 2 (over x), sub: 2 (over core).
Axes of the slice: x: 2, y: 2, z: 4, core: 2. Of those that a mesh axis runs over, the one named last changes fastest.
Arguments:
- inverse_slabs: bfloat16 [2, 384, 160000], P(None, 'wide', ('narrow', 'sub')), may hold values from -40 to 40
- potential_noise: bfloat16 [512, 160000], P(('grp', 'wide'), ('narrow', 'sub')), parts along dimension 0, may hold values from -6 to 6
- electrode_volts: float32 [512, 2], P(('grp', 'wide')), parts along dimension 0, may hold values from -3 to 3
- labels: int32 [160000], P(('narrow', 'sub')), may hold values from 0 to 1
- profile: float32 [2, 384], P(None, ('narrow', 'sub')), may hold values from 0.5 to 5
Outputs:
- neutral_charges: float32 [2, 384, 512], P(None, ('narrow', 'sub'), ('grp', 'wide')), parts along dimension 2
There are 2 independent parts, one for each index of `grp`. A program takes and returns all parts, laid end to end along the dimension named above; an argument that names none is the same for every part. Nothing has to cross between parts.
All inputs are finite; a program needn't handle non-finite values.
Results may differ from a plain program's by a relative error of at most 0.003.
Values may be sent and summed in bfloat16 or wider, within the bound.
No kernel may reach another device: no remote copies, remote signals or barrier semaphores. Data moves between devices by JAX's collectives and lax.ppermute only.
A program may use at most 192 MiB of HBM per device.

v0:
```python
import jax
import jax.numpy as jnp
from jax import lax
from jax.sharding import PartitionSpec as P


def local(inverse_slabs, potential_noise, electrode_volts, labels, profile):
    kind_ids = jnp.arange(electrode_volts.shape[1], dtype=jnp.int32)
    onehot = (labels[None, :] == kind_ids[:, None]).astype(jnp.float32)
    potential = (
        jnp.dot(electrode_volts, onehot, precision=lax.Precision.HIGHEST)
        + potential_noise.astype(jnp.float32)
    ).astype(jnp.bfloat16)
    panels = inverse_slabs.shape[0]
    owned_rows = []
    for number in range(panels):
        slab_piece = lax.all_gather(inverse_slabs[number], "wide", axis=0, tiled=True)
        product_block = lax.dot_general(
            slab_piece,
            potential,
            (((slab_piece.ndim - 1,), (1,)), ((), ())),
            preferred_element_type=jnp.float32,
        )
        owned_rows.append(
            lax.psum_scatter(product_block, ("narrow", "sub"), scatter_dimension=0, tiled=True)
        )
    charges = jnp.stack(owned_rows)
    charge_total, weight_sum = lax.psum(
        (jnp.sum(charges, axis=(0, 1)), jnp.sum(profile)), ("narrow", "sub")
    )
    return charges - profile[:, :, None] * (charge_total / weight_sum)[None, None, :]


def solution(mesh):
    return jax.shard_map(
        local,
        mesh=mesh,
        in_specs=(
            P(None, "wide", ("narrow", "sub")),
            P(("grp", "wide"), ("narrow", "sub")),
            P(("grp", "wide"), None),
            P(("narrow", "sub")),
            P(None, ("narrow", "sub")),
        ),
        out_specs=P(None, ("narrow", "sub"), ("grp", "wide")),
        check_vma=False,
    )
```

profile of v0, /device:TPU:3, one launch (start us, length us, event | category | flops | bytes accessed | tf_op | source)
XLA Modules:
  0.0 1108.6 jit_solution(2313723613728020214)
XLA Ops:
  6.5 10.6 fusion.15
  17.2 0.0 all-gather.5.cloned.1.call-update
  17.2 0.0 all-gather.7.cloned.1.call-start
  17.2 0.7 all-gather.7.cloned.1.call-update
  17.9 0.0 reduce-scatter.7.cloned.1.call-start
  18.0 0.1 copy-done.2
  18.1 7.9 fusion.1
  26.0 508.7 %all-gather.5.cloned.1.call-done = bf16[1,384,40000]{2,1,0:T(8,128)(2,1)} async-done(((bf16[1,96,40000]{2,1,0:T(8,128)(2,1)}), bf16[1,384,40000]{2,1,0:T(8,128)(2,1)}) %all-gather.5.cloned.1.call-update) | async-done | bytes 30720016 | tf_op jit(solution)/shard_map/all_gather | solution.py:17
  534.8 18.9 %fusion.6 = f32[384,64]{0,1:T(8,128)S(1)} fusion(bf16[64,40000]{1,0:T(8,128)(2,1)} %fusion.1, bf16[1,384,40000]{2,1,0:T(8,128)(2,1)} %all-gather.5.cloned.1.call-done), kind=kOutput, calls=%fused_computation.7 | convolution fusion | flops 1966080000 | bytes 35938304 | tf_op jit(solution)/shard_map/dot_general | solution.py:18
  553.6 0.8 copy.6
  554.5 0.0 reduce-scatter.9.cloned.1.call-start
  554.5 496.0 %all-gather.7.cloned.1.call-done = bf16[1,384,40000]{2,1,0:T(8,128)(2,1)} async-done(((bf16[1,96,40000]{2,1,0:T(8,128)(2,1)}), bf16[1,384,40000]{2,1,0:T(8,128)(2,1)}) %all-gather.7.cloned.1.call-update) | async-done | bytes 30720016 | tf_op jit(solution)/shard_map/all_gather | solution.py:17
  1050.5 15.6 %fusion.9 = f32[384,64]{0,1:T(8,128)S(1)} fusion(bf16[64,40000]{1,0:T(8,128)(2,1)} %fusion.1, bf16[1,384,40000]{2,1,0:T(8,128)(2,1)} %all-gather.7.cloned.1.call-done), kind=kOutput, calls=%fused_computation.8 | convolution fusion | flops 1966080000 | bytes 35938304 | tf_op jit(solution)/shard_map/dot_general | solution.py:18
  1066.1 0.8 copy.8
  1066.9 0.6 reduce_sum.29
  1067.5 2.0 reduce-scatter.7.cloned.1.call-done
  1069.6 0.8 reduce_sum.26
  1070.4 21.3 %reduce-scatter.9.cloned.1.call-done = f32[96,64]{1,0:T(8,128)} async-done(((f32[384,64]{1,0:T(8,128)}), f32[96,64]{1,0:T(8,128)}) %reduce-scatter.9.cloned.1.call-update) | async-done | bytes 24592
  1091.7 0.8 reduce_sum.27
  1092.5 6.4 all-reduce
  1098.9 0.6 broadcast_divide_fusion
  1099.5 0.9 copy.7
  1100.4 0.9 copy.9
  1101.3 0.7 maximum_subtract_fusion
  (11 shorter events, 0.1 us)
Async XLA Ops:
  6.5 11.5 %copy-start = (f32[64,2]{0,1:T(2,128)S(1)}, f32[64,2]{0,1:T(2,128)}, u32[]{:S(2)}) copy-start(f32[64,2]{0,1:T(2,128)} %param.7) | copy-start | bytes 1540
  6.5 528.2 %all-gather.5.cloned.1.call-start = ((), (), s32[]{:S(2)}) async-start(), calls=%async_computation.2 | async-start | bytes 38461440 | tf_op jit(solution)/shard_map/all_gather | solution.py:17
  17.2 0.9 copy-start.2
  17.2 1033.3 %all-gather.7.cloned.1.call-start = ((), (), s32[]{:S(2)}) async-start(), calls=%async_computation.3 | async-start | bytes 38461440 | tf_op jit(solution)/shard_map/all_gather | solution.py:17
  17.9 1051.6 %reduce-scatter.7.cloned.1.call-start = ((), (), s32[]{:S(2)}) async-start(), calls=%async_computation.4 | async-start | bytes 245760
  554.5 512.5 %copy-start.3 = (f32[2,96]{1,0:T(2,128)S(1)}, f32[2,96]{1,0:T(2,128)}, u32[]{:S(2)}) copy-start(f32[2,96]{1,0:T(2,128)} %param.9) | copy-start | bytes 2308
  554.5 537.2 %reduce-scatter.9.cloned.1.call-start = ((), (), s32[]{:S(2)}) async-start(), calls=%async_computation.5 | async-start | bytes 245760
  1050.5 51.5 %copy-start.1 = (f32[64,2]{0,1:T(2,128)S(1)}, f32[64,2]{0,1:T(2,128)}, u32[]{:S(2)}) copy-start(f32[64,2]{0,1:T(2,128)} %param.7) | copy-start | bytes 1540
Sparse Core Ops, SparseCore 0:
  17.3 517.3 all-gather.4
  536.3 514.1 all-gather.6
  1053.0 16.5 reduce-scatter.6
  1071.9 19.7 reduce-scatter.8
where the time goes:
time: 1110 us
  waiting for transfers between devices  1030 us (93%)
  matrix products  42.3 us (4%)
  local copies, waits for them, and re-layouts  14.1 us (1%)
  between operations  13.2 us (1%)
    all_gather x2, waiting for transfers between devices, local(): lax.all_gather(inverse_slabs[number], 'wide', axis=0, tiled=True)  1000 us
    dot_general x2, matrix products, local(): lax.dot_general(slab_piece, potential, (((slab_piece.ndim - 1,), (1,)), (...  34.4 us
    unnamed x6, waiting for transfers between devices  24.1 us
  transfers between devices with their start and end apart: 4, of which 4 were waited for; matrix products, arithmetic and copies ran while one was open for 4% of the time, Pallas kernels for 0%

commit v1 on v0

v1 whole, which is shorter than its diff:
```python
import jax
import jax.numpy as jnp
from jax import lax
from jax.sharding import PartitionSpec as P

SITES = ("narrow", "sub")
ALL = ("wide", "narrow", "sub")


def dot_t(a, b):
    return lax.dot_general(a, b, (((1,), (1,)), ((), ())), preferred_element_type=jnp.float32)


def potential_of(noise, volts, labels):
    value = volts[:, 0:1]
    for kind in range(1, volts.shape[1]):
        value = jnp.where(labels[None, :] == kind, volts[:, kind:kind + 1], value)
    return (value + noise.astype(jnp.float32)).astype(jnp.bfloat16)


def finish(charges, total, weight_sum, profile):
    return charges - profile[:, :, None] * (total / weight_sum)[None, None, :]


def gather_plan(slab, noise, volts, labels, profile, sizes):
    wide, owners = sizes
    panels, rows, _ = slab.shape
    frames = noise.shape[0]
    pot = lax.all_gather(potential_of(noise, volts, labels), "wide", axis=0, tiled=True)
    part = dot_t(slab.reshape(panels * rows, -1), pot).reshape(panels, rows, wide, frames)
    mine = lax.all_to_all(part, "wide", 2, 1, tiled=True).reshape(panels, wide * rows, frames)
    charges = lax.psum_scatter(mine, SITES, scatter_dimension=1, tiled=True)
    total, weight_sum = lax.psum((jnp.sum(charges, axis=(0, 1)), jnp.sum(profile)), SITES)
    return finish(charges, total, weight_sum, profile)


def line_plan(slab, noise, volts, labels, profile, sizes):
    wide, owners = sizes
    panels, rows, sites = slab.shape
    frames = noise.shape[0]
    nrows = panels * rows
    part_rows = nrows // 3
    third = sites // 3 // 128 * 128
    cuts = (0, third, 2 * third, sites)
    z = lax.axis_index("wide")
    k = lax.axis_index(SITES)
    slab = slab.reshape(nrows, sites)
    cut = [slab[:, cuts[s]:cuts[s + 1]] for s in range(3)]

    def after(x, *others):
        return lax.optimization_barrier((x,) + others)[0]

    def potential_at(s, source):
        return potential_of(source[:, cuts[s]:cuts[s + 1]], volts, labels[cuts[s]:cuts[s + 1]])

    def send(x, pairs):
        return lax.ppermute(x, "wide", pairs)

    own0 = potential_at(0, noise)
    own1 = potential_at(1, after(noise, own0))
    own2 = potential_at(2, after(noise, own1))
    spare = [slab[part_rows * i:part_rows * (i + 1), cuts[2]:] for i in range(3)]
    ends_in = [(0, 1), (3, 2)]
    across = [(1, 2), (2, 1)]
    right = [(0, 1), (1, 2), (2, 3)]
    left = [(3, 2), (2, 1), (1, 0)]
    f1a_r, f1a_l = send(own0, right), send(own0, left)
    f1b_r, f1b_l = send(own1, right), send(own1, left)
    f2a_r, f2a_l = send(f1a_r, right[1:]), send(f1a_l, left[1:])
    g0 = send(after(own2, f1a_r, f1a_l), ends_in)
    f2b_r, f2b_l = send(f1b_r, right[1:]), send(f1b_l, left[1:])
    h1 = send(after(spare[0], f1b_r, f1b_l), ends_in)
    f3a_r, f3a_l = send(f2a_r, right[2:]), send(f2a_l, left[2:])
    g1 = send(after(own2, f2a_r, f2a_l), across)
    h2 = send(after(spare[1], f2a_r, f2a_l), ends_in)
    f3b_r, f3b_l = send(f2b_r, right[2:]), send(f2b_l, left[2:])
    g2 = send(after(g0, f2b_r, f2b_l), across)
    h3 = send(after(spare[2], f2b_r, f2b_l), ends_in)
    weight_sum = lax.psum(jnp.sum(after(profile, f1a_r, f1a_l)), SITES)

    own_part = dot_t(cut[0], own0) + dot_t(cut[1], own1) + dot_t(cut[2], own2)
    terms = [
        (z, own_part),
        (z - 1, dot_t(cut[0], f1a_r) + dot_t(cut[1], f1b_r)),
        (z + 1, dot_t(cut[0], f1a_l) + dot_t(cut[1], f1b_l)),
        (z - 2, dot_t(cut[0], f2a_r) + dot_t(cut[1], f2b_r)),
        (z + 2, dot_t(cut[0], f2a_l) + dot_t(cut[1], f2b_l)),
        (jnp.where(z == 0, 3, 0), dot_t(cut[0], f3a_r + f3a_l) + dot_t(cut[1], f3b_r + f3b_l)),
        (jnp.where(z == 1, 0, 3), dot_t(cut[2], g0)),
        (3 - z, dot_t(cut[2], g1)),
        (jnp.where(z == 1, 3, 0), dot_t(cut[2], g2)),
    ]
    brought = jnp.concatenate([h1, h2, h3], axis=0)
    extra_terms = [
        (z, dot_t(brought, own2)),
        (3 - z, dot_t(brought, g1)),
        (jnp.where(z == 1, 3, 0), dot_t(brought, g2)),
    ]

    def block_of(b):
        mine = sum(jnp.where(b == at, x, 0.0) for at, x in terms)
        extra = sum(jnp.where(b == at, x, 0.0) for at, x in extra_terms)
        return jnp.concatenate([mine, extra], axis=0)

    summed = block_of(k)
    for turn in range(1, owners):
        summed += lax.ppermute(block_of(k ^ turn), SITES, [(i, i ^ turn) for i in range(owners)])
    frame_sum = jnp.sum(summed, axis=0)
    flip = [(a * owners + b, b * owners + a) for a in range(wide) for b in range(owners)]
    flip_end = [(a * owners + b, b * owners + e) for a, e in ((1, 0), (2, 3)) for b in range(owners)]
    charges = lax.ppermute(summed[:nrows], ALL, flip) + lax.ppermute(summed[nrows:], ALL, flip_end)
    total = 0.0
    for turn in range(owners):
        pairs = [(a * owners + b, b * owners + (a ^ turn)) for a in range(wide) for b in range(owners)]
        total += lax.ppermute(frame_sum, ALL, pairs)
    return finish(charges.reshape(panels, rows, frames), total, weight_sum, profile)


def solution(mesh):
    wide = mesh.shape["wide"]
    owners = mesh.shape["narrow"] * mesh.shape["sub"]
    plan = line_plan if wide == owners == 4 else gather_plan

    def local(slab, noise, volts, labels, profile):
        return plan(slab, noise, volts, labels, profile, (wide, owners))

    return jax.shard_map(
        local,
        mesh=mesh,
        in_specs=(
            P(None, "wide", ("narrow", "sub")),
            P(("grp", "wide"), ("narrow", "sub")),
            P(("grp", "wide"), None),
            P(("narrow", "sub")),
            P(None, ("narrow", "sub")),
        ),
        out_specs=P(None, ("narrow", "sub"), ("grp", "wide")),
        check_vma=False,
    )
```

time: 1110 us -> 326 us (0.29)
  waiting for transfers between devices: 1030 us -> 179 us
  starting transfers between devices: 0.12 us -> 57.6 us
  matrix products: 42.3 us -> 60.8 us
  between operations: 13.2 us -> 0.58 us
    all_gather x2 -> x0, waiting for transfers between devices: 1000 us -> none  [local(): lax.all_gather(inverse_slabs[number], 'wide', axis=0, tiled=True)]
    ppermute x0 -> x27, waiting for transfers between devices: none -> 179 us  [the longest x18 171 us: send(): return lax.ppermute(x, 'wide', pairs)]
    ppermute x0 -> x27, starting transfers between devices: none -> 57.6 us  [the longest x18 37.4 us: send(): return lax.ppermute(x, 'wide', pairs)]
    unnamed x6 -> x0, waiting for transfers between devices: 24.1 us -> none
    dot_general x3 -> x19, matrix products: 42.3 us -> 60.8 us  [dot_t(): lax.dot_general(a, b, (((1,), (1,)), ((), ())), preferred_element_type=jn...]
  transfers between devices with their start and end apart: 4 -> 27, of which waited for: 4 -> 11; matrix products, arithmetic and copies ran while one was open for 4% -> 21% of each run, Pallas kernels for 0% -> 0%
where the time goes in v1:
time: 326 us; the launch traced here: 324 us
  waiting for transfers between devices  179 us (55%)
  matrix products  60.8 us (19%)
  starting transfers between devices  57.6 us (18%)
  other arithmetic  12.6 us (4%)
  blocking collectives  7.49 us (2%)
  local copies, waits for them, and re-layouts  6.08 us (2%)
    ppermute x18, waiting for transfers between devices, send(): return lax.ppermute(x, 'wide', pairs)  171 us
    dot_general x19, matrix products, dot_t(): lax.dot_general(a, b, (((1,), (1,)), ((), ())), preferred_element_type=jn...  60.8 us
    ppermute x18, starting transfers between devices, send(): return lax.ppermute(x, 'wide', pairs)  37.4 us
    ppermute x4, starting transfers between devices, line_plan(): total += lax.ppermute(frame_sum, ALL, pairs)  9.9 us
    convert_element_type x3, other arithmetic, potential_of(): return (value + noise.astype(jnp.float32)).astype(jnp.bfloat16)  8.26 us
    psum x1, blocking collectives, line_plan(): weight_sum = lax.psum(jnp.sum(after(profile, f1a_r, f1a_l)), SITES)  7.49 us
  transfers between devices with their start and end apart: 27, of which 11 were waited for; matrix products, arithmetic and copies ran while one was open for 21% of the time, Pallas kernels for 0%

profile of v1, /device:TPU:3, one launch (start us, length us, event | category | flops | bytes accessed | tf_op | source)
XLA Modules:
  0.0 324.1 jit_solution(3658006840628794802)
XLA Ops:
  9.2 5.3 %collective-permute-start.1 = (bf16[64,13312]{1,0:T(8,128)(2,1)}, bf16[64,13312]{1,0:T(8,128)(2,1)}, u32[]{:S(2)}, u32[]{:S(2)}) collective-permute-start(bf16[64,13312]{1,0:T(8,128)(2,1)} %add_convert_fusion.1), channel_id=1, source_target_pairs={{0,4},{4,8},{8,12},{1,5},{5,9},{9,13},{2,6},{6,10},{10,14},{3,7},{... | collective-permute-start | bytes 5111816 | tf_op jit(solution)/shard_map/ppermute | solution.py:57
  15.8 5.2 %collective-permute-start = (bf16[64,13312]{1,0:T(8,128)(2,1)}, bf16[64,13312]{1,0:T(8,128)(2,1)}, u32[]{:S(2)}, u32[]{:S(2)}) collective-permute-start(bf16[64,13312]{1,0:T(8,128)(2,1)} %add_convert_fusion.2), channel_id=1, source_target_pairs={{0,4},{4,8},{8,12},{1,5},{5,9},{9,13},{2,6},{6,10},{10,14},{3,7},{... | collective-permute-start | bytes 5111816 | tf_op jit(solution)/shard_map/ppermute | solution.py:57
  21.8 4.6 %fusion.61 = (bf16[64,13376]{1,0:T(8,128)(2,1)S(1)}, bf16[64,13376]{1,0:T(8,128)(2,1)}, bf16[64,13376]{1,0:T(8,128)(2,1)}) fusion(bf16[192,40000]{1,0:T(8,128)(2,1)} %bitcast.35), kind=kLoop, calls=%fused_computation.69 | loop fusion | bytes 10272768 | tf_op jit(solution)/shard_map/slice | solution.py:62
  28.4 4.2 %fusion.6 = f32[64,192]{1,0:T(8,128)S(1)} fusion(bf16[64,13376]{1,0:T(8,128)(2,1)S(1)} %add_convert_fusion, bf16[192,40000]{1,0:T(8,128)(2,1)} %bitcast.36), kind=kOutput, calls=%fused_computation.9 | convolution fusion | flops 328728576 | bytes 6922240 | tf_op jit(solution)/shard_map/dot_general | solution.py:11
  32.6 4.7 %fusion.18 = f32[64,192]{1,0:T(8,128)S(1)} fusion(bf16[64,13312]{1,0:T(8,128)(2,1)} %add_convert_fusion.1, bf16[192,40000]{1,0:T(8,128)(2,1)} %bitcast.37), kind=kOutput, calls=%fused_computation.21 | convolution fusion | flops 327155712 | bytes 6864896 | tf_op jit(solution)/shard_map/dot_general | solution.py:11
  37.4 4.7 %fusion.37 = f32[64,192]{1,0:T(8,128)S(1)} fusion(f32[64,192]{1,0:T(8,128)S(1)} %fusion.6, f32[64,192]{1,0:T(8,128)S(1)} %fusion.18, bf16[64,13312]{1,0:T(8,128)(2,1)} %add_convert_fusion.2, bf16[192,40000]{1,0:T(8,128)(2,1)} %bitcast.38), kind=kOutput, calls=%fused_computation.38 | convolution fusion | flops 327180288 | bytes 6963200 | tf_op jit(solution)/shard_map/dot_general | solution.py:11
  42.1 42.6 %collective-permute-done.2 = bf16[64,13312]{1,0:T(8,128)(2,1)} collective-permute-done((bf16[64,13312]{1,0:T(8,128)(2,1)}, bf16[64,13312]{1,0:T(8,128)(2,1)}, u32[]{:S(2)}, u32[]{:S(2)}) %collective-permute-start.2) | collective-permute-done | bytes 1703968 | tf_op jit(solution)/shard_map/ppermute | solution.py:57
  86.2 7.5 %psum.7 = f32[]{:T(128)} all-reduce(f32[]{:T(128)} %reduce_sum.19), channel_id=1, replica_groups=mesh['grp'=2,'wide'=4,'narrow'=2,'sub'=2] {'narrow','sub'}, use_global_device_ids=true, to_apply=%region_2.3 | all-reduce | flops 1 | bytes 8 | tf_op jit(solution)/shard_map/psum | solution.py:79
  93.7 4.2 %collective-permute-start.12 = (bf16[64,13376]{1,0:T(8,128)(2,1)S(1)}, bf16[64,13376]{1,0:T(8,128)(2,1)S(1)}, u32[]{:S(2)}, u32[]{:S(2)}) collective-permute-start(bf16[64,13376]{1,0:T(8,128)(2,1)S(1)} %add_convert_fusion), channel_id=1, source_target_pairs={{0,4},{12,8},{1,5},{13,9},{2,6},{14,10},{3,7},{15,11},{16,20},{28,... | collective-permute-start | bytes 5136392 | tf_op jit(solution)/shard_map/ppermute | solution.py:57
  103.2 4.9 %fusion.14 = f32[64,192]{1,0:T(8,128)S(1)} fusion(bf16[64,13312]{1,0:T(8,128)(2,1)} %collective-permute-done.3, bf16[192,40000]{1,0:T(8,128)(2,1)} %bitcast.39), kind=kOutput, calls=%fused_computation.17 | convolution fusion | flops 327155712 | bytes 6864896 | tf_op jit(solution)/shard_map/dot_general | solution.py:11
  108.0 4.9 %fusion.16 = f32[64,192]{1,0:T(8,128)S(1)} fusion(bf16[64,13312]{1,0:T(8,128)(2,1)} %collective-permute-done.1, bf16[192,40000]{1,0:T(8,128)(2,1)} %bitcast.40), kind=kOutput, calls=%fused_computation.19 | convolution fusion | flops 327155712 | bytes 6864896 | tf_op jit(solution)/shard_map/dot_general | solution.py:11
  112.9 4.9 %fusion.43 = f32[64,192]{1,0:T(8,128)S(1)} fusion(f32[64,192]{1,0:T(8,128)S(1)} %fusion.14, bf16[64,13312]{1,0:T(8,128)(2,1)} %collective-permute-done.2, bf16[192,40000]{1,0:T(8,128)(2,1)} %bitcast.41), kind=kOutput, calls=%fused_computation.40 | convolution fusion | flops 327168000 | bytes 6914048 | tf_op jit(solution)/shard_map/dot_general | solution.py:11
  117.8 4.9 %fusion.40 = f32[64,192]{1,0:T(8,128)S(1)} fusion(f32[64,192]{1,0:T(8,128)S(1)} %fusion.16, bf16[64,13312]{1,0:T(8,128)(2,1)} %collective-permute-done, bf16[192,40000]{1,0:T(8,128)(2,1)} %bitcast.42), kind=kOutput, calls=%fused_computation.39 | convolution fusion | flops 327168000 | bytes 6914048 | tf_op jit(solution)/shard_map/dot_general | solution.py:11
  122.7 51.6 %collective-permute-done.6 = bf16[64,13312]{1,0:T(8,128)(2,1)} collective-permute-done((bf16[64,13312]{1,0:T(8,128)(2,1)}, bf16[64,13312]{1,0:T(8,128)(2,1)}, u32[]{:S(2)}, u32[]{:S(2)}) %collective-permute-start.6) | collective-permute-done | bytes 1703968 | tf_op jit(solution)/shard_map/ppermute | solution.py:57
  187.3 3.2 fusion.46
  191.8 19.2 %collective-permute-done.15 = bf16[64,13376]{1,0:T(8,128)(2,1)S(1)} collective-permute-done((bf16[64,13376]{1,0:T(8,128)(2,1)S(1)}, bf16[64,13376]{1,0:T(8,128)(2,1)S(1)}, u32[]{:S(2)}, u32[]{:S(2)}) %collective-permute-start.15) | collective-permute-done | bytes 1712160 | tf_op jit(solution)/shard_map/ppermute | solution.py:57
  216.9 4.0 %collective-permute-start.17 = (bf16[64,13376]{1,0:T(8,128)(2,1)S(1)}, bf16[64,13376]{1,0:T(8,128)(2,1)S(1)}, u32[]{:S(2)}, u32[]{:S(2)}) collective-permute-start(bf16[64,13376]{1,0:T(8,128)(2,1)S(1)} %get-tuple-element.21), channel_id=1, source_target_pairs={{0,4},{12,8},{1,5},{13,9},{2,6},{14,10},{3,7},{15,11},{16,20},{28,... | collective-permute-start | bytes 5136392 | tf_op jit(solution)/shard_map/ppermute | solution.py:57
  220.9 3.7 %fusion.8 = f32[64,192]{1,0:T(8,128)S(1)} fusion(bf16[192,40000]{1,0:T(8,128)(2,1)S(1)} %bitcast.50, bf16[64,13312]{1,0:T(8,128)(2,1)} %collective-permute-done.10, bf16[64,13312]{1,0:T(8,128)(2,1)} %collective-permute-done.11), kind=kOutput, calls=%fused_computation.11 | convolution fusion | flops 328007680 | bytes 8568832 | tf_op jit(solution)/shard_map/dot_general | solution.py:11
  224.6 28.1 %collective-permute-done.9 = bf16[64,13312]{1,0:T(8,128)(2,1)} collective-permute-done((bf16[64,13312]{1,0:T(8,128)(2,1)}, bf16[64,13312]{1,0:T(8,128)(2,1)}, u32[]{:S(2)}, u32[]{:S(2)}) %collective-permute-start.9) | collective-permute-done | bytes 1703968 | tf_op jit(solution)/shard_map/ppermute | solution.py:57
  253.4 3.7 %fusion.52 = f32[64,192]{1,0:T(8,128)S(1)} fusion(f32[64,192]{1,0:T(8,128)S(1)} %fusion.8, bf16[192,40000]{1,0:T(8,128)(2,1)S(1)} %bitcast.51, bf16[64,13312]{1,0:T(8,128)(2,1)} %collective-permute-done.8, bf16[64,13312]{1,0:T(8,128)(2,1)} %collective-permute-done.9), kind=kOutput, calls=%fused_computation.43 | convolution fusion | flops 328019968 | bytes 8634368 | tf_op jit(solution)/shard_map/dot_general | solution.py:11
  257.4 27.4 %collective-permute-done.17 = bf16[64,13376]{1,0:T(8,128)(2,1)S(1)} collective-permute-done((bf16[64,13376]{1,0:T(8,128)(2,1)S(1)}, bf16[64,13376]{1,0:T(8,128)(2,1)S(1)}, u32[]{:S(2)}, u32[]{:S(2)}) %collective-permute-start.17) | collective-permute-done | bytes 1712160 | tf_op jit(solution)/shard_map/ppermute | solution.py:57
  303.8 4.1 %collective-permute-start.25 = (f32[64]{0:T(128)S(1)}, f32[64]{0:T(128)S(1)}, u32[]{:S(2)}, u32[]{:S(2)}) collective-permute-start(f32[64]{0:T(128)S(1)} %get-tuple-element.23), channel_id=1, source_target_pairs={{0,2},{1,6},{2,10},{3,14},{4,3},{5,7},{6,11},{7,15},{8,0},{9,4},{1... | collective-permute-start | bytes 776 | tf_op jit(solution)/shard_map/ppermute | solution.py:115
  309.9 3.6 %collective-permute-start.23 = (f32[64]{0:T(128)S(1)}, f32[64]{0:T(128)S(1)}, u32[]{:S(2)}, u32[]{:S(2)}) collective-permute-start(f32[64]{0:T(128)S(1)} %get-tuple-element.23), channel_id=1, source_target_pairs={{0,0},{1,4},{2,8},{3,12},{4,1},{5,5},{6,9},{7,13},{8,2},{9,6},{10,... | collective-permute-start | bytes 776 | tf_op jit(solution)/shard_map/ppermute | solution.py:115
  314.9 4.7 %collective-permute-start.21 = (f32[192,64]{0,1:T(8,128)S(1)}, f32[192,64]{0,1:T(8,128)S(1)}, u32[]{:S(2)}, u32[]{:S(2)}) collective-permute-start(f32[192,64]{0,1:T(8,128)S(1)} %get-tuple-element.35), channel_id=1, source_target_pairs={{0,0},{1,4},{2,8},{3,12},{4,1},{5,5},{6,9},{7,13},{8,2},{9,6},{10,... | collective-permute-start | bytes 147464 | tf_op jit(solution)/shard_map/ppermute | solution.py:111
  (89 shorter events, 67.9 us)
Async XLA Ops:
  7.9 90.0 %collective-permute-start.3 = (bf16[64,13312]{1,0:T(8,128)(2,1)}, bf16[64,13312]{1,0:T(8,128)(2,1)}, u32[]{:S(2)}, u32[]{:S(2)}) collective-permute-start(bf16[64,13312]{1,0:T(8,128)(2,1)} %add_convert_fusion.1), channel_id=1, source_target_pairs={{12,8},{8,4},{4,0},{13,9},{9,5},{5,1},{14,10},{10,6},{6,2},{15,11}... | collective-permute-start | bytes 5111816 | tf_op jit(solution)/shard_map/ppermute | solution.py:57
  9.2 88.7 %collective-permute-start.1 = (bf16[64,13312]{1,0:T(8,128)(2,1)}, bf16[64,13312]{1,0:T(8,128)(2,1)}, u32[]{:S(2)}, u32[]{:S(2)}) collective-permute-start(bf16[64,13312]{1,0:T(8,128)(2,1)} %add_convert_fusion.1), channel_id=1, source_target_pairs={{0,4},{4,8},{8,12},{1,5},{5,9},{9,13},{2,6},{6,10},{10,14},{3,7},{... | collective-permute-start | bytes 5111816 | tf_op jit(solution)/shard_map/ppermute | solution.py:57
  14.5 70.2 %collective-permute-start.2 = (bf16[64,13312]{1,0:T(8,128)(2,1)}, bf16[64,13312]{1,0:T(8,128)(2,1)}, u32[]{:S(2)}, u32[]{:S(2)}) collective-permute-start(bf16[64,13312]{1,0:T(8,128)(2,1)} %add_convert_fusion.2), channel_id=1, source_target_pairs={{12,8},{8,4},{4,0},{13,9},{9,5},{5,1},{14,10},{10,6},{6,2},{15,11}... | collective-permute-start | bytes 5111816 | tf_op jit(solution)/shard_map/ppermute | solution.py:57
  15.8 69.8 %collective-permute-start = (bf16[64,13312]{1,0:T(8,128)(2,1)}, bf16[64,13312]{1,0:T(8,128)(2,1)}, u32[]{:S(2)}, u32[]{:S(2)}) collective-permute-start(bf16[64,13312]{1,0:T(8,128)(2,1)} %add_convert_fusion.2), channel_id=1, source_target_pairs={{0,4},{4,8},{8,12},{1,5},{5,9},{9,13},{2,6},{6,10},{10,14},{3,7},{... | collective-permute-start | bytes 5111816 | tf_op jit(solution)/shard_map/ppermute | solution.py:57
  93.7 96.8 %collective-permute-start.12 = (bf16[64,13376]{1,0:T(8,128)(2,1)S(1)}, bf16[64,13376]{1,0:T(8,128)(2,1)S(1)}, u32[]{:S(2)}, u32[]{:S(2)}) collective-permute-start(bf16[64,13376]{1,0:T(8,128)(2,1)S(1)} %add_convert_fusion), channel_id=1, source_target_pairs={{0,4},{12,8},{1,5},{13,9},{2,6},{14,10},{3,7},{15,11},{16,20},{28,... | collective-permute-start | bytes 5136392 | tf_op jit(solution)/shard_map/ppermute | solution.py:57
  97.9 78.0 %collective-permute-start.7 = (bf16[64,13312]{1,0:T(8,128)(2,1)}, bf16[64,13312]{1,0:T(8,128)(2,1)S(1)}, u32[]{:S(2)}, u32[]{:S(2)}) collective-permute-start(bf16[64,13312]{1,0:T(8,128)(2,1)} %collective-permute-done.3), channel_id=1, source_target_pairs={{8,4},{4,0},{9,5},{5,1},{10,6},{6,2},{11,7},{7,3},{24,20},{20,16},... | collective-permute-start | bytes 5111816 | tf_op jit(solution)/shard_map/ppermute | solution.py:57
  99.2 76.7 %collective-permute-start.5 = (bf16[64,13312]{1,0:T(8,128)(2,1)}, bf16[64,13312]{1,0:T(8,128)(2,1)S(1)}, u32[]{:S(2)}, u32[]{:S(2)}) collective-permute-start(bf16[64,13312]{1,0:T(8,128)(2,1)} %collective-permute-done.1), channel_id=1, source_target_pairs={{4,8},{8,12},{5,9},{9,13},{6,10},{10,14},{7,11},{11,15},{20,24},{2... | collective-permute-start | bytes 5111816 | tf_op jit(solution)/shard_map/ppermute | solution.py:57
  100.0 74.3 %collective-permute-start.6 = (bf16[64,13312]{1,0:T(8,128)(2,1)}, bf16[64,13312]{1,0:T(8,128)(2,1)}, u32[]{:S(2)}, u32[]{:S(2)}) collective-permute-start(bf16[64,13312]{1,0:T(8,128)(2,1)} %collective-permute-done.2), channel_id=1, source_target_pairs={{8,4},{4,0},{9,5},{5,1},{10,6},{6,2},{11,7},{7,3},{24,20},{20,16},... | collective-permute-start | bytes 5111816 | tf_op jit(solution)/shard_map/ppermute | solution.py:57
  101.3 74.6 %collective-permute-start.4 = (bf16[64,13312]{1,0:T(8,128)(2,1)}, bf16[64,13312]{1,0:T(8,128)(2,1)}, u32[]{:S(2)}, u32[]{:S(2)}) collective-permute-start(bf16[64,13312]{1,0:T(8,128)(2,1)} %collective-permute-done), channel_id=1, source_target_pairs={{4,8},{8,12},{5,9},{9,13},{6,10},{10,14},{7,11},{11,15},{20,24},{2... | collective-permute-start | bytes 5111816 | tf_op jit(solution)/shard_map/ppermute | solution.py:57
  174.3 36.7 %collective-permute-start.15 = (bf16[64,13376]{1,0:T(8,128)(2,1)S(1)}, bf16[64,13376]{1,0:T(8,128)(2,1)S(1)}, u32[]{:S(2)}, u32[]{:S(2)}) collective-permute-start(bf16[64,13376]{1,0:T(8,128)(2,1)S(1)} %copy-done.1), channel_id=1, source_target_pairs={{0,4},{12,8},{1,5},{13,9},{2,6},{14,10},{3,7},{15,11},{16,20},{28,... | collective-permute-start | bytes 5136392 | tf_op jit(solution)/shard_map/ppermute | solution.py:57
  176.0 81.2 %collective-permute-start.16 = (bf16[64,13376]{1,0:T(8,128)(2,1)S(1)}, bf16[64,13376]{1,0:T(8,128)(2,1)S(1)}, u32[]{:S(2)}, u32[]{:S(2)}) collective-permute-start(bf16[64,13376]{1,0:T(8,128)(2,1)S(1)} %copy-done), channel_id=1, source_target_pairs={{0,4},{12,8},{1,5},{13,9},{2,6},{14,10},{3,7},{15,11},{16,20},{28,... | collective-permute-start | bytes 5136392 | tf_op jit(solution)/shard_map/ppermute | solution.py:57
  177.4 38.8 %collective-permute-start.11 = (bf16[64,13312]{1,0:T(8,128)(2,1)S(1)}, bf16[64,13312]{1,0:T(8,128)(2,1)}, u32[]{:S(2)}, u32[]{:S(2)}) collective-permute-start(bf16[64,13312]{1,0:T(8,128)(2,1)S(1)} %collective-permute-done.7), channel_id=1, source_target_pairs={{4,0},{5,1},{6,2},{7,3},{20,16},{21,17},{22,18},{23,19}} | collective-permute-start | bytes 5111816 | tf_op jit(solution)/shard_map/ppermute | solution.py:57
  178.7 38.3 %collective-permute-start.10 = (bf16[64,13312]{1,0:T(8,128)(2,1)S(1)}, bf16[64,13312]{1,0:T(8,128)(2,1)}, u32[]{:S(2)}, u32[]{:S(2)}) collective-permute-start(bf16[64,13312]{1,0:T(8,128)(2,1)S(1)} %collective-permute-done.5), channel_id=1, source_target_pairs={{8,12},{9,13},{10,14},{11,15},{24,28},{25,29},{26,30},{27,31}} | collective-permute-start | bytes 5111816 | tf_op jit(solution)/shard_map/ppermute | solution.py:57
  190.5 62.2 %collective-permute-start.9 = (bf16[64,13312]{1,0:T(8,128)(2,1)}, bf16[64,13312]{1,0:T(8,128)(2,1)}, u32[]{:S(2)}, u32[]{:S(2)}) collective-permute-start(bf16[64,13312]{1,0:T(8,128)(2,1)} %collective-permute-done.6), channel_id=1, source_target_pairs={{4,0},{5,1},{6,2},{7,3},{20,16},{21,17},{22,18},{23,19}} | collective-permute-start | bytes 5111816 | tf_op jit(solution)/shard_map/ppermute | solution.py:57
  211.0 42.4 %collective-permute-start.8 = (bf16[64,13312]{1,0:T(8,128)(2,1)}, bf16[64,13312]{1,0:T(8,128)(2,1)}, u32[]{:S(2)}, u32[]{:S(2)}) collective-permute-start(bf16[64,13312]{1,0:T(8,128)(2,1)} %collective-permute-done.4), channel_id=1, source_target_pairs={{8,12},{9,13},{10,14},{11,15},{24,28},{25,29},{26,30},{27,31}} | collective-permute-start | bytes 5111816 | tf_op jit(solution)/shard_map/ppermute | solution.py:57
  216.1 70.6 %collective-permute-start.13 = (bf16[64,13376]{1,0:T(8,128)(2,1)S(1)}, bf16[64,13376]{1,0:T(8,128)(2,1)S(1)}, u32[]{:S(2)}, u32[]{:S(2)}) collective-permute-start(bf16[64,13376]{1,0:T(8,128)(2,1)S(1)} %add_convert_fusion), channel_id=1, source_target_pairs={{4,8},{8,4},{5,9},{9,5},{6,10},{10,6},{7,11},{11,7},{20,24},{24,20... | collective-permute-start | bytes 5136392 | tf_op jit(solution)/shard_map/ppermute | solution.py:57
  216.9 67.8 %collective-permute-start.17 = (bf16[64,13376]{1,0:T(8,128)(2,1)S(1)}, bf16[64,13376]{1,0:T(8,128)(2,1)S(1)}, u32[]{:S(2)}, u32[]{:S(2)}) collective-permute-start(bf16[64,13376]{1,0:T(8,128)(2,1)S(1)} %get-tuple-element.21), channel_id=1, source_target_pairs={{0,4},{12,8},{1,5},{13,9},{2,6},{14,10},{3,7},{15,11},{16,20},{28,... | collective-permute-start | bytes 5136392 | tf_op jit(solution)/shard_map/ppermute | solution.py:57
  252.7 37.6 %collective-permute-start.14 = (bf16[64,13376]{1,0:T(8,128)(2,1)S(1)}, bf16[64,13376]{1,0:T(8,128)(2,1)S(1)}, u32[]{:S(2)}, u32[]{:S(2)}) collective-permute-start(bf16[64,13376]{1,0:T(8,128)(2,1)S(1)} %collective-permute-done.12), channel_id=1, source_target_pairs={{4,8},{8,4},{5,9},{9,5},{6,10},{10,6},{7,11},{11,7},{20,24},{24,20... | collective-permute-start | bytes 5136392 | tf_op jit(solution)/shard_map/ppermute | solution.py:57
  303.6 11.3 %collective-permute-start.26 = (f32[64]{0:T(128)S(1)}, f32[64]{0:T(128)S(1)}, u32[]{:S(2)}, u32[]{:S(2)}) collective-permute-start(f32[64]{0:T(128)S(1)} %get-tuple-element.23), channel_id=1, source_target_pairs={{0,3},{1,7},{2,11},{3,15},{4,2},{5,6},{6,10},{7,14},{8,1},{9,5},{1... | collective-permute-start | bytes 776 | tf_op jit(solution)/shard_map/ppermute | solution.py:115
  303.8 15.8 %collective-permute-start.25 = (f32[64]{0:T(128)S(1)}, f32[64]{0:T(128)S(1)}, u32[]{:S(2)}, u32[]{:S(2)}) collective-permute-start(f32[64]{0:T(128)S(1)} %get-tuple-element.23), channel_id=1, source_target_pairs={{0,2},{1,6},{2,10},{3,14},{4,3},{5,7},{6,11},{7,15},{8,0},{9,4},{1... | collective-permute-start | bytes 776 | tf_op jit(solution)/shard_map/ppermute | solution.py:115
  308.0 11.6 %collective-permute-start.24 = (f32[64]{0:T(128)S(1)}, f32[64]{0:T(128)S(1)}, u32[]{:S(2)}, u32[]{:S(2)}) collective-permute-start(f32[64]{0:T(128)S(1)} %get-tuple-element.23), channel_id=1, source_target_pairs={{0,1},{1,5},{2,9},{3,13},{4,0},{5,4},{6,8},{7,12},{8,3},{9,7},{10,... | collective-permute-start | bytes 776 | tf_op jit(solution)/shard_map/ppermute | solution.py:115
  309.9 9.7 %collective-permute-start.23 = (f32[64]{0:T(128)S(1)}, f32[64]{0:T(128)S(1)}, u32[]{:S(2)}, u32[]{:S(2)}) collective-permute-start(f32[64]{0:T(128)S(1)} %get-tuple-element.23), channel_id=1, source_target_pairs={{0,0},{1,4},{2,8},{3,12},{4,1},{5,5},{6,9},{7,13},{8,2},{9,6},{10,... | collective-permute-start | bytes 776 | tf_op jit(solution)/shard_map/ppermute | solution.py:115
  313.6 7.4 %collective-permute-start.22 = (f32[192,64]{0,1:T(8,128)S(1)}, f32[192,64]{0,1:T(8,128)S(1)}, u32[]{:S(2)}, u32[]{:S(2)}) collective-permute-start(f32[192,64]{0,1:T(8,128)S(1)} %get-tuple-element.34), channel_id=1, source_target_pairs={{4,0},{5,4},{6,8},{7,12},{8,3},{9,7},{10,11},{11,15},{20,16},{21,2... | collective-permute-start | bytes 147464 | tf_op jit(solution)/shard_map/ppermute | solution.py:111
  314.9 8.4 %collective-permute-start.21 = (f32[192,64]{0,1:T(8,128)S(1)}, f32[192,64]{0,1:T(8,128)S(1)}, u32[]{:S(2)}, u32[]{:S(2)}) collective-permute-start(f32[192,64]{0,1:T(8,128)S(1)} %get-tuple-element.35), channel_id=1, source_target_pairs={{0,0},{1,4},{2,8},{3,12},{4,1},{5,5},{6,9},{7,13},{8,2},{9,6},{10,... | collective-permute-start | bytes 147464 | tf_op jit(solution)/shard_map/ppermute | solution.py:111
  (10 other events, 458.9 us)

commit v2 on v1

--- a/solution.py
+++ b/solution.py
@@ -50,47 +50,42 @@
     def after(x, *others):
         return lax.optimization_barrier((x,) + others)[0]
 
-    def potential_at(s, source):
-        return potential_of(source[:, cuts[s]:cuts[s + 1]], volts, labels[cuts[s]:cuts[s + 1]])
-
     def send(x, pairs):
         return lax.ppermute(x, "wide", pairs)
 
-    own0 = potential_at(0, noise)
-    own1 = potential_at(1, after(noise, own0))
-    own2 = potential_at(2, after(noise, own1))
-    spare = [slab[part_rows * i:part_rows * (i + 1), cuts[2]:] for i in range(3)]
+    own01 = potential_of(noise[:, :cuts[2]], volts, labels[:cuts[2]])
+    own2 = potential_of(after(noise, own01)[:, cuts[2]:], volts, labels[cuts[2]:])
+    is_end = (z == 0) | (z == wide - 1)
+    spare1, spare23 = (jnp.where(is_end, x[:, cuts[2]:], 0) for x in (slab[:part_rows], slab[part_rows:]))
     ends_in = [(0, 1), (3, 2)]
     across = [(1, 2), (2, 1)]
     right = [(0, 1), (1, 2), (2, 3)]
     left = [(3, 2), (2, 1), (1, 0)]
-    f1a_r, f1a_l = send(own0, right), send(own0, left)
-    f1b_r, f1b_l = send(own1, right), send(own1, left)
-    f2a_r, f2a_l = send(f1a_r, right[1:]), send(f1a_l, left[1:])
-    g0 = send(after(own2, f1a_r, f1a_l), ends_in)
-    f2b_r, f2b_l = send(f1b_r, right[1:]), send(f1b_l, left[1:])
-    h1 = send(after(spare[0], f1b_r, f1b_l), ends_in)
-    f3a_r, f3a_l = send(f2a_r, right[2:]), send(f2a_l, left[2:])
-    g1 = send(after(own2, f2a_r, f2a_l), across)
-    h2 = send(after(spare[1], f2a_r, f2a_l), ends_in)
-    f3b_r, f3b_l = send(f2b_r, right[2:]), send(f2b_l, left[2:])
-    g2 = send(after(g0, f2b_r, f2b_l), across)
-    h3 = send(after(spare[2], f2b_r, f2b_l), ends_in)
-    weight_sum = lax.psum(jnp.sum(after(profile, f1a_r, f1a_l)), SITES)
+    f1_r, f1_l = send(own01, right), send(own01, left)
+    f1_r, f1_l, own2, spare1 = lax.optimization_barrier((f1_r, f1_l, own2, spare1))
+    f2_r, f2_l = send(f1_r, right[1:]), send(f1_l, left[1:])
+    g0, h1 = send(own2, ends_in), send(spare1, ends_in)
+    f2_r, f2_l, g0, h1, own2, spare23 = lax.optimization_barrier((f2_r, f2_l, g0, h1, own2, spare23))
+    f3_r, f3_l = send(f2_r, right[2:]), send(f2_l, left[2:])
+    g1, g2 = send(own2, across), send(g0, across)
+    h23 = send(spare23, ends_in)
+    f3_r, f3_l, g1, g2, h23 = lax.optimization_barrier((f3_r, f3_l, g1, g2, h23))
 
-    own_part = dot_t(cut[0], own0) + dot_t(cut[1], own1) + dot_t(cut[2], own2)
+    both = slab[:, :cuts[2]]
+    own_part = dot_t(both, own01) + dot_t(cut[2], own2)
+    weight_sum = lax.psum(jnp.sum(profile), SITES)
     terms = [
         (z, own_part),
-        (z - 1, dot_t(cut[0], f1a_r) + dot_t(cut[1], f1b_r)),
-        (z + 1, dot_t(cut[0], f1a_l) + dot_t(cut[1], f1b_l)),
-        (z - 2, dot_t(cut[0], f2a_r) + dot_t(cut[1], f2b_r)),
-        (z + 2, dot_t(cut[0], f2a_l) + dot_t(cut[1], f2b_l)),
-        (jnp.where(z == 0, 3, 0), dot_t(cut[0], f3a_r + f3a_l) + dot_t(cut[1], f3b_r + f3b_l)),
+        (z - 1, dot_t(both, f1_r)),
+        (z + 1, dot_t(both, f1_l)),
+        (z - 2, dot_t(both, f2_r)),
+        (z + 2, dot_t(both, f2_l)),
+        (jnp.where(z == 0, 3, 0), dot_t(both, f3_r + f3_l)),
         (jnp.where(z == 1, 0, 3), dot_t(cut[2], g0)),
         (3 - z, dot_t(cut[2], g1)),
         (jnp.where(z == 1, 3, 0), dot_t(cut[2], g2)),
     ]
-    brought = jnp.concatenate([h1, h2, h3], axis=0)
+    brought = jnp.concatenate([h1, h23], axis=0)
     extra_terms = [
         (z, dot_t(brought, own2)),
         (3 - z, dot_t(brought, g1)),

time: 326 us -> 326 us (level)
  waiting for transfers between devices: 179 us -> 141 us
  matrix products: 60.8 us -> 84.8 us
  starting transfers between devices: 57.6 us -> 65.7 us
    ppermute x18 -> x11, waiting for transfers between devices: 171 us -> 133 us  [send(): return lax.ppermute(x, 'wide', pairs)]
    dot_general x19 -> x13, matrix products: 60.8 us -> 84.8 us  [dot_t(): lax.dot_general(a, b, (((1,), (1,)), ((), ())), preferred_element_type=jn...]
    ppermute x4, starting transfers between devices: 9.9 us -> 20.2 us  [line_plan(): total += lax.ppermute(frame_sum, ALL, pairs)]
    optimization_barrier x0 -> x2, local copies, waits for them, and re-layouts: none -> 8.03 us  [line_plan(): lax.optimization_barrier((f2_r, f2_l, g0, h1, own2, spare23))]
    select_n x0 -> x2, other arithmetic: none -> 5.14 us  [line_plan(): jnp.where(is_end, x[:, cuts[2]:], 0)]
    slice x1 -> x0, local copies, waits for them, and re-layouts: 4.55 us -> none  [line_plan(): slab[part_rows * i:part_rows * (i + 1), cuts[2]:]]
    ppermute x18 -> x11, starting transfers between devices: 37.4 us -> 33.8 us  [send(): return lax.ppermute(x, 'wide', pairs)]
    convert_element_type x3 -> x2, other arithmetic: 8.26 us -> 6.09 us  [potential_of(): return (value + noise.astype(jnp.float32)).astype(jnp.bfloat16)]
  transfers between devices with their start and end apart: 27 -> 20, of which waited for: 11 -> 11; matrix products, arithmetic and copies ran while one was open for 21% -> 21% of each run, Pallas kernels for 0% -> 0%
where the time goes in v2:
time: 326 us; the launch traced here: 325 us
  waiting for transfers between devices  141 us (43%)
  matrix products  84.8 us (26%)
  starting transfers between devices  65.7 us (20%)
  other arithmetic  15.6 us (5%)
  local copies, waits for them, and re-layouts  9.03 us (3%)
  blocking collectives  7.88 us (2%)
    ppermute x11, waiting for transfers between devices, send(): return lax.ppermute(x, 'wide', pairs)  133 us
    dot_general x13, matrix products, dot_t(): lax.dot_general(a, b, (((1,), (1,)), ((), ())), preferred_element_type=jn...  84.8 us
    ppermute x11, starting transfers between devices, send(): return lax.ppermute(x, 'wide', pairs)  33.8 us
    ppermute x4, starting transfers between devices, line_plan(): total += lax.ppermute(frame_sum, ALL, pairs)  20.2 us
    optimization_barrier x2, local copies, waits for them, and re-layouts, line_plan(): lax.optimization_barrier((f2_r, f2_l, g0, h1, own2, spare23))  8.03 us
    psum x1, blocking collectives, line_plan(): weight_sum = lax.psum(jnp.sum(profile), SITES)  7.88 us
  transfers between devices with their start and end apart: 20, of which 11 were waited for; matrix products, arithmetic and copies ran while one was open for 21% of the time, Pallas kernels for 0%

profile of v2, /device:TPU:3, one launch (start us, length us, event | category | flops | bytes accessed | tf_op | source)
XLA Modules:
  0.0 324.5 jit_solution(3520880771420439971)
XLA Ops:
  6.0 5.7 %collective-permute-start = (bf16[64,26624]{1,0:T(8,128)(2,1)S(1)}, bf16[64,26624]{1,0:T(8,128)(2,1)}, u32[]{:S(2)}, u32[]{:S(2)}) collective-permute-start(bf16[64,26624]{1,0:T(8,128)(2,1)S(1)} %add_convert_fusion), channel_id=1, source_target_pairs={{0,4},{4,8},{8,12},{1,5},{5,9},{9,13},{2,6},{6,10},{10,14},{3,7},{... | collective-permute-start | bytes 10223624 | tf_op jit(solution)/shard_map/ppermute | solution.py:54
  19.2 62.1 %collective-permute-done.1 = bf16[64,26624]{1,0:T(8,128)(2,1)} collective-permute-done((bf16[64,26624]{1,0:T(8,128)(2,1)S(1)}, bf16[64,26624]{1,0:T(8,128)(2,1)}, u32[]{:S(2)}, u32[]{:S(2)}) %collective-permute-start.1) | collective-permute-done | bytes 3407904 | tf_op jit(solution)/shard_map/ppermute | solution.py:54
  82.1 5.4 %collective-permute-start.5 = (bf16[64,13376]{1,0:T(8,128)(2,1)}, bf16[64,13376]{1,0:T(8,128)(2,1)}, u32[]{:S(2)}, u32[]{:S(2)}) collective-permute-start(bf16[64,13376]{1,0:T(8,128)(2,1)} %slice_select_fusion.1), channel_id=1, source_target_pairs={{0,4},{12,8},{1,5},{13,9},{2,6},{14,10},{3,7},{15,11},{16,20},{28,... | collective-permute-start | bytes 5136392 | tf_op jit(solution)/shard_map/ppermute | solution.py:54
  96.0 7.9 %psum.7 = f32[]{:T(128)} all-reduce(f32[]{:T(128)} %reduce_sum.19), channel_id=1, replica_groups=mesh['grp'=2,'wide'=4,'narrow'=2,'sub'=2] {'narrow','sub'}, use_global_device_ids=true, to_apply=%region_2.3 | all-reduce | flops 1 | bytes 8 | tf_op jit(solution)/shard_map/psum | solution.py:76
  103.9 8.9 %fusion.10 = f32[64,192]{1,0:T(8,128)} fusion(bf16[64,26624]{1,0:T(8,128)(2,1)} %copy-done, bf16[192,40000]{1,0:T(8,128)(2,1)} %bitcast.29), kind=kOutput, calls=%fused_computation.12 | convolution fusion | flops 654311424 | bytes 13680640 | tf_op jit(solution)/shard_map/dot_general | solution.py:11
  112.8 8.3 %fusion.8 = f32[64,192]{1,0:T(8,128)S(1)} fusion(bf16[64,26624]{1,0:T(8,128)(2,1)} %collective-permute-done, bf16[192,40000]{1,0:T(8,128)(2,1)} %bitcast.30), kind=kOutput, calls=%fused_computation.10 | convolution fusion | flops 654311424 | bytes 13680640 | tf_op jit(solution)/shard_map/dot_general | solution.py:11
  121.5 36.9 %collective-permute-done.4 = bf16[64,13376]{1,0:T(8,128)(2,1)} collective-permute-done((bf16[64,13376]{1,0:T(8,128)(2,1)}, bf16[64,13376]{1,0:T(8,128)(2,1)}, u32[]{:S(2)}, u32[]{:S(2)}) %collective-permute-start.4) | collective-permute-done | bytes 1712160 | tf_op jit(solution)/shard_map/ppermute | solution.py:54
  158.4 9.3 %collective-permute-done.3 = bf16[64,26624]{1,0:T(8,128)(2,1)} collective-permute-done((bf16[64,26624]{1,0:T(8,128)(2,1)}, bf16[64,26624]{1,0:T(8,128)(2,1)}, u32[]{:S(2)}, u32[]{:S(2)}) %collective-permute-start.3) | collective-permute-done | bytes 3407904 | tf_op jit(solution)/shard_map/ppermute | solution.py:54
  175.0 7.5 %collective-permute-start.10 = (bf16[128,13376]{0,1:T(8,128)(2,1)}, bf16[128,13376]{0,1:T(8,128)(2,1)}, u32[]{:S(2)}, u32[]{:S(2)}) collective-permute-start(bf16[128,13376]{0,1:T(8,128)(2,1)} %copy.9), channel_id=1, source_target_pairs={{0,4},{12,8},{1,5},{13,9},{2,6},{14,10},{3,7},{15,11},{16,20},{28,... | collective-permute-start | bytes 10272776 | tf_op jit(solution)/shard_map/ppermute | solution.py:54
  182.5 8.9 %fusion.6 = f32[64,192]{1,0:T(8,128)} fusion(bf16[64,26624]{1,0:T(8,128)(2,1)} %collective-permute-done.1, bf16[192,40000]{1,0:T(8,128)(2,1)} %bitcast.31), kind=kOutput, calls=%fused_computation.8 | convolution fusion | flops 654311424 | bytes 13680640 | tf_op jit(solution)/shard_map/dot_general | solution.py:11
  195.2 5.4 %fusion.24 = f32[64,192]{1,0:T(8,128)} fusion(f32[64,192]{1,0:T(8,128)S(1)} %copy-done.5, bf16[64,13376]{1,0:T(8,128)(2,1)} %add_convert_fusion.1, bf16[192,40000]{1,0:T(8,128)(2,1)} %bitcast.32), kind=kOutput, calls=%fused_computation.29 | convolution fusion | flops 328740864 | bytes 6979584 | tf_op jit(solution)/shard_map/dot_general | solution.py:11
  200.6 5.4 %fusion.17 = f32[64,192]{1,0:T(8,128)} fusion(bf16[64,13376]{1,0:T(8,128)(2,1)} %collective-permute-done.4, bf16[192,40000]{1,0:T(8,128)(2,1)} %bitcast.33), kind=kOutput, calls=%fused_computation.21 | convolution fusion | flops 328728576 | bytes 6930432 | tf_op jit(solution)/shard_map/dot_general | solution.py:11
  205.9 4.5 %copy.10 = bf16[64,13376]{0,1:T(8,128)(2,1)S(1)} copy(bf16[64,13376]{1,0:T(8,128)(2,1)} %collective-permute-done.5) | data formatting | bytes 3424256 | tf_op jit(solution)/shard_map/optimization_barrier | solution.py:68
  210.4 8.4 %fusion.4 = f32[64,192]{1,0:T(8,128)S(1)} fusion(bf16[64,26624]{1,0:T(8,128)(2,1)} %collective-permute-done.2, bf16[192,40000]{1,0:T(8,128)(2,1)} %bitcast.34), kind=kOutput, calls=%fused_computation.6 | convolution fusion | flops 654311424 | bytes 13680640 | tf_op jit(solution)/shard_map/dot_general | solution.py:11
  218.9 8.4 %fusion.2 = f32[64,192]{1,0:T(8,128)S(1)} fusion(bf16[64,26624]{1,0:T(8,128)(2,1)} %collective-permute-done.3, bf16[192,40000]{1,0:T(8,128)(2,1)} %bitcast.35), kind=kOutput, calls=%fused_computation.4 | convolution fusion | flops 654311424 | bytes 13680640 | tf_op jit(solution)/shard_map/dot_general | solution.py:11
  227.4 20.7 %collective-permute-done.7 = bf16[64,26624]{1,0:T(8,128)(2,1)} collective-permute-done((bf16[64,26624]{1,0:T(8,128)(2,1)}, bf16[64,26624]{1,0:T(8,128)(2,1)}, u32[]{:S(2)}, u32[]{:S(2)}) %collective-permute-start.7) | collective-permute-done | bytes 3407904 | tf_op jit(solution)/shard_map/ppermute | solution.py:54
  254.3 5.0 %fusion.21 = f32[192,64]{0,1:T(8,128)S(1)} fusion(bf16[64,13376]{1,0:T(8,128)(2,1)} %add_convert_fusion.1, bf16[128,13376]{0,1:T(8,128)(2,1)} %collective-permute-done.10, bf16[64,13376]{0,1:T(8,128)(2,1)S(1)} %copy.10), kind=kOutput, calls=%fused_computation.25 | convolution fusion | flops 339001344 | bytes 6897664 | tf_op jit(solution)/shard_map/dot_general | solution.py:11
  259.3 5.0 %fusion.22 = f32[192,64]{0,1:T(8,128)S(1)} fusion(bf16[64,13376]{1,0:T(8,128)(2,1)} %collective-permute-done.8, bf16[128,13376]{0,1:T(8,128)(2,1)} %collective-permute-done.10, bf16[64,13376]{0,1:T(8,128)(2,1)S(1)} %copy.10), kind=kOutput, calls=%fused_computation.26 | convolution fusion | flops 339001344 | bytes 6897664 | tf_op jit(solution)/shard_map/dot_general | solution.py:11
  267.5 9.5 %fusion = f32[64,192]{1,0:T(8,128)S(1)} fusion(bf16[192,40000]{1,0:T(8,128)(2,1)} %bitcast.36, bf16[64,26624]{1,0:T(8,128)(2,1)} %collective-permute-done.6, bf16[64,26624]{1,0:T(8,128)(2,1)} %collective-permute-done.7), kind=kOutput, calls=%fused_computation.2 | convolution fusion | flops 656015360 | bytes 17088512 | tf_op jit(solution)/shard_map/dot_general | solution.py:11
  277.1 5.1 %select_add_fusion.3 = (f32[192,64]{0,1:T(8,128)S(1)}, f32[192,64]{0,1:T(8,128)S(1)}, f32[192,64]{0,1:T(8,128)S(1)}, f32[192,64]{0,1:T(8,128)S(1)}) fusion(f32[192,64]{0,1:T(8,128)S(1)} %fusion.22, f32[192,64]{0,1:T(8,128)S(1)} %fusion.21, pred[]{:T(512)S(6)} %eq.161, pred[]{:T(512)S(6)} %eq.160, pred[]{:T(512)S(6)} %eq.146, pred[]{:T(512)S(6)} %eq.188, ...), kind=kOutput, calls=%fused_computation.45 | convolution fusion | flops 339247104 | bytes 7143436 | tf_op jit(solution)/shard_map/dot_general | solution.py:11
  282.3 4.3 %collective-permute-start.11 = (f32[384,64]{0,1:T(8,128)S(1)}, f32[384,64]{0,1:T(8,128)S(1)}, u32[]{:S(2)}, u32[]{:S(2)}) collective-permute-start(f32[384,64]{0,1:T(8,128)S(1)} %pad_maximum_fusion.4), channel_id=1, source_target_pairs={{0,1},{1,0},{2,3},{3,2},{4,5},{5,4},{6,7},{7,6},{8,9},{9,8},{10,11... | collective-permute-start | bytes 294920 | tf_op jit(solution)/shard_map/ppermute | solution.py:102
  294.7 13.6 %collective-permute-start.18 = (f32[64]{0:T(128)S(1)}, f32[64]{0:T(128)S(1)}, u32[]{:S(2)}, u32[]{:S(2)}) collective-permute-start(f32[64]{0:T(128)S(1)} %get-tuple-element.37), channel_id=1, source_target_pairs={{0,2},{1,6},{2,10},{3,14},{4,3},{5,7},{6,11},{7,15},{8,0},{9,4},{1... | collective-permute-start | bytes 776 | tf_op jit(solution)/shard_map/ppermute | solution.py:110
  310.0 3.9 %collective-permute-start.16 = (f32[64]{0:T(128)S(1)}, f32[64]{0:T(128)S(1)}, u32[]{:S(2)}, u32[]{:S(2)}) collective-permute-start(f32[64]{0:T(128)S(1)} %get-tuple-element.37), channel_id=1, source_target_pairs={{0,0},{1,4},{2,8},{3,12},{4,1},{5,5},{6,9},{7,13},{8,2},{9,6},{10,... | collective-permute-start | bytes 776 | tf_op jit(solution)/shard_map/ppermute | solution.py:110
  315.3 4.3 %collective-permute-start.14 = (f32[192,64]{0,1:T(8,128)S(1)}, f32[192,64]{0,1:T(8,128)S(1)}, u32[]{:S(2)}, u32[]{:S(2)}) collective-permute-start(f32[192,64]{0,1:T(8,128)S(1)} %get-tuple-element.44), channel_id=1, source_target_pairs={{0,0},{1,4},{2,8},{3,12},{4,1},{5,5},{6,9},{7,13},{8,2},{9,6},{10,... | collective-permute-start | bytes 147464 | tf_op jit(solution)/shard_map/ppermute | solution.py:106
  (74 shorter events, 59.7 us)
Async XLA Ops:
  4.6 76.7 %collective-permute-start.1 = (bf16[64,26624]{1,0:T(8,128)(2,1)S(1)}, bf16[64,26624]{1,0:T(8,128)(2,1)}, u32[]{:S(2)}, u32[]{:S(2)}) collective-permute-start(bf16[64,26624]{1,0:T(8,128)(2,1)S(1)} %add_convert_fusion), channel_id=1, source_target_pairs={{12,8},{8,4},{4,0},{13,9},{9,5},{5,1},{14,10},{10,6},{6,2},{15,11}... | collective-permute-start | bytes 10223624 | tf_op jit(solution)/shard_map/ppermute | solution.py:54
  6.0 76.0 %collective-permute-start = (bf16[64,26624]{1,0:T(8,128)(2,1)S(1)}, bf16[64,26624]{1,0:T(8,128)(2,1)}, u32[]{:S(2)}, u32[]{:S(2)}) collective-permute-start(bf16[64,26624]{1,0:T(8,128)(2,1)S(1)} %add_convert_fusion), channel_id=1, source_target_pairs={{0,4},{4,8},{8,12},{1,5},{5,9},{9,13},{2,6},{6,10},{10,14},{3,7},{... | collective-permute-start | bytes 10223624 | tf_op jit(solution)/shard_map/ppermute | solution.py:54
  82.1 39.5 %collective-permute-start.5 = (bf16[64,13376]{1,0:T(8,128)(2,1)}, bf16[64,13376]{1,0:T(8,128)(2,1)}, u32[]{:S(2)}, u32[]{:S(2)}) collective-permute-start(bf16[64,13376]{1,0:T(8,128)(2,1)} %slice_select_fusion.1), channel_id=1, source_target_pairs={{0,4},{12,8},{1,5},{13,9},{2,6},{14,10},{3,7},{15,11},{16,20},{28,... | collective-permute-start | bytes 5136392 | tf_op jit(solution)/shard_map/ppermute | solution.py:54
  87.5 70.9 %collective-permute-start.4 = (bf16[64,13376]{1,0:T(8,128)(2,1)}, bf16[64,13376]{1,0:T(8,128)(2,1)}, u32[]{:S(2)}, u32[]{:S(2)}) collective-permute-start(bf16[64,13376]{1,0:T(8,128)(2,1)} %add_convert_fusion.1), channel_id=1, source_target_pairs={{0,4},{12,8},{1,5},{13,9},{2,6},{14,10},{3,7},{15,11},{16,20},{28,... | collective-permute-start | bytes 5136392 | tf_op jit(solution)/shard_map/ppermute | solution.py:54
  90.0 68.4 %collective-permute-start.2 = (bf16[64,26624]{1,0:T(8,128)(2,1)}, bf16[64,26624]{1,0:T(8,128)(2,1)}, u32[]{:S(2)}, u32[]{:S(2)}) collective-permute-start(bf16[64,26624]{1,0:T(8,128)(2,1)} %collective-permute-done), channel_id=1, source_target_pairs={{4,8},{8,12},{5,9},{9,13},{6,10},{10,14},{7,11},{11,15},{20,24},{2... | collective-permute-start | bytes 10223624 | tf_op jit(solution)/shard_map/ppermute | solution.py:54
  92.4 75.3 %collective-permute-start.3 = (bf16[64,26624]{1,0:T(8,128)(2,1)}, bf16[64,26624]{1,0:T(8,128)(2,1)}, u32[]{:S(2)}, u32[]{:S(2)}) collective-permute-start(bf16[64,26624]{1,0:T(8,128)(2,1)} %collective-permute-done.1), channel_id=1, source_target_pairs={{8,4},{4,0},{9,5},{5,1},{10,6},{6,2},{11,7},{7,3},{24,20},{20,16},... | collective-permute-start | bytes 10223624 | tf_op jit(solution)/shard_map/ppermute | solution.py:54
  171.3 56.1 %collective-permute-start.6 = (bf16[64,26624]{1,0:T(8,128)(2,1)}, bf16[64,26624]{1,0:T(8,128)(2,1)}, u32[]{:S(2)}, u32[]{:S(2)}) collective-permute-start(bf16[64,26624]{1,0:T(8,128)(2,1)} %collective-permute-done.2), channel_id=1, source_target_pairs={{8,12},{9,13},{10,14},{11,15},{24,28},{25,29},{26,30},{27,31}} | collective-permute-start | bytes 10223624 | tf_op jit(solution)/shard_map/ppermute | solution.py:54
  173.8 74.3 %collective-permute-start.7 = (bf16[64,26624]{1,0:T(8,128)(2,1)}, bf16[64,26624]{1,0:T(8,128)(2,1)}, u32[]{:S(2)}, u32[]{:S(2)}) collective-permute-start(bf16[64,26624]{1,0:T(8,128)(2,1)} %collective-permute-done.3), channel_id=1, source_target_pairs={{4,0},{5,1},{6,2},{7,3},{20,16},{21,17},{22,18},{23,19}} | collective-permute-start | bytes 10223624 | tf_op jit(solution)/shard_map/ppermute | solution.py:54
  175.0 76.1 %collective-permute-start.10 = (bf16[128,13376]{0,1:T(8,128)(2,1)}, bf16[128,13376]{0,1:T(8,128)(2,1)}, u32[]{:S(2)}, u32[]{:S(2)}) collective-permute-start(bf16[128,13376]{0,1:T(8,128)(2,1)} %copy.9), channel_id=1, source_target_pairs={{0,4},{12,8},{1,5},{13,9},{2,6},{14,10},{3,7},{15,11},{16,20},{28,... | collective-permute-start | bytes 10272776 | tf_op jit(solution)/shard_map/ppermute | solution.py:54
  191.5 35.9 %collective-permute-start.9 = (bf16[64,13376]{1,0:T(8,128)(2,1)}, bf16[64,13376]{1,0:T(8,128)(2,1)}, u32[]{:S(2)}, u32[]{:S(2)}) collective-permute-start(bf16[64,13376]{1,0:T(8,128)(2,1)} %collective-permute-done.4), channel_id=1, source_target_pairs={{4,8},{8,4},{5,9},{9,5},{6,10},{10,6},{7,11},{11,7},{20,24},{24,20... | collective-permute-start | bytes 5136392 | tf_op jit(solution)/shard_map/ppermute | solution.py:54
  193.3 34.1 %collective-permute-start.8 = (bf16[64,13376]{1,0:T(8,128)(2,1)}, bf16[64,13376]{1,0:T(8,128)(2,1)}, u32[]{:S(2)}, u32[]{:S(2)}) collective-permute-start(bf16[64,13376]{1,0:T(8,128)(2,1)} %add_convert_fusion.1), channel_id=1, source_target_pairs={{4,8},{8,4},{5,9},{9,5},{6,10},{10,6},{7,11},{11,7},{20,24},{24,20... | collective-permute-start | bytes 5136392 | tf_op jit(solution)/shard_map/ppermute | solution.py:54
  210.4 40.7 %slice-start = ((s8[15384576]{0:T(1024)(128)(4,1)}), s8[4194304]{0:T(1024)(128)(4,1)S(1)}, s32[]{:S(2)}) async-start(s8[15384576]{0:T(1024)(128)(4,1)} %bitcast.37), calls=%async_computation | async-start | bytes 8388608
  210.4 40.7 %slice-start.1 = ((s8[15384576]{0:T(1024)(128)(4,1)}), s8[4194304]{0:T(1024)(128)(4,1)S(1)}, s32[]{:S(2)}) async-start(s8[15384576]{0:T(1024)(128)(4,1)} %bitcast.37), calls=%async_computation.1 | async-start | bytes 8388608
  218.9 32.2 %slice-start.2 = ((s8[15384576]{0:T(1024)(128)(4,1)}), s8[4194304]{0:T(1024)(128)(4,1)S(1)}, s32[]{:S(2)}) async-start(s8[15384576]{0:T(1024)(128)(4,1)} %bitcast.37), calls=%async_computation.2 | async-start | bytes 8388608
  218.9 32.2 %slice-start.3 = ((s8[15384576]{0:T(1024)(128)(4,1)}), s8[2801664]{0:T(1024)(128)(4,1)S(1)}, s32[]{:S(2)}) async-start(s8[15384576]{0:T(1024)(128)(4,1)} %bitcast.37), calls=%async_computation.3 | async-start | bytes 5603328
  282.3 6.5 %collective-permute-start.11 = (f32[384,64]{0,1:T(8,128)S(1)}, f32[384,64]{0,1:T(8,128)S(1)}, u32[]{:S(2)}, u32[]{:S(2)}) collective-permute-start(f32[384,64]{0,1:T(8,128)S(1)} %pad_maximum_fusion.4), channel_id=1, source_target_pairs={{0,1},{1,0},{2,3},{3,2},{4,5},{5,4},{6,7},{7,6},{8,9},{9,8},{10,11... | collective-permute-start | bytes 294920 | tf_op jit(solution)/shard_map/ppermute | solution.py:102
  286.8 4.5 %collective-permute-start.12 = (f32[384,64]{0,1:T(8,128)S(1)}, f32[384,64]{0,1:T(8,128)S(1)}, u32[]{:S(2)}, u32[]{:S(2)}) collective-permute-start(f32[384,64]{0,1:T(8,128)S(1)} %pad_maximum_fusion.5), channel_id=1, source_target_pairs={{0,2},{1,3},{2,0},{3,1},{4,6},{5,7},{6,4},{7,5},{8,10},{9,11},{10,... | collective-permute-start | bytes 294920 | tf_op jit(solution)/shard_map/ppermute | solution.py:102
  287.7 5.8 %collective-permute-start.13 = (f32[384,64]{0,1:T(8,128)S(1)}, f32[384,64]{0,1:T(8,128)S(1)}, u32[]{:S(2)}, u32[]{:S(2)}) collective-permute-start(f32[384,64]{0,1:T(8,128)S(1)} %pad_maximum_fusion.6), channel_id=1, source_target_pairs={{0,3},{1,2},{2,1},{3,0},{4,7},{5,6},{6,5},{7,4},{8,11},{9,10},{10,... | collective-permute-start | bytes 294920 | tf_op jit(solution)/shard_map/ppermute | solution.py:102
  293.7 21.6 %collective-permute-start.19 = (f32[64]{0:T(128)S(1)}, f32[64]{0:T(128)S(1)}, u32[]{:S(2)}, u32[]{:S(2)}) collective-permute-start(f32[64]{0:T(128)S(1)} %get-tuple-element.37), channel_id=1, source_target_pairs={{0,3},{1,7},{2,11},{3,15},{4,2},{5,6},{6,10},{7,14},{8,1},{9,5},{1... | collective-permute-start | bytes 776 | tf_op jit(solution)/shard_map/ppermute | solution.py:110
  294.7 24.9 %collective-permute-start.18 = (f32[64]{0:T(128)S(1)}, f32[64]{0:T(128)S(1)}, u32[]{:S(2)}, u32[]{:S(2)}) collective-permute-start(f32[64]{0:T(128)S(1)} %get-tuple-element.37), channel_id=1, source_target_pairs={{0,2},{1,6},{2,10},{3,14},{4,3},{5,7},{6,11},{7,15},{8,0},{9,4},{1... | collective-permute-start | bytes 776 | tf_op jit(solution)/shard_map/ppermute | solution.py:110
  308.4 11.3 %collective-permute-start.17 = (f32[64]{0:T(128)S(1)}, f32[64]{0:T(128)S(1)}, u32[]{:S(2)}, u32[]{:S(2)}) collective-permute-start(f32[64]{0:T(128)S(1)} %get-tuple-element.37), channel_id=1, source_target_pairs={{0,1},{1,5},{2,9},{3,13},{4,0},{5,4},{6,8},{7,12},{8,3},{9,7},{10,... | collective-permute-start | bytes 776 | tf_op jit(solution)/shard_map/ppermute | solution.py:110
  310.0 9.7 %collective-permute-start.16 = (f32[64]{0:T(128)S(1)}, f32[64]{0:T(128)S(1)}, u32[]{:S(2)}, u32[]{:S(2)}) collective-permute-start(f32[64]{0:T(128)S(1)} %get-tuple-element.37), channel_id=1, source_target_pairs={{0,0},{1,4},{2,8},{3,12},{4,1},{5,5},{6,9},{7,13},{8,2},{9,6},{10,... | collective-permute-start | bytes 776 | tf_op jit(solution)/shard_map/ppermute | solution.py:110
  314.0 7.4 %collective-permute-start.15 = (f32[192,64]{0,1:T(8,128)S(1)}, f32[192,64]{0,1:T(8,128)S(1)}, u32[]{:S(2)}, u32[]{:S(2)}) collective-permute-start(f32[192,64]{0,1:T(8,128)S(1)} %get-tuple-element.43), channel_id=1, source_target_pairs={{4,0},{5,4},{6,8},{7,12},{8,3},{9,7},{10,11},{11,15},{20,16},{21,2... | collective-permute-start | bytes 147464 | tf_op jit(solution)/shard_map/ppermute | solution.py:106
  315.3 8.4 %collective-permute-start.14 = (f32[192,64]{0,1:T(8,128)S(1)}, f32[192,64]{0,1:T(8,128)S(1)}, u32[]{:S(2)}, u32[]{:S(2)}) collective-permute-start(f32[192,64]{0,1:T(8,128)S(1)} %get-tuple-element.44), channel_id=1, source_target_pairs={{0,0},{1,4},{2,8},{3,12},{4,1},{5,5},{6,9},{7,13},{8,2},{9,6},{10,... | collective-permute-start | bytes 147464 | tf_op jit(solution)/shard_map/ppermute | solution.py:106
  (6 other events, 64.8 us)

commit v3 on v1

v3 whole, which is shorter than its diff:
```python
import jax
import jax.numpy as jnp
from jax import lax
from jax.experimental import pallas as pl
from jax.experimental.pallas import tpu as pltpu
from jax.sharding import PartitionSpec as P

SITES = ("narrow", "sub")
ALL = ("wide", "narrow", "sub")


def dot_t(a, b):
    return lax.dot_general(a, b, (((1,), (1,)), ((), ())), preferred_element_type=jnp.float32)


def potential_of(noise, volts, labels):
    value = volts[:, 0:1]
    for kind in range(1, volts.shape[1]):
        value = jnp.where(labels[None, :] == kind, volts[:, kind:kind + 1], value)
    return (value + noise.astype(jnp.float32)).astype(jnp.bfloat16)


def finish(charges, total, weight_sum, profile):
    return charges - profile[:, :, None] * (total / weight_sum)[None, None, :]


def gather_plan(slab, noise, volts, labels, profile, sizes):
    wide, owners = sizes
    panels, rows, _ = slab.shape
    frames = noise.shape[0]
    pot = lax.all_gather(potential_of(noise, volts, labels), "wide", axis=0, tiled=True)
    part = dot_t(slab.reshape(panels * rows, -1), pot).reshape(panels, rows, wide, frames)
    mine = lax.all_to_all(part, "wide", 2, 1, tiled=True).reshape(panels, wide * rows, frames)
    charges = lax.psum_scatter(mine, SITES, scatter_dimension=1, tiled=True)
    total, weight_sum = lax.psum((jnp.sum(charges, axis=(0, 1)), jnp.sum(profile)), SITES)
    return finish(charges, total, weight_sum, profile)


LANES = 128
STEPS = 4
WIDTH = 4 * LANES


def is_end(z):
    return (z == 0) | (z == 3)


def is_mid(z):
    return (z == 1) | (z == 2)


def far_block(z):
    return jnp.where(z < 2, 3, 0)


def across_block(z):
    return 3 - z


def absorb(place, slab, third_of, units, brought, sums, last=None):
    nrows, sites = slab.shape
    tile = sites // 3 // LANES * LANES // STEPS
    frames = units[0][0].shape[0]
    arrays = [x for x, _, _ in units]
    valid = [v for _, v, _ in units]
    row_sets, extra = [], []
    for number, rows, lane, block in brought:
        at = []
        for x in rows:
            known = [n for n, y in enumerate(row_sets) if y is x]
            at.append(known[0] if known else len(row_sets))
            if not known:
                row_sets.append(x)
        extra.append((number, at, lane, block))
    count, nsets = len(units), len(row_sets)
    blocks = 4
    whole = tile * STEPS
    rest = sites - 3 * whole
    rest_width = rest + -rest % LANES
    long = [n for n in range(count) if arrays[n].shape[1] > whole]

    def dot(a, b):
        return lax.dot_general(a, b, (((1,), (1,)), ((), ())), preferred_element_type=jnp.float32)

    def kernel(place_ref, slab_ref, *refs):
        xs, rows = refs[:count], refs[count:count + nsets]
        refs = refs[count + nsets:]
        if sums is not None:
            sums_ref, refs = refs[0], refs[1:]
        if long:
            slab_rest, rests, refs = refs[0], refs[1:1 + len(long)], refs[1 + len(long):]
        if last is None:
            acc, = refs
        else:
            profile_ref, outs, acc = refs[0], refs[1:-1], refs[-1]
        z, k = place_ref[0], place_ref[1]
        step = pl.program_id(0)

        @pl.when(step == 0)
        def _():
            acc[...] = jnp.zeros(acc.shape, acc.dtype) if sums is None else sums_ref[...]
            if long:
                column = lax.broadcasted_iota(jnp.int32, (nrows, rest_width), 1)
                piece = jnp.where(column < rest, slab_rest[...].astype(jnp.float32), 0.0).astype(jnp.bfloat16)
            for n, x in zip(long, rests if long else ()):
                @pl.when(valid[n](z))
                def _(n=n, x=x):
                    acc[units[n][2](z), :, 0:nrows] += dot(x[...], piece)

        for n in range(count):
            if units[n][2] is None:
                continue

            @pl.when(valid[n](z))
            def _(n=n):
                acc[units[n][2](z), :, 0:nrows] += dot(xs[n][...], slab_ref[...])

        if extra:
            @pl.when(is_mid(z))
            def _():
                for number, at, lane, block in extra:
                    piece = [rows[i][...] for i in at]
                    piece = piece[0] if len(piece) == 1 else jnp.concatenate(piece, axis=0)
                    acc[block(z), :, lane:lane + piece.shape[0]] += dot(xs[number][...], piece)

        if last is not None:
            @pl.when(step == STEPS - 1)
            def _():
                weight = jnp.sum(profile_ref[...])
                lane = lax.broadcasted_iota(jnp.int32, (frames, LANES), 1)
                for turn, out in enumerate(outs):
                    at = k ^ turn
                    out[:, :WIDTH - LANES] = acc[at, :, :WIDTH - LANES]
                    end = acc[at, :, WIDTH - LANES:]
                    out[:, WIDTH - LANES:] = jnp.where(lane >= nrows - LANES, weight, end)

    def unit_spec(ok):
        return pl.BlockSpec((frames, tile), lambda i, s: (0, jnp.where(ok(s[0]), i, 0)))

    in_specs = [pl.BlockSpec((nrows, tile), lambda i, s: (0, third_of(s[0]) * STEPS + i))]
    in_specs += [unit_spec(v) for v in valid]
    in_specs += [pl.BlockSpec((x.shape[0], tile), lambda i, s: (0, jnp.where(is_mid(s[0]), i, 0))) for x in row_sets]
    operands = [slab] + arrays + row_sets
    sums_shape = (blocks, frames, WIDTH)
    if sums is not None:
        in_specs.append(pl.BlockSpec(sums_shape, lambda i, s: (0, 0, 0)))
        operands.append(sums)
    if long:
        in_specs.append(pl.BlockSpec((nrows, rest_width), lambda i, s: (0, 3 * whole // rest_width)))
        in_specs += [pl.BlockSpec((frames, rest_width), lambda i, s: (0, whole // rest_width))] * len(long)
        operands += [slab] + [arrays[n] for n in long]
    if last is None:
        out_shape = jax.ShapeDtypeStruct(sums_shape, jnp.float32)
        out_specs = pl.BlockSpec(sums_shape, lambda i, s: (0, 0, 0))
        scratch = []
    else:
        in_specs.append(pl.BlockSpec(last.shape, lambda i, s: (0, 0)))
        operands.append(last)
        out_shape = [jax.ShapeDtypeStruct(sums_shape[1:], jnp.float32)] * blocks
        out_specs = [pl.BlockSpec(sums_shape[1:], lambda i, s: (0, 0))] * blocks
        scratch = [pltpu.VMEM(sums_shape, jnp.float32)]
    return pl.pallas_call(
        kernel,
        grid_spec=pltpu.PrefetchScalarGridSpec(
            num_scalar_prefetch=1, grid=(STEPS,), in_specs=in_specs, out_specs=out_specs, scratch_shapes=scratch),
        out_shape=out_shape,
        compiler_params=pltpu.CompilerParams(vmem_limit_bytes=32 * 1024 * 1024),
        cost_estimate=pl.CostEstimate(flops=1000, bytes_accessed=1000, transcendentals=0),
    )(place, *operands)


def line_plan(slab, noise, volts, labels, profile, sizes):
    wide, owners = sizes
    panels, rows, sites = slab.shape
    frames = noise.shape[0]
    nrows = panels * rows
    part_rows = nrows // 3
    third = sites // 3 // LANES * LANES
    z = lax.axis_index("wide")
    k = lax.axis_index(SITES)
    place = jnp.stack([z, k]).astype(jnp.int32)
    slab = slab.reshape(nrows, sites)

    def after(x, *others):
        return lax.optimization_barrier((x,) + others)[0]

    def potential_at(first, end, small):
        return potential_of(noise[:, first:end], small, labels[first:end])

    def send(x, pairs):
        return lax.ppermute(x, "wide", pairs)

    def spare(i, *others):
        return after(slab[part_rows * i:part_rows * (i + 1), 2 * third:3 * third], *others)

    ends_in = [(0, 1), (3, 2)]
    across = [(1, 2), (2, 1)]
    right = [(0, 1), (1, 2), (2, 3)]
    left = [(3, 2), (2, 1), (1, 0)]
    rest = sites - 3 * third
    own0 = jnp.concatenate([
        potential_at(0, third, volts), potential_at(3 * third, sites, volts),
        jnp.zeros((frames, -rest % LANES), jnp.bfloat16)], axis=1)
    own1 = potential_at(third, 2 * third, after(volts, own0))
    f1a_r, f1a_l = send(own0, right), send(own0, left)
    f1b_r, f1b_l = send(own1, right), send(own1, left)
    own2 = potential_at(2 * third, 3 * third, after(volts, own1))
    f2a_r, f2a_l = send(f1a_r, right[1:]), send(f1a_l, left[1:])
    g0 = send(after(own2, f1a_r, f1a_l), ends_in)
    f2b_r, f2b_l = send(f1b_r, right[1:]), send(f1b_l, left[1:])
    h1 = send(spare(0, f1b_r, f1b_l), ends_in)
    f3a_r, f3a_l = send(f2a_r, right[2:]), send(f2a_l, left[2:])
    g1 = send(after(own2, f2a_r, f2a_l), across)
    h2 = send(spare(1, f2a_r, f2a_l), ends_in)
    f3b_r, f3b_l = send(f2b_r, right[2:]), send(f2b_l, left[2:])
    g2 = send(after(g0, f2b_r, f2b_l), across)
    h3 = send(spare(2, f2b_r, f2b_l), ends_in)

    def always(z):
        return z >= 0

    def here(z):
        return z

    def pick(end_third, mid_third):
        return lambda z: jnp.where(is_mid(z), mid_third, end_third)

    def chain(x_r, x_l, hop):
        return [(x_r, lambda z: z >= hop, lambda z: z - hop), (x_l, lambda z: z < 4 - hop, lambda z: z + hop)]

    sums = absorb(place, slab, pick(0, 0), [(own0, always, here)] + chain(f1a_r, f1a_l, 1), [], None)
    sums = absorb(place, slab, pick(1, 1), [(own1, always, here)] + chain(f1b_r, f1b_l, 1), [], sums)
    sums = absorb(place, slab, pick(2, 2), [(own2, always, here), (g0, is_mid, lambda z: jnp.where(z == 1, 0, 3))], [], sums)
    sums = absorb(place, slab, pick(0, 0), chain(f2a_r, f2a_l, 2), [], sums)
    sums = absorb(place, slab, pick(1, 1), chain(f2b_r, f2b_l, 2), [], sums)
    sums = absorb(
        place, slab, pick(0, 2),
        chain(f3a_r, f3a_l, 3) + [(g1, is_mid, across_block), (own2, is_mid, None)],
        [(2, (h1, h2), 2 * LANES, across_block), (3, (h1, h2), 2 * LANES, here)], sums)
    messages = absorb(
        place, slab, pick(1, 2),
        chain(f3b_r, f3b_l, 3) + [(g2, is_mid, far_block), (g1, is_mid, None), (own2, is_mid, None)],
        [(2, (h1, h2, h3), 2 * LANES, far_block), (3, (h3,), 3 * LANES, across_block), (4, (h3,), 3 * LANES, here)], sums, profile)

    summed = messages[0]
    for turn in range(1, owners):
        summed += lax.ppermute(messages[turn], SITES, [(i, i ^ turn) for i in range(owners)])
    weight_sum = summed[0, WIDTH - 1]
    mine, extra = summed[:, :nrows], summed[:, 2 * LANES:2 * LANES + nrows]
    frame_sum = jnp.sum(mine, axis=1) + jnp.sum(extra, axis=1)
    flip = [(a * owners + b, b * owners + a) for a in range(wide) for b in range(owners)]
    flip_end = [(a * owners + b, b * owners + e) for a, e in ((1, 0), (2, 3)) for b in range(owners)]
    charges = lax.ppermute(mine, ALL, flip) + lax.ppermute(extra, ALL, flip_end)
    total = 0.0
    for turn in range(owners):
        pairs = [(a * owners + b, b * owners + (a ^ turn)) for a in range(wide) for b in range(owners)]
        total += lax.ppermute(frame_sum, ALL, pairs)
    charges = charges.reshape(frames, panels, rows).transpose(1, 2, 0)
    return finish(charges, total, weight_sum, profile)


def solution(mesh):
    wide = mesh.shape["wide"]
    owners = mesh.shape["narrow"] * mesh.shape["sub"]
    plan = line_plan if wide == owners == 4 else gather_plan

    def local(slab, noise, volts, labels, profile):
        return plan(slab, noise, volts, labels, profile, (wide, owners))

    return jax.shard_map(
        local,
        mesh=mesh,
        in_specs=(
            P(None, "wide", ("narrow", "sub")),
            P(("grp", "wide"), ("narrow", "sub")),
            P(("grp", "wide"), None),
            P(("narrow", "sub")),
            P(None, ("narrow", "sub")),
        ),
        out_specs=P(None, ("narrow", "sub"), ("grp", "wide")),
        check_vma=False,
    )
```

time: 326 us -> 339 us (1.040)
  matrix products: 60.8 us -> 0 us
  Pallas kernels: 0 us -> 38.1 us
  starting transfers between devices: 57.6 us -> 78 us
  local copies, waits for them, and re-layouts: 6.08 us -> 19.1 us
  waiting for transfers between devices: 179 us -> 192 us
  blocking collectives: 7.49 us -> 0 us
    dot_general x19 -> x0, matrix products: 60.8 us -> none  [dot_t(): lax.dot_general(a, b, (((1,), (1,)), ((), ())), preferred_element_type=jn...]
    pallas_call x0 -> x7, Pallas kernels: none -> 38.1 us  [absorb(): pl.pallas_call(kernel, grid_spec=pltpu.PrefetchScalarGridSpec(num_scalar_...]
    unnamed x16 -> x46, local copies, waits for them, and re-layouts: 0.37 us -> 13.1 us
    ppermute x4, starting transfers between devices: 9.9 us -> 20.9 us  [line_plan(): total += lax.ppermute(frame_sum, ALL, pairs)]
    ppermute x18, waiting for transfers between devices: 171 us -> 180 us  [send(): return lax.ppermute(x, 'wide', pairs)]
    psum x1 -> x0, blocking collectives: 7.49 us -> none  [line_plan(): weight_sum = lax.psum(jnp.sum(after(profile, f1a_r, f1a_l)), SITES)]
    ppermute x5, starting transfers between devices: 10.4 us -> 16.7 us  [the longest x3 11 us: line_plan(): lax.ppermute(messages[turn], SITES, [(i, i ^ turn) for i in range(owners)])]
    ppermute x5, waiting for transfers between devices: 7.72 us -> 11.7 us  [the longest x3 6.33 us: line_plan(): lax.ppermute(messages[turn], SITES, [(i, i ^ turn) for i in range(owners)])]
  transfers between devices with their start and end apart: 27 -> 27, of which waited for: 11 -> 10; matrix products, arithmetic and copies ran while one was open for 21% -> 3% of each run, Pallas kernels for 0% -> 10%
where the time goes in v3:
time: 339 us; the launch traced here: 338 us
  waiting for transfers between devices  192 us (57%)
  starting transfers between devices  78 us (23%)
  Pallas kernels  38.1 us (11%)
  local copies, waits for them, and re-layouts  19.1 us (6%)
  other arithmetic  9.8 us (3%)
    ppermute x18, waiting for transfers between devices, send(): return lax.ppermute(x, 'wide', pairs)  180 us
    ppermute x18, starting transfers between devices, send(): return lax.ppermute(x, 'wide', pairs)  40.3 us
    pallas_call x7, Pallas kernels, absorb(): pl.pallas_call(kernel, grid_spec=pltpu.PrefetchScalarGridSpec(num_scalar_...  38.1 us
    ppermute x4, starting transfers between devices, line_plan(): total += lax.ppermute(frame_sum, ALL, pairs)  20.9 us
    unnamed x46, local copies, waits for them, and re-layouts  13.1 us
    ppermute x3, starting transfers between devices, line_plan(): lax.ppermute(messages[turn], SITES, [(i, i ^ turn) for i in range(owners)])  11 us
  transfers between devices with their start and end apart: 27, of which 10 were waited for; matrix products, arithmetic and copies ran while one was open for 3% of the time, Pallas kernels for 10%

profile of v3, /device:TPU:3, one launch (start us, length us, event | category | flops | bytes accessed | tf_op | source)
XLA Modules:
  0.0 337.7 jit_solution(15683851612030261405)
XLA Ops:
  5.6 3.3 collective-permute-start.6
  12.2 4.1 %collective-permute-start = (bf16[64,13312]{1,0:T(8,128)(2,1)S(1)}, bf16[64,13312]{1,0:T(8,128)(2,1)S(1)}, u32[]{:S(2)}, u32[]{:S(2)}) collective-permute-start(bf16[64,13312]{1,0:T(8,128)(2,1)S(1)} %add_convert_fusion.1.refs_0_), channel_id=1, source_target_pairs={{0,4},{4,8},{8,12},{1,5},{5,9},{9,13},{2,6},{6,10},{10,14},{3,7},{... | collective-permute-start | bytes 5111816 | tf_op jit(solution)/shard_map/ppermute | solution.py:191
  17.6 27.4 %collective-permute-done.6.refs_1_.refs_5_ = bf16[64,13440]{1,0:T(8,128)(2,1)S(1)} collective-permute-done((bf16[64,13440]{1,0:T(8,128)(2,1)S(1)}, bf16[64,13440]{1,0:T(8,128)(2,1)S(1)}, u32[]{:S(2)}, u32[]{:S(2)}) %collective-permute-start.6) | collective-permute-done | bytes 1720352 | tf_op jit(solution)/shard_map/ppermute | solution.py:191
  47.7 33.8 %collective-permute-done.refs_1_ = bf16[64,13312]{1,0:T(8,128)(2,1)S(1)} collective-permute-done((bf16[64,13312]{1,0:T(8,128)(2,1)S(1)}, bf16[64,13312]{1,0:T(8,128)(2,1)S(1)}, u32[]{:S(2)}, u32[]{:S(2)}) %collective-permute-start) | collective-permute-done | bytes 1703968 | tf_op jit(solution)/shard_map/ppermute | solution.py:191
  86.8 6.5 %collective-permute-start.8 = (bf16[64,13312]{1,0:T(8,128)(2,1)S(1)}, bf16[64,13312]{1,0:T(8,128)(2,1)}, u32[]{:S(2)}, u32[]{:S(2)}) collective-permute-start(bf16[64,13312]{1,0:T(8,128)(2,1)S(1)} %add_convert_fusion.refs_0_.refs_3_.refs_4_), channel_id=1, source_target_pairs={{0,4},{12,8},{1,5},{13,9},{2,6},{14,10},{3,7},{15,11},{16,20},{28,... | collective-permute-start | bytes 5111816 | tf_op jit(solution)/shard_map/ppermute | solution.py:191
  95.3 4.0 %fusion = (bf16[64,13312]{1,0:T(8,128)(2,1)}, bf16[64,13312]{1,0:T(8,128)(2,1)S(1)}, bf16[64,13312]{1,0:T(8,128)(2,1)S(1)}) fusion(bf16[192,40000]{1,0:T(8,128)(2,1)} %bitcast.18), kind=kLoop, calls=%fused_computation.20 | loop fusion | bytes 10223616 | tf_op jit(solution)/shard_map/slice | solution.py:194
  99.3 62.2 %collective-permute-done.11.refs_1_.refs_5_ = bf16[64,13440]{1,0:T(8,128)(2,1)} collective-permute-done((bf16[64,13440]{1,0:T(8,128)(2,1)S(1)}, bf16[64,13440]{1,0:T(8,128)(2,1)}, u32[]{:S(2)}, u32[]{:S(2)}) %collective-permute-start.11) | collective-permute-done | bytes 1720352 | tf_op jit(solution)/shard_map/ppermute | solution.py:191
  161.6 3.2 collective-permute-start.13
  169.3 27.9 %collective-permute-done.13.refs_4_.refs_5_ = bf16[64,13312]{1,0:T(8,128)(2,1)S(1)} collective-permute-done((bf16[64,13312]{1,0:T(8,128)(2,1)S(1)}, bf16[64,13312]{1,0:T(8,128)(2,1)S(1)}, u32[]{:S(2)}, u32[]{:S(2)}) %collective-permute-start.13) | collective-permute-done | bytes 1703968 | tf_op jit(solution)/shard_map/ppermute | solution.py:191
  198.4 5.3 %collective-permute-start.15 = (bf16[64,13312]{1,0:T(8,128)(2,1)}, bf16[64,13312]{1,0:T(8,128)(2,1)}, u32[]{:S(2)}, u32[]{:S(2)}) collective-permute-start(bf16[64,13312]{1,0:T(8,128)(2,1)} %get-tuple-element.24), channel_id=1, source_target_pairs={{0,4},{12,8},{1,5},{13,9},{2,6},{14,10},{3,7},{15,11},{16,20},{28,... | collective-permute-start | bytes 5111816 | tf_op jit(solution)/shard_map/ppermute | solution.py:191
  206.7 27.0 %collective-permute-done.14.refs_5_.refs_6_ = bf16[64,13312]{1,0:T(8,128)(2,1)S(1)} collective-permute-done((bf16[64,13312]{1,0:T(8,128)(2,1)S(1)}, bf16[64,13312]{1,0:T(8,128)(2,1)S(1)}, u32[]{:S(2)}, u32[]{:S(2)}) %collective-permute-start.14) | collective-permute-done | bytes 1703968 | tf_op jit(solution)/shard_map/ppermute | solution.py:191
  239.3 5.4 %copy-done = bf16[2,96,40000]{2,1,0:T(8,128)(2,1)S(1)} copy-done((bf16[2,96,40000]{2,1,0:T(8,128)(2,1)S(1)}, bf16[2,96,40000]{2,1,0:T(8,128)(2,1)}, u32[]{:S(2)}) %copy-start) | copy-done | bytes 15360024
  247.6 6.5 %shard_map.55.refs_3_ = f32[4,64,512]{2,1,0:T(8,128)S(1)} custom-call(s32[2]{0:T(128)S(1)} %pad_add_fusion.place_ref, bf16[192,40000]{1,0:T(8,128)(2,1)S(1)} %bitcast.22, bf16[64,13440]{1,0:T(8,128)(2,1)S(1)} %concatenate.3.refs_0_.refs_4_, bf16[64,13440]{1,0:T(8,128)(2,1)S(1)} %copy-done.2, bf16[64,13440]{1,0:T(8,128)(2,1)S(1)} %copy-done.4, ...), custom_call_target="tpu_custom_call" | custom-call | flops 1000 | bytes 1000 | tf_op jit(solution)/shard_map/pallas_call | solution.py:162
  254.2 5.8 %shard_map.56.refs_2_ = f32[4,64,512]{2,1,0:T(8,128)S(1)} custom-call(s32[2]{0:T(128)S(1)} %pad_add_fusion.place_ref, bf16[192,40000]{1,0:T(8,128)(2,1)S(1)} %bitcast.24, bf16[64,13312]{1,0:T(8,128)(2,1)S(1)} %copy-done.10, bf16[64,13312]{1,0:T(8,128)(2,1)S(1)} %copy-done.18, bf16[64,13312]{1,0:T(8,128)(2,1)S(1)} %copy-done.20, ...), custom_call_target="tpu_custom_call" | custom-call | flops 1000 | bytes 1000 | tf_op jit(solution)/shard_map/pallas_call | solution.py:162
  260.0 4.3 %shard_map.57.refs_2_ = f32[4,64,512]{2,1,0:T(8,128)S(1)} custom-call(s32[2]{0:T(128)S(1)} %pad_add_fusion.place_ref, bf16[192,40000]{1,0:T(8,128)(2,1)S(1)} %bitcast.25, bf16[64,13312]{1,0:T(8,128)(2,1)S(1)} %add_convert_fusion.refs_0_.refs_3_.refs_4_, bf16[64,13312]{1,0:T(8,128)(2,1)} %collective-permute-done.8.refs_1_, f32[4,64,512]{2,1,0:T(8,128)S(1)} %shard_map.56.refs_2_), custom_call_target="tpu_custom_call" | custom-call | flops 1000 | bytes 1000 | tf_op jit(solution)/shard_map/pallas_call | solution.py:162
  264.3 4.9 %shard_map.58.refs_2_ = f32[4,64,512]{2,1,0:T(8,128)S(1)} custom-call(s32[2]{0:T(128)S(1)} %pad_add_fusion.place_ref, bf16[192,40000]{1,0:T(8,128)(2,1)S(1)} %bitcast.26, bf16[64,13440]{1,0:T(8,128)(2,1)S(1)} %copy-done.6, bf16[64,13440]{1,0:T(8,128)(2,1)} %collective-permute-done.11.refs_1_.refs_5_, f32[4,64,512]{2,1,0:T(8,128)S(1)} %shard_map.57.refs_2_, ...), custom_call_target="tpu_custom_call" | custom-call | flops 1000 | bytes 1000 | tf_op jit(solution)/shard_map/pallas_call | solution.py:162
  269.3 5.1 %shard_map.59.refs_6_ = f32[4,64,512]{2,1,0:T(8,128)S(1)} custom-call(s32[2]{0:T(128)S(1)} %pad_add_fusion.place_ref, bf16[192,40000]{1,0:T(8,128)(2,1)S(1)} %bitcast.28, bf16[64,13312]{1,0:T(8,128)(2,1)} %collective-permute-done.1.refs_0_, bf16[64,13312]{1,0:T(8,128)(2,1)} %collective-permute-done.4.refs_1_, f32[4,64,512]{2,1,0:T(8,128)S(1)} %shard_map.58.refs_2_), custom_call_target="tpu_custom_call" | custom-call | flops 1000 | bytes 1000 | tf_op jit(solution)/shard_map/pallas_call | solution.py:162
  274.4 5.5 %shard_map.60.refs_8_ = f32[4,64,512]{2,1,0:T(8,128)S(1)} custom-call(s32[2]{0:T(128)S(1)} %pad_add_fusion.place_ref, bf16[192,40000]{1,0:T(8,128)(2,1)} %bitcast.19, bf16[64,13440]{1,0:T(8,128)(2,1)S(1)} %copy-done.8, bf16[64,13440]{1,0:T(8,128)(2,1)} %collective-permute-done.17.refs_1_.refs_9_, bf16[64,13312]{1,0:T(8,128)(2,1)S(1)} %copy-done.14, ...), custom_call_target="tpu_custom_call" | custom-call | flops 1000 | bytes 1000 | tf_op jit(solution)/shard_map/pallas_call | solution.py:162
  280.0 6.0 %shard_map.61 = (f32[64,512]{1,0:T(8,128)S(1)}, f32[64,512]{1,0:T(8,128)S(1)}, f32[64,512]{1,0:T(8,128)S(1)}, f32[64,512]{1,0:T(8,128)S(1)}) custom-call(s32[2]{0:T(128)S(1)} %pad_add_fusion.place_ref, bf16[192,40000]{1,0:T(8,128)(2,1)} %bitcast.21, bf16[64,13312]{1,0:T(8,128)(2,1)} %collective-permute-done.2.refs_0_, ...), custom_call_target="tpu_custom_call" | custom-call | flops 1000 | bytes 1000 | tf_op jit(solution)/shard_map/pallas_call | solution.py:162
  286.0 9.3 %collective-permute-start.18 = (f32[64,512]{1,0:T(8,128)S(1)}, f32[64,512]{1,0:T(8,128)S(1)}, u32[]{:S(2)}, u32[]{:S(2)}) collective-permute-start(f32[64,512]{1,0:T(8,128)S(1)} %get-tuple-element.26), channel_id=1, source_target_pairs={{0,1},{1,0},{2,3},{3,2},{4,5},{5,4},{6,7},{7,6},{8,9},{9,8},{10,11... | collective-permute-start | bytes 393224 | tf_op jit(solution)/shard_map/ppermute | solution.py:247
  297.0 3.4 collective-permute-done.19
  305.8 16.7 %collective-permute-start.24 = (f32[64]{0:T(128)S(1)}, f32[64]{0:T(128)S(1)}, u32[]{:S(2)}, u32[]{:S(2)}) collective-permute-start(f32[64]{0:T(128)S(1)} %add.48), channel_id=1, source_target_pairs={{0,1},{1,5},{2,9},{3,13},{4,0},{5,4},{6,8},{7,12},{8,3},{9,7},{10,... | collective-permute-start | bytes 776 | tf_op jit(solution)/shard_map/ppermute | solution.py:257
  325.0 4.5 %collective-permute-start.21 = (f32[64,192]{1,0:T(8,128)S(1)}, f32[64,192]{1,0:T(8,128)S(1)}, u32[]{:S(2)}, u32[]{:S(2)}) collective-permute-start(f32[64,192]{1,0:T(8,128)S(1)} %get-tuple-element.38), channel_id=1, source_target_pairs={{0,0},{1,4},{2,8},{3,12},{4,1},{5,5},{6,9},{7,13},{8,2},{9,6},{10,... | collective-permute-start | bytes 147464 | tf_op jit(solution)/shard_map/ppermute | solution.py:253
  333.3 3.6 %collective-permute-done.22 = f32[64,192]{1,0:T(8,128)S(1)} collective-permute-done((f32[64,192]{1,0:T(8,128)S(1)}, f32[64,192]{1,0:T(8,128)S(1)}, u32[]{:S(2)}, u32[]{:S(2)}) %collective-permute-start.22) | collective-permute-done | bytes 49184 | tf_op jit(solution)/shard_map/ppermute | solution.py:253
  (104 shorter events, 51.6 us)
Async XLA Ops:
  5.6 39.4 %collective-permute-start.6 = (bf16[64,13440]{1,0:T(8,128)(2,1)S(1)}, bf16[64,13440]{1,0:T(8,128)(2,1)S(1)}, u32[]{:S(2)}, u32[]{:S(2)}) collective-permute-start(bf16[64,13440]{1,0:T(8,128)(2,1)S(1)} %concatenate.3.refs_0_.refs_4_), channel_id=1, source_target_pairs={{0,4},{4,8},{8,12},{1,5},{5,9},{9,13},{2,6},{6,10},{10,14},{3,7},{... | collective-permute-start | bytes 5160968 | tf_op jit(solution)/shard_map/ppermute | solution.py:191
  8.9 77.8 %collective-permute-start.7 = (bf16[64,13440]{1,0:T(8,128)(2,1)S(1)}, bf16[64,13440]{1,0:T(8,128)(2,1)S(1)}, u32[]{:S(2)}, u32[]{:S(2)}) collective-permute-start(bf16[64,13440]{1,0:T(8,128)(2,1)S(1)} %concatenate.3.refs_0_.refs_4_), channel_id=1, source_target_pairs={{12,8},{8,4},{4,0},{13,9},{9,5},{5,1},{14,10},{10,6},{6,2},{15,11}... | collective-permute-start | bytes 5160968 | tf_op jit(solution)/shard_map/ppermute | solution.py:191
  12.2 69.3 %collective-permute-start = (bf16[64,13312]{1,0:T(8,128)(2,1)S(1)}, bf16[64,13312]{1,0:T(8,128)(2,1)S(1)}, u32[]{:S(2)}, u32[]{:S(2)}) collective-permute-start(bf16[64,13312]{1,0:T(8,128)(2,1)S(1)} %add_convert_fusion.1.refs_0_), channel_id=1, source_target_pairs={{0,4},{4,8},{8,12},{1,5},{5,9},{9,13},{2,6},{6,10},{10,14},{3,7},{... | collective-permute-start | bytes 5111816 | tf_op jit(solution)/shard_map/ppermute | solution.py:191
  16.3 69.1 %collective-permute-start.3 = (bf16[64,13312]{1,0:T(8,128)(2,1)S(1)}, bf16[64,13312]{1,0:T(8,128)(2,1)S(1)}, u32[]{:S(2)}, u32[]{:S(2)}) collective-permute-start(bf16[64,13312]{1,0:T(8,128)(2,1)S(1)} %add_convert_fusion.1.refs_0_), channel_id=1, source_target_pairs={{12,8},{8,4},{4,0},{13,9},{9,5},{5,1},{14,10},{10,6},{6,2},{15,11}... | collective-permute-start | bytes 5111816 | tf_op jit(solution)/shard_map/ppermute | solution.py:191
  45.0 49.5 %collective-permute-start.10 = (bf16[64,13440]{1,0:T(8,128)(2,1)S(1)}, bf16[64,13440]{1,0:T(8,128)(2,1)S(1)}, u32[]{:S(2)}, u32[]{:S(2)}) collective-permute-start(bf16[64,13440]{1,0:T(8,128)(2,1)S(1)} %collective-permute-done.6.refs_1_.refs_5_), channel_id=1, source_target_pairs={{4,8},{8,12},{5,9},{9,13},{6,10},{10,14},{7,11},{11,15},{20,24},{2... | collective-permute-start | bytes 5160968 | tf_op jit(solution)/shard_map/ppermute | solution.py:191
  81.5 83.2 %collective-permute-start.1 = (bf16[64,13312]{1,0:T(8,128)(2,1)S(1)}, bf16[64,13312]{1,0:T(8,128)(2,1)}, u32[]{:S(2)}, u32[]{:S(2)}) collective-permute-start(bf16[64,13312]{1,0:T(8,128)(2,1)S(1)} %collective-permute-done.refs_1_), channel_id=1, source_target_pairs={{4,8},{8,12},{5,9},{9,13},{6,10},{10,14},{7,11},{11,15},{20,24},{2... | collective-permute-start | bytes 5111816 | tf_op jit(solution)/shard_map/ppermute | solution.py:191
  85.4 80.1 %collective-permute-start.4 = (bf16[64,13312]{1,0:T(8,128)(2,1)S(1)}, bf16[64,13312]{1,0:T(8,128)(2,1)}, u32[]{:S(2)}, u32[]{:S(2)}) collective-permute-start(bf16[64,13312]{1,0:T(8,128)(2,1)S(1)} %collective-permute-done.3.refs_2_), channel_id=1, source_target_pairs={{8,4},{4,0},{9,5},{5,1},{10,6},{6,2},{11,7},{7,3},{24,20},{20,16},... | collective-permute-start | bytes 5111816 | tf_op jit(solution)/shard_map/ppermute | solution.py:191
  86.8 81.2 %collective-permute-start.8 = (bf16[64,13312]{1,0:T(8,128)(2,1)S(1)}, bf16[64,13312]{1,0:T(8,128)(2,1)}, u32[]{:S(2)}, u32[]{:S(2)}) collective-permute-start(bf16[64,13312]{1,0:T(8,128)(2,1)S(1)} %add_convert_fusion.refs_0_.refs_3_.refs_4_), channel_id=1, source_target_pairs={{0,4},{12,8},{1,5},{13,9},{2,6},{14,10},{3,7},{15,11},{16,20},{28,... | collective-permute-start | bytes 5111816 | tf_op jit(solution)/shard_map/ppermute | solution.py:191
  93.2 68.3 %collective-permute-start.11 = (bf16[64,13440]{1,0:T(8,128)(2,1)S(1)}, bf16[64,13440]{1,0:T(8,128)(2,1)}, u32[]{:S(2)}, u32[]{:S(2)}) collective-permute-start(bf16[64,13440]{1,0:T(8,128)(2,1)S(1)} %collective-permute-done.7.refs_2_.refs_6_), channel_id=1, source_target_pairs={{8,4},{4,0},{9,5},{5,1},{10,6},{6,2},{11,7},{7,3},{24,20},{20,16},... | collective-permute-start | bytes 5160968 | tf_op jit(solution)/shard_map/ppermute | solution.py:191
  94.5 141.7 %collective-permute-start.16 = (bf16[64,13440]{1,0:T(8,128)(2,1)S(1)}, bf16[64,13440]{1,0:T(8,128)(2,1)S(1)}, u32[]{:S(2)}, u32[]{:S(2)}) collective-permute-start(bf16[64,13440]{1,0:T(8,128)(2,1)S(1)} %collective-permute-done.10.refs_0_.refs_4_), channel_id=1, source_target_pairs={{8,12},{9,13},{10,14},{11,15},{24,28},{25,29},{26,30},{27,31}} | collective-permute-start | bytes 5160968 | tf_op jit(solution)/shard_map/ppermute | solution.py:191
  161.6 35.7 %collective-permute-start.13 = (bf16[64,13312]{1,0:T(8,128)(2,1)S(1)}, bf16[64,13312]{1,0:T(8,128)(2,1)S(1)}, u32[]{:S(2)}, u32[]{:S(2)}) collective-permute-start(bf16[64,13312]{1,0:T(8,128)(2,1)S(1)} %get-tuple-element.22), channel_id=1, source_target_pairs={{0,4},{12,8},{1,5},{13,9},{2,6},{14,10},{3,7},{15,11},{16,20},{28,... | collective-permute-start | bytes 5111816 | tf_op jit(solution)/shard_map/ppermute | solution.py:191
  164.8 38.9 %collective-permute-start.12 = (bf16[64,13312]{1,0:T(8,128)(2,1)S(1)}, bf16[64,13312]{1,0:T(8,128)(2,1)S(1)}, u32[]{:S(2)}, u32[]{:S(2)}) collective-permute-start(bf16[64,13312]{1,0:T(8,128)(2,1)S(1)} %add_convert_fusion.refs_0_.refs_3_.refs_4_), channel_id=1, source_target_pairs={{4,8},{8,4},{5,9},{9,5},{6,10},{10,6},{7,11},{11,7},{20,24},{24,20... | collective-permute-start | bytes 5111816 | tf_op jit(solution)/shard_map/ppermute | solution.py:191
  165.5 68.2 %collective-permute-start.14 = (bf16[64,13312]{1,0:T(8,128)(2,1)S(1)}, bf16[64,13312]{1,0:T(8,128)(2,1)S(1)}, u32[]{:S(2)}, u32[]{:S(2)}) collective-permute-start(bf16[64,13312]{1,0:T(8,128)(2,1)S(1)} %get-tuple-element.23), channel_id=1, source_target_pairs={{0,4},{12,8},{1,5},{13,9},{2,6},{14,10},{3,7},{15,11},{16,20},{28,... | collective-permute-start | bytes 5111816 | tf_op jit(solution)/shard_map/ppermute | solution.py:191
  168.0 106.4 %collective-permute-start.17 = (bf16[64,13440]{1,0:T(8,128)(2,1)}, bf16[64,13440]{1,0:T(8,128)(2,1)}, u32[]{:S(2)}, u32[]{:S(2)}) collective-permute-start(bf16[64,13440]{1,0:T(8,128)(2,1)} %collective-permute-done.11.refs_1_.refs_5_), channel_id=1, source_target_pairs={{4,0},{5,1},{6,2},{7,3},{20,16},{21,17},{22,18},{23,19}} | collective-permute-start | bytes 5160968 | tf_op jit(solution)/shard_map/ppermute | solution.py:191
  198.4 81.6 %collective-permute-start.15 = (bf16[64,13312]{1,0:T(8,128)(2,1)}, bf16[64,13312]{1,0:T(8,128)(2,1)}, u32[]{:S(2)}, u32[]{:S(2)}) collective-permute-start(bf16[64,13312]{1,0:T(8,128)(2,1)} %get-tuple-element.24), channel_id=1, source_target_pairs={{0,4},{12,8},{1,5},{13,9},{2,6},{14,10},{3,7},{15,11},{16,20},{28,... | collective-permute-start | bytes 5111816 | tf_op jit(solution)/shard_map/ppermute | solution.py:191
  204.9 75.1 %collective-permute-start.2 = (bf16[64,13312]{1,0:T(8,128)(2,1)}, bf16[64,13312]{1,0:T(8,128)(2,1)}, u32[]{:S(2)}, u32[]{:S(2)}) collective-permute-start(bf16[64,13312]{1,0:T(8,128)(2,1)} %collective-permute-done.1.refs_0_), channel_id=1, source_target_pairs={{8,12},{9,13},{10,14},{11,15},{24,28},{25,29},{26,30},{27,31}} | collective-permute-start | bytes 5111816 | tf_op jit(solution)/shard_map/ppermute | solution.py:191
  234.9 45.1 %collective-permute-start.5 = (bf16[64,13312]{1,0:T(8,128)(2,1)}, bf16[64,13312]{1,0:T(8,128)(2,1)}, u32[]{:S(2)}, u32[]{:S(2)}) collective-permute-start(bf16[64,13312]{1,0:T(8,128)(2,1)} %collective-permute-done.4.refs_1_), channel_id=1, source_target_pairs={{4,0},{5,1},{6,2},{7,3},{20,16},{21,17},{22,18},{23,19}} | collective-permute-start | bytes 5111816 | tf_op jit(solution)/shard_map/ppermute | solution.py:191
  237.4 42.6 %collective-permute-start.9 = (bf16[64,13312]{1,0:T(8,128)(2,1)}, bf16[64,13312]{1,0:T(8,128)(2,1)}, u32[]{:S(2)}, u32[]{:S(2)}) collective-permute-start(bf16[64,13312]{1,0:T(8,128)(2,1)} %collective-permute-done.8.refs_1_), channel_id=1, source_target_pairs={{4,8},{8,4},{5,9},{9,5},{6,10},{10,6},{7,11},{11,7},{20,24},{24,20... | collective-permute-start | bytes 5111816 | tf_op jit(solution)/shard_map/ppermute | solution.py:191
  286.0 11.0 %collective-permute-start.18 = (f32[64,512]{1,0:T(8,128)S(1)}, f32[64,512]{1,0:T(8,128)S(1)}, u32[]{:S(2)}, u32[]{:S(2)}) collective-permute-start(f32[64,512]{1,0:T(8,128)S(1)} %get-tuple-element.26), channel_id=1, source_target_pairs={{0,1},{1,0},{2,3},{3,2},{4,5},{5,4},{6,7},{7,6},{8,9},{9,8},{10,11... | collective-permute-start | bytes 393224 | tf_op jit(solution)/shard_map/ppermute | solution.py:247
  303.5 26.0 %collective-permute-start.23 = (f32[64]{0:T(128)S(1)}, f32[64]{0:T(128)S(1)}, u32[]{:S(2)}, u32[]{:S(2)}) collective-permute-start(f32[64]{0:T(128)S(1)} %add.48), channel_id=1, source_target_pairs={{0,0},{1,4},{2,8},{3,12},{4,1},{5,5},{6,9},{7,13},{8,2},{9,6},{10,... | collective-permute-start | bytes 776 | tf_op jit(solution)/shard_map/ppermute | solution.py:257
  305.8 25.0 %collective-permute-start.24 = (f32[64]{0:T(128)S(1)}, f32[64]{0:T(128)S(1)}, u32[]{:S(2)}, u32[]{:S(2)}) collective-permute-start(f32[64]{0:T(128)S(1)} %add.48), channel_id=1, source_target_pairs={{0,1},{1,5},{2,9},{3,13},{4,0},{5,4},{6,8},{7,12},{8,3},{9,7},{10,... | collective-permute-start | bytes 776 | tf_op jit(solution)/shard_map/ppermute | solution.py:257
  322.5 8.3 %collective-permute-start.25 = (f32[64]{0:T(128)S(1)}, f32[64]{0:T(128)S(1)}, u32[]{:S(2)}, u32[]{:S(2)}) collective-permute-start(f32[64]{0:T(128)S(1)} %add.48), channel_id=1, source_target_pairs={{0,2},{1,6},{2,10},{3,14},{4,3},{5,7},{6,11},{7,15},{8,0},{9,4},{1... | collective-permute-start | bytes 776 | tf_op jit(solution)/shard_map/ppermute | solution.py:257
  322.5 8.3 %collective-permute-start.26 = (f32[64]{0:T(128)S(1)}, f32[64]{0:T(128)S(1)}, u32[]{:S(2)}, u32[]{:S(2)}) collective-permute-start(f32[64]{0:T(128)S(1)} %add.48), channel_id=1, source_target_pairs={{0,3},{1,7},{2,11},{3,15},{4,2},{5,6},{6,10},{7,14},{8,1},{9,5},{1... | collective-permute-start | bytes 776 | tf_op jit(solution)/shard_map/ppermute | solution.py:257
  325.0 8.3 %collective-permute-start.21 = (f32[64,192]{1,0:T(8,128)S(1)}, f32[64,192]{1,0:T(8,128)S(1)}, u32[]{:S(2)}, u32[]{:S(2)}) collective-permute-start(f32[64,192]{1,0:T(8,128)S(1)} %get-tuple-element.38), channel_id=1, source_target_pairs={{0,0},{1,4},{2,8},{3,12},{4,1},{5,5},{6,9},{7,13},{8,2},{9,6},{10,... | collective-permute-start | bytes 147464 | tf_op jit(solution)/shard_map/ppermute | solution.py:253
  (26 other events, 261.9 us)

commit v4 on v2

v4 whole, which is shorter than its diff:
```python
import jax
import jax.numpy as jnp
from jax import lax
from jax.experimental import pallas as pl
from jax.experimental.pallas import tpu as pltpu
from jax.sharding import PartitionSpec as P

SITES = ("narrow", "sub")
ALL = ("wide", "narrow", "sub")


def dot_t(a, b):
    return lax.dot_general(a, b, (((1,), (1,)), ((), ())), preferred_element_type=jnp.float32)


def potential_of(noise, volts, labels):
    value = volts[:, 0:1]
    for kind in range(1, volts.shape[1]):
        value = jnp.where(labels[None, :] == kind, volts[:, kind:kind + 1], value)
    return (value + noise.astype(jnp.float32)).astype(jnp.bfloat16)


def finish(charges, total, weight_sum, profile):
    return charges - profile[:, :, None] * (total / weight_sum)[None, None, :]


def gather_plan(slab, noise, volts, labels, profile, sizes):
    wide, owners = sizes
    panels, rows, _ = slab.shape
    frames = noise.shape[0]
    pot = lax.all_gather(potential_of(noise, volts, labels), "wide", axis=0, tiled=True)
    part = dot_t(slab.reshape(panels * rows, -1), pot).reshape(panels, rows, wide, frames)
    mine = lax.all_to_all(part, "wide", 2, 1, tiled=True).reshape(panels, wide * rows, frames)
    charges = lax.psum_scatter(mine, SITES, scatter_dimension=1, tiled=True)
    total, weight_sum = lax.psum((jnp.sum(charges, axis=(0, 1)), jnp.sum(profile)), SITES)
    return finish(charges, total, weight_sum, profile)


LANES = 128
STEPS = 4
WIDTH = 4 * LANES
FREE = LANES * 2 - 1
PARAMS = pltpu.CompilerParams(vmem_limit_bytes=56 * 1024 * 1024)
SMALL = pl.CostEstimate(flops=1000, bytes_accessed=1000, transcendentals=0)


def always(z):
    return z >= 0


def is_mid(z):
    return (z == 1) | (z == 2)


def is_end(z):
    return (z == 0) | (z == 3)


def dot(a, b):
    return lax.dot_general(a, b, (((1,), (1,)), ((), ())), preferred_element_type=jnp.float32)


def first_potential(noise, volts, labels, third):
    frames, sites = noise.shape
    tile = third // STEPS
    rest = sites - 3 * third
    rest_width = rest + -rest % LANES
    labels = labels.reshape(1, sites)

    def kernel(noise_ref, labels_ref, volts_ref, noise_rest, labels_rest, out):
        def potential(noise, labels):
            value = jnp.broadcast_to(volts_ref[:, 0:1], noise.shape)
            for kind in range(1, volts_ref.shape[1]):
                value = jnp.where(labels == kind, volts_ref[:, kind:kind + 1], value)
            return value + noise.astype(jnp.float32)

        step = pl.program_id(0)
        at = pl.multiple_of(step * tile, LANES)
        out[:, pl.ds(at, tile)] = potential(noise_ref[...], labels_ref[...]).astype(jnp.bfloat16)

        @pl.when(step == 0)
        def _():
            column = lax.broadcasted_iota(jnp.int32, (frames, rest_width), 1)
            value = jnp.where(column < rest, potential(noise_rest[...], labels_rest[...]), 0.0)
            out[:, third:] = value.astype(jnp.bfloat16)

    last = 3 * third // rest_width
    return pl.pallas_call(
        kernel,
        grid=(STEPS,),
        in_specs=[
            pl.BlockSpec((frames, tile), lambda i: (0, i)),
            pl.BlockSpec((1, tile), lambda i: (0, i)),
            pl.BlockSpec(volts.shape, lambda i: (0, 0)),
            pl.BlockSpec((frames, rest_width), lambda i: (0, last)),
            pl.BlockSpec((1, rest_width), lambda i: (0, last)),
        ],
        out_specs=pl.BlockSpec((frames, third + rest_width), lambda i: (0, 0)),
        out_shape=jax.ShapeDtypeStruct((frames, third + rest_width), jnp.bfloat16),
        compiler_params=PARAMS,
        cost_estimate=SMALL,
    )(noise, labels, volts, noise, labels)


def route(place, sources, to_right, to_left, shape, tokens):
    arrays = [s[0] for s in sources]
    count = len(arrays)

    def kernel(place_ref, *refs):
        outs, sems = refs[count + len(tokens):-1], refs[-1]
        z = place_ref[0]
        for here in range(4):
            @pl.when(z == here)
            def _(here=here):
                copies = []
                for side, choice in enumerate((to_right[here], to_left[here])):
                    if choice is None:
                        continue
                    number, columns = choice
                    _, row, rows, column = sources[number]
                    copies.append(pltpu.make_async_copy(
                        refs[number].at[pl.ds(row, rows), pl.ds(column, columns)],
                        outs[side].at[pl.ds(0, rows), pl.ds(0, columns)], sems.at[side]))
                for copy in copies:
                    copy.start()
                for copy in copies:
                    copy.wait()

    anywhere = pl.BlockSpec(memory_space=pl.ANY)
    return pl.pallas_call(
        kernel,
        in_specs=[pl.BlockSpec(memory_space=pltpu.SMEM)] + [anywhere] * (count + len(tokens)),
        out_specs=[anywhere] * 2,
        out_shape=[jax.ShapeDtypeStruct(shape, jnp.bfloat16)] * 2,
        scratch_shapes=[pltpu.SemaphoreType.DMA((2,))],
        compiler_params=PARAMS,
        cost_estimate=SMALL,
    )(place, *arrays, *tokens)


def absorb(place, whole, streams, work, sums_shape, sums, first=None, profile=None):
    tile = whole // STEPS
    names = list(streams)
    slab = streams["slab"][0]
    nrows, sites = slab.shape
    rest = sites - 3 * whole
    rest_width = rest + -rest % LANES
    long = [n for n in names if streams[n][0].shape[1] == whole + rest_width] if first else []
    blocks, frames, width = sums_shape

    def kernel(place_ref, *refs):
        tiles = dict(zip(names, refs))
        refs = refs[len(names):]
        if sums is not None:
            sums_ref, refs = refs[0], refs[1:]
        if first:
            slab_rest, refs = refs[0], refs[1:]
            rests = dict(zip(long, refs))
            refs = refs[len(long):]
        if profile is None:
            acc, = refs
        else:
            profile_ref, outs, acc = refs[0], refs[1:-1], refs[-1]
        z, k = place_ref[0], place_ref[1]
        step = pl.program_id(0)

        def add(block, lane, value):
            acc[block, :, lane:lane + value.shape[1]] += value

        @pl.when(step == 0)
        def _():
            acc[...] = jnp.zeros(acc.shape, acc.dtype) if sums is None else sums_ref[...]
            if first:
                column = lax.broadcasted_iota(jnp.int32, (nrows, rest_width), 1)
                piece = jnp.where(column < rest, slab_rest[...].astype(jnp.float32), 0.0).astype(jnp.bfloat16)
                first(z, dict(rests, slab=piece), add)

        work(z, tiles, add)

        if profile is not None:
            @pl.when(step == STEPS - 1)
            def _():
                weight = jnp.sum(profile_ref[...])
                lane = lax.broadcasted_iota(jnp.int32, (frames, LANES), 1)
                for turn, out in enumerate(outs):
                    out[:, :width - LANES] = acc[k ^ turn, :, :width - LANES]
                    end = acc[k ^ turn, :, width - LANES:]
                    out[:, width - LANES:] = jnp.where(lane == LANES - 2, weight, end)

    def spec(array, needed, third):
        return pl.BlockSpec(
            (array.shape[0], tile), lambda i, s: (0, third(s[0]) * STEPS + jnp.where(needed(s[0]), i, 0)))

    in_specs = [spec(*streams[n]) for n in names]
    operands = [streams[n][0] for n in names]
    if sums is not None:
        in_specs.append(pl.BlockSpec(sums_shape, lambda i, s: (0, 0, 0)))
        operands.append(sums)
    if first:
        in_specs.append(pl.BlockSpec((nrows, rest_width), lambda i, s: (0, 3 * whole // rest_width)))
        in_specs += [pl.BlockSpec((frames, rest_width), lambda i, s: (0, whole // rest_width))] * len(long)
        operands += [slab] + [streams[n][0] for n in long]
    if profile is None:
        out_shape = jax.ShapeDtypeStruct(sums_shape, jnp.float32)
        out_specs = pl.BlockSpec(sums_shape, lambda i, s: (0, 0, 0))
        scratch = []
    else:
        in_specs.append(pl.BlockSpec(profile.shape, lambda i, s: (0, 0)))
        operands.append(profile)
        out_shape = [jax.ShapeDtypeStruct(sums_shape[1:], jnp.float32)] * blocks
        out_specs = [pl.BlockSpec(sums_shape[1:], lambda i, s: (0, 0))] * blocks
        scratch = [pltpu.VMEM(sums_shape, jnp.float32)]
    return pl.pallas_call(
        kernel,
        grid_spec=pltpu.PrefetchScalarGridSpec(
            num_scalar_prefetch=1, grid=(STEPS,), in_specs=in_specs, out_specs=out_specs, scratch_shapes=scratch),
        out_shape=out_shape,
        compiler_params=PARAMS,
        cost_estimate=SMALL,
    )(place, *operands)


def line_plan(slab, noise, volts, labels, profile, sizes):
    wide, owners = sizes
    panels, rows, sites = slab.shape
    frames = noise.shape[0]
    nrows = panels * rows
    part = nrows // 3
    third = sites // 3 // LANES * LANES
    z = lax.axis_index("wide")
    k = lax.axis_index(SITES)
    place = jnp.stack([z, k]).astype(jnp.int32)
    slab = slab.reshape(nrows, sites)
    right = [(0, 1), (1, 2), (2, 3)]
    left = [(3, 2), (2, 1), (1, 0)]

    def send(pair):
        return lax.ppermute(pair[0], "wide", right), lax.ppermute(pair[1], "wide", left)

    def potential_at(first, end, before):
        small = lax.optimization_barrier((volts, before))[0]
        return potential_of(noise[:, first:end], small, labels[first:end])

    def mirror(choice):
        swap = {0: 0, 1: 2, 2: 1, 3: 4, 4: 3}
        return [None if c is None else (swap[c[0]], c[1]) for c in reversed(choice)]

    def routed(sources, choice, width, tokens):
        sources = [s if isinstance(s, tuple) else (s, 0, frames, 0) for s in sources]
        return send(route(place, sources, choice, mirror(choice), (frames, width), tokens))

    def spare(i):
        return (slab, part * i, part, 2 * third)

    own_a = first_potential(noise, volts, labels, third)
    long = own_a.shape[1]
    r1 = send((own_a, own_a))
    own_b = potential_at(third, 2 * third, own_a)
    r2 = send((own_b, own_b))
    own_c = potential_at(2 * third, 3 * third, own_b)

    sums_shape = (wide, frames, WIDTH)

    def at(number):
        return lambda z: number

    def thirds(end, mid):
        return lambda z: jnp.where(is_mid(z), mid, end)

    def from_left(z):
        return z >= 1

    def from_right(z):
        return z <= 2

    def far(z, refs, name):
        return jnp.where(z < 2, refs[name + "l"][...], refs[name + "r"][...])

    def near(z, refs, name):
        return jnp.where(z < 2, refs[name + "r"][...], refs[name + "l"][...])

    def both(name, pair, right_needed=from_left, left_needed=from_right):
        return {name + "r": (pair[0], right_needed, at(0)), name + "l": (pair[1], left_needed, at(0))}

    def work1(z, refs, add):
        add(z, 0, dot(refs["own"][...], refs["slab"][...]))

        @pl.when(z >= 1)
        def _():
            add(z - 1, 0, dot(refs["r"][...], refs["slab"][...]))

        @pl.when(z <= 2)
        def _():
            add(z + 1, 0, dot(refs["l"][...], refs["slab"][...]))

    def work3(z, refs, add):
        add(z, 0, dot(refs["own"][...], refs["slab2"][...]))
        add((z + 2) % 4, 0, dot(far(z, refs, ""), refs["slab"][...]))

        @pl.when(is_mid(z))
        def _():
            add(jnp.where(z < 2, 0, 3), 0, dot(near(z, refs, ""), refs["slab2"][...]))

    def work4(z, refs, add):
        add((z + 2) % 4, 0, dot(far(z, refs, ""), refs["slab"][...]))

    def work5(z, refs, add):
        came = far(z, refs, "")
        add(3 - z, 0, dot(came, refs["slab"][...]))

        @pl.when(is_mid(z))
        def _():
            brought = jnp.concatenate([near(z, refs, "4"), near(z, refs, "")], axis=0)
            add(z, 2 * LANES, dot(refs["own"][...], brought))
            add(3 - z, 2 * LANES, dot(came, brought))

    def first5(z, refs, add):
        @pl.when(is_end(z))
        def _():
            add(3 - z, 0, dot(far(z, refs, ""), refs["slab"]))

    def work6(z, refs, add):
        came = far(z, refs, "")
        block = jnp.where(z < 2, 3, 0)
        add(block, 0, dot(came, refs["slab"][...]))

        @pl.when(is_mid(z))
        def _():
            newest = near(z, refs, "")
            brought = jnp.concatenate([near(z, refs, "4"), near(z, refs, "5"), newest], axis=0)
            add(block, 2 * LANES, dot(came, brought))
            add(z, 3 * LANES, dot(refs["own"][...], newest))
            add(3 - z, 3 * LANES, dot(far(z, refs, "5"), newest))

    def near_right(z):
        return z == 1

    def near_left(z):
        return z == 2

    r3 = routed([own_c, r1[0], r1[1]], [(0, third), (1, long), (1, long), None], long, [])
    r4 = routed([spare(0), r2[0], r2[1]], [(0, third), (1, third), (1, third), None], third, [])
    sums = absorb(
        place, third, dict(both("", r1), slab=(slab, always, at(0)), own=(own_a, always, at(0))), work1, sums_shape, None,
        first=lambda z, refs, add: work1(z, refs, add))
    sums = absorb(
        place, third, dict(both("", r2), slab=(slab, always, at(1)), own=(own_b, always, at(0))), work1, sums_shape, sums)
    r5 = routed([spare(1), r3[0], r3[1], own_c, own_c], [(0, third), (3, third), (1, long), None], long, [sums])
    sums = absorb(
        place, third,
        dict(both("", r3), slab=(slab, always, at(0)), slab2=(slab, always, at(2)), own=(own_c, always, at(0))),
        work3, sums_shape, sums, first=lambda z, refs, add: add((z + 2) % 4, 0, dot(far(z, refs, ""), refs["slab"])))
    r6 = routed([spare(2), r3[0], r3[1], r4[0], r4[1]], [(0, third), (1, third), (3, third), None], third, [sums])
    sums = absorb(place, third, dict(both("", r4), slab=(slab, always, at(1))), work4, sums_shape, sums)
    middle = dict(both("4", r4, near_right, near_left), own=(own_c, is_mid, at(0)))
    sums = absorb(
        place, third, dict(both("", r5), slab=(slab, always, thirds(0, 2)), **middle), work5, sums_shape, sums, first=first5)
    messages = absorb(
        place, third, dict(both("", r6), slab=(slab, always, thirds(1, 2)), **both("5", r5, is_mid, is_mid), **middle),
        work6, sums_shape, sums, profile=profile)

    summed = messages[0]
    for turn in range(1, owners):
        summed += lax.ppermute(messages[turn], SITES, [(i, i ^ turn) for i in range(owners)])
    weight_sum = summed[0, WIDTH - 2]
    half = WIDTH // 2
    frame_sum = jnp.sum(summed[:, :nrows], axis=1) + jnp.sum(summed[:, half:half + nrows], axis=1)
    lane = jnp.arange(half)
    mine, extra = (jnp.where(lane[None, :] == FREE, frame_sum[:, None], x) for x in (summed[:, :half], summed[:, half:]))
    def flip(turn):
        return [(a * owners + b, b * owners + (a ^ turn)) for a in range(wide) for b in range(owners)]

    mine, extra = lax.ppermute(mine, ALL, flip(0)), lax.ppermute(extra, ALL, flip(1))
    total = mine[:, FREE] + extra[:, FREE] + lax.ppermute(frame_sum, ALL, flip(2)) + lax.ppermute(frame_sum, ALL, flip(3))
    charges = (mine + extra)[:, :nrows].reshape(frames, panels, rows).transpose(1, 2, 0)
    return finish(charges, total, weight_sum, profile)


def solution(mesh):
    wide = mesh.shape["wide"]
    owners = mesh.shape["narrow"] * mesh.shape["sub"]
    plan = line_plan if wide == owners == 4 else gather_plan

    def local(slab, noise, volts, labels, profile):
        return plan(slab, noise, volts, labels, profile, (wide, owners))

    return jax.shard_map(
        local,
        mesh=mesh,
        in_specs=(
            P(None, "wide", ("narrow", "sub")),
            P(("grp", "wide"), ("narrow", "sub")),
            P(("grp", "wide"), None),
            P(("narrow", "sub")),
            P(None, ("narrow", "sub")),
        ),
        out_specs=P(None, ("narrow", "sub"), ("grp", "wide")),
        check_vma=False,
    )
```

time: 326 us -> 607 us (1.86)
  Pallas kernels: 0 us -> 265 us
  starting transfers between devices: 65.7 us -> 262 us
  waiting for transfers between devices: 141 us -> 52.6 us
  matrix products: 84.8 us -> 0 us
  blocking collectives: 7.88 us -> 0 us
    pallas_call x0 -> x11, Pallas kernels: none -> 265 us  [the longest x4 214 us: route(): pl.pallas_call(kernel, in_specs=[pl.BlockSpec(memory_space=pltpu.SMEM)] +...]
    ppermute x20 -> x19, starting transfers between devices: 65.7 us -> 262 us  [the longest x6 237 us: send(): lax.ppermute(pair[0], 'wide', right)]
    ppermute x20 -> x19, waiting for transfers between devices: 141 us -> 52.6 us  [the longest x6 36 us: send(): lax.ppermute(pair[0], 'wide', right)]
    dot_general x13 -> x0, matrix products: 84.8 us -> none  [dot_t(): lax.dot_general(a, b, (((1,), (1,)), ((), ())), preferred_element_type=jn...]
    unnamed x20 -> x27, local copies, waits for them, and re-layouts: 0.05 us -> 11.2 us
    optimization_barrier x2 -> x0, local copies, waits for them, and re-layouts: 8.03 us -> none  [line_plan(): lax.optimization_barrier((f2_r, f2_l, g0, h1, own2, spare23))]
    psum x1 -> x0, blocking collectives: 7.88 us -> none  [line_plan(): weight_sum = lax.psum(jnp.sum(profile), SITES)]
  transfers between devices with their start and end apart: 20 -> 19, of which waited for: 11 -> 8; matrix products, arithmetic and copies ran while one was open for 21% -> 1% of each run, Pallas kernels for 0% -> 42%
where the time goes in v4:
time: 607 us; the launch traced here: 603 us
  Pallas kernels  265 us (44%)
  starting transfers between devices  262 us (43%)
  waiting for transfers between devices  52.6 us (9%)
  local copies, waits for them, and re-layouts  13.6 us (2%)
  other arithmetic  9.62 us (2%)
    ppermute x6, starting transfers between devices, send(): lax.ppermute(pair[0], 'wide', right)  237 us
    pallas_call x4, Pallas kernels, route(): pl.pallas_call(kernel, in_specs=[pl.BlockSpec(memory_space=pltpu.SMEM)] +...  214 us
    pallas_call x6, Pallas kernels, absorb(): pl.pallas_call(kernel, grid_spec=pltpu.PrefetchScalarGridSpec(num_scalar_...  47.1 us
    ppermute x6, waiting for transfers between devices, send(): lax.ppermute(pair[0], 'wide', right)  36 us
  transfers between devices with their start and end apart: 19, of which 8 were waited for; matrix products, arithmetic and copies ran while one was open for 1% of the time, Pallas kernels for 42%

profile of v4, /device:TPU:3, one launch (start us, length us, event | category | flops | bytes accessed | tf_op | source)
XLA Modules:
  0.0 602.9 jit_solution(9529684960962331227)
XLA Ops:
  3.1 4.0 shard_map.55.refs_3_.refs_7_
  7.1 3.3 collective-permute-start
  14.9 5.2 collective-permute-start.4
  25.2 21.6 %collective-permute-done.refs_1_.refs_0_.refs_5_ = bf16[64,13440]{1,0:T(8,128)(2,1)S(1)} collective-permute-done((bf16[64,13440]{1,0:T(8,128)(2,1)}, bf16[64,13440]{1,0:T(8,128)(2,1)S(1)}, u32[]{:S(2)}, u32[]{:S(2)}) %collective-permute-start) | collective-permute-done | bytes 1720352 | tf_op jit(solution)/shard_map/ppermute | solution.py:238
  46.8 3.8 collective-permute-done.1.refs_2_.refs_1_.refs_6_
  51.9 53.4 %shard_map.56 = (bf16[64,13440]{1,0:T(8,128)(2,1)}, bf16[64,13440]{1,0:T(8,128)(2,1)}) custom-call(s32[2]{0:T(128)} %pad_add_fusion.place_ref, bf16[64,13312]{1,0:T(8,128)(2,1)} %add_convert_fusion.refs_0_.refs_4_.refs_3_.refs_5_.refs_7_, bf16[64,13440]{1,0:T(8,128)(2,1)} %copy-done.6, bf16[64,13440]{1,0:T(8,128)(2,1)} %copy-done.7), custom_call_target="tpu_custom_call" | custom-call | flops 1000 | bytes 1000 | tf_op jit(solution)/shard_map/pallas_call | solution.py:130
  105.3 55.9 %collective-permute-start.2 = (bf16[64,13440]{1,0:T(8,128)(2,1)}, bf16[64,13440]{1,0:T(8,128)(2,1)S(1)}, u32[]{:S(2)}, u32[]{:S(2)}) collective-permute-start(bf16[64,13440]{1,0:T(8,128)(2,1)} %get-tuple-element.21), channel_id=1, source_target_pairs={{0,4},{4,8},{8,12},{1,5},{5,9},{9,13},{2,6},{6,10},{10,14},{3,7},{... | collective-permute-start | bytes 5160968 | tf_op jit(solution)/shard_map/ppermute | solution.py:238
  162.6 53.4 %shard_map.57 = (bf16[64,13312]{1,0:T(8,128)(2,1)}, bf16[64,13312]{1,0:T(8,128)(2,1)}) custom-call(s32[2]{0:T(128)} %pad_add_fusion.place_ref, bf16[192,40000]{1,0:T(8,128)(2,1)} %bitcast.14, bf16[64,13312]{1,0:T(8,128)(2,1)} %collective-permute-done.4.refs_1_.refs_0_, bf16[64,13312]{1,0:T(8,128)(2,1)} %collective-permute-done.5.refs_2_.refs_1_), custom_call_target="tpu_custom_call" | custom-call | flops 1000 | bytes 1000 | tf_op jit(solution)/shard_map/pallas_call | solution.py:130
  216.0 55.7 %collective-permute-start.6 = (bf16[64,13312]{1,0:T(8,128)(2,1)}, bf16[64,13312]{1,0:T(8,128)(2,1)S(1)}, u32[]{:S(2)}, u32[]{:S(2)}) collective-permute-start(bf16[64,13312]{1,0:T(8,128)(2,1)} %get-tuple-element.23), channel_id=1, source_target_pairs={{0,4},{4,8},{8,12},{1,5},{5,9},{9,13},{2,6},{6,10},{10,14},{3,7},{... | collective-permute-start | bytes 5111816 | tf_op jit(solution)/shard_map/ppermute | solution.py:238
  273.0 8.6 %shard_map.58.refs_4_ = f32[4,64,512]{2,1,0:T(8,128)} custom-call(s32[2]{0:T(128)} %pad_add_fusion.place_ref, bf16[64,13440]{1,0:T(8,128)(2,1)} %copy-done.6, bf16[64,13440]{1,0:T(8,128)(2,1)} %copy-done.7, bf16[192,40000]{1,0:T(8,128)(2,1)} %bitcast.15, bf16[64,13440]{1,0:T(8,128)(2,1)} %shard_map.55.refs_3_.refs_7_, bf16[192,40000]{1,0:T(8,128)(2,1)} %bitcast.16, ...), custom_call_target="tpu_custom_call" | custom-call | flops 1000 | bytes 1000 | tf_op jit(solution)/shard_map/pallas_call | solution.py:213
  281.6 8.3 %shard_map.59.refs_5_ = f32[4,64,512]{2,1,0:T(8,128)} custom-call(s32[2]{0:T(128)} %pad_add_fusion.place_ref, bf16[64,13312]{1,0:T(8,128)(2,1)} %collective-permute-done.4.refs_1_.refs_0_, bf16[64,13312]{1,0:T(8,128)(2,1)} %collective-permute-done.5.refs_2_.refs_1_, bf16[192,40000]{1,0:T(8,128)(2,1)} %bitcast.17, ...), custom_call_target="tpu_custom_call" | custom-call | flops 1000 | bytes 1000 | tf_op jit(solution)/shard_map/pallas_call | solution.py:213
  292.3 53.4 %shard_map.62 = (bf16[64,13440]{1,0:T(8,128)(2,1)}, bf16[64,13440]{1,0:T(8,128)(2,1)}) custom-call(s32[2]{0:T(128)} %pad_add_fusion.place_ref, bf16[192,40000]{1,0:T(8,128)(2,1)} %bitcast.18, bf16[64,13440]{1,0:T(8,128)(2,1)} %copy-done, bf16[64,13440]{1,0:T(8,128)(2,1)} %copy-done.1, ...), custom_call_target="tpu_custom_call" | custom-call | flops 1000 | bytes 1000 | tf_op jit(solution)/shard_map/pallas_call | solution.py:130
  345.7 59.8 %collective-permute-start.10 = (bf16[64,13440]{1,0:T(8,128)(2,1)}, bf16[64,13440]{1,0:T(8,128)(2,1)S(1)}, u32[]{:S(2)}, u32[]{:S(2)}) collective-permute-start(bf16[64,13440]{1,0:T(8,128)(2,1)} %get-tuple-element.27), channel_id=1, source_target_pairs={{0,4},{4,8},{8,12},{1,5},{5,9},{9,13},{2,6},{6,10},{10,14},{3,7},{... | collective-permute-start | bytes 5160968 | tf_op jit(solution)/shard_map/ppermute | solution.py:238
  406.8 9.1 %shard_map.60.refs_5_.refs_3_ = f32[4,64,512]{2,1,0:T(8,128)} custom-call(s32[2]{0:T(128)} %pad_add_fusion.place_ref, bf16[64,13440]{1,0:T(8,128)(2,1)} %copy-done, bf16[64,13440]{1,0:T(8,128)(2,1)} %copy-done.1, bf16[192,40000]{1,0:T(8,128)(2,1)} %bitcast.19, bf16[192,40000]{1,0:T(8,128)(2,1)} %bitcast.20, ...), custom_call_target="tpu_custom_call" | custom-call | flops 1000 | bytes 1000 | tf_op jit(solution)/shard_map/pallas_call | solution.py:213
  418.3 53.4 %shard_map.61 = (bf16[64,13312]{1,0:T(8,128)(2,1)}, bf16[64,13312]{1,0:T(8,128)(2,1)}) custom-call(s32[2]{0:T(128)} %pad_add_fusion.place_ref, bf16[192,40000]{1,0:T(8,128)(2,1)} %bitcast.22, bf16[64,13440]{1,0:T(8,128)(2,1)} %copy-done, bf16[64,13440]{1,0:T(8,128)(2,1)} %copy-done.1, bf16[64,13312]{1,0:T(8,128)(2,1)} %copy-done.2, ...), custom_call_target="tpu_custom_call" | custom-call | flops 1000 | bytes 1000 | tf_op jit(solution)/shard_map/pallas_call | solution.py:130
  471.7 57.3 %collective-permute-start.8 = (bf16[64,13312]{1,0:T(8,128)(2,1)}, bf16[64,13312]{1,0:T(8,128)(2,1)S(1)}, u32[]{:S(2)}, u32[]{:S(2)}) collective-permute-start(bf16[64,13312]{1,0:T(8,128)(2,1)} %get-tuple-element.25), channel_id=1, source_target_pairs={{0,4},{4,8},{8,12},{1,5},{5,9},{9,13},{2,6},{6,10},{10,14},{3,7},{... | collective-permute-start | bytes 5111816 | tf_op jit(solution)/shard_map/ppermute | solution.py:238
  530.4 6.4 %shard_map.63.refs_6_ = f32[4,64,512]{2,1,0:T(8,128)} custom-call(s32[2]{0:T(128)} %pad_add_fusion.place_ref, bf16[64,13312]{1,0:T(8,128)(2,1)} %copy-done.2, bf16[64,13312]{1,0:T(8,128)(2,1)} %copy-done.3, bf16[192,40000]{1,0:T(8,128)(2,1)} %bitcast.23, f32[4,64,512]{2,1,0:T(8,128)} %shard_map.60.refs_5_.refs_3_), custom_call_target="tpu_custom_call" | custom-call | flops 1000 | bytes 1000 | tf_op jit(solution)/shard_map/pallas_call | solution.py:213
  539.2 7.2 %shard_map.64.refs_8_ = f32[4,64,512]{2,1,0:T(8,128)} custom-call(s32[2]{0:T(128)} %pad_add_fusion.place_ref, bf16[64,13440]{1,0:T(8,128)(2,1)} %copy-done.4, bf16[64,13440]{1,0:T(8,128)(2,1)} %copy-done.5, bf16[192,40000]{1,0:T(8,128)(2,1)} %bitcast.24, bf16[64,13312]{1,0:T(8,128)(2,1)} %copy-done.2, bf16[64,13312]{1,0:T(8,128)(2,1)} %copy-done.3, ...), custom_call_target="tpu_custom_call" | custom-call | flops 1000 | bytes 1000 | tf_op jit(solution)/shard_map/pallas_call | solution.py:213
  546.5 14.4 %collective-permute-done.8.refs_0_ = bf16[64,13312]{1,0:T(8,128)(2,1)S(1)} collective-permute-done((bf16[64,13312]{1,0:T(8,128)(2,1)}, bf16[64,13312]{1,0:T(8,128)(2,1)S(1)}, u32[]{:S(2)}, u32[]{:S(2)}) %collective-permute-start.8) | collective-permute-done | bytes 1703968 | tf_op jit(solution)/shard_map/ppermute | solution.py:238
  560.9 3.8 collective-permute-done.9.refs_1_
  565.9 7.5 %shard_map.65 = (f32[64,512]{1,0:T(8,128)}, f32[64,512]{1,0:T(8,128)}, f32[64,512]{1,0:T(8,128)}, f32[64,512]{1,0:T(8,128)}) custom-call(s32[2]{0:T(128)} %pad_add_fusion.place_ref, bf16[64,13312]{1,0:T(8,128)(2,1)} %copy-done.8, bf16[64,13312]{1,0:T(8,128)(2,1)} %copy-done.9, bf16[192,40000]{1,0:T(8,128)(2,1)} %bitcast.26, bf16[64,13440]{1,0:T(8,128)(2,1)} %copy-done.4, ...), custom_call_target="tpu_custom_call" | custom-call | flops 1000 | bytes 1000 | tf_op jit(solution)/shard_map/pallas_call | solution.py:213
  573.4 6.1 %collective-permute-start.12 = (f32[64,512]{1,0:T(8,128)}, f32[64,512]{1,0:T(8,128)S(1)}, u32[]{:S(2)}, u32[]{:S(2)}) collective-permute-start(f32[64,512]{1,0:T(8,128)} %get-tuple-element.30), channel_id=1, source_target_pairs={{0,1},{1,0},{2,3},{3,2},{4,5},{5,4},{6,7},{7,6},{8,9},{9,8},{10,11... | collective-permute-start | bytes 393224 | tf_op jit(solution)/shard_map/ppermute | solution.py:364
  581.3 3.6 collective-permute-done.13
  590.9 6.8 %collective-permute-start.16 = (f32[64,256]{1,0:T(8,128)S(1)}, f32[64,256]{1,0:T(8,128)S(1)}, u32[]{:S(2)}, u32[]{:S(2)}) collective-permute-start(f32[64,256]{1,0:T(8,128)S(1)} %get-tuple-element.38), channel_id=1, source_target_pairs={{0,1},{1,5},{2,9},{3,13},{4,0},{5,4},{6,8},{7,12},{8,3},{9,7},{10,... | collective-permute-start | bytes 196616 | tf_op jit(solution)/shard_map/ppermute | solution.py:373
  (70 shorter events, 40.5 us)
Async XLA Ops:
  3.1 8.7 %copy-start.10 = (s32[40000]{0:T(1024)S(1)}, s32[40000]{0:T(1024)}, u32[]{:S(2)}) copy-start(s32[40000]{0:T(1024)} %param.8) | copy-start | bytes 480004
  3.1 8.7 %copy-start.11 = (f32[64,2]{0,1:T(2,128)S(1)}, f32[64,2]{0,1:T(2,128)}, u32[]{:S(2)}) copy-start(f32[64,2]{0,1:T(2,128)} %param.7) | copy-start | bytes 1540
  7.1 39.7 %collective-permute-start = (bf16[64,13440]{1,0:T(8,128)(2,1)}, bf16[64,13440]{1,0:T(8,128)(2,1)S(1)}, u32[]{:S(2)}, u32[]{:S(2)}) collective-permute-start(bf16[64,13440]{1,0:T(8,128)(2,1)} %shard_map.55.refs_3_.refs_7_), channel_id=1, source_target_pairs={{0,4},{4,8},{8,12},{1,5},{5,9},{9,13},{2,6},{6,10},{10,14},{3,7},{... | collective-permute-start | bytes 5160968 | tf_op jit(solution)/shard_map/ppermute | solution.py:238
  10.4 40.2 %collective-permute-start.1 = (bf16[64,13440]{1,0:T(8,128)(2,1)}, bf16[64,13440]{1,0:T(8,128)(2,1)S(1)}, u32[]{:S(2)}, u32[]{:S(2)}) collective-permute-start(bf16[64,13440]{1,0:T(8,128)(2,1)} %shard_map.55.refs_3_.refs_7_), channel_id=1, source_target_pairs={{12,8},{8,4},{4,0},{13,9},{9,5},{5,1},{14,10},{10,6},{6,2},{15,11}... | collective-permute-start | bytes 5160968 | tf_op jit(solution)/shard_map/ppermute | solution.py:238
  14.9 147.6 %collective-permute-start.4 = (bf16[64,13312]{1,0:T(8,128)(2,1)}, bf16[64,13312]{1,0:T(8,128)(2,1)}, u32[]{:S(2)}, u32[]{:S(2)}) collective-permute-start(bf16[64,13312]{1,0:T(8,128)(2,1)} %add_convert_fusion.1.refs_3_), channel_id=1, source_target_pairs={{0,4},{4,8},{8,12},{1,5},{5,9},{9,13},{2,6},{6,10},{10,14},{3,7},{... | collective-permute-start | bytes 5111816 | tf_op jit(solution)/shard_map/ppermute | solution.py:238
  20.1 142.5 %collective-permute-start.5 = (bf16[64,13312]{1,0:T(8,128)(2,1)}, bf16[64,13312]{1,0:T(8,128)(2,1)}, u32[]{:S(2)}, u32[]{:S(2)}) collective-permute-start(bf16[64,13312]{1,0:T(8,128)(2,1)} %add_convert_fusion.1.refs_3_), channel_id=1, source_target_pairs={{12,8},{8,4},{4,0},{13,9},{9,5},{5,1},{14,10},{10,6},{6,2},{15,11}... | collective-permute-start | bytes 5111816 | tf_op jit(solution)/shard_map/ppermute | solution.py:238
  46.8 3.8 copy-start.6
  105.3 184.5 %collective-permute-start.2 = (bf16[64,13440]{1,0:T(8,128)(2,1)}, bf16[64,13440]{1,0:T(8,128)(2,1)S(1)}, u32[]{:S(2)}, u32[]{:S(2)}) collective-permute-start(bf16[64,13440]{1,0:T(8,128)(2,1)} %get-tuple-element.21), channel_id=1, source_target_pairs={{0,4},{4,8},{8,12},{1,5},{5,9},{9,13},{2,6},{6,10},{10,14},{3,7},{... | collective-permute-start | bytes 5160968 | tf_op jit(solution)/shard_map/ppermute | solution.py:238
  161.2 128.6 %collective-permute-start.3 = (bf16[64,13440]{1,0:T(8,128)(2,1)}, bf16[64,13440]{1,0:T(8,128)(2,1)S(1)}, u32[]{:S(2)}, u32[]{:S(2)}) collective-permute-start(bf16[64,13440]{1,0:T(8,128)(2,1)} %get-tuple-element.22), channel_id=1, source_target_pairs={{12,8},{8,4},{4,0},{13,9},{9,5},{5,1},{14,10},{10,6},{6,2},{15,11}... | collective-permute-start | bytes 5160968 | tf_op jit(solution)/shard_map/ppermute | solution.py:238
  216.0 199.9 %collective-permute-start.6 = (bf16[64,13312]{1,0:T(8,128)(2,1)}, bf16[64,13312]{1,0:T(8,128)(2,1)S(1)}, u32[]{:S(2)}, u32[]{:S(2)}) collective-permute-start(bf16[64,13312]{1,0:T(8,128)(2,1)} %get-tuple-element.23), channel_id=1, source_target_pairs={{0,4},{4,8},{8,12},{1,5},{5,9},{9,13},{2,6},{6,10},{10,14},{3,7},{... | collective-permute-start | bytes 5111816 | tf_op jit(solution)/shard_map/ppermute | solution.py:238
  271.7 144.2 %collective-permute-start.7 = (bf16[64,13312]{1,0:T(8,128)(2,1)}, bf16[64,13312]{1,0:T(8,128)(2,1)S(1)}, u32[]{:S(2)}, u32[]{:S(2)}) collective-permute-start(bf16[64,13312]{1,0:T(8,128)(2,1)} %get-tuple-element.24), channel_id=1, source_target_pairs={{12,8},{8,4},{4,0},{13,9},{9,5},{5,1},{14,10},{10,6},{6,2},{15,11}... | collective-permute-start | bytes 5111816 | tf_op jit(solution)/shard_map/ppermute | solution.py:238
  345.7 191.1 %collective-permute-start.10 = (bf16[64,13440]{1,0:T(8,128)(2,1)}, bf16[64,13440]{1,0:T(8,128)(2,1)S(1)}, u32[]{:S(2)}, u32[]{:S(2)}) collective-permute-start(bf16[64,13440]{1,0:T(8,128)(2,1)} %get-tuple-element.27), channel_id=1, source_target_pairs={{0,4},{4,8},{8,12},{1,5},{5,9},{9,13},{2,6},{6,10},{10,14},{3,7},{... | collective-permute-start | bytes 5160968 | tf_op jit(solution)/shard_map/ppermute | solution.py:238
  405.5 131.3 %collective-permute-start.11 = (bf16[64,13440]{1,0:T(8,128)(2,1)}, bf16[64,13440]{1,0:T(8,128)(2,1)S(1)}, u32[]{:S(2)}, u32[]{:S(2)}) collective-permute-start(bf16[64,13440]{1,0:T(8,128)(2,1)} %get-tuple-element.28), channel_id=1, source_target_pairs={{12,8},{8,4},{4,0},{13,9},{9,5},{5,1},{14,10},{10,6},{6,2},{15,11}... | collective-permute-start | bytes 5160968 | tf_op jit(solution)/shard_map/ppermute | solution.py:238
  471.7 89.1 %collective-permute-start.8 = (bf16[64,13312]{1,0:T(8,128)(2,1)}, bf16[64,13312]{1,0:T(8,128)(2,1)S(1)}, u32[]{:S(2)}, u32[]{:S(2)}) collective-permute-start(bf16[64,13312]{1,0:T(8,128)(2,1)} %get-tuple-element.25), channel_id=1, source_target_pairs={{0,4},{4,8},{8,12},{1,5},{5,9},{9,13},{2,6},{6,10},{10,14},{3,7},{... | collective-permute-start | bytes 5111816 | tf_op jit(solution)/shard_map/ppermute | solution.py:238
  529.1 35.6 %collective-permute-start.9 = (bf16[64,13312]{1,0:T(8,128)(2,1)}, bf16[64,13312]{1,0:T(8,128)(2,1)S(1)}, u32[]{:S(2)}, u32[]{:S(2)}) collective-permute-start(bf16[64,13312]{1,0:T(8,128)(2,1)} %get-tuple-element.26), channel_id=1, source_target_pairs={{12,8},{8,4},{4,0},{13,9},{9,5},{5,1},{14,10},{10,6},{6,2},{15,11}... | collective-permute-start | bytes 5111816 | tf_op jit(solution)/shard_map/ppermute | solution.py:238
  546.5 55.8 %copy-start.12 = (f32[2,96]{1,0:T(2,128)S(1)}, f32[2,96]{1,0:T(2,128)}, u32[]{:S(2)}) copy-start(f32[2,96]{1,0:T(2,128)} %refs_9_.1) | copy-start | bytes 2308
  560.9 3.8 copy-start.8
  573.4 7.9 %collective-permute-start.12 = (f32[64,512]{1,0:T(8,128)}, f32[64,512]{1,0:T(8,128)S(1)}, u32[]{:S(2)}, u32[]{:S(2)}) collective-permute-start(f32[64,512]{1,0:T(8,128)} %get-tuple-element.30), channel_id=1, source_target_pairs={{0,1},{1,0},{2,3},{3,2},{4,5},{5,4},{6,7},{7,6},{8,9},{9,8},{10,11... | collective-permute-start | bytes 393224 | tf_op jit(solution)/shard_map/ppermute | solution.py:364
  579.5 5.3 collective-permute-start.13
  579.8 8.0 %collective-permute-start.14 = (f32[64,512]{1,0:T(8,128)}, f32[64,512]{1,0:T(8,128)S(1)}, u32[]{:S(2)}, u32[]{:S(2)}) collective-permute-start(f32[64,512]{1,0:T(8,128)} %get-tuple-element.32), channel_id=1, source_target_pairs={{0,3},{1,2},{2,1},{3,0},{4,7},{5,6},{6,5},{7,4},{8,11},{9,10},{10,... | collective-permute-start | bytes 393224 | tf_op jit(solution)/shard_map/ppermute | solution.py:364
  589.0 9.9 %collective-permute-start.15 = (f32[64,256]{1,0:T(8,128)S(1)}, f32[64,256]{1,0:T(8,128)S(1)}, u32[]{:S(2)}, u32[]{:S(2)}) collective-permute-start(f32[64,256]{1,0:T(8,128)S(1)} %get-tuple-element.37), channel_id=1, source_target_pairs={{0,0},{1,4},{2,8},{3,12},{4,1},{5,5},{6,9},{7,13},{8,2},{9,6},{10,... | collective-permute-start | bytes 196616 | tf_op jit(solution)/shard_map/ppermute | solution.py:373
  590.9 8.5 %collective-permute-start.16 = (f32[64,256]{1,0:T(8,128)S(1)}, f32[64,256]{1,0:T(8,128)S(1)}, u32[]{:S(2)}, u32[]{:S(2)}) collective-permute-start(f32[64,256]{1,0:T(8,128)S(1)} %get-tuple-element.38), channel_id=1, source_target_pairs={{0,1},{1,5},{2,9},{3,13},{4,0},{5,4},{6,8},{7,12},{8,3},{9,7},{10,... | collective-permute-start | bytes 196616 | tf_op jit(solution)/shard_map/ppermute | solution.py:373
  597.7 3.9 collective-permute-start.17
  597.7 3.9 collective-permute-start.18
  (8 other events, 9.8 us)

commit v5 on v4

--- a/solution.py
+++ b/solution.py
@@ -38,6 +38,7 @@
 
 LANES = 128
 STEPS = 4
+ROWS = 64
 WIDTH = 4 * LANES
 FREE = LANES * 2 - 1
 PARAMS = pltpu.CompilerParams(vmem_limit_bytes=56 * 1024 * 1024)
@@ -66,12 +67,18 @@
     rest = sites - 3 * third
     rest_width = rest + -rest % LANES
     labels = labels.reshape(1, sites)
+    volts = volts.T
 
     def kernel(noise_ref, labels_ref, volts_ref, noise_rest, labels_rest, out):
+        def column_of(kind):
+            shape = (frames, frames)
+            diagonal = lax.broadcasted_iota(jnp.int32, shape, 0) == lax.broadcasted_iota(jnp.int32, shape, 1)
+            return jnp.sum(jnp.where(diagonal, volts_ref[kind:kind + 1, :], 0.0), axis=1, keepdims=True)
+
         def potential(noise, labels):
-            value = jnp.broadcast_to(volts_ref[:, 0:1], noise.shape)
-            for kind in range(1, volts_ref.shape[1]):
-                value = jnp.where(labels == kind, volts_ref[:, kind:kind + 1], value)
+            value = jnp.broadcast_to(column_of(0), noise.shape)
+            for kind in range(1, volts_ref.shape[0]):
+                value = jnp.where(labels == kind, column_of(kind), value)
             return value + noise.astype(jnp.float32)
 
         step = pl.program_id(0)
@@ -102,40 +109,43 @@
     )(noise, labels, volts, noise, labels)
 
 
-def route(place, sources, to_right, to_left, shape, tokens):
-    arrays = [s[0] for s in sources]
-    count = len(arrays)
+def route(place, whole, sources, to_right, to_left, width, tokens):
+    tile = whole // STEPS
+    count = len(sources)
+    frames = ROWS
 
     def kernel(place_ref, *refs):
-        outs, sems = refs[count + len(tokens):-1], refs[-1]
+        outs = refs[count + len(tokens):]
         z = place_ref[0]
         for here in range(4):
             @pl.when(z == here)
             def _(here=here):
-                copies = []
-                for side, choice in enumerate((to_right[here], to_left[here])):
-                    if choice is None:
-                        continue
-                    number, columns = choice
-                    _, row, rows, column = sources[number]
-                    copies.append(pltpu.make_async_copy(
-                        refs[number].at[pl.ds(row, rows), pl.ds(column, columns)],
-                        outs[side].at[pl.ds(0, rows), pl.ds(0, columns)], sems.at[side]))
-                for copy in copies:
-                    copy.start()
-                for copy in copies:
-                    copy.wait()
-
-    anywhere = pl.BlockSpec(memory_space=pl.ANY)
+                for out, number in zip(outs, (to_right[here], to_left[here])):
+                    if number is not None:
+                        out[...] = refs[number][...]
+
+    def spec(number):
+        array, row, column = sources[number]
+        last = (array.shape[1] - 1) // tile if column == 0 else column + STEPS - 1
+        users = [here for here in range(4) if number in (to_right[here], to_left[here])]
+
+        def index(i, s):
+            used = sum((s[0] == here).astype(jnp.int32) for here in users)
+            return row, jnp.minimum(column + i * used, last)
+
+        return pl.BlockSpec((frames, tile), index)
+
+    out_spec = pl.BlockSpec((frames, tile), lambda i, s: (0, i))
     return pl.pallas_call(
         kernel,
-        in_specs=[pl.BlockSpec(memory_space=pltpu.SMEM)] + [anywhere] * (count + len(tokens)),
-        out_specs=[anywhere] * 2,
-        out_shape=[jax.ShapeDtypeStruct(shape, jnp.bfloat16)] * 2,
-        scratch_shapes=[pltpu.SemaphoreType.DMA((2,))],
+        grid_spec=pltpu.PrefetchScalarGridSpec(
+            num_scalar_prefetch=1, grid=(pl.cdiv(width, tile),),
+            in_specs=[spec(n) for n in range(count)] + [pl.BlockSpec(memory_space=pl.ANY)] * len(tokens),
+            out_specs=[out_spec] * 2),
+        out_shape=[jax.ShapeDtypeStruct((frames, width), jnp.bfloat16)] * 2,
         compiler_params=PARAMS,
         cost_estimate=SMALL,
-    )(place, *arrays, *tokens)
+    )(place, *[s[0] for s in sources], *tokens)
 
 
 def absorb(place, whole, streams, work, sums_shape, sums, first=None, profile=None):
@@ -145,7 +155,7 @@
     nrows, sites = slab.shape
     rest = sites - 3 * whole
     rest_width = rest + -rest % LANES
-    long = [n for n in names if streams[n][0].shape[1] == whole + rest_width] if first else []
+    long = [n for n in names if n in ("r", "l", "own") and streams[n][0].shape[1] == whole + rest_width] if first else []
     blocks, frames, width = sums_shape
 
     def kernel(place_ref, *refs):
@@ -159,8 +169,9 @@
             refs = refs[len(long):]
         if profile is None:
             acc, = refs
+            turned = None
         else:
-            profile_ref, outs, acc = refs[0], refs[1:-1], refs[-1]
+            profile_ref, outs, acc, turned = refs[0], refs[1:-2], refs[-2], refs[-1]
         z, k = place_ref[0], place_ref[1]
         step = pl.program_id(0)
 
@@ -175,11 +186,17 @@
                 piece = jnp.where(column < rest, slab_rest[...].astype(jnp.float32), 0.0).astype(jnp.bfloat16)
                 first(z, dict(rests, slab=piece), add)
 
-        work(z, tiles, add)
+            if turned is not None:
+                turned[...] = jnp.zeros(turned.shape, turned.dtype)
+
+        work(z, tiles, add, *([] if turned is None else [turned]))
 
         if profile is not None:
             @pl.when(step == STEPS - 1)
             def _():
+                block = jnp.where(z < 2, 3, 0)
+                add(block, 0, turned[:nrows].T[:frames])
+                add(block, width // 2, turned[nrows:].T[:frames])
                 weight = jnp.sum(profile_ref[...])
                 lane = lax.broadcasted_iota(jnp.int32, (frames, LANES), 1)
                 for turn, out in enumerate(outs):
@@ -209,7 +226,7 @@
         operands.append(profile)
         out_shape = [jax.ShapeDtypeStruct(sums_shape[1:], jnp.float32)] * blocks
         out_specs = [pl.BlockSpec(sums_shape[1:], lambda i, s: (0, 0))] * blocks
-        scratch = [pltpu.VMEM(sums_shape, jnp.float32)]
+        scratch = [pltpu.VMEM(sums_shape, jnp.float32), pltpu.VMEM((2 * nrows, LANES), jnp.float32)]
     return pl.pallas_call(
         kernel,
         grid_spec=pltpu.PrefetchScalarGridSpec(
@@ -225,7 +242,6 @@
     panels, rows, sites = slab.shape
     frames = noise.shape[0]
     nrows = panels * rows
-    part = nrows // 3
     third = sites // 3 // LANES * LANES
     z = lax.axis_index("wide")
     k = lax.axis_index(SITES)
@@ -243,14 +259,15 @@
 
     def mirror(choice):
         swap = {0: 0, 1: 2, 2: 1, 3: 4, 4: 3}
-        return [None if c is None else (swap[c[0]], c[1]) for c in reversed(choice)]
+        return [swap.get(c) for c in reversed(choice)]
 
     def routed(sources, choice, width, tokens):
-        sources = [s if isinstance(s, tuple) else (s, 0, frames, 0) for s in sources]
-        return send(route(place, sources, choice, mirror(choice), (frames, width), tokens))
+        sources = [s if isinstance(s, tuple) else (s, 0, 0) for s in sources]
+        pair = route(place, third, sources, choice, mirror(choice), width, tokens)
+        return send(pair), pair[0]
 
     def spare(i):
-        return (slab, part * i, part, 2 * third)
+        return (slab, i, 2 * STEPS)
 
     own_a = first_potential(noise, volts, labels, third)
     long = own_a.shape[1]
@@ -314,23 +331,26 @@
             add(z, 2 * LANES, dot(refs["own"][...], brought))
             add(3 - z, 2 * LANES, dot(came, brought))
 
+    def first3(z, refs, add):
+        add((z + 2) % 4, 0, dot(far(z, refs, ""), refs["slab"]))
+
     def first5(z, refs, add):
         @pl.when(is_end(z))
         def _():
             add(3 - z, 0, dot(far(z, refs, ""), refs["slab"]))
 
-    def work6(z, refs, add):
+    def work6(z, refs, add, turned):
         came = far(z, refs, "")
-        block = jnp.where(z < 2, 3, 0)
-        add(block, 0, dot(came, refs["slab"][...]))
+        turned[:nrows, :frames] += dot(refs["slab"][...], came)
 
         @pl.when(is_mid(z))
         def _():
             newest = near(z, refs, "")
             brought = jnp.concatenate([near(z, refs, "4"), near(z, refs, "5"), newest], axis=0)
-            add(block, 2 * LANES, dot(came, brought))
-            add(z, 3 * LANES, dot(refs["own"][...], newest))
-            add(3 - z, 3 * LANES, dot(far(z, refs, "5"), newest))
+            turned[nrows:, :frames] += dot(brought, came)
+            both = dot(jnp.concatenate([refs["own"][...], far(z, refs, "5")], axis=0), newest)
+            add(z, 3 * LANES, both[:frames])
+            add(3 - z, 3 * LANES, both[frames:])
 
     def near_right(z):
         return z == 1
@@ -338,23 +358,24 @@
     def near_left(z):
         return z == 2
 
-    r3 = routed([own_c, r1[0], r1[1]], [(0, third), (1, long), (1, long), None], long, [])
-    r4 = routed([spare(0), r2[0], r2[1]], [(0, third), (1, third), (1, third), None], third, [])
+    r3, sent = routed([own_c, r1[0], r1[1]], [0, 1, 1, None], long, [])
+    r4, sent = routed([spare(0), r2[0], r2[1]], [0, 1, 1, None], third, [sent])
     sums = absorb(
         place, third, dict(both("", r1), slab=(slab, always, at(0)), own=(own_a, always, at(0))), work1, sums_shape, None,
-        first=lambda z, refs, add: work1(z, refs, add))
+        first=work1)
     sums = absorb(
         place, third, dict(both("", r2), slab=(slab, always, at(1)), own=(own_b, always, at(0))), work1, sums_shape, sums)
-    r5 = routed([spare(1), r3[0], r3[1], own_c, own_c], [(0, third), (3, third), (1, long), None], long, [sums])
+    r5, sent = routed([spare(1), r3[0], r3[1], own_c, own_c], [0, 3, 1, None], long, [sent, sums])
     sums = absorb(
         place, third,
         dict(both("", r3), slab=(slab, always, at(0)), slab2=(slab, always, at(2)), own=(own_c, always, at(0))),
-        work3, sums_shape, sums, first=lambda z, refs, add: add((z + 2) % 4, 0, dot(far(z, refs, ""), refs["slab"])))
-    r6 = routed([spare(2), r3[0], r3[1], r4[0], r4[1]], [(0, third), (1, third), (3, third), None], third, [sums])
-    sums = absorb(place, third, dict(both("", r4), slab=(slab, always, at(1))), work4, sums_shape, sums)
+        work3, sums_shape, sums, first=first3)
+    r6, sent = routed([spare(2), r3[0], r3[1], r4[0], r4[1]], [0, 1, 3, None], third, [sent, sums])
+    sums = absorb(
+        place, third, dict(both("", r4), slab=(slab, always, at(1))), work4, sums_shape, sums)
     middle = dict(both("4", r4, near_right, near_left), own=(own_c, is_mid, at(0)))
-    sums = absorb(
-        place, third, dict(both("", r5), slab=(slab, always, thirds(0, 2)), **middle), work5, sums_shape, sums, first=first5)
+    sums = absorb(place, third, dict(both("", r5), slab=(slab, always, thirds(0, 2)), **middle), work5, sums_shape, sums,
+        first=first5)
     messages = absorb(
         place, third, dict(both("", r6), slab=(slab, always, thirds(1, 2)), **both("5", r5, is_mid, is_mid), **middle),
         work6, sums_shape, sums, profile=profile)

time: 607 us -> 287 us (0.47)
  starting transfers between devices: 262 us -> 52.5 us
  Pallas kernels: 265 us -> 71.8 us
  waiting for transfers between devices: 52.6 us -> 138 us
    ppermute x6, starting transfers between devices: 237 us -> 28.7 us  [send(): lax.ppermute(pair[0], 'wide', right)]
    pallas_call x4, Pallas kernels: 214 us -> 20.7 us  [route(): pl.pallas_call(kernel, grid_spec=pltpu.PrefetchScalarGridSpec(num_scalar_...]
    ppermute x6, waiting for transfers between devices: 7.64 us -> 97.7 us  [send(): lax.ppermute(pair[1], 'wide', left)]
  transfers between devices with their start and end apart: 19 -> 19, of which waited for: 8 -> 13; matrix products, arithmetic and copies ran while one was open for 1% -> 2% of each run, Pallas kernels for 42% -> 21%
where the time goes in v5:
time: 287 us; the launch traced here: 283 us
  waiting for transfers between devices  138 us (48%)
  Pallas kernels  71.8 us (25%)
  starting transfers between devices  52.5 us (18%)
  other arithmetic  10.6 us (4%)
  local copies, waits for them, and re-layouts  9.61 us (3%)
    ppermute x6, waiting for transfers between devices, send(): lax.ppermute(pair[1], 'wide', left)  97.7 us
    pallas_call x6, Pallas kernels, absorb(): pl.pallas_call(kernel, grid_spec=pltpu.PrefetchScalarGridSpec(num_scalar_...  47 us
    ppermute x6, waiting for transfers between devices, send(): lax.ppermute(pair[0], 'wide', right)  31.7 us
    ppermute x6, starting transfers between devices, send(): lax.ppermute(pair[0], 'wide', right)  28.7 us
    pallas_call x4, Pallas kernels, route(): pl.pallas_call(kernel, grid_spec=pltpu.PrefetchScalarGridSpec(num_scalar_...  20.7 us
    ppermute x6, starting transfers between devices, send(): lax.ppermute(pair[1], 'wide', left)  7.69 us
    unnamed x24, local copies, waits for them, and re-layouts  7.21 us
    ppermute x3, waiting for transfers between devices, line_plan(): lax.ppermute(messages[turn], SITES, [(i, i ^ turn) for i in range(owners)])  6.54 us
  transfers between devices with their start and end apart: 19, of which 13 were waited for; matrix products, arithmetic and copies ran while one was open for 2% of the time, Pallas kernels for 21%

profile of v5, /device:TPU:3, one launch (start us, length us, event | category | flops | bytes accessed | tf_op | source)
XLA Modules:
  0.0 282.7 jit_solution(14070924071620943416)
XLA Ops:
  2.6 4.0 %shard_map.55.refs_3_.refs_7_ = bf16[64,13440]{1,0:T(8,128)(2,1)} custom-call(bf16[64,40000]{1,0:T(8,128)(2,1)} %noise_rest.1, s32[1,40000]{1,0:T(1,128)} %reshape.27.labels_ref.labels_rest, f32[2,64]{1,0:T(2,128)} %bitcast.28, bf16[64,40000]{1,0:T(8,128)(2,1)} %noise_rest.1, s32[1,40000]{1,0:T(1,128)} %reshape.27.labels_ref.labels_rest), custom_call_target="tpu_custom_call" | custom-call | flops 1000 | bytes 1000 | tf_op jit(solution)/shard_map/pallas_call | solution.py:95
  11.2 5.2 %collective-permute-start.4 = (bf16[64,13312]{1,0:T(8,128)(2,1)}, bf16[64,13312]{1,0:T(8,128)(2,1)}, u32[]{:S(2)}, u32[]{:S(2)}) collective-permute-start(bf16[64,13312]{1,0:T(8,128)(2,1)} %add_convert_fusion.1.refs_3_), channel_id=1, source_target_pairs={{0,4},{4,8},{8,12},{1,5},{5,9},{9,13},{2,6},{6,10},{10,14},{3,7},{... | collective-permute-start | bytes 5111816 | tf_op jit(solution)/shard_map/ppermute | solution.py:254
  17.6 5.2 %collective-permute-start = (bf16[64,13440]{1,0:T(8,128)(2,1)S(1)}, bf16[64,13440]{1,0:T(8,128)(2,1)}, u32[]{:S(2)}, u32[]{:S(2)}) collective-permute-start(bf16[64,13440]{1,0:T(8,128)(2,1)S(1)} %copy-done.6), channel_id=1, source_target_pairs={{0,4},{4,8},{8,12},{1,5},{5,9},{9,13},{2,6},{6,10},{10,14},{3,7},{... | collective-permute-start | bytes 5160968 | tf_op jit(solution)/shard_map/ppermute | solution.py:254
  26.6 60.3 %collective-permute-done.1.refs_2_.refs_1_.refs_6_ = bf16[64,13440]{1,0:T(8,128)(2,1)S(1)} collective-permute-done((bf16[64,13440]{1,0:T(8,128)(2,1)S(1)}, bf16[64,13440]{1,0:T(8,128)(2,1)S(1)}, u32[]{:S(2)}, u32[]{:S(2)}) %collective-permute-start.1) | collective-permute-done | bytes 1720352 | tf_op jit(solution)/shard_map/ppermute | solution.py:254
  88.2 5.0 %shard_map.56 = (bf16[64,13440]{1,0:T(8,128)(2,1)}, bf16[64,13440]{1,0:T(8,128)(2,1)}) custom-call(s32[2]{0:T(128)} %pad_add_fusion.place_ref, bf16[64,13312]{1,0:T(8,128)(2,1)} %add_convert_fusion.refs_0_.refs_3_.refs_4_.refs_5_.refs_7_, bf16[64,13440]{1,0:T(8,128)(2,1)} %collective-permute-done.refs_1_.refs_0_.refs_5_, bf16[64,13440]{1,0:T(8,128)(2,1)} %copy-done.7), custom_call_target="tpu_custom_call" | custom-call | flops 1000 | bytes 1000 | tf_op jit(solution)/shard_map/pallas_call | solution.py:139
  94.5 5.0 %collective-permute-start.2 = (bf16[64,13440]{1,0:T(8,128)(2,1)}, bf16[64,13440]{1,0:T(8,128)(2,1)S(1)}, u32[]{:S(2)}, u32[]{:S(2)}) collective-permute-start(bf16[64,13440]{1,0:T(8,128)(2,1)} %get-tuple-element.21.refs_3_), channel_id=1, source_target_pairs={{0,4},{4,8},{8,12},{1,5},{5,9},{9,13},{2,6},{6,10},{10,14},{3,7},{... | collective-permute-start | bytes 5160968 | tf_op jit(solution)/shard_map/ppermute | solution.py:254
  99.6 5.0 %shard_map.57 = (bf16[64,13312]{1,0:T(8,128)(2,1)}, bf16[64,13312]{1,0:T(8,128)(2,1)}) custom-call(s32[2]{0:T(128)} %pad_add_fusion.place_ref, bf16[192,40000]{1,0:T(8,128)(2,1)} %bitcast.15, bf16[64,13312]{1,0:T(8,128)(2,1)} %collective-permute-done.4.refs_1_.refs_0_, bf16[64,13312]{1,0:T(8,128)(2,1)} %collective-permute-done.5.refs_2_.refs_1_, ...), custom_call_target="tpu_custom_call" | custom-call | flops 1000 | bytes 1000 | tf_op jit(solution)/shard_map/pallas_call | solution.py:139
  105.9 4.2 %collective-permute-start.6 = (bf16[64,13312]{1,0:T(8,128)(2,1)}, bf16[64,13312]{1,0:T(8,128)(2,1)S(1)}, u32[]{:S(2)}, u32[]{:S(2)}) collective-permute-start(bf16[64,13312]{1,0:T(8,128)(2,1)} %get-tuple-element.23.refs_5_), channel_id=1, source_target_pairs={{0,4},{4,8},{8,12},{1,5},{5,9},{9,13},{2,6},{6,10},{10,14},{3,7},{... | collective-permute-start | bytes 5111816 | tf_op jit(solution)/shard_map/ppermute | solution.py:254
  110.1 8.5 %shard_map.58.refs_4_ = f32[4,64,512]{2,1,0:T(8,128)} custom-call(s32[2]{0:T(128)} %pad_add_fusion.place_ref, bf16[64,13440]{1,0:T(8,128)(2,1)} %collective-permute-done.refs_1_.refs_0_.refs_5_, bf16[64,13440]{1,0:T(8,128)(2,1)} %copy-done.7, bf16[192,40000]{1,0:T(8,128)(2,1)} %bitcast.16, bf16[64,13440]{1,0:T(8,128)(2,1)} %shard_map.55.refs_3_.refs_7_, ...), custom_call_target="tpu_custom_call" | custom-call | flops 1000 | bytes 1000 | tf_op jit(solution)/shard_map/pallas_call | solution.py:230
  118.7 8.3 %shard_map.59.refs_6_.refs_5_ = f32[4,64,512]{2,1,0:T(8,128)} custom-call(s32[2]{0:T(128)} %pad_add_fusion.place_ref, bf16[64,13312]{1,0:T(8,128)(2,1)} %collective-permute-done.4.refs_1_.refs_0_, bf16[64,13312]{1,0:T(8,128)(2,1)} %collective-permute-done.5.refs_2_.refs_1_, bf16[192,40000]{1,0:T(8,128)(2,1)} %bitcast.18, ...), custom_call_target="tpu_custom_call" | custom-call | flops 1000 | bytes 1000 | tf_op jit(solution)/shard_map/pallas_call | solution.py:230
  126.9 6.8 %collective-permute-done.3.refs_2_.refs_1_.refs_8_ = bf16[64,13440]{1,0:T(8,128)(2,1)S(1)} collective-permute-done((bf16[64,13440]{1,0:T(8,128)(2,1)}, bf16[64,13440]{1,0:T(8,128)(2,1)S(1)}, u32[]{:S(2)}, u32[]{:S(2)}) %collective-permute-start.3) | collective-permute-done | bytes 1720352 | tf_op jit(solution)/shard_map/ppermute | solution.py:254
  136.2 5.3 %shard_map.60 = (bf16[64,13440]{1,0:T(8,128)(2,1)}, bf16[64,13440]{1,0:T(8,128)(2,1)}) custom-call(s32[2]{0:T(128)} %pad_add_fusion.place_ref, bf16[192,40000]{1,0:T(8,128)(2,1)} %bitcast.19, bf16[64,13440]{1,0:T(8,128)(2,1)} %copy-done.1, bf16[64,13440]{1,0:T(8,128)(2,1)} %copy-done, ...), custom_call_target="tpu_custom_call" | custom-call | flops 1000 | bytes 1000 | tf_op jit(solution)/shard_map/pallas_call | solution.py:139
  142.8 5.0 %collective-permute-start.10 = (bf16[64,13440]{1,0:T(8,128)(2,1)}, bf16[64,13440]{1,0:T(8,128)(2,1)S(1)}, u32[]{:S(2)}, u32[]{:S(2)}) collective-permute-start(bf16[64,13440]{1,0:T(8,128)(2,1)} %get-tuple-element.25.refs_5_), channel_id=1, source_target_pairs={{0,4},{4,8},{8,12},{1,5},{5,9},{9,13},{2,6},{6,10},{10,14},{3,7},{... | collective-permute-start | bytes 5160968 | tf_op jit(solution)/shard_map/ppermute | solution.py:254
  147.8 9.1 %shard_map.61.refs_6_.refs_3_ = f32[4,64,512]{2,1,0:T(8,128)} custom-call(s32[2]{0:T(128)} %pad_add_fusion.place_ref, bf16[64,13440]{1,0:T(8,128)(2,1)} %copy-done.1, bf16[64,13440]{1,0:T(8,128)(2,1)} %copy-done, bf16[192,40000]{1,0:T(8,128)(2,1)} %bitcast.20, bf16[192,40000]{1,0:T(8,128)(2,1)} %bitcast.21, ...), custom_call_target="tpu_custom_call" | custom-call | flops 1000 | bytes 1000 | tf_op jit(solution)/shard_map/pallas_call | solution.py:230
  156.9 13.4 %collective-permute-done.7.refs_4_.refs_1_.refs_6_ = bf16[64,13312]{1,0:T(8,128)(2,1)S(1)} collective-permute-done((bf16[64,13312]{1,0:T(8,128)(2,1)}, bf16[64,13312]{1,0:T(8,128)(2,1)S(1)}, u32[]{:S(2)}, u32[]{:S(2)}) %collective-permute-start.7) | collective-permute-done | bytes 1703968 | tf_op jit(solution)/shard_map/ppermute | solution.py:254
  172.7 5.3 %shard_map.62 = (bf16[64,13312]{1,0:T(8,128)(2,1)}, bf16[64,13312]{1,0:T(8,128)(2,1)}) custom-call(s32[2]{0:T(128)} %pad_add_fusion.place_ref, bf16[192,40000]{1,0:T(8,128)(2,1)} %bitcast.23, bf16[64,13440]{1,0:T(8,128)(2,1)} %copy-done.1, bf16[64,13440]{1,0:T(8,128)(2,1)} %copy-done, bf16[64,13312]{1,0:T(8,128)(2,1)} %copy-done.3, ...), custom_call_target="tpu_custom_call" | custom-call | flops 1000 | bytes 1000 | tf_op jit(solution)/shard_map/pallas_call | solution.py:139
  178.0 4.0 %collective-permute-start.8 = (bf16[64,13312]{1,0:T(8,128)(2,1)}, bf16[64,13312]{1,0:T(8,128)(2,1)S(1)}, u32[]{:S(2)}, u32[]{:S(2)}) collective-permute-start(bf16[64,13312]{1,0:T(8,128)(2,1)} %get-tuple-element.26), channel_id=1, source_target_pairs={{0,4},{4,8},{8,12},{1,5},{5,9},{9,13},{2,6},{6,10},{10,14},{3,7},{... | collective-permute-start | bytes 5111816 | tf_op jit(solution)/shard_map/ppermute | solution.py:254
  183.3 6.4 %shard_map.63.refs_6_ = f32[4,64,512]{2,1,0:T(8,128)} custom-call(s32[2]{0:T(128)} %pad_add_fusion.place_ref, bf16[64,13312]{1,0:T(8,128)(2,1)} %copy-done.3, bf16[64,13312]{1,0:T(8,128)(2,1)} %copy-done.2, bf16[192,40000]{1,0:T(8,128)(2,1)} %bitcast.24, f32[4,64,512]{2,1,0:T(8,128)} %shard_map.61.refs_6_.refs_3_), custom_call_target="tpu_custom_call" | custom-call | flops 1000 | bytes 1000 | tf_op jit(solution)/shard_map/pallas_call | solution.py:230
  189.8 17.3 %collective-permute-done.11.refs_1_.refs_9_.refs_4_ = bf16[64,13440]{1,0:T(8,128)(2,1)S(1)} collective-permute-done((bf16[64,13440]{1,0:T(8,128)(2,1)}, bf16[64,13440]{1,0:T(8,128)(2,1)S(1)}, u32[]{:S(2)}, u32[]{:S(2)}) %collective-permute-start.11) | collective-permute-done | bytes 1720352 | tf_op jit(solution)/shard_map/ppermute | solution.py:254
  209.5 7.2 %shard_map.64.refs_8_ = f32[4,64,512]{2,1,0:T(8,128)} custom-call(s32[2]{0:T(128)} %pad_add_fusion.place_ref, bf16[64,13440]{1,0:T(8,128)(2,1)} %copy-done.5, bf16[64,13440]{1,0:T(8,128)(2,1)} %copy-done.4, bf16[192,40000]{1,0:T(8,128)(2,1)} %bitcast.25, bf16[64,13312]{1,0:T(8,128)(2,1)} %copy-done.3, bf16[64,13312]{1,0:T(8,128)(2,1)} %copy-done.2, ...), custom_call_target="tpu_custom_call" | custom-call | flops 1000 | bytes 1000 | tf_op jit(solution)/shard_map/pallas_call | solution.py:230
  216.8 27.9 %collective-permute-done.8.refs_0_ = bf16[64,13312]{1,0:T(8,128)(2,1)S(1)} collective-permute-done((bf16[64,13312]{1,0:T(8,128)(2,1)}, bf16[64,13312]{1,0:T(8,128)(2,1)S(1)}, u32[]{:S(2)}, u32[]{:S(2)}) %collective-permute-start.8) | collective-permute-done | bytes 1703968 | tf_op jit(solution)/shard_map/ppermute | solution.py:254
  247.1 7.4 %shard_map.65 = (f32[64,512]{1,0:T(8,128)}, f32[64,512]{1,0:T(8,128)}, f32[64,512]{1,0:T(8,128)}, f32[64,512]{1,0:T(8,128)}) custom-call(s32[2]{0:T(128)} %pad_add_fusion.place_ref, bf16[64,13312]{1,0:T(8,128)(2,1)} %copy-done.8, bf16[64,13312]{1,0:T(8,128)(2,1)} %copy-done.9, bf16[192,40000]{1,0:T(8,128)(2,1)} %bitcast.27, bf16[64,13440]{1,0:T(8,128)(2,1)} %copy-done.5, ...), custom_call_target="tpu_custom_call" | custom-call | flops 1000 | bytes 1000 | tf_op jit(solution)/shard_map/pallas_call | solution.py:230
  259.0 3.6 %collective-permute-done.13 = f32[64,512]{1,0:T(8,128)S(1)} collective-permute-done((f32[64,512]{1,0:T(8,128)}, f32[64,512]{1,0:T(8,128)S(1)}, u32[]{:S(2)}, u32[]{:S(2)}) %collective-permute-start.13) | collective-permute-done | bytes 131104 | tf_op jit(solution)/shard_map/ppermute | solution.py:385
  266.7 6.5 %collective-permute-start.15 = (f32[64,256]{1,0:T(8,128)S(1)}, f32[64,256]{1,0:T(8,128)S(1)}, u32[]{:S(2)}, u32[]{:S(2)}) collective-permute-start(f32[64,256]{1,0:T(8,128)S(1)} %get-tuple-element.37), channel_id=1, source_target_pairs={{0,0},{1,4},{2,8},{3,12},{4,1},{5,5},{6,9},{7,13},{8,2},{9,6},{10,... | collective-permute-start | bytes 196616 | tf_op jit(solution)/shard_map/ppermute | solution.py:394
  (67 shorter events, 46.4 us)
Async XLA Ops:
  2.6 4.1 %copy-start.10 = (f32[64,2]{0,1:T(2,128)S(1)}, f32[64,2]{0,1:T(2,128)}, u32[]{:S(2)}) copy-start(f32[64,2]{0,1:T(2,128)} %param.7) | copy-start | bytes 1540
  6.6 9.7 %copy-start.6 = (bf16[64,13440]{1,0:T(8,128)(2,1)S(1)}, bf16[64,13440]{1,0:T(8,128)(2,1)}, u32[]{:S(2)}) copy-start(bf16[64,13440]{1,0:T(8,128)(2,1)} %shard_map.55.refs_3_.refs_7_) | copy-start | bytes 5160964
  9.9 89.7 %collective-permute-start.5 = (bf16[64,13312]{1,0:T(8,128)(2,1)}, bf16[64,13312]{1,0:T(8,128)(2,1)}, u32[]{:S(2)}, u32[]{:S(2)}) collective-permute-start(bf16[64,13312]{1,0:T(8,128)(2,1)} %add_convert_fusion.1.refs_3_), channel_id=1, source_target_pairs={{12,8},{8,4},{4,0},{13,9},{9,5},{5,1},{14,10},{10,6},{6,2},{15,11}... | collective-permute-start | bytes 5111816 | tf_op jit(solution)/shard_map/ppermute | solution.py:254
  11.2 88.4 %collective-permute-start.4 = (bf16[64,13312]{1,0:T(8,128)(2,1)}, bf16[64,13312]{1,0:T(8,128)(2,1)}, u32[]{:S(2)}, u32[]{:S(2)}) collective-permute-start(bf16[64,13312]{1,0:T(8,128)(2,1)} %add_convert_fusion.1.refs_3_), channel_id=1, source_target_pairs={{0,4},{4,8},{8,12},{1,5},{5,9},{9,13},{2,6},{6,10},{10,14},{3,7},{... | collective-permute-start | bytes 5111816 | tf_op jit(solution)/shard_map/ppermute | solution.py:254
  16.3 70.6 %collective-permute-start.1 = (bf16[64,13440]{1,0:T(8,128)(2,1)S(1)}, bf16[64,13440]{1,0:T(8,128)(2,1)S(1)}, u32[]{:S(2)}, u32[]{:S(2)}) collective-permute-start(bf16[64,13440]{1,0:T(8,128)(2,1)S(1)} %copy-done.6), channel_id=1, source_target_pairs={{12,8},{8,4},{4,0},{13,9},{9,5},{5,1},{14,10},{10,6},{6,2},{15,11}... | collective-permute-start | bytes 5160968 | tf_op jit(solution)/shard_map/ppermute | solution.py:254
  17.6 70.1 %collective-permute-start = (bf16[64,13440]{1,0:T(8,128)(2,1)S(1)}, bf16[64,13440]{1,0:T(8,128)(2,1)}, u32[]{:S(2)}, u32[]{:S(2)}) collective-permute-start(bf16[64,13440]{1,0:T(8,128)(2,1)S(1)} %copy-done.6), channel_id=1, source_target_pairs={{0,4},{4,8},{8,12},{1,5},{5,9},{9,13},{2,6},{6,10},{10,14},{3,7},{... | collective-permute-start | bytes 5160968 | tf_op jit(solution)/shard_map/ppermute | solution.py:254
  86.9 1.3 copy-start.7
  93.2 40.5 %collective-permute-start.3 = (bf16[64,13440]{1,0:T(8,128)(2,1)}, bf16[64,13440]{1,0:T(8,128)(2,1)S(1)}, u32[]{:S(2)}, u32[]{:S(2)}) collective-permute-start(bf16[64,13440]{1,0:T(8,128)(2,1)} %get-tuple-element.22), channel_id=1, source_target_pairs={{12,8},{8,4},{4,0},{13,9},{9,5},{5,1},{14,10},{10,6},{6,2},{15,11}... | collective-permute-start | bytes 5160968 | tf_op jit(solution)/shard_map/ppermute | solution.py:254
  94.5 40.2 %collective-permute-start.2 = (bf16[64,13440]{1,0:T(8,128)(2,1)}, bf16[64,13440]{1,0:T(8,128)(2,1)S(1)}, u32[]{:S(2)}, u32[]{:S(2)}) collective-permute-start(bf16[64,13440]{1,0:T(8,128)(2,1)} %get-tuple-element.21.refs_3_), channel_id=1, source_target_pairs={{0,4},{4,8},{8,12},{1,5},{5,9},{9,13},{2,6},{6,10},{10,14},{3,7},{... | collective-permute-start | bytes 5160968 | tf_op jit(solution)/shard_map/ppermute | solution.py:254
  104.6 65.6 %collective-permute-start.7 = (bf16[64,13312]{1,0:T(8,128)(2,1)}, bf16[64,13312]{1,0:T(8,128)(2,1)S(1)}, u32[]{:S(2)}, u32[]{:S(2)}) collective-permute-start(bf16[64,13312]{1,0:T(8,128)(2,1)} %get-tuple-element.24), channel_id=1, source_target_pairs={{12,8},{8,4},{4,0},{13,9},{9,5},{5,1},{14,10},{10,6},{6,2},{15,11}... | collective-permute-start | bytes 5111816 | tf_op jit(solution)/shard_map/ppermute | solution.py:254
  105.9 65.4 %collective-permute-start.6 = (bf16[64,13312]{1,0:T(8,128)(2,1)}, bf16[64,13312]{1,0:T(8,128)(2,1)S(1)}, u32[]{:S(2)}, u32[]{:S(2)}) collective-permute-start(bf16[64,13312]{1,0:T(8,128)(2,1)} %get-tuple-element.23.refs_5_), channel_id=1, source_target_pairs={{0,4},{4,8},{8,12},{1,5},{5,9},{9,13},{2,6},{6,10},{10,14},{3,7},{... | collective-permute-start | bytes 5111816 | tf_op jit(solution)/shard_map/ppermute | solution.py:254
  141.5 65.6 %collective-permute-start.11 = (bf16[64,13440]{1,0:T(8,128)(2,1)}, bf16[64,13440]{1,0:T(8,128)(2,1)S(1)}, u32[]{:S(2)}, u32[]{:S(2)}) collective-permute-start(bf16[64,13440]{1,0:T(8,128)(2,1)} %get-tuple-element.28), channel_id=1, source_target_pairs={{12,8},{8,4},{4,0},{13,9},{9,5},{5,1},{14,10},{10,6},{6,2},{15,11}... | collective-permute-start | bytes 5160968 | tf_op jit(solution)/shard_map/ppermute | solution.py:254
  142.8 65.3 %collective-permute-start.10 = (bf16[64,13440]{1,0:T(8,128)(2,1)}, bf16[64,13440]{1,0:T(8,128)(2,1)S(1)}, u32[]{:S(2)}, u32[]{:S(2)}) collective-permute-start(bf16[64,13440]{1,0:T(8,128)(2,1)} %get-tuple-element.25.refs_5_), channel_id=1, source_target_pairs={{0,4},{4,8},{8,12},{1,5},{5,9},{9,13},{2,6},{6,10},{10,14},{3,7},{... | collective-permute-start | bytes 5160968 | tf_op jit(solution)/shard_map/ppermute | solution.py:254
  170.2 1.3 copy-start.2
  178.0 66.6 %collective-permute-start.8 = (bf16[64,13312]{1,0:T(8,128)(2,1)}, bf16[64,13312]{1,0:T(8,128)(2,1)S(1)}, u32[]{:S(2)}, u32[]{:S(2)}) collective-permute-start(bf16[64,13312]{1,0:T(8,128)(2,1)} %get-tuple-element.26), channel_id=1, source_target_pairs={{0,4},{4,8},{8,12},{1,5},{5,9},{9,13},{2,6},{6,10},{10,14},{3,7},{... | collective-permute-start | bytes 5111816 | tf_op jit(solution)/shard_map/ppermute | solution.py:254
  182.0 62.6 %collective-permute-start.9 = (bf16[64,13312]{1,0:T(8,128)(2,1)}, bf16[64,13312]{1,0:T(8,128)(2,1)S(1)}, u32[]{:S(2)}, u32[]{:S(2)}) collective-permute-start(bf16[64,13312]{1,0:T(8,128)(2,1)} %get-tuple-element.27), channel_id=1, source_target_pairs={{12,8},{8,4},{4,0},{13,9},{9,5},{5,1},{14,10},{10,6},{6,2},{15,11}... | collective-permute-start | bytes 5111816 | tf_op jit(solution)/shard_map/ppermute | solution.py:254
  216.8 65.2 %copy-start.11 = (f32[2,96]{1,0:T(2,128)S(1)}, f32[2,96]{1,0:T(2,128)}, u32[]{:S(2)}) copy-start(f32[2,96]{1,0:T(2,128)} %refs_9_.1) | copy-start | bytes 2308
  254.5 4.6 %collective-permute-start.12 = (f32[64,512]{1,0:T(8,128)}, f32[64,512]{1,0:T(8,128)S(1)}, u32[]{:S(2)}, u32[]{:S(2)}) collective-permute-start(f32[64,512]{1,0:T(8,128)} %get-tuple-element.30), channel_id=1, source_target_pairs={{0,1},{1,0},{2,3},{3,2},{4,5},{5,4},{6,7},{7,6},{8,9},{9,8},{10,11... | collective-permute-start | bytes 393224 | tf_op jit(solution)/shard_map/ppermute | solution.py:385
  257.3 5.3 %collective-permute-start.13 = (f32[64,512]{1,0:T(8,128)}, f32[64,512]{1,0:T(8,128)S(1)}, u32[]{:S(2)}, u32[]{:S(2)}) collective-permute-start(f32[64,512]{1,0:T(8,128)} %get-tuple-element.31), channel_id=1, source_target_pairs={{0,2},{1,3},{2,0},{3,1},{4,6},{5,7},{6,4},{7,5},{8,10},{9,11},{10,... | collective-permute-start | bytes 393224 | tf_op jit(solution)/shard_map/ppermute | solution.py:385
  257.7 7.8 %collective-permute-start.14 = (f32[64,512]{1,0:T(8,128)}, f32[64,512]{1,0:T(8,128)S(1)}, u32[]{:S(2)}, u32[]{:S(2)}) collective-permute-start(f32[64,512]{1,0:T(8,128)} %get-tuple-element.32), channel_id=1, source_target_pairs={{0,3},{1,2},{2,1},{3,0},{4,7},{5,6},{6,5},{7,4},{8,11},{9,10},{10,... | collective-permute-start | bytes 393224 | tf_op jit(solution)/shard_map/ppermute | solution.py:385
  266.7 12.2 %collective-permute-start.15 = (f32[64,256]{1,0:T(8,128)S(1)}, f32[64,256]{1,0:T(8,128)S(1)}, u32[]{:S(2)}, u32[]{:S(2)}) collective-permute-start(f32[64,256]{1,0:T(8,128)S(1)} %get-tuple-element.37), channel_id=1, source_target_pairs={{0,0},{1,4},{2,8},{3,12},{4,1},{5,5},{6,9},{7,13},{8,2},{9,6},{10,... | collective-permute-start | bytes 196616 | tf_op jit(solution)/shard_map/ppermute | solution.py:394
  273.3 7.1 %collective-permute-start.16 = (f32[64,256]{1,0:T(8,128)S(1)}, f32[64,256]{1,0:T(8,128)S(1)}, u32[]{:S(2)}, u32[]{:S(2)}) collective-permute-start(f32[64,256]{1,0:T(8,128)S(1)} %get-tuple-element.38), channel_id=1, source_target_pairs={{0,1},{1,5},{2,9},{3,13},{4,0},{5,4},{6,8},{7,12},{8,3},{9,7},{10,... | collective-permute-start | bytes 196616 | tf_op jit(solution)/shard_map/ppermute | solution.py:394
  277.1 3.5 %collective-permute-start.18 = (f32[64]{0:T(128)S(1)}, f32[64]{0:T(128)S(1)}, u32[]{:S(2)}, u32[]{:S(2)}) collective-permute-start(f32[64]{0:T(128)S(1)} %add.46), channel_id=1, source_target_pairs={{0,3},{1,7},{2,11},{3,15},{4,2},{5,6},{6,10},{7,14},{8,1},{9,5},{1... | collective-permute-start | bytes 776 | tf_op jit(solution)/shard_map/ppermute | solution.py:395
  277.1 4.2 %collective-permute-start.17 = (f32[64]{0:T(128)S(1)}, f32[64]{0:T(128)S(1)}, u32[]{:S(2)}, u32[]{:S(2)}) collective-permute-start(f32[64]{0:T(128)S(1)} %add.46), channel_id=1, source_target_pairs={{0,2},{1,6},{2,10},{3,14},{4,3},{5,7},{6,11},{7,15},{8,0},{9,4},{1... | collective-permute-start | bytes 776 | tf_op jit(solution)/shard_map/ppermute | solution.py:395
  (7 other events, 8.5 us)

commit v6 on v5

--- a/solution.py
+++ b/solution.py
@@ -41,7 +41,7 @@
 ROWS = 64
 WIDTH = 4 * LANES
 FREE = LANES * 2 - 1
-PARAMS = pltpu.CompilerParams(vmem_limit_bytes=56 * 1024 * 1024)
+PARAMS = pltpu.CompilerParams(vmem_limit_bytes=16 * 1024 * 1024)
 SMALL = pl.CostEstimate(flops=1000, bytes_accessed=1000, transcendentals=0)
 
 
@@ -61,7 +61,7 @@
     return lax.dot_general(a, b, (((1,), (1,)), ((), ())), preferred_element_type=jnp.float32)
 
 
-def first_potential(noise, volts, labels, third):
+def later_potentials(noise, volts, labels, third, token):
     frames, sites = noise.shape
     tile = third // STEPS
     rest = sites - 3 * third
@@ -69,44 +69,50 @@
     labels = labels.reshape(1, sites)
     volts = volts.T
 
-    def kernel(noise_ref, labels_ref, volts_ref, noise_rest, labels_rest, out):
-        def column_of(kind):
-            shape = (frames, frames)
-            diagonal = lax.broadcasted_iota(jnp.int32, shape, 0) == lax.broadcasted_iota(jnp.int32, shape, 1)
-            return jnp.sum(jnp.where(diagonal, volts_ref[kind:kind + 1, :], 0.0), axis=1, keepdims=True)
+    def kernel(noise_b, labels_b, noise_c, labels_c, noise_rest, labels_rest, volts_ref, token_ref, out_b, out_c):
+        diagonal = (lax.broadcasted_iota(jnp.int32, (frames, frames), 0)
+                    == lax.broadcasted_iota(jnp.int32, (frames, frames), 1))
+        columns = [jnp.sum(jnp.where(diagonal, volts_ref[kind:kind + 1, :], 0.0), axis=1, keepdims=True)
+                   for kind in range(volts_ref.shape[0])]
 
         def potential(noise, labels):
-            value = jnp.broadcast_to(column_of(0), noise.shape)
-            for kind in range(1, volts_ref.shape[0]):
-                value = jnp.where(labels == kind, column_of(kind), value)
+            value = jnp.broadcast_to(columns[0], noise.shape)
+            for kind in range(1, len(columns)):
+                value = jnp.where(labels == kind, columns[kind], value)
             return value + noise.astype(jnp.float32)
 
         step = pl.program_id(0)
         at = pl.multiple_of(step * tile, LANES)
-        out[:, pl.ds(at, tile)] = potential(noise_ref[...], labels_ref[...]).astype(jnp.bfloat16)
+        out_b[:, pl.ds(at, tile)] = potential(noise_b[...], labels_b[...]).astype(jnp.bfloat16)
+        out_c[...] = potential(noise_c[...], labels_c[...]).astype(jnp.bfloat16)
 
         @pl.when(step == 0)
         def _():
             column = lax.broadcasted_iota(jnp.int32, (frames, rest_width), 1)
             value = jnp.where(column < rest, potential(noise_rest[...], labels_rest[...]), 0.0)
-            out[:, third:] = value.astype(jnp.bfloat16)
+            out_b[:, third:] = value.astype(jnp.bfloat16)
 
     last = 3 * third // rest_width
     return pl.pallas_call(
         kernel,
         grid=(STEPS,),
         in_specs=[
-            pl.BlockSpec((frames, tile), lambda i: (0, i)),
-            pl.BlockSpec((1, tile), lambda i: (0, i)),
-            pl.BlockSpec(volts.shape, lambda i: (0, 0)),
+            pl.BlockSpec((frames, tile), lambda i: (0, STEPS + i)),
+            pl.BlockSpec((1, tile), lambda i: (0, STEPS + i)),
+            pl.BlockSpec((frames, tile), lambda i: (0, 2 * STEPS + i)),
+            pl.BlockSpec((1, tile), lambda i: (0, 2 * STEPS + i)),
             pl.BlockSpec((frames, rest_width), lambda i: (0, last)),
             pl.BlockSpec((1, rest_width), lambda i: (0, last)),
+            pl.BlockSpec(volts.shape, lambda i: (0, 0)),
+            pl.BlockSpec(memory_space=pl.ANY),
         ],
-        out_specs=pl.BlockSpec((frames, third + rest_width), lambda i: (0, 0)),
-        out_shape=jax.ShapeDtypeStruct((frames, third + rest_width), jnp.bfloat16),
+        out_specs=[pl.BlockSpec((frames, third + rest_width), lambda i: (0, 0)),
+                   pl.BlockSpec((frames, tile), lambda i: (0, i))],
+        out_shape=[jax.ShapeDtypeStruct((frames, third + rest_width), jnp.bfloat16),
+                   jax.ShapeDtypeStruct((frames, third), jnp.bfloat16)],
         compiler_params=PARAMS,
         cost_estimate=SMALL,
-    )(noise, labels, volts, noise, labels)
+    )(noise, labels, noise, labels, noise, labels, volts, token)
 
 
 def route(place, whole, sources, to_right, to_left, width, tokens):
@@ -181,15 +187,15 @@
         @pl.when(step == 0)
         def _():
             acc[...] = jnp.zeros(acc.shape, acc.dtype) if sums is None else sums_ref[...]
+            if turned is not None:
+                turned[...] = jnp.zeros(turned.shape, turned.dtype)
             if first:
                 column = lax.broadcasted_iota(jnp.int32, (nrows, rest_width), 1)
                 piece = jnp.where(column < rest, slab_rest[...].astype(jnp.float32), 0.0).astype(jnp.bfloat16)
-                first(z, dict(rests, slab=piece), add)
-
-            if turned is not None:
-                turned[...] = jnp.zeros(turned.shape, turned.dtype)
-
-        work(z, tiles, add, *([] if turned is None else [turned]))
+                first(z, dict(rests, slab=piece), add, turned)
+
+
+        work(z, tiles, add, turned)
 
         if profile is not None:
             @pl.when(step == STEPS - 1)
@@ -253,10 +259,6 @@
     def send(pair):
         return lax.ppermute(pair[0], "wide", right), lax.ppermute(pair[1], "wide", left)
 
-    def potential_at(first, end, before):
-        small = lax.optimization_barrier((volts, before))[0]
-        return potential_of(noise[:, first:end], small, labels[first:end])
-
     def mirror(choice):
         swap = {0: 0, 1: 2, 2: 1, 3: 4, 4: 3}
         return [swap.get(c) for c in reversed(choice)]
@@ -269,12 +271,12 @@
     def spare(i):
         return (slab, i, 2 * STEPS)
 
-    own_a = first_potential(noise, volts, labels, third)
-    long = own_a.shape[1]
+    rest = sites - 3 * third
+    long = third + rest + -rest % LANES
+    own_a = potential_of(noise[:, :long], volts, labels[:long])
     r1 = send((own_a, own_a))
-    own_b = potential_at(third, 2 * third, own_a)
+    own_b, own_c = later_potentials(noise, volts, labels, third, own_a)
     r2 = send((own_b, own_b))
-    own_c = potential_at(2 * third, 3 * third, own_b)
 
     sums_shape = (wide, frames, WIDTH)
 
@@ -299,7 +301,7 @@
     def both(name, pair, right_needed=from_left, left_needed=from_right):
         return {name + "r": (pair[0], right_needed, at(0)), name + "l": (pair[1], left_needed, at(0))}
 
-    def work1(z, refs, add):
+    def work1(z, refs, add, turned):
         add(z, 0, dot(refs["own"][...], refs["slab"][...]))
 
         @pl.when(z >= 1)
@@ -310,7 +312,7 @@
         def _():
             add(z + 1, 0, dot(refs["l"][...], refs["slab"][...]))
 
-    def work3(z, refs, add):
+    def work3(z, refs, add, turned):
         add(z, 0, dot(refs["own"][...], refs["slab2"][...]))
         add((z + 2) % 4, 0, dot(far(z, refs, ""), refs["slab"][...]))
 
@@ -318,10 +320,10 @@
         def _():
             add(jnp.where(z < 2, 0, 3), 0, dot(near(z, refs, ""), refs["slab2"][...]))
 
-    def work4(z, refs, add):
+    def work4(z, refs, add, turned):
         add((z + 2) % 4, 0, dot(far(z, refs, ""), refs["slab"][...]))
 
-    def work5(z, refs, add):
+    def work5(z, refs, add, turned):
         came = far(z, refs, "")
         add(3 - z, 0, dot(came, refs["slab"][...]))
 
@@ -331,13 +333,13 @@
             add(z, 2 * LANES, dot(refs["own"][...], brought))
             add(3 - z, 2 * LANES, dot(came, brought))
 
-    def first3(z, refs, add):
+    def first4(z, refs, add, turned):
         add((z + 2) % 4, 0, dot(far(z, refs, ""), refs["slab"]))
 
-    def first5(z, refs, add):
+    def first6(z, refs, add, turned):
         @pl.when(is_end(z))
         def _():
-            add(3 - z, 0, dot(far(z, refs, ""), refs["slab"]))
+            turned[:nrows, :frames] += dot(refs["slab"], far(z, refs, ""))
 
     def work6(z, refs, add, turned):
         came = far(z, refs, "")
@@ -359,26 +361,25 @@
         return z == 2
 
     r3, sent = routed([own_c, r1[0], r1[1]], [0, 1, 1, None], long, [])
-    r4, sent = routed([spare(0), r2[0], r2[1]], [0, 1, 1, None], third, [sent])
+    r4, sent = routed([spare(0), r2[0], r2[1]], [0, 1, 1, None], long, [sent])
     sums = absorb(
-        place, third, dict(both("", r1), slab=(slab, always, at(0)), own=(own_a, always, at(0))), work1, sums_shape, None,
+        place, third, dict(both("", r1), slab=(slab, always, at(0)), own=(own_a, always, at(0))), work1, sums_shape, None)
+    sums = absorb(
+        place, third, dict(both("", r2), slab=(slab, always, at(1)), own=(own_b, always, at(0))), work1, sums_shape, sums,
         first=work1)
-    sums = absorb(
-        place, third, dict(both("", r2), slab=(slab, always, at(1)), own=(own_b, always, at(0))), work1, sums_shape, sums)
     r5, sent = routed([spare(1), r3[0], r3[1], own_c, own_c], [0, 3, 1, None], long, [sent, sums])
     sums = absorb(
         place, third,
         dict(both("", r3), slab=(slab, always, at(0)), slab2=(slab, always, at(2)), own=(own_c, always, at(0))),
-        work3, sums_shape, sums, first=first3)
-    r6, sent = routed([spare(2), r3[0], r3[1], r4[0], r4[1]], [0, 1, 3, None], third, [sent, sums])
+        work3, sums_shape, sums)
+    r6, sent = routed([spare(2), r3[0], r3[1], r4[0], r4[1]], [0, 1, 3, None], long, [sent, sums])
     sums = absorb(
-        place, third, dict(both("", r4), slab=(slab, always, at(1))), work4, sums_shape, sums)
+        place, third, dict(both("", r4), slab=(slab, always, at(1))), work4, sums_shape, sums, first=first4)
     middle = dict(both("4", r4, near_right, near_left), own=(own_c, is_mid, at(0)))
-    sums = absorb(place, third, dict(both("", r5), slab=(slab, always, thirds(0, 2)), **middle), work5, sums_shape, sums,
-        first=first5)
+    sums = absorb(place, third, dict(both("", r5), slab=(slab, always, thirds(0, 2)), **middle), work5, sums_shape, sums)
     messages = absorb(
         place, third, dict(both("", r6), slab=(slab, always, thirds(1, 2)), **both("5", r5, is_mid, is_mid), **middle),
-        work6, sums_shape, sums, profile=profile)
+        work6, sums_shape, sums, first=first6, profile=profile)
 
     summed = messages[0]
     for turn in range(1, owners):

time: 287 us -> 264 us (0.920)
  Pallas kernels: 71.8 us -> 49.2 us
  other arithmetic: 10.6 us -> 4.67 us
  starting transfers between devices: 52.5 us -> 56.8 us
  local copies, waits for them, and re-layouts: 9.61 us -> 13.5 us
    pallas_call x6, Pallas kernels: 47 us -> 31.9 us  [absorb(): pl.pallas_call(kernel, grid_spec=pltpu.PrefetchScalarGridSpec(num_scalar_...]
    ppermute x6, waiting for transfers between devices: 97.7 us -> 90.5 us  [send(): lax.ppermute(pair[1], 'wide', left)]
    pallas_call x4, Pallas kernels: 20.7 us -> 13.8 us  [route(): pl.pallas_call(kernel, grid_spec=pltpu.PrefetchScalarGridSpec(num_scalar_...]
    ppermute x6, waiting for transfers between devices: 31.7 us -> 37.3 us  [send(): lax.ppermute(pair[0], 'wide', right)]
    unnamed x24 -> x22, local copies, waits for them, and re-layouts: 7.21 us -> 12 us
    convert_element_type x2 -> x1, other arithmetic: 6.39 us -> 1.99 us  [potential_of(): return (value + noise.astype(jnp.float32)).astype(jnp.bfloat16)]
    ppermute x6, starting transfers between devices: 28.7 us -> 32.5 us  [send(): lax.ppermute(pair[0], 'wide', right)]
  transfers between devices with their start and end apart: 19 -> 19, of which waited for: 13 -> 15; matrix products, arithmetic and copies ran while one was open for 2% -> 0% of each run, Pallas kernels for 21% -> 17%
where the time goes in v6:
time: 264 us; the launch traced here: 261 us
  waiting for transfers between devices  136 us (52%)
  starting transfers between devices  56.8 us (22%)
  Pallas kernels  49.2 us (19%)
  local copies, waits for them, and re-layouts  13.5 us (5%)
  other arithmetic  4.67 us (2%)
    ppermute x6, waiting for transfers between devices, send(): lax.ppermute(pair[1], 'wide', left)  90.5 us
    ppermute x6, waiting for transfers between devices, send(): lax.ppermute(pair[0], 'wide', right)  37.3 us
    ppermute x6, starting transfers between devices, send(): lax.ppermute(pair[0], 'wide', right)  32.5 us
    pallas_call x6, Pallas kernels, absorb(): pl.pallas_call(kernel, grid_spec=pltpu.PrefetchScalarGridSpec(num_scalar_...  31.9 us
    pallas_call x4, Pallas kernels, route(): pl.pallas_call(kernel, grid_spec=pltpu.PrefetchScalarGridSpec(num_scalar_...  13.8 us
    unnamed x22, local copies, waits for them, and re-layouts  12 us
    ppermute x6, starting transfers between devices, send(): lax.ppermute(pair[1], 'wide', left)  8.16 us
    ppermute x1, starting transfers between devices, line_plan(): lax.ppermute(mine, ALL, flip(0))  7.46 us
  transfers between devices with their start and end apart: 19, of which 15 were waited for; matrix products, arithmetic and copies ran while one was open for 0% of the time, Pallas kernels for 17%

profile of v6, /device:TPU:3, one launch (start us, length us, event | category | flops | bytes accessed | tf_op | source)
XLA Modules:
  0.0 260.8 jit_solution(2072325503629094515)
XLA Ops:
  4.9 5.2 %collective-permute-start = (bf16[64,13440]{1,0:T(8,128)(2,1)S(1)}, bf16[64,13440]{1,0:T(8,128)(2,1)}, u32[]{:S(2)}, u32[]{:S(2)}) collective-permute-start(bf16[64,13440]{1,0:T(8,128)(2,1)S(1)} %add_convert_fusion.token_ref.refs_3_), channel_id=1, source_target_pairs={{0,4},{4,8},{8,12},{1,5},{5,9},{9,13},{2,6},{6,10},{10,14},{3,7},{... | collective-permute-start | bytes 5160968 | tf_op jit(solution)/shard_map/ppermute | solution.py:260
  12.7 3.6 %shard_map.55 = (bf16[64,13440]{1,0:T(8,128)(2,1)}, bf16[64,13312]{1,0:T(8,128)(2,1)S(1)}) custom-call(bf16[64,40000]{1,0:T(8,128)(2,1)S(1)} %copy-done.2, s32[1,40000]{1,0:T(1,128)S(1)} %reshape.25.labels_b.labels_c.labels_rest, bf16[64,40000]{1,0:T(8,128)(2,1)S(1)} %copy-done.2, s32[1,40000]{1,0:T(1,128)S(1)} %reshape.25.labels_b.labels_c.labels_rest, ...), custom_call_target="tpu_custom_call" | custom-call | flops 1000 | bytes 1000 | tf_op jit(solution)/shard_map/pallas_call | solution.py:96
  17.5 5.2 %collective-permute-start.4 = (bf16[64,13440]{1,0:T(8,128)(2,1)}, bf16[64,13440]{1,0:T(8,128)(2,1)}, u32[]{:S(2)}, u32[]{:S(2)}) collective-permute-start(bf16[64,13440]{1,0:T(8,128)(2,1)} %get-tuple-element.22.refs_3_.refs_8_), channel_id=1, source_target_pairs={{0,4},{4,8},{8,12},{1,5},{5,9},{9,13},{2,6},{6,10},{10,14},{3,7},{... | collective-permute-start | bytes 5160968 | tf_op jit(solution)/shard_map/ppermute | solution.py:260
  22.8 21.2 %collective-permute-done.1.refs_2_.refs_1_ = bf16[64,13440]{1,0:T(8,128)(2,1)} collective-permute-done((bf16[64,13440]{1,0:T(8,128)(2,1)S(1)}, bf16[64,13440]{1,0:T(8,128)(2,1)}, u32[]{:S(2)}, u32[]{:S(2)}) %collective-permute-start.1) | collective-permute-done | bytes 1720352 | tf_op jit(solution)/shard_map/ppermute | solution.py:260
  44.8 4.4 %shard_map.56 = (bf16[64,13440]{1,0:T(8,128)(2,1)}, bf16[64,13440]{1,0:T(8,128)(2,1)}) custom-call(s32[2]{0:T(128)S(1)} %pad_add_fusion.place_ref, bf16[64,13312]{1,0:T(8,128)(2,1)S(1)} %get-tuple-element.19.refs_0_.refs_3_.refs_4_.refs_5_.refs_7_, bf16[64,13440]{1,0:T(8,128)(2,1)} %collective-permute-done.refs_1_.refs_0_, ...), custom_call_target="tpu_custom_call" | custom-call | flops 1000 | bytes 1000 | tf_op jit(solution)/shard_map/pallas_call | solution.py:145
  50.5 5.9 %collective-permute-start.2 = (bf16[64,13440]{1,0:T(8,128)(2,1)}, bf16[64,13440]{1,0:T(8,128)(2,1)S(1)}, u32[]{:S(2)}, u32[]{:S(2)}) collective-permute-start(bf16[64,13440]{1,0:T(8,128)(2,1)} %get-tuple-element.20.refs_3_), channel_id=1, source_target_pairs={{0,4},{4,8},{8,12},{1,5},{5,9},{9,13},{2,6},{6,10},{10,14},{3,7},{... | collective-permute-start | bytes 5160968 | tf_op jit(solution)/shard_map/ppermute | solution.py:260
  56.4 24.5 %collective-permute-done.5.refs_2_.refs_1_.refs_7_ = bf16[64,13440]{1,0:T(8,128)(2,1)} collective-permute-done((bf16[64,13440]{1,0:T(8,128)(2,1)}, bf16[64,13440]{1,0:T(8,128)(2,1)}, u32[]{:S(2)}, u32[]{:S(2)}) %collective-permute-start.5) | collective-permute-done | bytes 1720352 | tf_op jit(solution)/shard_map/ppermute | solution.py:260
  81.8 5.4 %copy-done = bf16[2,96,40000]{2,1,0:T(8,128)(2,1)S(1)} copy-done((bf16[2,96,40000]{2,1,0:T(8,128)(2,1)S(1)}, bf16[2,96,40000]{2,1,0:T(8,128)(2,1)}, u32[]{:S(2)}) %copy-start) | copy-done | bytes 15360024
  87.1 4.8 %shard_map.57 = (bf16[64,13440]{1,0:T(8,128)(2,1)}, bf16[64,13440]{1,0:T(8,128)(2,1)}) custom-call(s32[2]{0:T(128)S(1)} %pad_add_fusion.place_ref, bf16[192,40000]{1,0:T(8,128)(2,1)S(1)} %bitcast.11, bf16[64,13440]{1,0:T(8,128)(2,1)} %collective-permute-done.4.refs_1_.refs_0_.refs_6_, bf16[64,13440]{1,0:T(8,128)(2,1)} %collective-permute-done.5.refs_2_.refs_1_.refs_7_, ...), custom_call_target="tpu_custom_call" | custom-call | flops 1000 | bytes 1000 | tf_op jit(solution)/shard_map/pallas_call | solution.py:145
  93.5 6.6 %collective-permute-start.6 = (bf16[64,13440]{1,0:T(8,128)(2,1)}, bf16[64,13440]{1,0:T(8,128)(2,1)S(1)}, u32[]{:S(2)}, u32[]{:S(2)}) collective-permute-start(bf16[64,13440]{1,0:T(8,128)(2,1)} %get-tuple-element.23.refs_5_), channel_id=1, source_target_pairs={{0,4},{4,8},{8,12},{1,5},{5,9},{9,13},{2,6},{6,10},{10,14},{3,7},{... | collective-permute-start | bytes 5160968 | tf_op jit(solution)/shard_map/ppermute | solution.py:260
  100.1 6.5 %shard_map.58.refs_4_ = f32[4,64,512]{2,1,0:T(8,128)S(1)} custom-call(s32[2]{0:T(128)S(1)} %pad_add_fusion.place_ref, bf16[64,13440]{1,0:T(8,128)(2,1)} %collective-permute-done.refs_1_.refs_0_, bf16[64,13440]{1,0:T(8,128)(2,1)} %collective-permute-done.1.refs_2_.refs_1_, bf16[192,40000]{1,0:T(8,128)(2,1)S(1)} %bitcast.12, ...), custom_call_target="tpu_custom_call" | custom-call | flops 1000 | bytes 1000 | tf_op jit(solution)/shard_map/pallas_call | solution.py:236
  106.6 7.0 %shard_map.59.refs_6_.refs_5_ = f32[4,64,512]{2,1,0:T(8,128)S(1)} custom-call(s32[2]{0:T(128)S(1)} %pad_add_fusion.place_ref, bf16[64,13440]{1,0:T(8,128)(2,1)} %collective-permute-done.4.refs_1_.refs_0_.refs_6_, bf16[64,13440]{1,0:T(8,128)(2,1)} %collective-permute-done.5.refs_2_.refs_1_.refs_7_, bf16[192,40000]{1,0:T(8,128)(2,1)S(1)} %bitcast.13, ...), custom_call_target="tpu_custom_call" | custom-call | flops 1000 | bytes 1000 | tf_op jit(solution)/shard_map/pallas_call | solution.py:236
  113.6 4.0 %collective-permute-done.3.refs_2_.refs_1_ = bf16[64,13440]{1,0:T(8,128)(2,1)S(1)} collective-permute-done((bf16[64,13440]{1,0:T(8,128)(2,1)}, bf16[64,13440]{1,0:T(8,128)(2,1)S(1)}, u32[]{:S(2)}, u32[]{:S(2)}) %collective-permute-start.3) | collective-permute-done | bytes 1720352 | tf_op jit(solution)/shard_map/ppermute | solution.py:260
  124.9 5.1 %collective-permute-start.10 = (bf16[64,13440]{1,0:T(8,128)(2,1)S(1)}, bf16[64,13440]{1,0:T(8,128)(2,1)S(1)}, u32[]{:S(2)}, u32[]{:S(2)}) collective-permute-start(bf16[64,13440]{1,0:T(8,128)(2,1)S(1)} %get-tuple-element.25.refs_5_), channel_id=1, source_target_pairs={{0,4},{4,8},{8,12},{1,5},{5,9},{9,13},{2,6},{6,10},{10,14},{3,7},{... | collective-permute-start | bytes 5160968 | tf_op jit(solution)/shard_map/ppermute | solution.py:260
  130.0 6.0 %shard_map.61.refs_6_.refs_3_ = f32[4,64,512]{2,1,0:T(8,128)S(1)} custom-call(s32[2]{0:T(128)S(1)} %pad_add_fusion.place_ref, bf16[64,13440]{1,0:T(8,128)(2,1)S(1)} %copy-done.6, bf16[64,13440]{1,0:T(8,128)(2,1)S(1)} %collective-permute-done.3.refs_2_.refs_1_, bf16[192,40000]{1,0:T(8,128)(2,1)S(1)} %bitcast.16, bf16[192,40000]{1,0:T(8,128)(2,1)S(1)} %bitcast.17, ...), custom_call_target="tpu_custom_call" | custom-call | flops 1000 | bytes 1000 | tf_op jit(solution)/shard_map/pallas_call | solution.py:236
  136.0 18.5 %collective-permute-done.7.refs_4_.refs_1_.refs_6_ = bf16[64,13440]{1,0:T(8,128)(2,1)S(1)} collective-permute-done((bf16[64,13440]{1,0:T(8,128)(2,1)}, bf16[64,13440]{1,0:T(8,128)(2,1)S(1)}, u32[]{:S(2)}, u32[]{:S(2)}) %collective-permute-start.7) | collective-permute-done | bytes 1720352 | tf_op jit(solution)/shard_map/ppermute | solution.py:260
  159.3 4.5 %collective-permute-start.8 = (bf16[64,13440]{1,0:T(8,128)(2,1)S(1)}, bf16[64,13440]{1,0:T(8,128)(2,1)S(1)}, u32[]{:S(2)}, u32[]{:S(2)}) collective-permute-start(bf16[64,13440]{1,0:T(8,128)(2,1)S(1)} %get-tuple-element.26), channel_id=1, source_target_pairs={{0,4},{4,8},{8,12},{1,5},{5,9},{9,13},{2,6},{6,10},{10,14},{3,7},{... | collective-permute-start | bytes 5160968 | tf_op jit(solution)/shard_map/ppermute | solution.py:260
  165.3 3.9 %shard_map.63.refs_6_ = f32[4,64,512]{2,1,0:T(8,128)S(1)} custom-call(s32[2]{0:T(128)S(1)} %pad_add_fusion.place_ref, bf16[64,13440]{1,0:T(8,128)(2,1)S(1)} %collective-permute-done.6.refs_3_.refs_0_.refs_5_, bf16[64,13440]{1,0:T(8,128)(2,1)S(1)} %collective-permute-done.7.refs_4_.refs_1_.refs_6_, bf16[192,40000]{1,0:T(8,128)(2,1)S(1)} %bitcast.19, ...), custom_call_target="tpu_custom_call" | custom-call | flops 1000 | bytes 1000 | tf_op jit(solution)/shard_map/pallas_call | solution.py:236
  169.2 22.2 %collective-permute-done.11.refs_1_.refs_4_ = bf16[64,13440]{1,0:T(8,128)(2,1)S(1)} collective-permute-done((bf16[64,13440]{1,0:T(8,128)(2,1)S(1)}, bf16[64,13440]{1,0:T(8,128)(2,1)S(1)}, u32[]{:S(2)}, u32[]{:S(2)}) %collective-permute-start.11) | collective-permute-done | bytes 1720352 | tf_op jit(solution)/shard_map/ppermute | solution.py:260
  192.3 4.0 %shard_map.64.refs_8_ = f32[4,64,512]{2,1,0:T(8,128)S(1)} custom-call(s32[2]{0:T(128)S(1)} %pad_add_fusion.place_ref, bf16[64,13440]{1,0:T(8,128)(2,1)S(1)} %collective-permute-done.10.refs_0_.refs_3_, bf16[64,13440]{1,0:T(8,128)(2,1)S(1)} %collective-permute-done.11.refs_1_.refs_4_, bf16[192,40000]{1,0:T(8,128)(2,1)S(1)} %bitcast.21, ...), custom_call_target="tpu_custom_call" | custom-call | flops 1000 | bytes 1000 | tf_op jit(solution)/shard_map/pallas_call | solution.py:236
  196.2 32.9 %collective-permute-done.8.refs_0_.refs_10_ = bf16[64,13440]{1,0:T(8,128)(2,1)S(1)} collective-permute-done((bf16[64,13440]{1,0:T(8,128)(2,1)S(1)}, bf16[64,13440]{1,0:T(8,128)(2,1)S(1)}, u32[]{:S(2)}, u32[]{:S(2)}) %collective-permute-start.8) | collective-permute-done | bytes 1720352 | tf_op jit(solution)/shard_map/ppermute | solution.py:260
  229.1 4.5 %shard_map.65 = (f32[64,512]{1,0:T(8,128)S(1)}, f32[64,512]{1,0:T(8,128)S(1)}, f32[64,512]{1,0:T(8,128)S(1)}, f32[64,512]{1,0:T(8,128)S(1)}) custom-call(s32[2]{0:T(128)S(1)} %pad_add_fusion.place_ref, bf16[64,13440]{1,0:T(8,128)(2,1)S(1)} %collective-permute-done.8.refs_0_.refs_10_, bf16[64,13440]{1,0:T(8,128)(2,1)S(1)} %collective-permute-done.9.refs_1_.refs_11_, ...), custom_call_target="tpu_custom_call" | custom-call | flops 1000 | bytes 1000 | tf_op jit(solution)/shard_map/pallas_call | solution.py:236
  237.3 3.4 %collective-permute-done.13 = f32[64,512]{1,0:T(8,128)S(1)} collective-permute-done((f32[64,512]{1,0:T(8,128)S(1)}, f32[64,512]{1,0:T(8,128)S(1)}, u32[]{:S(2)}, u32[]{:S(2)}) %collective-permute-start.13) | collective-permute-done | bytes 131104 | tf_op jit(solution)/shard_map/ppermute | solution.py:386
  243.9 7.5 %collective-permute-start.15 = (f32[64,256]{1,0:T(8,128)S(1)}, f32[64,256]{1,0:T(8,128)S(1)}, u32[]{:S(2)}, u32[]{:S(2)}) collective-permute-start(f32[64,256]{1,0:T(8,128)S(1)} %get-tuple-element.35), channel_id=1, source_target_pairs={{0,0},{1,4},{2,8},{3,12},{4,1},{5,5},{6,9},{7,13},{8,2},{9,6},{10,... | collective-permute-start | bytes 196616 | tf_op jit(solution)/shard_map/ppermute | solution.py:395
  (63 shorter events, 43.8 us)
Async XLA Ops:
  1.6 8.6 %copy-start.9 = (f32[64,2]{0,1:T(2,128)S(1)}, f32[64,2]{0,1:T(2,128)}, u32[]{:S(2)}) copy-start(f32[64,2]{0,1:T(2,128)} %param.7) | copy-start | bytes 1540
  3.6 40.4 %collective-permute-start.1 = (bf16[64,13440]{1,0:T(8,128)(2,1)S(1)}, bf16[64,13440]{1,0:T(8,128)(2,1)}, u32[]{:S(2)}, u32[]{:S(2)}) collective-permute-start(bf16[64,13440]{1,0:T(8,128)(2,1)S(1)} %add_convert_fusion.token_ref.refs_3_), channel_id=1, source_target_pairs={{12,8},{8,4},{4,0},{13,9},{9,5},{5,1},{14,10},{10,6},{6,2},{15,11}... | collective-permute-start | bytes 5160968 | tf_op jit(solution)/shard_map/ppermute | solution.py:260
  4.9 39.9 %collective-permute-start = (bf16[64,13440]{1,0:T(8,128)(2,1)S(1)}, bf16[64,13440]{1,0:T(8,128)(2,1)}, u32[]{:S(2)}, u32[]{:S(2)}) collective-permute-start(bf16[64,13440]{1,0:T(8,128)(2,1)S(1)} %add_convert_fusion.token_ref.refs_3_), channel_id=1, source_target_pairs={{0,4},{4,8},{8,12},{1,5},{5,9},{9,13},{2,6},{6,10},{10,14},{3,7},{... | collective-permute-start | bytes 5160968 | tf_op jit(solution)/shard_map/ppermute | solution.py:260
  16.2 64.6 %collective-permute-start.5 = (bf16[64,13440]{1,0:T(8,128)(2,1)}, bf16[64,13440]{1,0:T(8,128)(2,1)}, u32[]{:S(2)}, u32[]{:S(2)}) collective-permute-start(bf16[64,13440]{1,0:T(8,128)(2,1)} %get-tuple-element.22.refs_3_.refs_8_), channel_id=1, source_target_pairs={{12,8},{8,4},{4,0},{13,9},{9,5},{5,1},{14,10},{10,6},{6,2},{15,11}... | collective-permute-start | bytes 5160968 | tf_op jit(solution)/shard_map/ppermute | solution.py:260
  17.5 64.2 %collective-permute-start.4 = (bf16[64,13440]{1,0:T(8,128)(2,1)}, bf16[64,13440]{1,0:T(8,128)(2,1)}, u32[]{:S(2)}, u32[]{:S(2)}) collective-permute-start(bf16[64,13440]{1,0:T(8,128)(2,1)} %get-tuple-element.22.refs_3_.refs_8_), channel_id=1, source_target_pairs={{0,4},{4,8},{8,12},{1,5},{5,9},{9,13},{2,6},{6,10},{10,14},{3,7},{... | collective-permute-start | bytes 5160968 | tf_op jit(solution)/shard_map/ppermute | solution.py:260
  49.2 68.4 %collective-permute-start.3 = (bf16[64,13440]{1,0:T(8,128)(2,1)}, bf16[64,13440]{1,0:T(8,128)(2,1)S(1)}, u32[]{:S(2)}, u32[]{:S(2)}) collective-permute-start(bf16[64,13440]{1,0:T(8,128)(2,1)} %get-tuple-element.21), channel_id=1, source_target_pairs={{12,8},{8,4},{4,0},{13,9},{9,5},{5,1},{14,10},{10,6},{6,2},{15,11}... | collective-permute-start | bytes 5160968 | tf_op jit(solution)/shard_map/ppermute | solution.py:260
  50.5 68.1 %collective-permute-start.2 = (bf16[64,13440]{1,0:T(8,128)(2,1)}, bf16[64,13440]{1,0:T(8,128)(2,1)S(1)}, u32[]{:S(2)}, u32[]{:S(2)}) collective-permute-start(bf16[64,13440]{1,0:T(8,128)(2,1)} %get-tuple-element.20.refs_3_), channel_id=1, source_target_pairs={{0,4},{4,8},{8,12},{1,5},{5,9},{9,13},{2,6},{6,10},{10,14},{3,7},{... | collective-permute-start | bytes 5160968 | tf_op jit(solution)/shard_map/ppermute | solution.py:260
  87.1 12.9 %copy-start.1 = (bf16[2,96,40000]{2,1,0:T(8,128)(2,1)S(1)}, bf16[2,96,40000]{2,1,0:T(8,128)(2,1)}, u32[]{:S(2)}) copy-start(bf16[2,96,40000]{2,1,0:T(8,128)(2,1)} %param.5) | copy-start | bytes 46080004
  91.9 62.6 %collective-permute-start.7 = (bf16[64,13440]{1,0:T(8,128)(2,1)}, bf16[64,13440]{1,0:T(8,128)(2,1)S(1)}, u32[]{:S(2)}, u32[]{:S(2)}) collective-permute-start(bf16[64,13440]{1,0:T(8,128)(2,1)} %get-tuple-element.24), channel_id=1, source_target_pairs={{12,8},{8,4},{4,0},{13,9},{9,5},{5,1},{14,10},{10,6},{6,2},{15,11}... | collective-permute-start | bytes 5160968 | tf_op jit(solution)/shard_map/ppermute | solution.py:260
  93.5 62.0 %collective-permute-start.6 = (bf16[64,13440]{1,0:T(8,128)(2,1)}, bf16[64,13440]{1,0:T(8,128)(2,1)S(1)}, u32[]{:S(2)}, u32[]{:S(2)}) collective-permute-start(bf16[64,13440]{1,0:T(8,128)(2,1)} %get-tuple-element.23.refs_5_), channel_id=1, source_target_pairs={{0,4},{4,8},{8,12},{1,5},{5,9},{9,13},{2,6},{6,10},{10,14},{3,7},{... | collective-permute-start | bytes 5160968 | tf_op jit(solution)/shard_map/ppermute | solution.py:260
  117.7 12.4 %copy-start.3 = (bf16[64,13440]{1,0:T(8,128)(2,1)}, bf16[64,13440]{1,0:T(8,128)(2,1)S(1)}, u32[]{:S(2)}) copy-start(bf16[64,13440]{1,0:T(8,128)(2,1)S(1)} %collective-permute-done.3.refs_2_.refs_1_) | copy-start | bytes 5160964
  123.6 67.8 %collective-permute-start.11 = (bf16[64,13440]{1,0:T(8,128)(2,1)S(1)}, bf16[64,13440]{1,0:T(8,128)(2,1)S(1)}, u32[]{:S(2)}, u32[]{:S(2)}) collective-permute-start(bf16[64,13440]{1,0:T(8,128)(2,1)S(1)} %get-tuple-element.28), channel_id=1, source_target_pairs={{12,8},{8,4},{4,0},{13,9},{9,5},{5,1},{14,10},{10,6},{6,2},{15,11}... | collective-permute-start | bytes 5160968 | tf_op jit(solution)/shard_map/ppermute | solution.py:260
  124.9 30.6 %copy-start.7 = (bf16[64,13440]{1,0:T(8,128)(2,1)S(1)}, bf16[64,13440]{1,0:T(8,128)(2,1)}, u32[]{:S(2)}) copy-start(bf16[64,13440]{1,0:T(8,128)(2,1)} %copy-done.5) | copy-start | bytes 5160964
  124.9 67.4 %collective-permute-start.10 = (bf16[64,13440]{1,0:T(8,128)(2,1)S(1)}, bf16[64,13440]{1,0:T(8,128)(2,1)S(1)}, u32[]{:S(2)}, u32[]{:S(2)}) collective-permute-start(bf16[64,13440]{1,0:T(8,128)(2,1)S(1)} %get-tuple-element.25.refs_5_), channel_id=1, source_target_pairs={{0,4},{4,8},{8,12},{1,5},{5,9},{9,13},{2,6},{6,10},{10,14},{3,7},{... | collective-permute-start | bytes 5160968 | tf_op jit(solution)/shard_map/ppermute | solution.py:260
  159.3 69.8 %collective-permute-start.8 = (bf16[64,13440]{1,0:T(8,128)(2,1)S(1)}, bf16[64,13440]{1,0:T(8,128)(2,1)S(1)}, u32[]{:S(2)}, u32[]{:S(2)}) collective-permute-start(bf16[64,13440]{1,0:T(8,128)(2,1)S(1)} %get-tuple-element.26), channel_id=1, source_target_pairs={{0,4},{4,8},{8,12},{1,5},{5,9},{9,13},{2,6},{6,10},{10,14},{3,7},{... | collective-permute-start | bytes 5160968 | tf_op jit(solution)/shard_map/ppermute | solution.py:260
  163.8 65.3 %collective-permute-start.9 = (bf16[64,13440]{1,0:T(8,128)(2,1)S(1)}, bf16[64,13440]{1,0:T(8,128)(2,1)S(1)}, u32[]{:S(2)}, u32[]{:S(2)}) collective-permute-start(bf16[64,13440]{1,0:T(8,128)(2,1)S(1)} %get-tuple-element.27), channel_id=1, source_target_pairs={{12,8},{8,4},{4,0},{13,9},{9,5},{5,1},{14,10},{10,6},{6,2},{15,11}... | collective-permute-start | bytes 5160968 | tf_op jit(solution)/shard_map/ppermute | solution.py:260
  169.1 60.0 %copy-start.8 = (f32[2,96]{1,0:T(2,128)S(1)}, f32[2,96]{1,0:T(2,128)}, u32[]{:S(2)}) copy-start(f32[2,96]{1,0:T(2,128)} %refs_12_.1) | copy-start | bytes 2308
  233.7 3.6 %collective-permute-start.12 = (f32[64,512]{1,0:T(8,128)S(1)}, f32[64,512]{1,0:T(8,128)S(1)}, u32[]{:S(2)}, u32[]{:S(2)}) collective-permute-start(f32[64,512]{1,0:T(8,128)S(1)} %get-tuple-element.30), channel_id=1, source_target_pairs={{0,1},{1,0},{2,3},{3,2},{4,5},{5,4},{6,7},{7,6},{8,9},{9,8},{10,11... | collective-permute-start | bytes 393224 | tf_op jit(solution)/shard_map/ppermute | solution.py:386
  235.6 5.1 %collective-permute-start.13 = (f32[64,512]{1,0:T(8,128)S(1)}, f32[64,512]{1,0:T(8,128)S(1)}, u32[]{:S(2)}, u32[]{:S(2)}) collective-permute-start(f32[64,512]{1,0:T(8,128)S(1)} %get-tuple-element.31), channel_id=1, source_target_pairs={{0,2},{1,3},{2,0},{3,1},{4,6},{5,7},{6,4},{7,5},{8,10},{9,11},{10,... | collective-permute-start | bytes 393224 | tf_op jit(solution)/shard_map/ppermute | solution.py:386
  235.7 7.9 %collective-permute-start.14 = (f32[64,512]{1,0:T(8,128)S(1)}, f32[64,512]{1,0:T(8,128)S(1)}, u32[]{:S(2)}, u32[]{:S(2)}) collective-permute-start(f32[64,512]{1,0:T(8,128)S(1)} %get-tuple-element.32), channel_id=1, source_target_pairs={{0,3},{1,2},{2,1},{3,0},{4,7},{5,6},{6,5},{7,4},{8,11},{9,10},{10,... | collective-permute-start | bytes 393224 | tf_op jit(solution)/shard_map/ppermute | solution.py:386
  243.9 13.1 %collective-permute-start.15 = (f32[64,256]{1,0:T(8,128)S(1)}, f32[64,256]{1,0:T(8,128)S(1)}, u32[]{:S(2)}, u32[]{:S(2)}) collective-permute-start(f32[64,256]{1,0:T(8,128)S(1)} %get-tuple-element.35), channel_id=1, source_target_pairs={{0,0},{1,4},{2,8},{3,12},{4,1},{5,5},{6,9},{7,13},{8,2},{9,6},{10,... | collective-permute-start | bytes 196616 | tf_op jit(solution)/shard_map/ppermute | solution.py:395
  251.4 7.1 %collective-permute-start.16 = (f32[64,256]{1,0:T(8,128)S(1)}, f32[64,256]{1,0:T(8,128)S(1)}, u32[]{:S(2)}, u32[]{:S(2)}) collective-permute-start(f32[64,256]{1,0:T(8,128)S(1)} %get-tuple-element.36), channel_id=1, source_target_pairs={{0,1},{1,5},{2,9},{3,13},{4,0},{5,4},{6,8},{7,12},{8,3},{9,7},{10,... | collective-permute-start | bytes 196616 | tf_op jit(solution)/shard_map/ppermute | solution.py:395
  255.2 3.6 %collective-permute-start.18 = (f32[64]{0:T(128)S(1)}, f32[64]{0:T(128)S(1)}, u32[]{:S(2)}, u32[]{:S(2)}) collective-permute-start(f32[64]{0:T(128)S(1)} %add.42), channel_id=1, source_target_pairs={{0,3},{1,7},{2,11},{3,15},{4,2},{5,6},{6,10},{7,14},{8,1},{9,5},{1... | collective-permute-start | bytes 776 | tf_op jit(solution)/shard_map/ppermute | solution.py:396
  255.2 4.2 %collective-permute-start.17 = (f32[64]{0:T(128)S(1)}, f32[64]{0:T(128)S(1)}, u32[]{:S(2)}, u32[]{:S(2)}) collective-permute-start(f32[64]{0:T(128)S(1)} %add.42), channel_id=1, source_target_pairs={{0,2},{1,6},{2,10},{3,14},{4,3},{5,7},{6,11},{7,15},{8,0},{9,4},{1... | collective-permute-start | bytes 776 | tf_op jit(solution)/shard_map/ppermute | solution.py:396
  (6 other events, 20.5 us)

commit v7 on v6

--- a/solution.py
+++ b/solution.py
@@ -115,7 +115,7 @@
     )(noise, labels, noise, labels, noise, labels, volts, token)
 
 
-def route(place, whole, sources, to_right, to_left, width, tokens):
+def route(place, whole, sources, to_right, to_left, start, width, tokens):
     tile = whole // STEPS
     count = len(sources)
     frames = ROWS
@@ -137,7 +137,7 @@
 
         def index(i, s):
             used = sum((s[0] == here).astype(jnp.int32) for here in users)
-            return row, jnp.minimum(column + i * used, last)
+            return row, jnp.minimum(column + start + i * used, last)
 
         return pl.BlockSpec((frames, tile), index)
 
@@ -154,18 +154,19 @@
     )(place, *[s[0] for s in sources], *tokens)
 
 
-def absorb(place, whole, streams, work, sums_shape, sums, first=None, profile=None):
+def absorb(place, whole, streams, work, sums_shape, sums, first=None, profile=None, tiles=(0, STEPS)):
+    start, count = tiles
     tile = whole // STEPS
     names = list(streams)
     slab = streams["slab"][0]
     nrows, sites = slab.shape
     rest = sites - 3 * whole
     rest_width = rest + -rest % LANES
-    long = [n for n in names if n in ("r", "l", "own") and streams[n][0].shape[1] == whole + rest_width] if first else []
+    long = [n for n in ("own", "r", "l") if n in names and streams[n][0].shape[1] % tile == rest_width] if first else []
     blocks, frames, width = sums_shape
 
     def kernel(place_ref, *refs):
-        tiles = dict(zip(names, refs))
+        now = dict(zip(names, refs))
         refs = refs[len(names):]
         if sums is not None:
             sums_ref, refs = refs[0], refs[1:]
@@ -175,9 +176,8 @@
             refs = refs[len(long):]
         if profile is None:
             acc, = refs
-            turned = None
         else:
-            profile_ref, outs, acc, turned = refs[0], refs[1:-2], refs[-2], refs[-1]
+            profile_ref, outs, acc = refs[0], refs[1:-1], refs[-1]
         z, k = place_ref[0], place_ref[1]
         step = pl.program_id(0)
 
@@ -187,32 +187,31 @@
         @pl.when(step == 0)
         def _():
             acc[...] = jnp.zeros(acc.shape, acc.dtype) if sums is None else sums_ref[...]
-            if turned is not None:
-                turned[...] = jnp.zeros(turned.shape, turned.dtype)
             if first:
                 column = lax.broadcasted_iota(jnp.int32, (nrows, rest_width), 1)
                 piece = jnp.where(column < rest, slab_rest[...].astype(jnp.float32), 0.0).astype(jnp.bfloat16)
-                first(z, dict(rests, slab=piece), add, turned)
-
-
-        work(z, tiles, add, turned)
+                first(z, dict(rests, slab=piece), add)
+
+
+        work(z, now, add)
 
         if profile is not None:
-            @pl.when(step == STEPS - 1)
+            @pl.when(step == count - 1)
             def _():
-                block = jnp.where(z < 2, 3, 0)
-                add(block, 0, turned[:nrows].T[:frames])
-                add(block, width // 2, turned[nrows:].T[:frames])
                 weight = jnp.sum(profile_ref[...])
                 lane = lax.broadcasted_iota(jnp.int32, (frames, LANES), 1)
                 for turn, out in enumerate(outs):
-                    out[:, :width - LANES] = acc[k ^ turn, :, :width - LANES]
-                    end = acc[k ^ turn, :, width - LANES:]
-                    out[:, width - LANES:] = jnp.where(lane == LANES - 2, weight, end)
+                    out[...] = acc[k ^ turn]
+                    middle = slice(LANES, 2 * LANES)
+                    out[:, middle] = jnp.where(lane == FREE - 1 - LANES, weight, acc[k ^ turn, :, middle])
+
+    def base(array):
+        return 0 if array.shape[1] <= count * tile + rest_width else start
 
     def spec(array, needed, third):
         return pl.BlockSpec(
-            (array.shape[0], tile), lambda i, s: (0, third(s[0]) * STEPS + jnp.where(needed(s[0]), i, 0)))
+            (array.shape[0], tile),
+            lambda i, s: (0, third(s[0]) * STEPS + jnp.where(needed(s[0]), base(array) + i, 0)))
 
     in_specs = [spec(*streams[n]) for n in names]
     operands = [streams[n][0] for n in names]
@@ -221,7 +220,7 @@
         operands.append(sums)
     if first:
         in_specs.append(pl.BlockSpec((nrows, rest_width), lambda i, s: (0, 3 * whole // rest_width)))
-        in_specs += [pl.BlockSpec((frames, rest_width), lambda i, s: (0, whole // rest_width))] * len(long)
+        in_specs += [pl.BlockSpec((frames, rest_width), lambda i, s, n=streams[n][0].shape[1]: (0, n // rest_width - 1)) for n in long]
         operands += [slab] + [streams[n][0] for n in long]
     if profile is None:
         out_shape = jax.ShapeDtypeStruct(sums_shape, jnp.float32)
@@ -232,11 +231,11 @@
         operands.append(profile)
         out_shape = [jax.ShapeDtypeStruct(sums_shape[1:], jnp.float32)] * blocks
         out_specs = [pl.BlockSpec(sums_shape[1:], lambda i, s: (0, 0))] * blocks
-        scratch = [pltpu.VMEM(sums_shape, jnp.float32), pltpu.VMEM((2 * nrows, LANES), jnp.float32)]
+        scratch = [pltpu.VMEM(sums_shape, jnp.float32)]
     return pl.pallas_call(
         kernel,
         grid_spec=pltpu.PrefetchScalarGridSpec(
-            num_scalar_prefetch=1, grid=(STEPS,), in_specs=in_specs, out_specs=out_specs, scratch_shapes=scratch),
+            num_scalar_prefetch=1, grid=(count,), in_specs=in_specs, out_specs=out_specs, scratch_shapes=scratch),
         out_shape=out_shape,
         compiler_params=PARAMS,
         cost_estimate=SMALL,
@@ -263,9 +262,9 @@
         swap = {0: 0, 1: 2, 2: 1, 3: 4, 4: 3}
         return [swap.get(c) for c in reversed(choice)]
 
-    def routed(sources, choice, width, tokens):
+    def routed(sources, choice, width, tokens, start=0):
         sources = [s if isinstance(s, tuple) else (s, 0, 0) for s in sources]
-        pair = route(place, third, sources, choice, mirror(choice), width, tokens)
+        pair = route(place, third, sources, choice, mirror(choice), start, width, tokens)
         return send(pair), pair[0]
 
     def spare(i):
@@ -301,7 +300,7 @@
     def both(name, pair, right_needed=from_left, left_needed=from_right):
         return {name + "r": (pair[0], right_needed, at(0)), name + "l": (pair[1], left_needed, at(0))}
 
-    def work1(z, refs, add, turned):
+    def work1(z, refs, add):
         add(z, 0, dot(refs["own"][...], refs["slab"][...]))
 
         @pl.when(z >= 1)
@@ -312,7 +311,7 @@
         def _():
             add(z + 1, 0, dot(refs["l"][...], refs["slab"][...]))
 
-    def work3(z, refs, add, turned):
+    def work3(z, refs, add):
         add(z, 0, dot(refs["own"][...], refs["slab2"][...]))
         add((z + 2) % 4, 0, dot(far(z, refs, ""), refs["slab"][...]))
 
@@ -320,10 +319,10 @@
         def _():
             add(jnp.where(z < 2, 0, 3), 0, dot(near(z, refs, ""), refs["slab2"][...]))
 
-    def work4(z, refs, add, turned):
+    def work4(z, refs, add):
         add((z + 2) % 4, 0, dot(far(z, refs, ""), refs["slab"][...]))
 
-    def work5(z, refs, add, turned):
+    def work5(z, refs, add):
         came = far(z, refs, "")
         add(3 - z, 0, dot(came, refs["slab"][...]))
 
@@ -333,23 +332,24 @@
             add(z, 2 * LANES, dot(refs["own"][...], brought))
             add(3 - z, 2 * LANES, dot(came, brought))
 
-    def first4(z, refs, add, turned):
+    def first4(z, refs, add):
         add((z + 2) % 4, 0, dot(far(z, refs, ""), refs["slab"]))
 
-    def first6(z, refs, add, turned):
+    def first6(z, refs, add):
         @pl.when(is_end(z))
         def _():
-            turned[:nrows, :frames] += dot(refs["slab"], far(z, refs, ""))
-
-    def work6(z, refs, add, turned):
+            add(3 - z, 0, dot(far(z, refs, ""), refs["slab"]))
+
+    def work6(z, refs, add):
         came = far(z, refs, "")
-        turned[:nrows, :frames] += dot(refs["slab"][...], came)
+        block = jnp.where(z < 2, 3, 0)
+        add(block, 0, dot(came, refs["slab"][...]))
 
         @pl.when(is_mid(z))
         def _():
             newest = near(z, refs, "")
             brought = jnp.concatenate([near(z, refs, "4"), near(z, refs, "5"), newest], axis=0)
-            turned[nrows:, :frames] += dot(brought, came)
+            add(block, 2 * LANES, dot(came, brought))
             both = dot(jnp.concatenate([refs["own"][...], far(z, refs, "5")], axis=0), newest)
             add(z, 3 * LANES, both[:frames])
             add(3 - z, 3 * LANES, both[frames:])
@@ -372,19 +372,25 @@
         place, third,
         dict(both("", r3), slab=(slab, always, at(0)), slab2=(slab, always, at(2)), own=(own_c, always, at(0))),
         work3, sums_shape, sums)
-    r6, sent = routed([spare(2), r3[0], r3[1], r4[0], r4[1]], [0, 1, 3, None], long, [sent, sums])
+    tile = third // STEPS
+    r6_sources, r6_choice = [spare(2), r3[0], r3[1], r4[0], r4[1]], [0, 1, 3, None]
+    r6, sent = routed(r6_sources, r6_choice, third - tile, [sent, sums])
+    r7, sent = routed(r6_sources, r6_choice, long - third + tile, [sent], STEPS - 1)
     sums = absorb(
         place, third, dict(both("", r4), slab=(slab, always, at(1))), work4, sums_shape, sums, first=first4)
     middle = dict(both("4", r4, near_right, near_left), own=(own_c, is_mid, at(0)))
     sums = absorb(place, third, dict(both("", r5), slab=(slab, always, thirds(0, 2)), **middle), work5, sums_shape, sums)
+    middle.update(both("5", r5, is_mid, is_mid))
+    sums = absorb(
+        place, third, dict(both("", r6), slab=(slab, always, thirds(1, 2)), **middle), work6, sums_shape, sums,
+        tiles=(0, STEPS - 1))
     messages = absorb(
-        place, third, dict(both("", r6), slab=(slab, always, thirds(1, 2)), **both("5", r5, is_mid, is_mid), **middle),
-        work6, sums_shape, sums, first=first6, profile=profile)
+        place, third, dict(both("", r7), slab=(slab, always, thirds(1, 2)), **middle), work6, sums_shape, sums,
+        first=first6, profile=profile, tiles=(STEPS - 1, 1))
 
     summed = messages[0]
     for turn in range(1, owners):
         summed += lax.ppermute(messages[turn], SITES, [(i, i ^ turn) for i in range(owners)])
-    weight_sum = summed[0, WIDTH - 2]
     half = WIDTH // 2
     frame_sum = jnp.sum(summed[:, :nrows], axis=1) + jnp.sum(summed[:, half:half + nrows], axis=1)
     lane = jnp.arange(half)
@@ -394,6 +400,7 @@
 
     mine, extra = lax.ppermute(mine, ALL, flip(0)), lax.ppermute(extra, ALL, flip(1))
     total = mine[:, FREE] + extra[:, FREE] + lax.ppermute(frame_sum, ALL, flip(2)) + lax.ppermute(frame_sum, ALL, flip(3))
+    weight_sum = mine[:, FREE - 1]
     charges = (mine + extra)[:, :nrows].reshape(frames, panels, rows).transpose(1, 2, 0)
     return finish(charges, total, weight_sum, profile)
 

time: 264 us -> 258 us (0.977)
  starting transfers between devices: 56.8 us -> 62.5 us
  local copies, waits for them, and re-layouts: 13.5 us -> 8.82 us
  waiting for transfers between devices: 136 us -> 132 us
    ppermute x6 -> x7, waiting for transfers between devices: 37.3 us -> 10.6 us  [send(): lax.ppermute(pair[0], 'wide', right)]
    ppermute x6 -> x7, waiting for transfers between devices: 90.5 us -> 114 us  [send(): lax.ppermute(pair[1], 'wide', left)]
    ppermute x6 -> x7, starting transfers between devices: 32.5 us -> 36.9 us  [send(): lax.ppermute(pair[0], 'wide', right)]
    unnamed x22 -> x12, local copies, waits for them, and re-layouts: 12 us -> 7.84 us
    ppermute x1, starting transfers between devices: 3.25 us -> 0.32 us  [line_plan(): lax.ppermute(extra, ALL, flip(1))]
    ppermute x1, starting transfers between devices: 1.82 us -> 4.75 us  [line_plan(): lax.ppermute(frame_sum, ALL, flip(2))]
    ppermute x6 -> x7, starting transfers between devices: 8.16 us -> 9.45 us  [send(): lax.ppermute(pair[1], 'wide', left)]
    pallas_call x4 -> x5, Pallas kernels: 13.8 us -> 12.6 us  [route(): pl.pallas_call(kernel, grid_spec=pltpu.PrefetchScalarGridSpec(num_scalar_...]
  transfers between devices with their start and end apart: 19 -> 21, of which waited for: 15 -> 15; matrix products, arithmetic and copies ran while one was open for 0% -> 0% of each run, Pallas kernels for 17% -> 18%
where the time goes in v7:
time: 258 us; the launch traced here: 256 us
  waiting for transfers between devices  132 us (51%)
  starting transfers between devices  62.5 us (24%)
  Pallas kernels  48.6 us (19%)
  local copies, waits for them, and re-layouts  8.82 us (3%)
  other arithmetic  4.04 us (2%)
    ppermute x7, waiting for transfers between devices, send(): lax.ppermute(pair[1], 'wide', left)  114 us
    ppermute x7, starting transfers between devices, send(): lax.ppermute(pair[0], 'wide', right)  36.9 us
    pallas_call x7, Pallas kernels, absorb(): pl.pallas_call(kernel, grid_spec=pltpu.PrefetchScalarGridSpec(num_scalar_...  32.4 us
    pallas_call x5, Pallas kernels, route(): pl.pallas_call(kernel, grid_spec=pltpu.PrefetchScalarGridSpec(num_scalar_...  12.6 us
    ppermute x7, waiting for transfers between devices, send(): lax.ppermute(pair[0], 'wide', right)  10.6 us
    ppermute x7, starting transfers between devices, send(): lax.ppermute(pair[1], 'wide', left)  9.45 us
    unnamed x12, local copies, waits for them, and re-layouts  7.84 us
    ppermute x1, starting transfers between devices, line_plan(): lax.ppermute(mine, ALL, flip(0))  7.42 us
  transfers between devices with their start and end apart: 21, of which 15 were waited for; matrix products, arithmetic and copies ran while one was open for 0% of the time, Pallas kernels for 18%

profile of v7, /device:TPU:3, one launch (start us, length us, event | category | flops | bytes accessed | tf_op | source)
XLA Modules:
  0.0 255.8 jit_solution(13105792049920183377)
XLA Ops:
  4.9 5.2 %collective-permute-start = (bf16[64,13440]{1,0:T(8,128)(2,1)S(1)}, bf16[64,13440]{1,0:T(8,128)(2,1)}, u32[]{:S(2)}, u32[]{:S(2)}) collective-permute-start(bf16[64,13440]{1,0:T(8,128)(2,1)S(1)} %add_convert_fusion.token_ref.refs_3_), channel_id=1, source_target_pairs={{0,4},{4,8},{8,12},{1,5},{5,9},{9,13},{2,6},{6,10},{10,14},{3,7},{... | collective-permute-start | bytes 5160968 | tf_op jit(solution)/shard_map/ppermute | solution.py:259
  12.7 3.5 %shard_map.55 = (bf16[64,13440]{1,0:T(8,128)(2,1)}, bf16[64,13312]{1,0:T(8,128)(2,1)S(1)}) custom-call(bf16[64,40000]{1,0:T(8,128)(2,1)S(1)} %copy-done.2, s32[1,40000]{1,0:T(1,128)S(1)} %reshape.25.labels_b.labels_c.labels_rest, bf16[64,40000]{1,0:T(8,128)(2,1)S(1)} %copy-done.2, s32[1,40000]{1,0:T(1,128)S(1)} %reshape.25.labels_b.labels_c.labels_rest, ...), custom_call_target="tpu_custom_call" | custom-call | flops 1000 | bytes 1000 | tf_op jit(solution)/shard_map/pallas_call | solution.py:96
  17.5 5.2 %collective-permute-start.4 = (bf16[64,13440]{1,0:T(8,128)(2,1)}, bf16[64,13440]{1,0:T(8,128)(2,1)}, u32[]{:S(2)}, u32[]{:S(2)}) collective-permute-start(bf16[64,13440]{1,0:T(8,128)(2,1)} %get-tuple-element.24.refs_3_.refs_6_), channel_id=1, source_target_pairs={{0,4},{4,8},{8,12},{1,5},{5,9},{9,13},{2,6},{6,10},{10,14},{3,7},{... | collective-permute-start | bytes 5160968 | tf_op jit(solution)/shard_map/ppermute | solution.py:259
  22.8 21.2 %collective-permute-done.1.refs_2_.refs_1_ = bf16[64,13440]{1,0:T(8,128)(2,1)} collective-permute-done((bf16[64,13440]{1,0:T(8,128)(2,1)S(1)}, bf16[64,13440]{1,0:T(8,128)(2,1)}, u32[]{:S(2)}, u32[]{:S(2)}) %collective-permute-start.1) | collective-permute-done | bytes 1720352 | tf_op jit(solution)/shard_map/ppermute | solution.py:259
  48.9 6.4 %collective-permute-start.2 = (bf16[64,13440]{1,0:T(8,128)(2,1)S(1)}, bf16[64,13440]{1,0:T(8,128)(2,1)S(1)}, u32[]{:S(2)}, u32[]{:S(2)}) collective-permute-start(bf16[64,13440]{1,0:T(8,128)(2,1)S(1)} %get-tuple-element.22.refs_3_), channel_id=1, source_target_pairs={{0,4},{4,8},{8,12},{1,5},{5,9},{9,13},{2,6},{6,10},{10,14},{3,7},{... | collective-permute-start | bytes 5160968 | tf_op jit(solution)/shard_map/ppermute | solution.py:259
  55.3 25.6 %collective-permute-done.5.refs_2_.refs_1_.refs_8_ = bf16[64,13440]{1,0:T(8,128)(2,1)} collective-permute-done((bf16[64,13440]{1,0:T(8,128)(2,1)}, bf16[64,13440]{1,0:T(8,128)(2,1)}, u32[]{:S(2)}, u32[]{:S(2)}) %collective-permute-start.5) | collective-permute-done | bytes 1720352 | tf_op jit(solution)/shard_map/ppermute | solution.py:259
  81.8 5.4 %copy-done = bf16[2,96,40000]{2,1,0:T(8,128)(2,1)S(1)} copy-done((bf16[2,96,40000]{2,1,0:T(8,128)(2,1)S(1)}, bf16[2,96,40000]{2,1,0:T(8,128)(2,1)}, u32[]{:S(2)}) %copy-start) | copy-done | bytes 15360024
  87.1 4.4 %shard_map.57 = (bf16[64,13440]{1,0:T(8,128)(2,1)}, bf16[64,13440]{1,0:T(8,128)(2,1)S(1)}) custom-call(s32[2]{0:T(128)S(1)} %pad_add_fusion.place_ref, bf16[192,40000]{1,0:T(8,128)(2,1)S(1)} %bitcast.10, bf16[64,13440]{1,0:T(8,128)(2,1)} %collective-permute-done.4.refs_1_.refs_0_.refs_7_, bf16[64,13440]{1,0:T(8,128)(2,1)} %collective-permute-done.5.refs_2_.refs_1_.refs_8_, ...), custom_call_target="tpu_custom_call" | custom-call | flops 1000 | bytes 1000 | tf_op jit(solution)/shard_map/pallas_call | solution.py:145
  93.1 6.5 %collective-permute-start.6 = (bf16[64,13440]{1,0:T(8,128)(2,1)}, bf16[64,13440]{1,0:T(8,128)(2,1)S(1)}, u32[]{:S(2)}, u32[]{:S(2)}) collective-permute-start(bf16[64,13440]{1,0:T(8,128)(2,1)} %get-tuple-element.25.refs_5_), channel_id=1, source_target_pairs={{0,4},{4,8},{8,12},{1,5},{5,9},{9,13},{2,6},{6,10},{10,14},{3,7},{... | collective-permute-start | bytes 5160968 | tf_op jit(solution)/shard_map/ppermute | solution.py:259
  99.6 6.5 %shard_map.58.refs_4_ = f32[4,64,512]{2,1,0:T(8,128)S(1)} custom-call(s32[2]{0:T(128)S(1)} %pad_add_fusion.place_ref, bf16[64,13440]{1,0:T(8,128)(2,1)} %collective-permute-done.refs_1_.refs_0_, bf16[64,13440]{1,0:T(8,128)(2,1)} %collective-permute-done.1.refs_2_.refs_1_, bf16[192,40000]{1,0:T(8,128)(2,1)S(1)} %bitcast.11, ...), custom_call_target="tpu_custom_call" | custom-call | flops 1000 | bytes 1000 | tf_op jit(solution)/shard_map/pallas_call | solution.py:235
  106.2 7.0 %shard_map.59.refs_6_.refs_5_ = f32[4,64,512]{2,1,0:T(8,128)S(1)} custom-call(s32[2]{0:T(128)S(1)} %pad_add_fusion.place_ref, bf16[64,13440]{1,0:T(8,128)(2,1)} %collective-permute-done.4.refs_1_.refs_0_.refs_7_, bf16[64,13440]{1,0:T(8,128)(2,1)} %collective-permute-done.5.refs_2_.refs_1_.refs_8_, bf16[192,40000]{1,0:T(8,128)(2,1)S(1)} %bitcast.12, ...), custom_call_target="tpu_custom_call" | custom-call | flops 1000 | bytes 1000 | tf_op jit(solution)/shard_map/pallas_call | solution.py:235
  113.2 4.5 %collective-permute-done.3.refs_2_.refs_1_ = bf16[64,13440]{1,0:T(8,128)(2,1)S(1)} collective-permute-done((bf16[64,13440]{1,0:T(8,128)(2,1)S(1)}, bf16[64,13440]{1,0:T(8,128)(2,1)S(1)}, u32[]{:S(2)}, u32[]{:S(2)}) %collective-permute-start.3) | collective-permute-done | bytes 1720352 | tf_op jit(solution)/shard_map/ppermute | solution.py:259
  122.1 5.1 %collective-permute-start.10 = (bf16[64,13440]{1,0:T(8,128)(2,1)S(1)}, bf16[64,13440]{1,0:T(8,128)(2,1)S(1)}, u32[]{:S(2)}, u32[]{:S(2)}) collective-permute-start(bf16[64,13440]{1,0:T(8,128)(2,1)S(1)} %get-tuple-element.27.refs_5_), channel_id=1, source_target_pairs={{0,4},{4,8},{8,12},{1,5},{5,9},{9,13},{2,6},{6,10},{10,14},{3,7},{... | collective-permute-start | bytes 5160968 | tf_op jit(solution)/shard_map/ppermute | solution.py:259
  127.2 6.0 %shard_map.61.refs_6_.refs_3_ = f32[4,64,512]{2,1,0:T(8,128)S(1)} custom-call(s32[2]{0:T(128)S(1)} %pad_add_fusion.place_ref, bf16[64,13440]{1,0:T(8,128)(2,1)S(1)} %collective-permute-done.2.refs_1_.refs_0_, bf16[64,13440]{1,0:T(8,128)(2,1)S(1)} %collective-permute-done.3.refs_2_.refs_1_, bf16[192,40000]{1,0:T(8,128)(2,1)S(1)} %bitcast.15, ...), custom_call_target="tpu_custom_call" | custom-call | flops 1000 | bytes 1000 | tf_op jit(solution)/shard_map/pallas_call | solution.py:235
  133.2 21.3 %collective-permute-done.7.refs_4_.refs_1_.refs_6_ = bf16[64,13440]{1,0:T(8,128)(2,1)S(1)} collective-permute-done((bf16[64,13440]{1,0:T(8,128)(2,1)S(1)}, bf16[64,13440]{1,0:T(8,128)(2,1)S(1)}, u32[]{:S(2)}, u32[]{:S(2)}) %collective-permute-start.7) | collective-permute-done | bytes 1720352 | tf_op jit(solution)/shard_map/ppermute | solution.py:259
  158.4 4.9 %collective-permute-start.12 = (bf16[64,9984]{1,0:T(8,128)(2,1)S(1)}, bf16[64,9984]{1,0:T(8,128)(2,1)S(1)}, u32[]{:S(2)}, u32[]{:S(2)}) collective-permute-start(bf16[64,9984]{1,0:T(8,128)(2,1)S(1)} %get-tuple-element.28.refs_5_), channel_id=1, source_target_pairs={{0,4},{4,8},{8,12},{1,5},{5,9},{9,13},{2,6},{6,10},{10,14},{3,7},{... | collective-permute-start | bytes 3833864 | tf_op jit(solution)/shard_map/ppermute | solution.py:259
  164.8 3.6 %collective-permute-start.8 = (bf16[64,3456]{1,0:T(8,128)(2,1)S(1)}, bf16[64,3456]{1,0:T(8,128)(2,1)S(1)}, u32[]{:S(2)}, u32[]{:S(2)}) collective-permute-start(bf16[64,3456]{1,0:T(8,128)(2,1)S(1)} %get-tuple-element.29), channel_id=1, source_target_pairs={{0,4},{4,8},{8,12},{1,5},{5,9},{9,13},{2,6},{6,10},{10,14},{3,7},{... | collective-permute-start | bytes 1327112 | tf_op jit(solution)/shard_map/ppermute | solution.py:259
  168.4 23.0 %collective-permute-done.11.refs_1_.refs_7_ = bf16[64,13440]{1,0:T(8,128)(2,1)S(1)} collective-permute-done((bf16[64,13440]{1,0:T(8,128)(2,1)S(1)}, bf16[64,13440]{1,0:T(8,128)(2,1)S(1)}, u32[]{:S(2)}, u32[]{:S(2)}) %collective-permute-start.11) | collective-permute-done | bytes 1720352 | tf_op jit(solution)/shard_map/ppermute | solution.py:259
  192.9 3.9 %shard_map.64.refs_6_ = f32[4,64,512]{2,1,0:T(8,128)S(1)} custom-call(s32[2]{0:T(128)S(1)} %pad_add_fusion.place_ref, bf16[64,13440]{1,0:T(8,128)(2,1)S(1)} %collective-permute-done.6.refs_3_.refs_0_.refs_5_, bf16[64,13440]{1,0:T(8,128)(2,1)S(1)} %collective-permute-done.7.refs_4_.refs_1_.refs_6_, bf16[192,40000]{1,0:T(8,128)(2,1)S(1)} %bitcast.19, ...), custom_call_target="tpu_custom_call" | custom-call | flops 1000 | bytes 1000 | tf_op jit(solution)/shard_map/pallas_call | solution.py:235
  196.7 4.0 %shard_map.65.refs_8_ = f32[4,64,512]{2,1,0:T(8,128)S(1)} custom-call(s32[2]{0:T(128)S(1)} %pad_add_fusion.place_ref, bf16[64,13440]{1,0:T(8,128)(2,1)S(1)} %collective-permute-done.10.refs_0_.refs_6_, bf16[64,13440]{1,0:T(8,128)(2,1)S(1)} %collective-permute-done.11.refs_1_.refs_7_, bf16[192,40000]{1,0:T(8,128)(2,1)S(1)} %bitcast.21, ...), custom_call_target="tpu_custom_call" | custom-call | flops 1000 | bytes 1000 | tf_op jit(solution)/shard_map/pallas_call | solution.py:235
  200.7 18.0 %collective-permute-done.13.refs_1_ = bf16[64,9984]{1,0:T(8,128)(2,1)S(1)} collective-permute-done((bf16[64,9984]{1,0:T(8,128)(2,1)S(1)}, bf16[64,9984]{1,0:T(8,128)(2,1)S(1)}, u32[]{:S(2)}, u32[]{:S(2)}) %collective-permute-start.13) | collective-permute-done | bytes 1277984 | tf_op jit(solution)/shard_map/ppermute | solution.py:259
  222.9 6.2 %collective-permute-done.8.refs_0_.refs_10_ = bf16[64,3456]{1,0:T(8,128)(2,1)S(1)} collective-permute-done((bf16[64,3456]{1,0:T(8,128)(2,1)S(1)}, bf16[64,3456]{1,0:T(8,128)(2,1)S(1)}, u32[]{:S(2)}, u32[]{:S(2)}) %collective-permute-start.8) | collective-permute-done | bytes 442400 | tf_op jit(solution)/shard_map/ppermute | solution.py:259
  241.2 7.4 %collective-permute-start.17 = (f32[64,256]{1,0:T(8,128)S(1)}, f32[64,256]{1,0:T(8,128)S(1)}, u32[]{:S(2)}, u32[]{:S(2)}) collective-permute-start(f32[64,256]{1,0:T(8,128)S(1)} %get-tuple-element.41), channel_id=1, source_target_pairs={{0,0},{1,4},{2,8},{3,12},{4,1},{5,5},{6,9},{7,13},{8,2},{9,6},{10,... | collective-permute-start | bytes 196616 | tf_op jit(solution)/shard_map/ppermute | solution.py:401
  249.0 4.8 %collective-permute-start.19 = (f32[64]{0:T(128)S(1)}, f32[64]{0:T(128)S(1)}, u32[]{:S(2)}, u32[]{:S(2)}) collective-permute-start(f32[64]{0:T(128)S(1)} %add.42), channel_id=1, source_target_pairs={{0,2},{1,6},{2,10},{3,14},{4,3},{5,7},{6,11},{7,15},{8,0},{9,4},{1... | collective-permute-start | bytes 776 | tf_op jit(solution)/shard_map/ppermute | solution.py:402
  (58 shorter events, 45.8 us)
Async XLA Ops:
  1.6 8.6 %copy-start.4 = (f32[64,2]{0,1:T(2,128)S(1)}, f32[64,2]{0,1:T(2,128)}, u32[]{:S(2)}) copy-start(f32[64,2]{0,1:T(2,128)} %param.7) | copy-start | bytes 1540
  3.6 40.4 %collective-permute-start.1 = (bf16[64,13440]{1,0:T(8,128)(2,1)S(1)}, bf16[64,13440]{1,0:T(8,128)(2,1)}, u32[]{:S(2)}, u32[]{:S(2)}) collective-permute-start(bf16[64,13440]{1,0:T(8,128)(2,1)S(1)} %add_convert_fusion.token_ref.refs_3_), channel_id=1, source_target_pairs={{12,8},{8,4},{4,0},{13,9},{9,5},{5,1},{14,10},{10,6},{6,2},{15,11}... | collective-permute-start | bytes 5160968 | tf_op jit(solution)/shard_map/ppermute | solution.py:259
  4.9 39.9 %collective-permute-start = (bf16[64,13440]{1,0:T(8,128)(2,1)S(1)}, bf16[64,13440]{1,0:T(8,128)(2,1)}, u32[]{:S(2)}, u32[]{:S(2)}) collective-permute-start(bf16[64,13440]{1,0:T(8,128)(2,1)S(1)} %add_convert_fusion.token_ref.refs_3_), channel_id=1, source_target_pairs={{0,4},{4,8},{8,12},{1,5},{5,9},{9,13},{2,6},{6,10},{10,14},{3,7},{... | collective-permute-start | bytes 5160968 | tf_op jit(solution)/shard_map/ppermute | solution.py:259
  16.2 64.7 %collective-permute-start.5 = (bf16[64,13440]{1,0:T(8,128)(2,1)}, bf16[64,13440]{1,0:T(8,128)(2,1)}, u32[]{:S(2)}, u32[]{:S(2)}) collective-permute-start(bf16[64,13440]{1,0:T(8,128)(2,1)} %get-tuple-element.24.refs_3_.refs_6_), channel_id=1, source_target_pairs={{12,8},{8,4},{4,0},{13,9},{9,5},{5,1},{14,10},{10,6},{6,2},{15,11}... | collective-permute-start | bytes 5160968 | tf_op jit(solution)/shard_map/ppermute | solution.py:259
  17.5 64.2 %collective-permute-start.4 = (bf16[64,13440]{1,0:T(8,128)(2,1)}, bf16[64,13440]{1,0:T(8,128)(2,1)}, u32[]{:S(2)}, u32[]{:S(2)}) collective-permute-start(bf16[64,13440]{1,0:T(8,128)(2,1)} %get-tuple-element.24.refs_3_.refs_6_), channel_id=1, source_target_pairs={{0,4},{4,8},{8,12},{1,5},{5,9},{9,13},{2,6},{6,10},{10,14},{3,7},{... | collective-permute-start | bytes 5160968 | tf_op jit(solution)/shard_map/ppermute | solution.py:259
  47.6 70.0 %collective-permute-start.3 = (bf16[64,13440]{1,0:T(8,128)(2,1)S(1)}, bf16[64,13440]{1,0:T(8,128)(2,1)S(1)}, u32[]{:S(2)}, u32[]{:S(2)}) collective-permute-start(bf16[64,13440]{1,0:T(8,128)(2,1)S(1)} %get-tuple-element.23), channel_id=1, source_target_pairs={{12,8},{8,4},{4,0},{13,9},{9,5},{5,1},{14,10},{10,6},{6,2},{15,11}... | collective-permute-start | bytes 5160968 | tf_op jit(solution)/shard_map/ppermute | solution.py:259
  48.9 69.6 %collective-permute-start.2 = (bf16[64,13440]{1,0:T(8,128)(2,1)S(1)}, bf16[64,13440]{1,0:T(8,128)(2,1)S(1)}, u32[]{:S(2)}, u32[]{:S(2)}) collective-permute-start(bf16[64,13440]{1,0:T(8,128)(2,1)S(1)} %get-tuple-element.22.refs_3_), channel_id=1, source_target_pairs={{0,4},{4,8},{8,12},{1,5},{5,9},{9,13},{2,6},{6,10},{10,14},{3,7},{... | collective-permute-start | bytes 5160968 | tf_op jit(solution)/shard_map/ppermute | solution.py:259
  87.1 12.5 %copy-start.1 = (bf16[2,96,40000]{2,1,0:T(8,128)(2,1)S(1)}, bf16[2,96,40000]{2,1,0:T(8,128)(2,1)}, u32[]{:S(2)}) copy-start(bf16[2,96,40000]{2,1,0:T(8,128)(2,1)} %param.5) | copy-start | bytes 46080004
  91.6 62.9 %collective-permute-start.7 = (bf16[64,13440]{1,0:T(8,128)(2,1)S(1)}, bf16[64,13440]{1,0:T(8,128)(2,1)S(1)}, u32[]{:S(2)}, u32[]{:S(2)}) collective-permute-start(bf16[64,13440]{1,0:T(8,128)(2,1)S(1)} %get-tuple-element.26), channel_id=1, source_target_pairs={{12,8},{8,4},{4,0},{13,9},{9,5},{5,1},{14,10},{10,6},{6,2},{15,11}... | collective-permute-start | bytes 5160968 | tf_op jit(solution)/shard_map/ppermute | solution.py:259
  93.1 62.4 %collective-permute-start.6 = (bf16[64,13440]{1,0:T(8,128)(2,1)}, bf16[64,13440]{1,0:T(8,128)(2,1)S(1)}, u32[]{:S(2)}, u32[]{:S(2)}) collective-permute-start(bf16[64,13440]{1,0:T(8,128)(2,1)} %get-tuple-element.25.refs_5_), channel_id=1, source_target_pairs={{0,4},{4,8},{8,12},{1,5},{5,9},{9,13},{2,6},{6,10},{10,14},{3,7},{... | collective-permute-start | bytes 5160968 | tf_op jit(solution)/shard_map/ppermute | solution.py:259
  120.8 70.6 %collective-permute-start.11 = (bf16[64,13440]{1,0:T(8,128)(2,1)S(1)}, bf16[64,13440]{1,0:T(8,128)(2,1)S(1)}, u32[]{:S(2)}, u32[]{:S(2)}) collective-permute-start(bf16[64,13440]{1,0:T(8,128)(2,1)S(1)} %get-tuple-element.31), channel_id=1, source_target_pairs={{12,8},{8,4},{4,0},{13,9},{9,5},{5,1},{14,10},{10,6},{6,2},{15,11}... | collective-permute-start | bytes 5160968 | tf_op jit(solution)/shard_map/ppermute | solution.py:259
  122.1 74.6 %collective-permute-start.10 = (bf16[64,13440]{1,0:T(8,128)(2,1)S(1)}, bf16[64,13440]{1,0:T(8,128)(2,1)S(1)}, u32[]{:S(2)}, u32[]{:S(2)}) collective-permute-start(bf16[64,13440]{1,0:T(8,128)(2,1)S(1)} %get-tuple-element.27.refs_5_), channel_id=1, source_target_pairs={{0,4},{4,8},{8,12},{1,5},{5,9},{9,13},{2,6},{6,10},{10,14},{3,7},{... | collective-permute-start | bytes 5160968 | tf_op jit(solution)/shard_map/ppermute | solution.py:259
  157.1 61.6 %collective-permute-start.13 = (bf16[64,9984]{1,0:T(8,128)(2,1)S(1)}, bf16[64,9984]{1,0:T(8,128)(2,1)S(1)}, u32[]{:S(2)}, u32[]{:S(2)}) collective-permute-start(bf16[64,9984]{1,0:T(8,128)(2,1)S(1)} %get-tuple-element.32), channel_id=1, source_target_pairs={{12,8},{8,4},{4,0},{13,9},{9,5},{5,1},{14,10},{10,6},{6,2},{15,11}... | collective-permute-start | bytes 3833864 | tf_op jit(solution)/shard_map/ppermute | solution.py:259
  158.4 61.2 %collective-permute-start.12 = (bf16[64,9984]{1,0:T(8,128)(2,1)S(1)}, bf16[64,9984]{1,0:T(8,128)(2,1)S(1)}, u32[]{:S(2)}, u32[]{:S(2)}) collective-permute-start(bf16[64,9984]{1,0:T(8,128)(2,1)S(1)} %get-tuple-element.28.refs_5_), channel_id=1, source_target_pairs={{0,4},{4,8},{8,12},{1,5},{5,9},{9,13},{2,6},{6,10},{10,14},{3,7},{... | collective-permute-start | bytes 3833864 | tf_op jit(solution)/shard_map/ppermute | solution.py:259
  164.8 64.4 %collective-permute-start.8 = (bf16[64,3456]{1,0:T(8,128)(2,1)S(1)}, bf16[64,3456]{1,0:T(8,128)(2,1)S(1)}, u32[]{:S(2)}, u32[]{:S(2)}) collective-permute-start(bf16[64,3456]{1,0:T(8,128)(2,1)S(1)} %get-tuple-element.29), channel_id=1, source_target_pairs={{0,4},{4,8},{8,12},{1,5},{5,9},{9,13},{2,6},{6,10},{10,14},{3,7},{... | collective-permute-start | bytes 1327112 | tf_op jit(solution)/shard_map/ppermute | solution.py:259
  191.4 37.7 %collective-permute-start.9 = (bf16[64,3456]{1,0:T(8,128)(2,1)S(1)}, bf16[64,3456]{1,0:T(8,128)(2,1)S(1)}, u32[]{:S(2)}, u32[]{:S(2)}) collective-permute-start(bf16[64,3456]{1,0:T(8,128)(2,1)S(1)} %get-tuple-element.30), channel_id=1, source_target_pairs={{12,8},{8,4},{4,0},{13,9},{9,5},{5,1},{14,10},{10,6},{6,2},{15,11}... | collective-permute-start | bytes 1327112 | tf_op jit(solution)/shard_map/ppermute | solution.py:259
  200.7 28.4 %copy-start.3 = (f32[2,96]{1,0:T(2,128)S(1)}, f32[2,96]{1,0:T(2,128)}, u32[]{:S(2)}) copy-start(f32[2,96]{1,0:T(2,128)} %refs_12_.1) | copy-start | bytes 2308
  231.0 3.6 %collective-permute-start.14 = (f32[64,512]{1,0:T(8,128)S(1)}, f32[64,512]{1,0:T(8,128)S(1)}, u32[]{:S(2)}, u32[]{:S(2)}) collective-permute-start(f32[64,512]{1,0:T(8,128)S(1)} %get-tuple-element.34), channel_id=1, source_target_pairs={{0,1},{1,0},{2,3},{3,2},{4,5},{5,4},{6,7},{7,6},{8,9},{9,8},{10,11... | collective-permute-start | bytes 393224 | tf_op jit(solution)/shard_map/ppermute | solution.py:393
  232.9 5.1 %collective-permute-start.15 = (f32[64,512]{1,0:T(8,128)S(1)}, f32[64,512]{1,0:T(8,128)S(1)}, u32[]{:S(2)}, u32[]{:S(2)}) collective-permute-start(f32[64,512]{1,0:T(8,128)S(1)} %get-tuple-element.35), channel_id=1, source_target_pairs={{0,2},{1,3},{2,0},{3,1},{4,6},{5,7},{6,4},{7,5},{8,10},{9,11},{10,... | collective-permute-start | bytes 393224 | tf_op jit(solution)/shard_map/ppermute | solution.py:393
  233.0 7.9 %collective-permute-start.16 = (f32[64,512]{1,0:T(8,128)S(1)}, f32[64,512]{1,0:T(8,128)S(1)}, u32[]{:S(2)}, u32[]{:S(2)}) collective-permute-start(f32[64,512]{1,0:T(8,128)S(1)} %get-tuple-element.36), channel_id=1, source_target_pairs={{0,3},{1,2},{2,1},{3,0},{4,7},{5,6},{6,5},{7,4},{8,11},{9,10},{10,... | collective-permute-start | bytes 393224 | tf_op jit(solution)/shard_map/ppermute | solution.py:393
  241.2 12.5 %collective-permute-start.17 = (f32[64,256]{1,0:T(8,128)S(1)}, f32[64,256]{1,0:T(8,128)S(1)}, u32[]{:S(2)}, u32[]{:S(2)}) collective-permute-start(f32[64,256]{1,0:T(8,128)S(1)} %get-tuple-element.41), channel_id=1, source_target_pairs={{0,0},{1,4},{2,8},{3,12},{4,1},{5,5},{6,9},{7,13},{8,2},{9,6},{10,... | collective-permute-start | bytes 196616 | tf_op jit(solution)/shard_map/ppermute | solution.py:401
  248.6 6.1 %collective-permute-start.18 = (f32[64,256]{1,0:T(8,128)S(1)}, f32[64,256]{1,0:T(8,128)S(1)}, u32[]{:S(2)}, u32[]{:S(2)}) collective-permute-start(f32[64,256]{1,0:T(8,128)S(1)} %get-tuple-element.42), channel_id=1, source_target_pairs={{0,1},{1,5},{2,9},{3,13},{4,0},{5,4},{6,8},{7,12},{8,3},{9,7},{10,... | collective-permute-start | bytes 196616 | tf_op jit(solution)/shard_map/ppermute | solution.py:401
  249.0 6.1 %collective-permute-start.20 = (f32[64]{0:T(128)S(1)}, f32[64]{0:T(128)S(1)}, u32[]{:S(2)}, u32[]{:S(2)}) collective-permute-start(f32[64]{0:T(128)S(1)} %add.42), channel_id=1, source_target_pairs={{0,3},{1,7},{2,11},{3,15},{4,2},{5,6},{6,10},{7,14},{8,1},{9,5},{1... | collective-permute-start | bytes 776 | tf_op jit(solution)/shard_map/ppermute | solution.py:402
  249.0 6.1 %collective-permute-start.19 = (f32[64]{0:T(128)S(1)}, f32[64]{0:T(128)S(1)}, u32[]{:S(2)}, u32[]{:S(2)}) collective-permute-start(f32[64]{0:T(128)S(1)} %add.42), channel_id=1, source_target_pairs={{0,2},{1,6},{2,10},{3,14},{4,3},{5,7},{6,11},{7,15},{8,0},{9,4},{1... | collective-permute-start | bytes 776 | tf_op jit(solution)/shard_map/ppermute | solution.py:402
  (3 other events, 16.4 us)

commit v8 on v7

--- a/solution.py
+++ b/solution.py
@@ -115,40 +115,41 @@
     )(noise, labels, noise, labels, noise, labels, volts, token)
 
 
-def route(place, whole, sources, to_right, to_left, start, width, tokens):
+def route(place, whole, sources, outer, inner, start, width, tokens):
     tile = whole // STEPS
     count = len(sources)
-    frames = ROWS
 
     def kernel(place_ref, *refs):
-        outs = refs[count + len(tokens):]
+        out_x, out_y = refs[count + len(tokens):]
         z = place_ref[0]
-        for here in range(4):
-            @pl.when(z == here)
-            def _(here=here):
-                for out, number in zip(outs, (to_right[here], to_left[here])):
-                    if number is not None:
-                        out[...] = refs[number][...]
+
+        @pl.when(is_end(z))
+        def _():
+            out_x[...] = refs[outer[0]][...]
+
+        @pl.when(is_mid(z))
+        def _():
+            out_x[...] = refs[outer[1]][...]
+            out_y[...] = refs[inner][...]
 
     def spec(number):
         array, row, column = sources[number]
         last = (array.shape[1] - 1) // tile if column == 0 else column + STEPS - 1
-        users = [here for here in range(4) if number in (to_right[here], to_left[here])]
 
         def index(i, s):
-            used = sum((s[0] == here).astype(jnp.int32) for here in users)
-            return row, jnp.minimum(column + start + i * used, last)
-
-        return pl.BlockSpec((frames, tile), index)
-
-    out_spec = pl.BlockSpec((frames, tile), lambda i, s: (0, i))
+            used = is_end(s[0]) if number == outer[0] else is_mid(s[0])
+            return row, jnp.where(used, jnp.minimum(column + start + i, last), column)
+
+        return pl.BlockSpec((ROWS, tile), index)
+
     return pl.pallas_call(
         kernel,
         grid_spec=pltpu.PrefetchScalarGridSpec(
             num_scalar_prefetch=1, grid=(pl.cdiv(width, tile),),
             in_specs=[spec(n) for n in range(count)] + [pl.BlockSpec(memory_space=pl.ANY)] * len(tokens),
-            out_specs=[out_spec] * 2),
-        out_shape=[jax.ShapeDtypeStruct((frames, width), jnp.bfloat16)] * 2,
+            out_specs=[pl.BlockSpec((ROWS, tile), lambda i, s: (0, i)),
+                       pl.BlockSpec((ROWS, tile), lambda i, s: (0, jnp.where(is_mid(s[0]), i, 0)))]),
+        out_shape=[jax.ShapeDtypeStruct((ROWS, width), jnp.bfloat16)] * 2,
         compiler_params=PARAMS,
         cost_estimate=SMALL,
     )(place, *[s[0] for s in sources], *tokens)
@@ -162,7 +163,7 @@
     nrows, sites = slab.shape
     rest = sites - 3 * whole
     rest_width = rest + -rest % LANES
-    long = [n for n in ("own", "r", "l") if n in names and streams[n][0].shape[1] % tile == rest_width] if first else []
+    long = [n for n in ("own", "x", "y") if n in names and streams[n][0].shape[1] % tile == rest_width] if first else []
     blocks, frames, width = sums_shape
 
     def kernel(place_ref, *refs):
@@ -252,19 +253,15 @@
     k = lax.axis_index(SITES)
     place = jnp.stack([z, k]).astype(jnp.int32)
     slab = slab.reshape(nrows, sites)
-    right = [(0, 1), (1, 2), (2, 3)]
-    left = [(3, 2), (2, 1), (1, 0)]
+    outer = [(0, 1), (1, 0), (2, 3), (3, 2)]
+    inner = [(1, 2), (2, 1)]
 
     def send(pair):
-        return lax.ppermute(pair[0], "wide", right), lax.ppermute(pair[1], "wide", left)
-
-    def mirror(choice):
-        swap = {0: 0, 1: 2, 2: 1, 3: 4, 4: 3}
-        return [swap.get(c) for c in reversed(choice)]
-
-    def routed(sources, choice, width, tokens, start=0):
+        return lax.ppermute(pair[0], "wide", outer), lax.ppermute(pair[1], "wide", inner)
+
+    def routed(sources, to_outer, to_inner, width, tokens, start=0):
         sources = [s if isinstance(s, tuple) else (s, 0, 0) for s in sources]
-        pair = route(place, third, sources, choice, mirror(choice), start, width, tokens)
+        pair = route(place, third, sources, to_outer, to_inner, start, width, tokens)
         return send(pair), pair[0]
 
     def spare(i):
@@ -285,31 +282,19 @@
     def thirds(end, mid):
         return lambda z: jnp.where(is_mid(z), mid, end)
 
-    def from_left(z):
-        return z >= 1
-
-    def from_right(z):
-        return z <= 2
-
     def far(z, refs, name):
-        return jnp.where(z < 2, refs[name + "l"][...], refs[name + "r"][...])
-
-    def near(z, refs, name):
-        return jnp.where(z < 2, refs[name + "r"][...], refs[name + "l"][...])
-
-    def both(name, pair, right_needed=from_left, left_needed=from_right):
-        return {name + "r": (pair[0], right_needed, at(0)), name + "l": (pair[1], left_needed, at(0))}
+        return jnp.where(is_end(z), refs[name + "x"][...], refs[name + "y"][...])
+
+    def both(name, pair, x_needed=always):
+        return {name + "x": (pair[0], x_needed, at(0)), name + "y": (pair[1], is_mid, at(0))}
 
     def work1(z, refs, add):
         add(z, 0, dot(refs["own"][...], refs["slab"][...]))
-
-        @pl.when(z >= 1)
-        def _():
-            add(z - 1, 0, dot(refs["r"][...], refs["slab"][...]))
-
-        @pl.when(z <= 2)
-        def _():
-            add(z + 1, 0, dot(refs["l"][...], refs["slab"][...]))
+        add(z ^ 1, 0, dot(refs["x"][...], refs["slab"][...]))
+
+        @pl.when(is_mid(z))
+        def _():
+            add(3 - z, 0, dot(refs["y"][...], refs["slab"][...]))
 
     def work3(z, refs, add):
         add(z, 0, dot(refs["own"][...], refs["slab2"][...]))
@@ -317,7 +302,7 @@
 
         @pl.when(is_mid(z))
         def _():
-            add(jnp.where(z < 2, 0, 3), 0, dot(near(z, refs, ""), refs["slab2"][...]))
+            add(z ^ 1, 0, dot(refs["x"][...], refs["slab2"][...]))
 
     def work4(z, refs, add):
         add((z + 2) % 4, 0, dot(far(z, refs, ""), refs["slab"][...]))
@@ -328,7 +313,7 @@
 
         @pl.when(is_mid(z))
         def _():
-            brought = jnp.concatenate([near(z, refs, "4"), near(z, refs, "")], axis=0)
+            brought = jnp.concatenate([refs["4"][...], refs["x"][...]], axis=0)
             add(z, 2 * LANES, dot(refs["own"][...], brought))
             add(3 - z, 2 * LANES, dot(came, brought))
 
@@ -347,40 +332,34 @@
 
         @pl.when(is_mid(z))
         def _():
-            newest = near(z, refs, "")
-            brought = jnp.concatenate([near(z, refs, "4"), near(z, refs, "5"), newest], axis=0)
+            newest = refs["x"][...]
+            brought = jnp.concatenate([refs["4"][...], refs["5x"][...], newest], axis=0)
             add(block, 2 * LANES, dot(came, brought))
-            both = dot(jnp.concatenate([refs["own"][...], far(z, refs, "5")], axis=0), newest)
+            both = dot(jnp.concatenate([refs["own"][...], refs["5y"][...]], axis=0), newest)
             add(z, 3 * LANES, both[:frames])
             add(3 - z, 3 * LANES, both[frames:])
 
-    def near_right(z):
-        return z == 1
-
-    def near_left(z):
-        return z == 2
-
-    r3, sent = routed([own_c, r1[0], r1[1]], [0, 1, 1, None], long, [])
-    r4, sent = routed([spare(0), r2[0], r2[1]], [0, 1, 1, None], long, [sent])
+    r3, sent = routed([own_c, r1[1], r1[0]], (0, 1), 2, long, [])
+    r4, sent = routed([spare(0), r2[1], r2[0]], (0, 1), 2, long, [sent])
     sums = absorb(
         place, third, dict(both("", r1), slab=(slab, always, at(0)), own=(own_a, always, at(0))), work1, sums_shape, None)
     sums = absorb(
         place, third, dict(both("", r2), slab=(slab, always, at(1)), own=(own_b, always, at(0))), work1, sums_shape, sums,
         first=work1)
-    r5, sent = routed([spare(1), r3[0], r3[1], own_c, own_c], [0, 3, 1, None], long, [sent, sums])
+    r5, sent = routed([spare(1), r3[1], own_c], (0, 1), 2, long, [sent, sums])
     sums = absorb(
         place, third,
         dict(both("", r3), slab=(slab, always, at(0)), slab2=(slab, always, at(2)), own=(own_c, always, at(0))),
         work3, sums_shape, sums)
     tile = third // STEPS
-    r6_sources, r6_choice = [spare(2), r3[0], r3[1], r4[0], r4[1]], [0, 1, 3, None]
-    r6, sent = routed(r6_sources, r6_choice, third - tile, [sent, sums])
-    r7, sent = routed(r6_sources, r6_choice, long - third + tile, [sent], STEPS - 1)
+    r6_sources = [spare(2), r4[1], r3[0]]
+    r6, sent = routed(r6_sources, (0, 1), 2, third - tile, [sent, sums])
+    r7, sent = routed(r6_sources, (0, 1), 2, long - third + tile, [sent], STEPS - 1)
     sums = absorb(
         place, third, dict(both("", r4), slab=(slab, always, at(1))), work4, sums_shape, sums, first=first4)
-    middle = dict(both("4", r4, near_right, near_left), own=(own_c, is_mid, at(0)))
+    middle = {"4": (r4[0], is_mid, at(0)), "own": (own_c, is_mid, at(0))}
     sums = absorb(place, third, dict(both("", r5), slab=(slab, always, thirds(0, 2)), **middle), work5, sums_shape, sums)
-    middle.update(both("5", r5, is_mid, is_mid))
+    middle.update(both("5", r5, is_mid))
     sums = absorb(
         place, third, dict(both("", r6), slab=(slab, always, thirds(1, 2)), **middle), work6, sums_shape, sums,
         tiles=(0, STEPS - 1))

time: 258 us -> 256 us (level)
  waiting for transfers between devices: 132 us -> 110 us
  starting transfers between devices: 62.5 us -> 79.2 us
  local copies, waits for them, and re-layouts: 8.82 us -> 11.7 us
    ppermute x14, waiting for transfers between devices: 124 us -> 101 us  [the longest x7 101 us: send(): lax.ppermute(pair[0], 'wide', outer)]
    ppermute x14, starting transfers between devices: 46.4 us -> 65.5 us  [the longest x7 57.9 us: send(): lax.ppermute(pair[0], 'wide', outer)]
    ppermute x1, starting transfers between devices: 0.32 us -> 4.52 us  [line_plan(): lax.ppermute(extra, ALL, flip(1))]
    ppermute x1, starting transfers between devices: 4.75 us -> 0.54 us  [line_plan(): lax.ppermute(frame_sum, ALL, flip(2))]
    unnamed x12 -> x20, local copies, waits for them, and re-layouts: 7.84 us -> 10.7 us
  transfers between devices with their start and end apart: 21 -> 21, of which waited for: 15 -> 10; matrix products, arithmetic and copies ran while one was open for 0% -> 0% of each run, Pallas kernels for 18% -> 18%
where the time goes in v8:
time: 256 us; the launch traced here: 253 us
  waiting for transfers between devices  110 us (43%)
  starting transfers between devices  79.2 us (31%)
  Pallas kernels  47.5 us (19%)
  local copies, waits for them, and re-layouts  11.7 us (5%)
  other arithmetic  4.04 us (2%)
    ppermute x7, waiting for transfers between devices, send(): lax.ppermute(pair[0], 'wide', outer)  101 us
    ppermute x7, starting transfers between devices, send(): lax.ppermute(pair[0], 'wide', outer)  57.9 us
    pallas_call x7, Pallas kernels, absorb(): pl.pallas_call(kernel, grid_spec=pltpu.PrefetchScalarGridSpec(num_scalar_...  30.9 us
    pallas_call x5, Pallas kernels, route(): pl.pallas_call(kernel, grid_spec=pltpu.PrefetchScalarGridSpec(num_scalar_...  13 us
    unnamed x20, local copies, waits for them, and re-layouts  10.7 us
    ppermute x7, starting transfers between devices, send(): lax.ppermute(pair[1], 'wide', inner)  7.58 us
    ppermute x3, waiting for transfers between devices, line_plan(): lax.ppermute(messages[turn], SITES, [(i, i ^ turn) for i in range(owners)])  6.33 us
    ppermute x1, starting transfers between devices, line_plan(): lax.ppermute(mine, ALL, flip(0))  5.32 us
  transfers between devices with their start and end apart: 21, of which 10 were waited for; matrix products, arithmetic and copies ran while one was open for 0% of the time, Pallas kernels for 18%

profile of v8, /device:TPU:3, one launch (start us, length us, event | category | flops | bytes accessed | tf_op | source)
XLA Modules:
  0.0 252.6 jit_solution(14367947700921520708)
XLA Ops:
  9.4 3.6 %shard_map.55 = (bf16[64,13440]{1,0:T(8,128)(2,1)}, bf16[64,13312]{1,0:T(8,128)(2,1)S(1)}) custom-call(bf16[64,40000]{1,0:T(8,128)(2,1)S(1)} %copy-done.2, s32[1,40000]{1,0:T(1,128)S(1)} %reshape.25.labels_b.labels_c.labels_rest, bf16[64,40000]{1,0:T(8,128)(2,1)S(1)} %copy-done.2, s32[1,40000]{1,0:T(1,128)S(1)} %reshape.25.labels_b.labels_c.labels_rest, ...), custom_call_target="tpu_custom_call" | custom-call | flops 1000 | bytes 1000 | tf_op jit(solution)/shard_map/pallas_call | solution.py:96
  13.0 2.6 %collective-permute-start.1 = (bf16[64,13440]{1,0:T(8,128)(2,1)}, bf16[64,13440]{1,0:T(8,128)(2,1)}, u32[]{:S(2)}, u32[]{:S(2)}) collective-permute-start(bf16[64,13440]{1,0:T(8,128)(2,1)} %get-tuple-element.21.refs_3_.refs_6_), channel_id=1, source_target_pairs={{0,4},{4,0},{8,12},{12,8},{1,5},{5,1},{9,13},{13,9},{2,6},{6,2},{1... | collective-permute-start | bytes 5160968 | tf_op jit(solution)/shard_map/ppermute | solution.py:260
  17.6 24.6 %collective-permute-done.3.refs_2_.refs_0_ = bf16[64,13440]{1,0:T(8,128)(2,1)} collective-permute-done((bf16[64,13440]{1,0:T(8,128)(2,1)S(1)}, bf16[64,13440]{1,0:T(8,128)(2,1)}, u32[]{:S(2)}, u32[]{:S(2)}) %collective-permute-start.3) | collective-permute-done | bytes 1720352 | tf_op jit(solution)/shard_map/ppermute | solution.py:260
  42.2 4.3 %shard_map.56 = (bf16[64,13440]{1,0:T(8,128)(2,1)}, bf16[64,13440]{1,0:T(8,128)(2,1)}) custom-call(s32[2]{0:T(128)S(1)} %pad_add_fusion.place_ref, bf16[64,13312]{1,0:T(8,128)(2,1)S(1)} %get-tuple-element.22.refs_0_.refs_2_.refs_4_, bf16[64,13440]{1,0:T(8,128)(2,1)} %collective-permute-done.2.refs_1_, bf16[64,13440]{1,0:T(8,128)(2,1)} %collective-permute-done.3.refs_2_.refs_0_), custom_call_target="tpu_custom_call" | custom-call | flops 1000 | bytes 1000 | tf_op jit(solution)/shard_map/pallas_call | solution.py:145
  47.3 7.7 %collective-permute-start.5 = (bf16[64,13440]{1,0:T(8,128)(2,1)}, bf16[64,13440]{1,0:T(8,128)(2,1)S(1)}, u32[]{:S(2)}, u32[]{:S(2)}) collective-permute-start(bf16[64,13440]{1,0:T(8,128)(2,1)} %get-tuple-element.23.refs_3_), channel_id=1, source_target_pairs={{0,4},{4,0},{8,12},{12,8},{1,5},{5,1},{9,13},{13,9},{2,6},{6,2},{1... | collective-permute-start | bytes 5160968 | tf_op jit(solution)/shard_map/ppermute | solution.py:260
  55.0 24.1 %collective-permute-done.1.refs_2_.refs_0_.refs_7_ = bf16[64,13440]{1,0:T(8,128)(2,1)} collective-permute-done((bf16[64,13440]{1,0:T(8,128)(2,1)}, bf16[64,13440]{1,0:T(8,128)(2,1)}, u32[]{:S(2)}, u32[]{:S(2)}) %collective-permute-start.1) | collective-permute-done | bytes 1720352 | tf_op jit(solution)/shard_map/ppermute | solution.py:260
  79.1 5.4 %copy-done = bf16[2,96,40000]{2,1,0:T(8,128)(2,1)S(1)} copy-done((bf16[2,96,40000]{2,1,0:T(8,128)(2,1)S(1)}, bf16[2,96,40000]{2,1,0:T(8,128)(2,1)}, u32[]{:S(2)}) %copy-start) | copy-done | bytes 15360024
  84.5 4.4 %shard_map.57 = (bf16[64,13440]{1,0:T(8,128)(2,1)}, bf16[64,13440]{1,0:T(8,128)(2,1)S(1)}) custom-call(s32[2]{0:T(128)S(1)} %pad_add_fusion.place_ref, bf16[192,40000]{1,0:T(8,128)(2,1)S(1)} %bitcast.10, bf16[64,13440]{1,0:T(8,128)(2,1)} %collective-permute-done.refs_1_.refs_8_, bf16[64,13440]{1,0:T(8,128)(2,1)} %collective-permute-done.1.refs_2_.refs_0_.refs_7_, ...), custom_call_target="tpu_custom_call" | custom-call | flops 1000 | bytes 1000 | tf_op jit(solution)/shard_map/pallas_call | solution.py:145
  91.2 6.0 %shard_map.58.refs_4_ = f32[4,64,512]{2,1,0:T(8,128)S(1)} custom-call(s32[2]{0:T(128)S(1)} %pad_add_fusion.place_ref, bf16[64,13440]{1,0:T(8,128)(2,1)} %collective-permute-done.3.refs_2_.refs_0_, bf16[64,13440]{1,0:T(8,128)(2,1)} %collective-permute-done.2.refs_1_, bf16[192,40000]{1,0:T(8,128)(2,1)S(1)} %bitcast.11, bf16[64,13440]{1,0:T(8,128)(2,1)S(1)} %copy-done.4), custom_call_target="tpu_custom_call" | custom-call | flops 1000 | bytes 1000 | tf_op jit(solution)/shard_map/pallas_call | solution.py:236
  97.2 9.9 %collective-permute-start.9 = (bf16[64,13440]{1,0:T(8,128)(2,1)}, bf16[64,13440]{1,0:T(8,128)(2,1)S(1)}, u32[]{:S(2)}, u32[]{:S(2)}) collective-permute-start(bf16[64,13440]{1,0:T(8,128)(2,1)} %get-tuple-element.26.refs_3_), channel_id=1, source_target_pairs={{0,4},{4,0},{8,12},{12,8},{1,5},{5,1},{9,13},{13,9},{2,6},{6,2},{1... | collective-permute-start | bytes 5160968 | tf_op jit(solution)/shard_map/ppermute | solution.py:260
  107.1 6.4 %shard_map.59.refs_4_.refs_5_ = f32[4,64,512]{2,1,0:T(8,128)S(1)} custom-call(s32[2]{0:T(128)S(1)} %pad_add_fusion.place_ref, bf16[64,13440]{1,0:T(8,128)(2,1)} %collective-permute-done.1.refs_2_.refs_0_.refs_7_, bf16[64,13440]{1,0:T(8,128)(2,1)} %collective-permute-done.refs_1_.refs_8_, bf16[192,40000]{1,0:T(8,128)(2,1)S(1)} %bitcast.12, ...), custom_call_target="tpu_custom_call" | custom-call | flops 1000 | bytes 1000 | tf_op jit(solution)/shard_map/pallas_call | solution.py:236
  116.1 9.5 %collective-permute-start.10 = (bf16[64,13440]{1,0:T(8,128)(2,1)S(1)}, bf16[64,13440]{1,0:T(8,128)(2,1)S(1)}, u32[]{:S(2)}, u32[]{:S(2)}) collective-permute-start(bf16[64,13440]{1,0:T(8,128)(2,1)S(1)} %get-tuple-element.27.refs_3_), channel_id=1, source_target_pairs={{0,4},{4,0},{8,12},{12,8},{1,5},{5,1},{9,13},{13,9},{2,6},{6,2},{1... | collective-permute-start | bytes 5160968 | tf_op jit(solution)/shard_map/ppermute | solution.py:260
  127.1 6.0 %shard_map.61.refs_4_.refs_3_ = f32[4,64,512]{2,1,0:T(8,128)S(1)} custom-call(s32[2]{0:T(128)S(1)} %pad_add_fusion.place_ref, bf16[64,13440]{1,0:T(8,128)(2,1)S(1)} %collective-permute-done.5.refs_0_.refs_2_, bf16[64,13440]{1,0:T(8,128)(2,1)S(1)} %copy-done.6, bf16[192,40000]{1,0:T(8,128)(2,1)S(1)} %bitcast.15, bf16[192,40000]{1,0:T(8,128)(2,1)S(1)} %bitcast.16, ...), custom_call_target="tpu_custom_call" | custom-call | flops 1000 | bytes 1000 | tf_op jit(solution)/shard_map/pallas_call | solution.py:236
  135.2 26.6 %collective-permute-start.12 = (bf16[64,9984]{1,0:T(8,128)(2,1)S(1)}, bf16[64,9984]{1,0:T(8,128)(2,1)S(1)}, u32[]{:S(2)}, u32[]{:S(2)}) collective-permute-start(bf16[64,9984]{1,0:T(8,128)(2,1)S(1)} %get-tuple-element.28.refs_3_), channel_id=1, source_target_pairs={{0,4},{4,0},{8,12},{12,8},{1,5},{5,1},{9,13},{13,9},{2,6},{6,2},{1... | collective-permute-start | bytes 3833864 | tf_op jit(solution)/shard_map/ppermute | solution.py:260
  163.8 3.8 %shard_map.64.refs_5_ = f32[4,64,512]{2,1,0:T(8,128)S(1)} custom-call(s32[2]{0:T(128)S(1)} %pad_add_fusion.place_ref, bf16[64,13440]{1,0:T(8,128)(2,1)S(1)} %collective-permute-done.9.refs_0_.refs_5_.refs_3_, bf16[64,13440]{1,0:T(8,128)(2,1)S(1)} %collective-permute-done.4.refs_1_.refs_6_, bf16[192,40000]{1,0:T(8,128)(2,1)S(1)} %bitcast.19, ...), custom_call_target="tpu_custom_call" | custom-call | flops 1000 | bytes 1000 | tf_op jit(solution)/shard_map/pallas_call | solution.py:236
  167.7 21.9 %collective-permute-done.10.refs_0_.refs_5_ = bf16[64,13440]{1,0:T(8,128)(2,1)S(1)} collective-permute-done((bf16[64,13440]{1,0:T(8,128)(2,1)S(1)}, bf16[64,13440]{1,0:T(8,128)(2,1)S(1)}, u32[]{:S(2)}, u32[]{:S(2)}) %collective-permute-start.10) | collective-permute-done | bytes 1720352 | tf_op jit(solution)/shard_map/ppermute | solution.py:260
  189.6 3.8 %shard_map.65.refs_7_ = f32[4,64,512]{2,1,0:T(8,128)S(1)} custom-call(s32[2]{0:T(128)S(1)} %pad_add_fusion.place_ref, bf16[64,13440]{1,0:T(8,128)(2,1)S(1)} %collective-permute-done.10.refs_0_.refs_5_, bf16[64,13440]{1,0:T(8,128)(2,1)S(1)} %collective-permute-done.11.refs_1_.refs_6_, bf16[192,40000]{1,0:T(8,128)(2,1)S(1)} %bitcast.21, ...), custom_call_target="tpu_custom_call" | custom-call | flops 1000 | bytes 1000 | tf_op jit(solution)/shard_map/pallas_call | solution.py:236
  193.4 23.5 %collective-permute-done.12.refs_0_ = bf16[64,9984]{1,0:T(8,128)(2,1)S(1)} collective-permute-done((bf16[64,9984]{1,0:T(8,128)(2,1)S(1)}, bf16[64,9984]{1,0:T(8,128)(2,1)S(1)}, u32[]{:S(2)}, u32[]{:S(2)}) %collective-permute-start.12) | collective-permute-done | bytes 1277984 | tf_op jit(solution)/shard_map/ppermute | solution.py:260
  217.0 3.1 %shard_map.66.refs_7_ = f32[4,64,512]{2,1,0:T(8,128)S(1)} custom-call(s32[2]{0:T(128)S(1)} %pad_add_fusion.place_ref, bf16[64,9984]{1,0:T(8,128)(2,1)S(1)} %collective-permute-done.12.refs_0_, bf16[64,9984]{1,0:T(8,128)(2,1)S(1)} %collective-permute-done.13.refs_1_, bf16[192,40000]{1,0:T(8,128)(2,1)S(1)} %bitcast.22, ...), custom_call_target="tpu_custom_call" | custom-call | flops 1000 | bytes 1000 | tf_op jit(solution)/shard_map/pallas_call | solution.py:236
  220.1 6.4 %collective-permute-done.7.refs_0_.refs_9_ = bf16[64,3456]{1,0:T(8,128)(2,1)S(1)} collective-permute-done((bf16[64,3456]{1,0:T(8,128)(2,1)S(1)}, bf16[64,3456]{1,0:T(8,128)(2,1)S(1)}, u32[]{:S(2)}, u32[]{:S(2)}) %collective-permute-start.7) | collective-permute-done | bytes 442400 | tf_op jit(solution)/shard_map/ppermute | solution.py:260
  231.6 3.4 %collective-permute-done.15 = f32[64,512]{1,0:T(8,128)S(1)} collective-permute-done((f32[64,512]{1,0:T(8,128)S(1)}, f32[64,512]{1,0:T(8,128)S(1)}, u32[]{:S(2)}, u32[]{:S(2)}) %collective-permute-start.15) | collective-permute-done | bytes 131104 | tf_op jit(solution)/shard_map/ppermute | solution.py:372
  234.9 3.0 %collective-permute-done.16 = f32[64,512]{1,0:T(8,128)S(1)} collective-permute-done((f32[64,512]{1,0:T(8,128)S(1)}, f32[64,512]{1,0:T(8,128)S(1)}, u32[]{:S(2)}, u32[]{:S(2)}) %collective-permute-start.16) | collective-permute-done | bytes 131104 | tf_op jit(solution)/shard_map/ppermute | solution.py:372
  238.2 5.3 %collective-permute-start.17 = (f32[64,256]{1,0:T(8,128)S(1)}, f32[64,256]{1,0:T(8,128)S(1)}, u32[]{:S(2)}, u32[]{:S(2)}) collective-permute-start(f32[64,256]{1,0:T(8,128)S(1)} %get-tuple-element.41), channel_id=1, source_target_pairs={{0,0},{1,4},{2,8},{3,12},{4,1},{5,5},{6,9},{7,13},{8,2},{9,6},{10,... | collective-permute-start | bytes 196616 | tf_op jit(solution)/shard_map/ppermute | solution.py:380
  243.5 4.5 %collective-permute-start.18 = (f32[64,256]{1,0:T(8,128)S(1)}, f32[64,256]{1,0:T(8,128)S(1)}, u32[]{:S(2)}, u32[]{:S(2)}) collective-permute-start(f32[64,256]{1,0:T(8,128)S(1)} %get-tuple-element.42), channel_id=1, source_target_pairs={{0,1},{1,5},{2,9},{3,13},{4,0},{5,4},{6,8},{7,12},{8,3},{9,7},{10,... | collective-permute-start | bytes 196616 | tf_op jit(solution)/shard_map/ppermute | solution.py:380
  (66 shorter events, 32.5 us)
Async XLA Ops:
  3.6 9.4 %copy-start.3 = (bf16[64,13440]{1,0:T(8,128)(2,1)}, bf16[64,13440]{1,0:T(8,128)(2,1)S(1)}, u32[]{:S(2)}) copy-start(bf16[64,13440]{1,0:T(8,128)(2,1)S(1)} %add_convert_fusion.token_ref.refs_3_) | copy-start | bytes 5160964
  3.6 38.6 %collective-permute-start.3 = (bf16[64,13440]{1,0:T(8,128)(2,1)S(1)}, bf16[64,13440]{1,0:T(8,128)(2,1)}, u32[]{:S(2)}, u32[]{:S(2)}) collective-permute-start(bf16[64,13440]{1,0:T(8,128)(2,1)S(1)} %add_convert_fusion.token_ref.refs_3_), channel_id=1, source_target_pairs={{0,4},{4,0},{8,12},{12,8},{1,5},{5,1},{9,13},{13,9},{2,6},{6,2},{1... | collective-permute-start | bytes 5160968 | tf_op jit(solution)/shard_map/ppermute | solution.py:260
  5.0 37.2 %collective-permute-start.2 = (bf16[64,13440]{1,0:T(8,128)(2,1)S(1)}, bf16[64,13440]{1,0:T(8,128)(2,1)}, u32[]{:S(2)}, u32[]{:S(2)}) collective-permute-start(bf16[64,13440]{1,0:T(8,128)(2,1)S(1)} %add_convert_fusion.token_ref.refs_3_), channel_id=1, source_target_pairs={{4,8},{8,4},{5,9},{9,5},{6,10},{10,6},{7,11},{11,7},{20,24},{24,20... | collective-permute-start | bytes 5160968 | tf_op jit(solution)/shard_map/ppermute | solution.py:260
  13.0 66.1 %collective-permute-start.1 = (bf16[64,13440]{1,0:T(8,128)(2,1)}, bf16[64,13440]{1,0:T(8,128)(2,1)}, u32[]{:S(2)}, u32[]{:S(2)}) collective-permute-start(bf16[64,13440]{1,0:T(8,128)(2,1)} %get-tuple-element.21.refs_3_.refs_6_), channel_id=1, source_target_pairs={{0,4},{4,0},{8,12},{12,8},{1,5},{5,1},{9,13},{13,9},{2,6},{6,2},{1... | collective-permute-start | bytes 5160968 | tf_op jit(solution)/shard_map/ppermute | solution.py:260
  15.6 63.4 %collective-permute-start = (bf16[64,13440]{1,0:T(8,128)(2,1)}, bf16[64,13440]{1,0:T(8,128)(2,1)}, u32[]{:S(2)}, u32[]{:S(2)}) collective-permute-start(bf16[64,13440]{1,0:T(8,128)(2,1)} %get-tuple-element.21.refs_3_.refs_6_), channel_id=1, source_target_pairs={{4,8},{8,4},{5,9},{9,5},{6,10},{10,6},{7,11},{11,7},{20,24},{24,20... | collective-permute-start | bytes 5160968 | tf_op jit(solution)/shard_map/ppermute | solution.py:260
  46.5 67.0 %collective-permute-start.6 = (bf16[64,13440]{1,0:T(8,128)(2,1)}, bf16[64,13440]{1,0:T(8,128)(2,1)S(1)}, u32[]{:S(2)}, u32[]{:S(2)}) collective-permute-start(bf16[64,13440]{1,0:T(8,128)(2,1)} %get-tuple-element.25), channel_id=1, source_target_pairs={{4,8},{8,4},{5,9},{9,5},{6,10},{10,6},{7,11},{11,7},{20,24},{24,20... | collective-permute-start | bytes 5160968 | tf_op jit(solution)/shard_map/ppermute | solution.py:260
  47.3 78.3 %collective-permute-start.5 = (bf16[64,13440]{1,0:T(8,128)(2,1)}, bf16[64,13440]{1,0:T(8,128)(2,1)S(1)}, u32[]{:S(2)}, u32[]{:S(2)}) collective-permute-start(bf16[64,13440]{1,0:T(8,128)(2,1)} %get-tuple-element.23.refs_3_), channel_id=1, source_target_pairs={{0,4},{4,0},{8,12},{12,8},{1,5},{5,1},{9,13},{13,9},{2,6},{6,2},{1... | collective-permute-start | bytes 5160968 | tf_op jit(solution)/shard_map/ppermute | solution.py:260
  84.5 6.7 %copy-start.4 = (bf16[64,13440]{1,0:T(8,128)(2,1)S(1)}, bf16[64,13440]{1,0:T(8,128)(2,1)}, u32[]{:S(2)}) copy-start(bf16[64,13440]{1,0:T(8,128)(2,1)} %copy-done.3) | copy-start | bytes 5160964
  88.9 44.2 %collective-permute-start.4 = (bf16[64,13440]{1,0:T(8,128)(2,1)S(1)}, bf16[64,13440]{1,0:T(8,128)(2,1)S(1)}, u32[]{:S(2)}, u32[]{:S(2)}) collective-permute-start(bf16[64,13440]{1,0:T(8,128)(2,1)S(1)} %get-tuple-element.24), channel_id=1, source_target_pairs={{4,8},{8,4},{5,9},{9,5},{6,10},{10,6},{7,11},{11,7},{20,24},{24,20... | collective-permute-start | bytes 5160968 | tf_op jit(solution)/shard_map/ppermute | solution.py:260
  97.2 65.7 %collective-permute-start.9 = (bf16[64,13440]{1,0:T(8,128)(2,1)}, bf16[64,13440]{1,0:T(8,128)(2,1)S(1)}, u32[]{:S(2)}, u32[]{:S(2)}) collective-permute-start(bf16[64,13440]{1,0:T(8,128)(2,1)} %get-tuple-element.26.refs_3_), channel_id=1, source_target_pairs={{0,4},{4,0},{8,12},{12,8},{1,5},{5,1},{9,13},{13,9},{2,6},{6,2},{1... | collective-permute-start | bytes 5160968 | tf_op jit(solution)/shard_map/ppermute | solution.py:260
  115.3 47.8 %collective-permute-start.11 = (bf16[64,13440]{1,0:T(8,128)(2,1)S(1)}, bf16[64,13440]{1,0:T(8,128)(2,1)S(1)}, u32[]{:S(2)}, u32[]{:S(2)}) collective-permute-start(bf16[64,13440]{1,0:T(8,128)(2,1)S(1)} %get-tuple-element.31), channel_id=1, source_target_pairs={{4,8},{8,4},{5,9},{9,5},{6,10},{10,6},{7,11},{11,7},{20,24},{24,20... | collective-permute-start | bytes 5160968 | tf_op jit(solution)/shard_map/ppermute | solution.py:260
  116.1 73.5 %collective-permute-start.10 = (bf16[64,13440]{1,0:T(8,128)(2,1)S(1)}, bf16[64,13440]{1,0:T(8,128)(2,1)S(1)}, u32[]{:S(2)}, u32[]{:S(2)}) collective-permute-start(bf16[64,13440]{1,0:T(8,128)(2,1)S(1)} %get-tuple-element.27.refs_3_), channel_id=1, source_target_pairs={{0,4},{4,0},{8,12},{12,8},{1,5},{5,1},{9,13},{13,9},{2,6},{6,2},{1... | collective-permute-start | bytes 5160968 | tf_op jit(solution)/shard_map/ppermute | solution.py:260
  134.4 59.0 %collective-permute-start.13 = (bf16[64,9984]{1,0:T(8,128)(2,1)S(1)}, bf16[64,9984]{1,0:T(8,128)(2,1)S(1)}, u32[]{:S(2)}, u32[]{:S(2)}) collective-permute-start(bf16[64,9984]{1,0:T(8,128)(2,1)S(1)} %get-tuple-element.32), channel_id=1, source_target_pairs={{4,8},{8,4},{5,9},{9,5},{6,10},{10,6},{7,11},{11,7},{20,24},{24,20... | collective-permute-start | bytes 3833864 | tf_op jit(solution)/shard_map/ppermute | solution.py:260
  135.2 81.8 %collective-permute-start.12 = (bf16[64,9984]{1,0:T(8,128)(2,1)S(1)}, bf16[64,9984]{1,0:T(8,128)(2,1)S(1)}, u32[]{:S(2)}, u32[]{:S(2)}) collective-permute-start(bf16[64,9984]{1,0:T(8,128)(2,1)S(1)} %get-tuple-element.28.refs_3_), channel_id=1, source_target_pairs={{0,4},{4,0},{8,12},{12,8},{1,5},{5,1},{9,13},{13,9},{2,6},{6,2},{1... | collective-permute-start | bytes 3833864 | tf_op jit(solution)/shard_map/ppermute | solution.py:260
  163.0 63.5 %collective-permute-start.7 = (bf16[64,3456]{1,0:T(8,128)(2,1)S(1)}, bf16[64,3456]{1,0:T(8,128)(2,1)S(1)}, u32[]{:S(2)}, u32[]{:S(2)}) collective-permute-start(bf16[64,3456]{1,0:T(8,128)(2,1)S(1)} %get-tuple-element.29), channel_id=1, source_target_pairs={{0,4},{4,0},{8,12},{12,8},{1,5},{5,1},{9,13},{13,9},{2,6},{6,2},{1... | collective-permute-start | bytes 1327112 | tf_op jit(solution)/shard_map/ppermute | solution.py:260
  163.2 63.3 %collective-permute-start.8 = (bf16[64,3456]{1,0:T(8,128)(2,1)S(1)}, bf16[64,3456]{1,0:T(8,128)(2,1)S(1)}, u32[]{:S(2)}, u32[]{:S(2)}) collective-permute-start(bf16[64,3456]{1,0:T(8,128)(2,1)S(1)} %get-tuple-element.30), channel_id=1, source_target_pairs={{4,8},{8,4},{5,9},{9,5},{6,10},{10,6},{7,11},{11,7},{20,24},{24,20... | collective-permute-start | bytes 1327112 | tf_op jit(solution)/shard_map/ppermute | solution.py:260
  193.4 33.0 %copy-start.7 = (f32[2,96]{1,0:T(2,128)S(1)}, f32[2,96]{1,0:T(2,128)}, u32[]{:S(2)}) copy-start(f32[2,96]{1,0:T(2,128)} %refs_11_.1) | copy-start | bytes 2308
  228.3 3.3 %collective-permute-start.14 = (f32[64,512]{1,0:T(8,128)S(1)}, f32[64,512]{1,0:T(8,128)S(1)}, u32[]{:S(2)}, u32[]{:S(2)}) collective-permute-start(f32[64,512]{1,0:T(8,128)S(1)} %get-tuple-element.34), channel_id=1, source_target_pairs={{0,1},{1,0},{2,3},{3,2},{4,5},{5,4},{6,7},{7,6},{8,9},{9,8},{10,11... | collective-permute-start | bytes 393224 | tf_op jit(solution)/shard_map/ppermute | solution.py:372
  229.9 5.1 %collective-permute-start.15 = (f32[64,512]{1,0:T(8,128)S(1)}, f32[64,512]{1,0:T(8,128)S(1)}, u32[]{:S(2)}, u32[]{:S(2)}) collective-permute-start(f32[64,512]{1,0:T(8,128)S(1)} %get-tuple-element.35), channel_id=1, source_target_pairs={{0,2},{1,3},{2,0},{3,1},{4,6},{5,7},{6,4},{7,5},{8,10},{9,11},{10,... | collective-permute-start | bytes 393224 | tf_op jit(solution)/shard_map/ppermute | solution.py:372
  230.0 7.9 %collective-permute-start.16 = (f32[64,512]{1,0:T(8,128)S(1)}, f32[64,512]{1,0:T(8,128)S(1)}, u32[]{:S(2)}, u32[]{:S(2)}) collective-permute-start(f32[64,512]{1,0:T(8,128)S(1)} %get-tuple-element.36), channel_id=1, source_target_pairs={{0,3},{1,2},{2,1},{3,0},{4,7},{5,6},{6,5},{7,4},{8,11},{9,10},{10,... | collective-permute-start | bytes 393224 | tf_op jit(solution)/shard_map/ppermute | solution.py:372
  238.2 10.4 %collective-permute-start.17 = (f32[64,256]{1,0:T(8,128)S(1)}, f32[64,256]{1,0:T(8,128)S(1)}, u32[]{:S(2)}, u32[]{:S(2)}) collective-permute-start(f32[64,256]{1,0:T(8,128)S(1)} %get-tuple-element.41), channel_id=1, source_target_pairs={{0,0},{1,4},{2,8},{3,12},{4,1},{5,5},{6,9},{7,13},{8,2},{9,6},{10,... | collective-permute-start | bytes 196616 | tf_op jit(solution)/shard_map/ppermute | solution.py:380
  243.5 7.0 %collective-permute-start.18 = (f32[64,256]{1,0:T(8,128)S(1)}, f32[64,256]{1,0:T(8,128)S(1)}, u32[]{:S(2)}, u32[]{:S(2)}) collective-permute-start(f32[64,256]{1,0:T(8,128)S(1)} %get-tuple-element.42), channel_id=1, source_target_pairs={{0,1},{1,5},{2,9},{3,13},{4,0},{5,4},{6,8},{7,12},{8,3},{9,7},{10,... | collective-permute-start | bytes 196616 | tf_op jit(solution)/shard_map/ppermute | solution.py:380
  248.0 3.0 %collective-permute-start.20 = (f32[64]{0:T(128)S(1)}, f32[64]{0:T(128)S(1)}, u32[]{:S(2)}, u32[]{:S(2)}) collective-permute-start(f32[64]{0:T(128)S(1)} %add.42), channel_id=1, source_target_pairs={{0,3},{1,7},{2,11},{3,15},{4,2},{5,6},{6,10},{7,14},{8,1},{9,5},{1... | collective-permute-start | bytes 776 | tf_op jit(solution)/shard_map/ppermute | solution.py:381
  248.0 3.9 %collective-permute-start.19 = (f32[64]{0:T(128)S(1)}, f32[64]{0:T(128)S(1)}, u32[]{:S(2)}, u32[]{:S(2)}) collective-permute-start(f32[64]{0:T(128)S(1)} %add.42), channel_id=1, source_target_pairs={{0,2},{1,6},{2,10},{3,14},{4,3},{5,7},{6,11},{7,15},{8,0},{9,4},{1... | collective-permute-start | bytes 776 | tf_op jit(solution)/shard_map/ppermute | solution.py:381
  (7 other events, 28.0 us)

commit v9 on v8

--- a/solution.py
+++ b/solution.py
@@ -257,7 +257,8 @@
     inner = [(1, 2), (2, 1)]
 
     def send(pair):
-        return lax.ppermute(pair[0], "wide", outer), lax.ppermute(pair[1], "wide", inner)
+        y = lax.ppermute(pair[1], "wide", inner)
+        return lax.ppermute(pair[0], "wide", outer), y
 
     def routed(sources, to_outer, to_inner, width, tokens, start=0):
         sources = [s if isinstance(s, tuple) else (s, 0, 0) for s in sources]
@@ -339,8 +340,8 @@
             add(z, 3 * LANES, both[:frames])
             add(3 - z, 3 * LANES, both[frames:])
 
-    r3, sent = routed([own_c, r1[1], r1[0]], (0, 1), 2, long, [])
-    r4, sent = routed([spare(0), r2[1], r2[0]], (0, 1), 2, long, [sent])
+    r3, sent = routed([own_c, r1[0], r1[1]], (0, 2), 1, long, [])
+    r4, sent = routed([spare(0), r2[0], r2[1]], (0, 2), 1, long, [sent])
     sums = absorb(
         place, third, dict(both("", r1), slab=(slab, always, at(0)), own=(own_a, always, at(0))), work1, sums_shape, None)
     sums = absorb(
@@ -378,7 +379,8 @@
         return [(a * owners + b, b * owners + (a ^ turn)) for a in range(wide) for b in range(owners)]
 
     mine, extra = lax.ppermute(mine, ALL, flip(0)), lax.ppermute(extra, ALL, flip(1))
-    total = mine[:, FREE] + extra[:, FREE] + lax.ppermute(frame_sum, ALL, flip(2)) + lax.ppermute(frame_sum, ALL, flip(3))
+    total = mine[:, FREE] + extra[:, FREE]
+    total += lax.ppermute(total, SITES, [(i, i ^ 2) for i in range(owners)])
     weight_sum = mine[:, FREE - 1]
     charges = (mine + extra)[:, :nrows].reshape(frames, panels, rows).transpose(1, 2, 0)
     return finish(charges, total, weight_sum, profile)

time: 256 us -> 258 us (level)
  waiting for transfers between devices: 110 us -> 125 us
  starting transfers between devices: 79.2 us -> 67.8 us
    ppermute x16 -> x15, waiting for transfers between devices: 102 us -> 114 us  [the longest x7 112 us: send(): return (lax.ppermute(pair[0], 'wide', outer), y)]
    ppermute x16 -> x15, starting transfers between devices: 66 us -> 57.5 us  [the longest x7 49.7 us: send(): return (lax.ppermute(pair[0], 'wide', outer), y)]
  transfers between devices with their start and end apart: 21 -> 20, of which waited for: 10 -> 10; matrix products, arithmetic and copies ran while one was open for 0% -> 0% of each run, Pallas kernels for 18% -> 18%
where the time goes in v9:
time: 258 us; the launch traced here: 257 us
  waiting for transfers between devices  125 us (48%)
  starting transfers between devices  67.8 us (26%)
  Pallas kernels  47.6 us (18%)
  local copies, waits for them, and re-layouts  11.6 us (4%)
  other arithmetic  4.04 us (2%)
    ppermute x7, waiting for transfers between devices, send(): return (lax.ppermute(pair[0], 'wide', outer), y)  112 us
    ppermute x7, starting transfers between devices, send(): return (lax.ppermute(pair[0], 'wide', outer), y)  49.7 us
    pallas_call x7, Pallas kernels, absorb(): pl.pallas_call(kernel, grid_spec=pltpu.PrefetchScalarGridSpec(num_scalar_...  30.9 us
    pallas_call x5, Pallas kernels, route(): pl.pallas_call(kernel, grid_spec=pltpu.PrefetchScalarGridSpec(num_scalar_...  13.1 us
    unnamed x20, local copies, waits for them, and re-layouts  10.7 us
    ppermute x7, starting transfers between devices, send(): y = lax.ppermute(pair[1], 'wide', inner)  7.72 us
    ppermute x3, waiting for transfers between devices, line_plan(): lax.ppermute(messages[turn], SITES, [(i, i ^ turn) for i in range(owners)])  6.33 us
  transfers between devices with their start and end apart: 20, of which 10 were waited for; matrix products, arithmetic and copies ran while one was open for 0% of the time, Pallas kernels for 18%

profile of v9, /device:TPU:3, one launch (start us, length us, event | category | flops | bytes accessed | tf_op | source)
XLA Modules:
  0.0 256.7 jit_solution(16401774119917992847)
XLA Ops:
  10.8 3.6 %shard_map.55 = (bf16[64,13440]{1,0:T(8,128)(2,1)}, bf16[64,13312]{1,0:T(8,128)(2,1)S(1)}) custom-call(bf16[64,40000]{1,0:T(8,128)(2,1)S(1)} %copy-done.2, s32[1,40000]{1,0:T(1,128)S(1)} %reshape.25.labels_b.labels_c.labels_rest, bf16[64,40000]{1,0:T(8,128)(2,1)S(1)} %copy-done.2, s32[1,40000]{1,0:T(1,128)S(1)} %reshape.25.labels_b.labels_c.labels_rest, ...), custom_call_target="tpu_custom_call" | custom-call | flops 1000 | bytes 1000 | tf_op jit(solution)/shard_map/pallas_call | solution.py:96
  17.7 27.6 %collective-permute-done.2.refs_1_.refs_0_ = bf16[64,13440]{1,0:T(8,128)(2,1)} collective-permute-done((bf16[64,13440]{1,0:T(8,128)(2,1)S(1)}, bf16[64,13440]{1,0:T(8,128)(2,1)}, u32[]{:S(2)}, u32[]{:S(2)}) %collective-permute-start.2) | collective-permute-done | bytes 1720352 | tf_op jit(solution)/shard_map/ppermute | solution.py:261
  45.3 4.3 %shard_map.56 = (bf16[64,13440]{1,0:T(8,128)(2,1)}, bf16[64,13440]{1,0:T(8,128)(2,1)}) custom-call(s32[2]{0:T(128)S(1)} %pad_add_fusion.place_ref, bf16[64,13312]{1,0:T(8,128)(2,1)S(1)} %get-tuple-element.22.refs_0_.refs_2_.refs_4_, bf16[64,13440]{1,0:T(8,128)(2,1)} %collective-permute-done.2.refs_1_.refs_0_, ...), custom_call_target="tpu_custom_call" | custom-call | flops 1000 | bytes 1000 | tf_op jit(solution)/shard_map/pallas_call | solution.py:145
  50.3 3.7 %collective-permute-start.5 = (bf16[64,13440]{1,0:T(8,128)(2,1)}, bf16[64,13440]{1,0:T(8,128)(2,1)S(1)}, u32[]{:S(2)}, u32[]{:S(2)}) collective-permute-start(bf16[64,13440]{1,0:T(8,128)(2,1)} %get-tuple-element.23.refs_3_), channel_id=1, source_target_pairs={{0,4},{4,0},{8,12},{12,8},{1,5},{5,1},{9,13},{13,9},{2,6},{6,2},{1... | collective-permute-start | bytes 5160968 | tf_op jit(solution)/shard_map/ppermute | solution.py:261
  54.0 28.2 %collective-permute-done.refs_1_.refs_0_.refs_7_ = bf16[64,13440]{1,0:T(8,128)(2,1)} collective-permute-done((bf16[64,13440]{1,0:T(8,128)(2,1)}, bf16[64,13440]{1,0:T(8,128)(2,1)}, u32[]{:S(2)}, u32[]{:S(2)}) %collective-permute-start) | collective-permute-done | bytes 1720352 | tf_op jit(solution)/shard_map/ppermute | solution.py:261
  82.1 5.4 %copy-done = bf16[2,96,40000]{2,1,0:T(8,128)(2,1)S(1)} copy-done((bf16[2,96,40000]{2,1,0:T(8,128)(2,1)S(1)}, bf16[2,96,40000]{2,1,0:T(8,128)(2,1)}, u32[]{:S(2)}) %copy-start) | copy-done | bytes 15360024
  87.5 4.4 %shard_map.57 = (bf16[64,13440]{1,0:T(8,128)(2,1)}, bf16[64,13440]{1,0:T(8,128)(2,1)S(1)}) custom-call(s32[2]{0:T(128)S(1)} %pad_add_fusion.place_ref, bf16[192,40000]{1,0:T(8,128)(2,1)S(1)} %bitcast.10, bf16[64,13440]{1,0:T(8,128)(2,1)} %collective-permute-done.refs_1_.refs_0_.refs_7_, bf16[64,13440]{1,0:T(8,128)(2,1)} %collective-permute-done.1.refs_2_.refs_1_.refs_8_, ...), custom_call_target="tpu_custom_call" | custom-call | flops 1000 | bytes 1000 | tf_op jit(solution)/shard_map/pallas_call | solution.py:145
  94.2 6.0 %shard_map.58.refs_4_ = f32[4,64,512]{2,1,0:T(8,128)S(1)} custom-call(s32[2]{0:T(128)S(1)} %pad_add_fusion.place_ref, bf16[64,13440]{1,0:T(8,128)(2,1)} %collective-permute-done.2.refs_1_.refs_0_, bf16[64,13440]{1,0:T(8,128)(2,1)} %collective-permute-done.3.refs_2_.refs_1_, bf16[192,40000]{1,0:T(8,128)(2,1)S(1)} %bitcast.11, bf16[64,13440]{1,0:T(8,128)(2,1)S(1)} %copy-done.4), custom_call_target="tpu_custom_call" | custom-call | flops 1000 | bytes 1000 | tf_op jit(solution)/shard_map/pallas_call | solution.py:236
  100.3 5.8 %collective-permute-start.9 = (bf16[64,13440]{1,0:T(8,128)(2,1)}, bf16[64,13440]{1,0:T(8,128)(2,1)S(1)}, u32[]{:S(2)}, u32[]{:S(2)}) collective-permute-start(bf16[64,13440]{1,0:T(8,128)(2,1)} %get-tuple-element.26.refs_3_), channel_id=1, source_target_pairs={{0,4},{4,0},{8,12},{12,8},{1,5},{5,1},{9,13},{13,9},{2,6},{6,2},{1... | collective-permute-start | bytes 5160968 | tf_op jit(solution)/shard_map/ppermute | solution.py:261
  106.1 6.4 %shard_map.59.refs_4_.refs_5_ = f32[4,64,512]{2,1,0:T(8,128)S(1)} custom-call(s32[2]{0:T(128)S(1)} %pad_add_fusion.place_ref, bf16[64,13440]{1,0:T(8,128)(2,1)} %collective-permute-done.refs_1_.refs_0_.refs_7_, bf16[64,13440]{1,0:T(8,128)(2,1)} %collective-permute-done.1.refs_2_.refs_1_.refs_8_, bf16[192,40000]{1,0:T(8,128)(2,1)S(1)} %bitcast.12, ...), custom_call_target="tpu_custom_call" | custom-call | flops 1000 | bytes 1000 | tf_op jit(solution)/shard_map/pallas_call | solution.py:236
  115.1 9.5 %collective-permute-start.10 = (bf16[64,13440]{1,0:T(8,128)(2,1)S(1)}, bf16[64,13440]{1,0:T(8,128)(2,1)S(1)}, u32[]{:S(2)}, u32[]{:S(2)}) collective-permute-start(bf16[64,13440]{1,0:T(8,128)(2,1)S(1)} %get-tuple-element.27.refs_3_), channel_id=1, source_target_pairs={{0,4},{4,0},{8,12},{12,8},{1,5},{5,1},{9,13},{13,9},{2,6},{6,2},{1... | collective-permute-start | bytes 5160968 | tf_op jit(solution)/shard_map/ppermute | solution.py:261
  126.0 6.0 %shard_map.61.refs_4_.refs_3_ = f32[4,64,512]{2,1,0:T(8,128)S(1)} custom-call(s32[2]{0:T(128)S(1)} %pad_add_fusion.place_ref, bf16[64,13440]{1,0:T(8,128)(2,1)S(1)} %collective-permute-done.5.refs_0_.refs_2_, bf16[64,13440]{1,0:T(8,128)(2,1)S(1)} %copy-done.6, bf16[192,40000]{1,0:T(8,128)(2,1)S(1)} %bitcast.15, bf16[192,40000]{1,0:T(8,128)(2,1)S(1)} %bitcast.16, ...), custom_call_target="tpu_custom_call" | custom-call | flops 1000 | bytes 1000 | tf_op jit(solution)/shard_map/pallas_call | solution.py:236
  134.1 26.6 %collective-permute-start.12 = (bf16[64,9984]{1,0:T(8,128)(2,1)S(1)}, bf16[64,9984]{1,0:T(8,128)(2,1)S(1)}, u32[]{:S(2)}, u32[]{:S(2)}) collective-permute-start(bf16[64,9984]{1,0:T(8,128)(2,1)S(1)} %get-tuple-element.28.refs_3_), channel_id=1, source_target_pairs={{0,4},{4,0},{8,12},{12,8},{1,5},{5,1},{9,13},{13,9},{2,6},{6,2},{1... | collective-permute-start | bytes 3833864 | tf_op jit(solution)/shard_map/ppermute | solution.py:261
  162.8 3.9 %shard_map.64.refs_5_ = f32[4,64,512]{2,1,0:T(8,128)S(1)} custom-call(s32[2]{0:T(128)S(1)} %pad_add_fusion.place_ref, bf16[64,13440]{1,0:T(8,128)(2,1)S(1)} %collective-permute-done.9.refs_0_.refs_5_.refs_3_, bf16[64,13440]{1,0:T(8,128)(2,1)S(1)} %collective-permute-done.4.refs_1_.refs_6_, bf16[192,40000]{1,0:T(8,128)(2,1)S(1)} %bitcast.19, ...), custom_call_target="tpu_custom_call" | custom-call | flops 1000 | bytes 1000 | tf_op jit(solution)/shard_map/pallas_call | solution.py:236
  166.7 26.0 %collective-permute-done.10.refs_0_.refs_5_ = bf16[64,13440]{1,0:T(8,128)(2,1)S(1)} collective-permute-done((bf16[64,13440]{1,0:T(8,128)(2,1)S(1)}, bf16[64,13440]{1,0:T(8,128)(2,1)S(1)}, u32[]{:S(2)}, u32[]{:S(2)}) %collective-permute-start.10) | collective-permute-done | bytes 1720352 | tf_op jit(solution)/shard_map/ppermute | solution.py:261
  192.6 3.8 %shard_map.65.refs_7_ = f32[4,64,512]{2,1,0:T(8,128)S(1)} custom-call(s32[2]{0:T(128)S(1)} %pad_add_fusion.place_ref, bf16[64,13440]{1,0:T(8,128)(2,1)S(1)} %collective-permute-done.10.refs_0_.refs_5_, bf16[64,13440]{1,0:T(8,128)(2,1)S(1)} %collective-permute-done.11.refs_1_.refs_6_, bf16[192,40000]{1,0:T(8,128)(2,1)S(1)} %bitcast.21, ...), custom_call_target="tpu_custom_call" | custom-call | flops 1000 | bytes 1000 | tf_op jit(solution)/shard_map/pallas_call | solution.py:236
  196.5 23.5 %collective-permute-done.12.refs_0_ = bf16[64,9984]{1,0:T(8,128)(2,1)S(1)} collective-permute-done((bf16[64,9984]{1,0:T(8,128)(2,1)S(1)}, bf16[64,9984]{1,0:T(8,128)(2,1)S(1)}, u32[]{:S(2)}, u32[]{:S(2)}) %collective-permute-start.12) | collective-permute-done | bytes 1277984 | tf_op jit(solution)/shard_map/ppermute | solution.py:261
  220.0 3.1 %shard_map.66.refs_7_ = f32[4,64,512]{2,1,0:T(8,128)S(1)} custom-call(s32[2]{0:T(128)S(1)} %pad_add_fusion.place_ref, bf16[64,9984]{1,0:T(8,128)(2,1)S(1)} %collective-permute-done.12.refs_0_, bf16[64,9984]{1,0:T(8,128)(2,1)S(1)} %collective-permute-done.13.refs_1_, bf16[192,40000]{1,0:T(8,128)(2,1)S(1)} %bitcast.22, ...), custom_call_target="tpu_custom_call" | custom-call | flops 1000 | bytes 1000 | tf_op jit(solution)/shard_map/pallas_call | solution.py:236
  223.1 6.4 %collective-permute-done.7.refs_0_.refs_9_ = bf16[64,3456]{1,0:T(8,128)(2,1)S(1)} collective-permute-done((bf16[64,3456]{1,0:T(8,128)(2,1)S(1)}, bf16[64,3456]{1,0:T(8,128)(2,1)S(1)}, u32[]{:S(2)}, u32[]{:S(2)}) %collective-permute-start.7) | collective-permute-done | bytes 442400 | tf_op jit(solution)/shard_map/ppermute | solution.py:261
  234.6 3.4 %collective-permute-done.15 = f32[64,512]{1,0:T(8,128)S(1)} collective-permute-done((f32[64,512]{1,0:T(8,128)S(1)}, f32[64,512]{1,0:T(8,128)S(1)}, u32[]{:S(2)}, u32[]{:S(2)}) %collective-permute-start.15) | collective-permute-done | bytes 131104 | tf_op jit(solution)/shard_map/ppermute | solution.py:373
  238.0 3.0 %collective-permute-done.16 = f32[64,512]{1,0:T(8,128)S(1)} collective-permute-done((f32[64,512]{1,0:T(8,128)S(1)}, f32[64,512]{1,0:T(8,128)S(1)}, u32[]{:S(2)}, u32[]{:S(2)}) %collective-permute-start.16) | collective-permute-done | bytes 131104 | tf_op jit(solution)/shard_map/ppermute | solution.py:373
  241.2 4.2 %collective-permute-start.17 = (f32[64,256]{1,0:T(8,128)S(1)}, f32[64,256]{1,0:T(8,128)S(1)}, u32[]{:S(2)}, u32[]{:S(2)}) collective-permute-start(f32[64,256]{1,0:T(8,128)S(1)} %get-tuple-element.41), channel_id=1, source_target_pairs={{0,0},{1,4},{2,8},{3,12},{4,1},{5,5},{6,9},{7,13},{8,2},{9,6},{10,... | collective-permute-start | bytes 196616 | tf_op jit(solution)/shard_map/ppermute | solution.py:381
  245.4 2.8 %collective-permute-start.18 = (f32[64,256]{1,0:T(8,128)S(1)}, f32[64,256]{1,0:T(8,128)S(1)}, u32[]{:S(2)}, u32[]{:S(2)}) collective-permute-start(f32[64,256]{1,0:T(8,128)S(1)} %get-tuple-element.42), channel_id=1, source_target_pairs={{0,1},{1,5},{2,9},{3,13},{4,0},{5,4},{6,8},{7,12},{8,3},{9,7},{10,... | collective-permute-start | bytes 196616 | tf_op jit(solution)/shard_map/ppermute | solution.py:381
  250.0 3.3 %collective-permute-done.18 = f32[64,256]{1,0:T(8,128)S(1)} collective-permute-done((f32[64,256]{1,0:T(8,128)S(1)}, f32[64,256]{1,0:T(8,128)S(1)}, u32[]{:S(2)}, u32[]{:S(2)}) %collective-permute-start.18) | collective-permute-done | bytes 65568 | tf_op jit(solution)/shard_map/ppermute | solution.py:381
  (64 shorter events, 35.8 us)
Async XLA Ops:
  1.6 6.7 %copy-start.8 = (f32[64,2]{0,1:T(2,128)S(1)}, f32[64,2]{0,1:T(2,128)}, u32[]{:S(2)}) copy-start(f32[64,2]{0,1:T(2,128)} %param.7) | copy-start | bytes 1540
  3.6 10.7 %copy-start.3 = (bf16[64,13440]{1,0:T(8,128)(2,1)}, bf16[64,13440]{1,0:T(8,128)(2,1)S(1)}, u32[]{:S(2)}) copy-start(bf16[64,13440]{1,0:T(8,128)(2,1)S(1)} %add_convert_fusion.token_ref.refs_3_) | copy-start | bytes 5160964
  3.6 14.1 %collective-permute-start.3 = (bf16[64,13440]{1,0:T(8,128)(2,1)S(1)}, bf16[64,13440]{1,0:T(8,128)(2,1)}, u32[]{:S(2)}, u32[]{:S(2)}) collective-permute-start(bf16[64,13440]{1,0:T(8,128)(2,1)S(1)} %add_convert_fusion.token_ref.refs_3_), channel_id=1, source_target_pairs={{4,8},{8,4},{5,9},{9,5},{6,10},{10,6},{7,11},{11,7},{20,24},{24,20... | collective-permute-start | bytes 5160968 | tf_op jit(solution)/shard_map/ppermute | solution.py:260
  5.6 39.7 %collective-permute-start.2 = (bf16[64,13440]{1,0:T(8,128)(2,1)S(1)}, bf16[64,13440]{1,0:T(8,128)(2,1)}, u32[]{:S(2)}, u32[]{:S(2)}) collective-permute-start(bf16[64,13440]{1,0:T(8,128)(2,1)S(1)} %add_convert_fusion.token_ref.refs_3_), channel_id=1, source_target_pairs={{0,4},{4,0},{8,12},{12,8},{1,5},{5,1},{9,13},{13,9},{2,6},{6,2},{1... | collective-permute-start | bytes 5160968 | tf_op jit(solution)/shard_map/ppermute | solution.py:261
  14.3 39.6 %collective-permute-start.1 = (bf16[64,13440]{1,0:T(8,128)(2,1)}, bf16[64,13440]{1,0:T(8,128)(2,1)}, u32[]{:S(2)}, u32[]{:S(2)}) collective-permute-start(bf16[64,13440]{1,0:T(8,128)(2,1)} %get-tuple-element.21.refs_3_.refs_6_), channel_id=1, source_target_pairs={{4,8},{8,4},{5,9},{9,5},{6,10},{10,6},{7,11},{11,7},{20,24},{24,20... | collective-permute-start | bytes 5160968 | tf_op jit(solution)/shard_map/ppermute | solution.py:260
  16.3 65.9 %collective-permute-start = (bf16[64,13440]{1,0:T(8,128)(2,1)}, bf16[64,13440]{1,0:T(8,128)(2,1)}, u32[]{:S(2)}, u32[]{:S(2)}) collective-permute-start(bf16[64,13440]{1,0:T(8,128)(2,1)} %get-tuple-element.21.refs_3_.refs_6_), channel_id=1, source_target_pairs={{0,4},{4,0},{8,12},{12,8},{1,5},{5,1},{9,13},{13,9},{2,6},{6,2},{1... | collective-permute-start | bytes 5160968 | tf_op jit(solution)/shard_map/ppermute | solution.py:261
  49.5 62.9 %collective-permute-start.6 = (bf16[64,13440]{1,0:T(8,128)(2,1)}, bf16[64,13440]{1,0:T(8,128)(2,1)S(1)}, u32[]{:S(2)}, u32[]{:S(2)}) collective-permute-start(bf16[64,13440]{1,0:T(8,128)(2,1)} %get-tuple-element.25), channel_id=1, source_target_pairs={{4,8},{8,4},{5,9},{9,5},{6,10},{10,6},{7,11},{11,7},{20,24},{24,20... | collective-permute-start | bytes 5160968 | tf_op jit(solution)/shard_map/ppermute | solution.py:260
  50.3 74.3 %collective-permute-start.5 = (bf16[64,13440]{1,0:T(8,128)(2,1)}, bf16[64,13440]{1,0:T(8,128)(2,1)S(1)}, u32[]{:S(2)}, u32[]{:S(2)}) collective-permute-start(bf16[64,13440]{1,0:T(8,128)(2,1)} %get-tuple-element.23.refs_3_), channel_id=1, source_target_pairs={{0,4},{4,0},{8,12},{12,8},{1,5},{5,1},{9,13},{13,9},{2,6},{6,2},{1... | collective-permute-start | bytes 5160968 | tf_op jit(solution)/shard_map/ppermute | solution.py:261
  87.5 6.7 %copy-start.4 = (bf16[64,13440]{1,0:T(8,128)(2,1)S(1)}, bf16[64,13440]{1,0:T(8,128)(2,1)}, u32[]{:S(2)}) copy-start(bf16[64,13440]{1,0:T(8,128)(2,1)} %copy-done.3) | copy-start | bytes 5160964
  92.0 40.0 %collective-permute-start.4 = (bf16[64,13440]{1,0:T(8,128)(2,1)S(1)}, bf16[64,13440]{1,0:T(8,128)(2,1)S(1)}, u32[]{:S(2)}, u32[]{:S(2)}) collective-permute-start(bf16[64,13440]{1,0:T(8,128)(2,1)S(1)} %get-tuple-element.24), channel_id=1, source_target_pairs={{4,8},{8,4},{5,9},{9,5},{6,10},{10,6},{7,11},{11,7},{20,24},{24,20... | collective-permute-start | bytes 5160968 | tf_op jit(solution)/shard_map/ppermute | solution.py:260
  100.3 61.7 %collective-permute-start.9 = (bf16[64,13440]{1,0:T(8,128)(2,1)}, bf16[64,13440]{1,0:T(8,128)(2,1)S(1)}, u32[]{:S(2)}, u32[]{:S(2)}) collective-permute-start(bf16[64,13440]{1,0:T(8,128)(2,1)} %get-tuple-element.26.refs_3_), channel_id=1, source_target_pairs={{0,4},{4,0},{8,12},{12,8},{1,5},{5,1},{9,13},{13,9},{2,6},{6,2},{1... | collective-permute-start | bytes 5160968 | tf_op jit(solution)/shard_map/ppermute | solution.py:261
  114.3 47.8 %collective-permute-start.11 = (bf16[64,13440]{1,0:T(8,128)(2,1)S(1)}, bf16[64,13440]{1,0:T(8,128)(2,1)S(1)}, u32[]{:S(2)}, u32[]{:S(2)}) collective-permute-start(bf16[64,13440]{1,0:T(8,128)(2,1)S(1)} %get-tuple-element.31), channel_id=1, source_target_pairs={{4,8},{8,4},{5,9},{9,5},{6,10},{10,6},{7,11},{11,7},{20,24},{24,20... | collective-permute-start | bytes 5160968 | tf_op jit(solution)/shard_map/ppermute | solution.py:260
  115.1 77.5 %collective-permute-start.10 = (bf16[64,13440]{1,0:T(8,128)(2,1)S(1)}, bf16[64,13440]{1,0:T(8,128)(2,1)S(1)}, u32[]{:S(2)}, u32[]{:S(2)}) collective-permute-start(bf16[64,13440]{1,0:T(8,128)(2,1)S(1)} %get-tuple-element.27.refs_3_), channel_id=1, source_target_pairs={{0,4},{4,0},{8,12},{12,8},{1,5},{5,1},{9,13},{13,9},{2,6},{6,2},{1... | collective-permute-start | bytes 5160968 | tf_op jit(solution)/shard_map/ppermute | solution.py:261
  133.4 63.1 %collective-permute-start.13 = (bf16[64,9984]{1,0:T(8,128)(2,1)S(1)}, bf16[64,9984]{1,0:T(8,128)(2,1)S(1)}, u32[]{:S(2)}, u32[]{:S(2)}) collective-permute-start(bf16[64,9984]{1,0:T(8,128)(2,1)S(1)} %get-tuple-element.32), channel_id=1, source_target_pairs={{4,8},{8,4},{5,9},{9,5},{6,10},{10,6},{7,11},{11,7},{20,24},{24,20... | collective-permute-start | bytes 3833864 | tf_op jit(solution)/shard_map/ppermute | solution.py:260
  134.1 85.9 %collective-permute-start.12 = (bf16[64,9984]{1,0:T(8,128)(2,1)S(1)}, bf16[64,9984]{1,0:T(8,128)(2,1)S(1)}, u32[]{:S(2)}, u32[]{:S(2)}) collective-permute-start(bf16[64,9984]{1,0:T(8,128)(2,1)S(1)} %get-tuple-element.28.refs_3_), channel_id=1, source_target_pairs={{0,4},{4,0},{8,12},{12,8},{1,5},{5,1},{9,13},{13,9},{2,6},{6,2},{1... | collective-permute-start | bytes 3833864 | tf_op jit(solution)/shard_map/ppermute | solution.py:261
  161.9 67.6 %collective-permute-start.7 = (bf16[64,3456]{1,0:T(8,128)(2,1)S(1)}, bf16[64,3456]{1,0:T(8,128)(2,1)S(1)}, u32[]{:S(2)}, u32[]{:S(2)}) collective-permute-start(bf16[64,3456]{1,0:T(8,128)(2,1)S(1)} %get-tuple-element.29), channel_id=1, source_target_pairs={{0,4},{4,0},{8,12},{12,8},{1,5},{5,1},{9,13},{13,9},{2,6},{6,2},{1... | collective-permute-start | bytes 1327112 | tf_op jit(solution)/shard_map/ppermute | solution.py:261
  162.1 67.4 %collective-permute-start.8 = (bf16[64,3456]{1,0:T(8,128)(2,1)S(1)}, bf16[64,3456]{1,0:T(8,128)(2,1)S(1)}, u32[]{:S(2)}, u32[]{:S(2)}) collective-permute-start(bf16[64,3456]{1,0:T(8,128)(2,1)S(1)} %get-tuple-element.30), channel_id=1, source_target_pairs={{4,8},{8,4},{5,9},{9,5},{6,10},{10,6},{7,11},{11,7},{20,24},{24,20... | collective-permute-start | bytes 1327112 | tf_op jit(solution)/shard_map/ppermute | solution.py:260
  196.5 33.0 %copy-start.7 = (f32[2,96]{1,0:T(2,128)S(1)}, f32[2,96]{1,0:T(2,128)}, u32[]{:S(2)}) copy-start(f32[2,96]{1,0:T(2,128)} %refs_11_.1) | copy-start | bytes 2308
  231.3 3.3 %collective-permute-start.14 = (f32[64,512]{1,0:T(8,128)S(1)}, f32[64,512]{1,0:T(8,128)S(1)}, u32[]{:S(2)}, u32[]{:S(2)}) collective-permute-start(f32[64,512]{1,0:T(8,128)S(1)} %get-tuple-element.34), channel_id=1, source_target_pairs={{0,1},{1,0},{2,3},{3,2},{4,5},{5,4},{6,7},{7,6},{8,9},{9,8},{10,11... | collective-permute-start | bytes 393224 | tf_op jit(solution)/shard_map/ppermute | solution.py:373
  232.9 5.1 %collective-permute-start.15 = (f32[64,512]{1,0:T(8,128)S(1)}, f32[64,512]{1,0:T(8,128)S(1)}, u32[]{:S(2)}, u32[]{:S(2)}) collective-permute-start(f32[64,512]{1,0:T(8,128)S(1)} %get-tuple-element.35), channel_id=1, source_target_pairs={{0,2},{1,3},{2,0},{3,1},{4,6},{5,7},{6,4},{7,5},{8,10},{9,11},{10,... | collective-permute-start | bytes 393224 | tf_op jit(solution)/shard_map/ppermute | solution.py:373
  233.2 7.8 %collective-permute-start.16 = (f32[64,512]{1,0:T(8,128)S(1)}, f32[64,512]{1,0:T(8,128)S(1)}, u32[]{:S(2)}, u32[]{:S(2)}) collective-permute-start(f32[64,512]{1,0:T(8,128)S(1)} %get-tuple-element.36), channel_id=1, source_target_pairs={{0,3},{1,2},{2,1},{3,0},{4,7},{5,6},{6,5},{7,4},{8,11},{9,10},{10,... | collective-permute-start | bytes 393224 | tf_op jit(solution)/shard_map/ppermute | solution.py:373
  241.2 8.8 %collective-permute-start.17 = (f32[64,256]{1,0:T(8,128)S(1)}, f32[64,256]{1,0:T(8,128)S(1)}, u32[]{:S(2)}, u32[]{:S(2)}) collective-permute-start(f32[64,256]{1,0:T(8,128)S(1)} %get-tuple-element.41), channel_id=1, source_target_pairs={{0,0},{1,4},{2,8},{3,12},{4,1},{5,5},{6,9},{7,13},{8,2},{9,6},{10,... | collective-permute-start | bytes 196616 | tf_op jit(solution)/shard_map/ppermute | solution.py:381
  245.4 8.0 %collective-permute-start.18 = (f32[64,256]{1,0:T(8,128)S(1)}, f32[64,256]{1,0:T(8,128)S(1)}, u32[]{:S(2)}, u32[]{:S(2)}) collective-permute-start(f32[64,256]{1,0:T(8,128)S(1)} %get-tuple-element.42), channel_id=1, source_target_pairs={{0,1},{1,5},{2,9},{3,13},{4,0},{5,4},{6,8},{7,12},{8,3},{9,7},{10,... | collective-permute-start | bytes 196616 | tf_op jit(solution)/shard_map/ppermute | solution.py:381
  253.5 2.5 collective-permute-start.19
  (6 other events, 24.0 us)

commit v10 on v9

--- a/solution.py
+++ b/solution.py
@@ -373,14 +373,17 @@
         summed += lax.ppermute(messages[turn], SITES, [(i, i ^ turn) for i in range(owners)])
     half = WIDTH // 2
     frame_sum = jnp.sum(summed[:, :nrows], axis=1) + jnp.sum(summed[:, half:half + nrows], axis=1)
-    lane = jnp.arange(half)
-    mine, extra = (jnp.where(lane[None, :] == FREE, frame_sum[:, None], x) for x in (summed[:, :half], summed[:, half:]))
-    def flip(turn):
-        return [(a * owners + b, b * owners + (a ^ turn)) for a in range(wide) for b in range(owners)]
-
-    mine, extra = lax.ppermute(mine, ALL, flip(0)), lax.ppermute(extra, ALL, flip(1))
-    total = mine[:, FREE] + extra[:, FREE]
-    total += lax.ppermute(total, SITES, [(i, i ^ 2) for i in range(owners)])
+    lane = jnp.arange(WIDTH) % half
+    sent = jnp.where(lane[None, :] == FREE, frame_sum[:, None], summed)
+    flip = [(a * owners + b, b * owners + a) for a in range(wide) for b in range(owners)]
+    got = lax.ppermute(sent, ALL, flip)
+
+    def beside(x, turn):
+        return lax.ppermute(x, SITES, [(i, i ^ turn) for i in range(owners)])
+
+    mine, frame_sum = got[:, :half], got[:, FREE]
+    extra = beside(got[:, half:], 1)
+    total = frame_sum + extra[:, FREE] + beside(frame_sum, 2) + beside(frame_sum, 3)
     weight_sum = mine[:, FREE - 1]
     charges = (mine + extra)[:, :nrows].reshape(frames, panels, rows).transpose(1, 2, 0)
     return finish(charges, total, weight_sum, profile)

time: 258 us -> 262 us (1.016); the launches traced: 257 us -> 258 us
    ppermute x3 -> x4, starting transfers between devices: 7.06 us -> 8.27 us  [the longest x1 4.16 us: line_plan(): got = lax.ppermute(sent, ALL, flip)]
    ppermute x3 -> x4, waiting for transfers between devices: 7.39 us -> 7.35 us  [the longest x1 6.04 us: line_plan(): got = lax.ppermute(sent, ALL, flip)]
  transfers between devices with their start and end apart: 20 -> 21, of which waited for: 10 -> 9; matrix products, arithmetic and copies ran while one was open for 0% -> 0% of each run, Pallas kernels for 18% -> 18%
where the time goes in v10:
time: 262 us; the launch traced here: 258 us
  waiting for transfers between devices  125 us (48%)
  starting transfers between devices  69 us (26%)
  Pallas kernels  47.5 us (18%)
  local copies, waits for them, and re-layouts  12 us (5%)
  other arithmetic  3.85 us (1%)
    ppermute x7, waiting for transfers between devices, send(): return (lax.ppermute(pair[0], 'wide', outer), y)  112 us
    ppermute x7, starting transfers between devices, send(): return (lax.ppermute(pair[0], 'wide', outer), y)  49.7 us
    pallas_call x7, Pallas kernels, absorb(): pl.pallas_call(kernel, grid_spec=pltpu.PrefetchScalarGridSpec(num_scalar_...  30.9 us
    pallas_call x5, Pallas kernels, route(): pl.pallas_call(kernel, grid_spec=pltpu.PrefetchScalarGridSpec(num_scalar_...  13.1 us
    unnamed x20, local copies, waits for them, and re-layouts  10.7 us
    ppermute x7, starting transfers between devices, send(): y = lax.ppermute(pair[1], 'wide', inner)  7.66 us
    ppermute x3, waiting for transfers between devices, line_plan(): lax.ppermute(messages[turn], SITES, [(i, i ^ turn) for i in range(owners)])  6.33 us
    ppermute x1, waiting for transfers between devices, line_plan(): got = lax.ppermute(sent, ALL, flip)  6.04 us
  transfers between devices with their start and end apart: 21, of which 9 were waited for; matrix products, arithmetic and copies ran while one was open for 0% of the time, Pallas kernels for 18%

profile of v10, /device:TPU:3, one launch (start us, length us, event | category | flops | bytes accessed | tf_op | source)
XLA Modules:
  0.0 258.1 jit_solution(11411872757389740271)
XLA Ops:
  10.8 3.5 %shard_map.55 = (bf16[64,13440]{1,0:T(8,128)(2,1)}, bf16[64,13312]{1,0:T(8,128)(2,1)S(1)}) custom-call(bf16[64,40000]{1,0:T(8,128)(2,1)S(1)} %copy-done.2, s32[1,40000]{1,0:T(1,128)S(1)} %reshape.30.labels_b.labels_c.labels_rest, bf16[64,40000]{1,0:T(8,128)(2,1)S(1)} %copy-done.2, s32[1,40000]{1,0:T(1,128)S(1)} %reshape.30.labels_b.labels_c.labels_rest, ...), custom_call_target="tpu_custom_call" | custom-call | flops 1000 | bytes 1000 | tf_op jit(solution)/shard_map/pallas_call | solution.py:96
  17.6 27.6 %collective-permute-done.2.refs_1_.refs_0_ = bf16[64,13440]{1,0:T(8,128)(2,1)} collective-permute-done((bf16[64,13440]{1,0:T(8,128)(2,1)S(1)}, bf16[64,13440]{1,0:T(8,128)(2,1)}, u32[]{:S(2)}, u32[]{:S(2)}) %collective-permute-start.2) | collective-permute-done | bytes 1720352 | tf_op jit(solution)/shard_map/ppermute | solution.py:261
  45.3 4.3 %shard_map.56 = (bf16[64,13440]{1,0:T(8,128)(2,1)}, bf16[64,13440]{1,0:T(8,128)(2,1)}) custom-call(s32[2]{0:T(128)S(1)} %pad_add_fusion.place_ref, bf16[64,13312]{1,0:T(8,128)(2,1)S(1)} %get-tuple-element.22.refs_0_.refs_2_.refs_4_, bf16[64,13440]{1,0:T(8,128)(2,1)} %collective-permute-done.2.refs_1_.refs_0_, ...), custom_call_target="tpu_custom_call" | custom-call | flops 1000 | bytes 1000 | tf_op jit(solution)/shard_map/pallas_call | solution.py:145
  50.3 3.6 %collective-permute-start.5 = (bf16[64,13440]{1,0:T(8,128)(2,1)}, bf16[64,13440]{1,0:T(8,128)(2,1)S(1)}, u32[]{:S(2)}, u32[]{:S(2)}) collective-permute-start(bf16[64,13440]{1,0:T(8,128)(2,1)} %get-tuple-element.23.refs_3_), channel_id=1, source_target_pairs={{0,4},{4,0},{8,12},{12,8},{1,5},{5,1},{9,13},{13,9},{2,6},{6,2},{1... | collective-permute-start | bytes 5160968 | tf_op jit(solution)/shard_map/ppermute | solution.py:261
  53.9 28.2 %collective-permute-done.refs_1_.refs_0_.refs_7_ = bf16[64,13440]{1,0:T(8,128)(2,1)} collective-permute-done((bf16[64,13440]{1,0:T(8,128)(2,1)}, bf16[64,13440]{1,0:T(8,128)(2,1)}, u32[]{:S(2)}, u32[]{:S(2)}) %collective-permute-start) | collective-permute-done | bytes 1720352 | tf_op jit(solution)/shard_map/ppermute | solution.py:261
  82.1 5.4 %copy-done = bf16[2,96,40000]{2,1,0:T(8,128)(2,1)S(1)} copy-done((bf16[2,96,40000]{2,1,0:T(8,128)(2,1)S(1)}, bf16[2,96,40000]{2,1,0:T(8,128)(2,1)}, u32[]{:S(2)}) %copy-start) | copy-done | bytes 15360024
  87.5 4.4 %shard_map.57 = (bf16[64,13440]{1,0:T(8,128)(2,1)}, bf16[64,13440]{1,0:T(8,128)(2,1)S(1)}) custom-call(s32[2]{0:T(128)S(1)} %pad_add_fusion.place_ref, bf16[192,40000]{1,0:T(8,128)(2,1)S(1)} %bitcast.10, bf16[64,13440]{1,0:T(8,128)(2,1)} %collective-permute-done.refs_1_.refs_0_.refs_7_, bf16[64,13440]{1,0:T(8,128)(2,1)} %collective-permute-done.1.refs_2_.refs_1_.refs_8_, ...), custom_call_target="tpu_custom_call" | custom-call | flops 1000 | bytes 1000 | tf_op jit(solution)/shard_map/pallas_call | solution.py:145
  94.2 6.0 %shard_map.58.refs_4_ = f32[4,64,512]{2,1,0:T(8,128)S(1)} custom-call(s32[2]{0:T(128)S(1)} %pad_add_fusion.place_ref, bf16[64,13440]{1,0:T(8,128)(2,1)} %collective-permute-done.2.refs_1_.refs_0_, bf16[64,13440]{1,0:T(8,128)(2,1)} %collective-permute-done.3.refs_2_.refs_1_, bf16[192,40000]{1,0:T(8,128)(2,1)S(1)} %bitcast.11, bf16[64,13440]{1,0:T(8,128)(2,1)S(1)} %copy-done.4), custom_call_target="tpu_custom_call" | custom-call | flops 1000 | bytes 1000 | tf_op jit(solution)/shard_map/pallas_call | solution.py:236
  100.3 5.8 %collective-permute-start.9 = (bf16[64,13440]{1,0:T(8,128)(2,1)}, bf16[64,13440]{1,0:T(8,128)(2,1)S(1)}, u32[]{:S(2)}, u32[]{:S(2)}) collective-permute-start(bf16[64,13440]{1,0:T(8,128)(2,1)} %get-tuple-element.26.refs_3_), channel_id=1, source_target_pairs={{0,4},{4,0},{8,12},{12,8},{1,5},{5,1},{9,13},{13,9},{2,6},{6,2},{1... | collective-permute-start | bytes 5160968 | tf_op jit(solution)/shard_map/ppermute | solution.py:261
  106.1 6.4 %shard_map.59.refs_4_.refs_5_ = f32[4,64,512]{2,1,0:T(8,128)S(1)} custom-call(s32[2]{0:T(128)S(1)} %pad_add_fusion.place_ref, bf16[64,13440]{1,0:T(8,128)(2,1)} %collective-permute-done.refs_1_.refs_0_.refs_7_, bf16[64,13440]{1,0:T(8,128)(2,1)} %collective-permute-done.1.refs_2_.refs_1_.refs_8_, bf16[192,40000]{1,0:T(8,128)(2,1)S(1)} %bitcast.12, ...), custom_call_target="tpu_custom_call" | custom-call | flops 1000 | bytes 1000 | tf_op jit(solution)/shard_map/pallas_call | solution.py:236
  115.1 9.5 %collective-permute-start.10 = (bf16[64,13440]{1,0:T(8,128)(2,1)S(1)}, bf16[64,13440]{1,0:T(8,128)(2,1)S(1)}, u32[]{:S(2)}, u32[]{:S(2)}) collective-permute-start(bf16[64,13440]{1,0:T(8,128)(2,1)S(1)} %get-tuple-element.27.refs_3_), channel_id=1, source_target_pairs={{0,4},{4,0},{8,12},{12,8},{1,5},{5,1},{9,13},{13,9},{2,6},{6,2},{1... | collective-permute-start | bytes 5160968 | tf_op jit(solution)/shard_map/ppermute | solution.py:261
  126.0 6.0 %shard_map.61.refs_4_.refs_3_ = f32[4,64,512]{2,1,0:T(8,128)S(1)} custom-call(s32[2]{0:T(128)S(1)} %pad_add_fusion.place_ref, bf16[64,13440]{1,0:T(8,128)(2,1)S(1)} %collective-permute-done.5.refs_0_.refs_2_, bf16[64,13440]{1,0:T(8,128)(2,1)S(1)} %copy-done.6, bf16[192,40000]{1,0:T(8,128)(2,1)S(1)} %bitcast.15, bf16[192,40000]{1,0:T(8,128)(2,1)S(1)} %bitcast.16, ...), custom_call_target="tpu_custom_call" | custom-call | flops 1000 | bytes 1000 | tf_op jit(solution)/shard_map/pallas_call | solution.py:236
  134.1 26.6 %collective-permute-start.12 = (bf16[64,9984]{1,0:T(8,128)(2,1)S(1)}, bf16[64,9984]{1,0:T(8,128)(2,1)S(1)}, u32[]{:S(2)}, u32[]{:S(2)}) collective-permute-start(bf16[64,9984]{1,0:T(8,128)(2,1)S(1)} %get-tuple-element.28.refs_3_), channel_id=1, source_target_pairs={{0,4},{4,0},{8,12},{12,8},{1,5},{5,1},{9,13},{13,9},{2,6},{6,2},{1... | collective-permute-start | bytes 3833864 | tf_op jit(solution)/shard_map/ppermute | solution.py:261
  162.8 3.9 %shard_map.64.refs_5_ = f32[4,64,512]{2,1,0:T(8,128)S(1)} custom-call(s32[2]{0:T(128)S(1)} %pad_add_fusion.place_ref, bf16[64,13440]{1,0:T(8,128)(2,1)S(1)} %collective-permute-done.9.refs_0_.refs_5_.refs_3_, bf16[64,13440]{1,0:T(8,128)(2,1)S(1)} %collective-permute-done.4.refs_1_.refs_6_, bf16[192,40000]{1,0:T(8,128)(2,1)S(1)} %bitcast.19, ...), custom_call_target="tpu_custom_call" | custom-call | flops 1000 | bytes 1000 | tf_op jit(solution)/shard_map/pallas_call | solution.py:236
  166.7 26.0 %collective-permute-done.10.refs_0_.refs_5_ = bf16[64,13440]{1,0:T(8,128)(2,1)S(1)} collective-permute-done((bf16[64,13440]{1,0:T(8,128)(2,1)S(1)}, bf16[64,13440]{1,0:T(8,128)(2,1)S(1)}, u32[]{:S(2)}, u32[]{:S(2)}) %collective-permute-start.10) | collective-permute-done | bytes 1720352 | tf_op jit(solution)/shard_map/ppermute | solution.py:261
  192.6 3.8 %shard_map.65.refs_7_ = f32[4,64,512]{2,1,0:T(8,128)S(1)} custom-call(s32[2]{0:T(128)S(1)} %pad_add_fusion.place_ref, bf16[64,13440]{1,0:T(8,128)(2,1)S(1)} %collective-permute-done.10.refs_0_.refs_5_, bf16[64,13440]{1,0:T(8,128)(2,1)S(1)} %collective-permute-done.11.refs_1_.refs_6_, bf16[192,40000]{1,0:T(8,128)(2,1)S(1)} %bitcast.21, ...), custom_call_target="tpu_custom_call" | custom-call | flops 1000 | bytes 1000 | tf_op jit(solution)/shard_map/pallas_call | solution.py:236
  196.5 23.5 %collective-permute-done.12.refs_0_ = bf16[64,9984]{1,0:T(8,128)(2,1)S(1)} collective-permute-done((bf16[64,9984]{1,0:T(8,128)(2,1)S(1)}, bf16[64,9984]{1,0:T(8,128)(2,1)S(1)}, u32[]{:S(2)}, u32[]{:S(2)}) %collective-permute-start.12) | collective-permute-done | bytes 1277984 | tf_op jit(solution)/shard_map/ppermute | solution.py:261
  220.0 3.1 %shard_map.66.refs_7_ = f32[4,64,512]{2,1,0:T(8,128)S(1)} custom-call(s32[2]{0:T(128)S(1)} %pad_add_fusion.place_ref, bf16[64,9984]{1,0:T(8,128)(2,1)S(1)} %collective-permute-done.12.refs_0_, bf16[64,9984]{1,0:T(8,128)(2,1)S(1)} %collective-permute-done.13.refs_1_, bf16[192,40000]{1,0:T(8,128)(2,1)S(1)} %bitcast.22, ...), custom_call_target="tpu_custom_call" | custom-call | flops 1000 | bytes 1000 | tf_op jit(solution)/shard_map/pallas_call | solution.py:236
  223.1 6.4 %collective-permute-done.7.refs_0_.refs_9_ = bf16[64,3456]{1,0:T(8,128)(2,1)S(1)} collective-permute-done((bf16[64,3456]{1,0:T(8,128)(2,1)S(1)}, bf16[64,3456]{1,0:T(8,128)(2,1)S(1)}, u32[]{:S(2)}, u32[]{:S(2)}) %collective-permute-start.7) | collective-permute-done | bytes 442400 | tf_op jit(solution)/shard_map/ppermute | solution.py:261
  234.6 3.4 %collective-permute-done.15 = f32[64,512]{1,0:T(8,128)S(1)} collective-permute-done((f32[64,512]{1,0:T(8,128)S(1)}, f32[64,512]{1,0:T(8,128)S(1)}, u32[]{:S(2)}, u32[]{:S(2)}) %collective-permute-start.15) | collective-permute-done | bytes 131104 | tf_op jit(solution)/shard_map/ppermute | solution.py:373
  238.0 3.0 %collective-permute-done.16 = f32[64,512]{1,0:T(8,128)S(1)} collective-permute-done((f32[64,512]{1,0:T(8,128)S(1)}, f32[64,512]{1,0:T(8,128)S(1)}, u32[]{:S(2)}, u32[]{:S(2)}) %collective-permute-start.16) | collective-permute-done | bytes 131104 | tf_op jit(solution)/shard_map/ppermute | solution.py:373
  241.2 4.2 %collective-permute-start.17 = (f32[64,512]{1,0:T(8,128)S(1)}, f32[64,512]{1,0:T(8,128)S(1)}, u32[]{:S(2)}, u32[]{:S(2)}) collective-permute-start(f32[64,512]{1,0:T(8,128)S(1)} %broadcast_select_fusion), channel_id=1, source_target_pairs={{0,0},{1,4},{2,8},{3,12},{4,1},{5,5},{6,9},{7,13},{8,2},{9,6},{10,... | collective-permute-start | bytes 393224 | tf_op jit(solution)/shard_map/ppermute | solution.py:379
  245.4 6.0 %collective-permute-done.17 = f32[64,512]{1,0:T(8,128)S(1)} collective-permute-done((f32[64,512]{1,0:T(8,128)S(1)}, f32[64,512]{1,0:T(8,128)S(1)}, u32[]{:S(2)}, u32[]{:S(2)}) %collective-permute-start.17) | collective-permute-done | bytes 131104 | tf_op jit(solution)/shard_map/ppermute | solution.py:379
  251.4 2.7 %collective-permute-start.18 = (f32[64,256]{1,0:T(8,128)S(1)}, f32[64,256]{1,0:T(8,128)S(1)}, u32[]{:S(2)}, u32[]{:S(2)}) collective-permute-start(f32[64,256]{1,0:T(8,128)S(1)} %get-tuple-element.42), channel_id=1, source_target_pairs={{0,1},{1,0},{2,3},{3,2},{4,5},{5,4},{6,7},{7,6},{8,9},{9,8},{10,11... | collective-permute-start | bytes 196616 | tf_op jit(solution)/shard_map/ppermute | solution.py:382
  (68 shorter events, 34.6 us)
Async XLA Ops:
  3.6 10.7 %copy-start.3 = (bf16[64,13440]{1,0:T(8,128)(2,1)}, bf16[64,13440]{1,0:T(8,128)(2,1)S(1)}, u32[]{:S(2)}) copy-start(bf16[64,13440]{1,0:T(8,128)(2,1)S(1)} %add_convert_fusion.token_ref.refs_3_) | copy-start | bytes 5160964
  3.6 14.0 %collective-permute-start.3 = (bf16[64,13440]{1,0:T(8,128)(2,1)S(1)}, bf16[64,13440]{1,0:T(8,128)(2,1)}, u32[]{:S(2)}, u32[]{:S(2)}) collective-permute-start(bf16[64,13440]{1,0:T(8,128)(2,1)S(1)} %add_convert_fusion.token_ref.refs_3_), channel_id=1, source_target_pairs={{4,8},{8,4},{5,9},{9,5},{6,10},{10,6},{7,11},{11,7},{20,24},{24,20... | collective-permute-start | bytes 5160968 | tf_op jit(solution)/shard_map/ppermute | solution.py:260
  5.6 39.7 %collective-permute-start.2 = (bf16[64,13440]{1,0:T(8,128)(2,1)S(1)}, bf16[64,13440]{1,0:T(8,128)(2,1)}, u32[]{:S(2)}, u32[]{:S(2)}) collective-permute-start(bf16[64,13440]{1,0:T(8,128)(2,1)S(1)} %add_convert_fusion.token_ref.refs_3_), channel_id=1, source_target_pairs={{0,4},{4,0},{8,12},{12,8},{1,5},{5,1},{9,13},{13,9},{2,6},{6,2},{1... | collective-permute-start | bytes 5160968 | tf_op jit(solution)/shard_map/ppermute | solution.py:261
  14.3 39.6 %collective-permute-start.1 = (bf16[64,13440]{1,0:T(8,128)(2,1)}, bf16[64,13440]{1,0:T(8,128)(2,1)}, u32[]{:S(2)}, u32[]{:S(2)}) collective-permute-start(bf16[64,13440]{1,0:T(8,128)(2,1)} %get-tuple-element.21.refs_3_.refs_6_), channel_id=1, source_target_pairs={{4,8},{8,4},{5,9},{9,5},{6,10},{10,6},{7,11},{11,7},{20,24},{24,20... | collective-permute-start | bytes 5160968 | tf_op jit(solution)/shard_map/ppermute | solution.py:260
  16.2 65.9 %collective-permute-start = (bf16[64,13440]{1,0:T(8,128)(2,1)}, bf16[64,13440]{1,0:T(8,128)(2,1)}, u32[]{:S(2)}, u32[]{:S(2)}) collective-permute-start(bf16[64,13440]{1,0:T(8,128)(2,1)} %get-tuple-element.21.refs_3_.refs_6_), channel_id=1, source_target_pairs={{0,4},{4,0},{8,12},{12,8},{1,5},{5,1},{9,13},{13,9},{2,6},{6,2},{1... | collective-permute-start | bytes 5160968 | tf_op jit(solution)/shard_map/ppermute | solution.py:261
  49.6 62.9 %collective-permute-start.6 = (bf16[64,13440]{1,0:T(8,128)(2,1)}, bf16[64,13440]{1,0:T(8,128)(2,1)S(1)}, u32[]{:S(2)}, u32[]{:S(2)}) collective-permute-start(bf16[64,13440]{1,0:T(8,128)(2,1)} %get-tuple-element.25), channel_id=1, source_target_pairs={{4,8},{8,4},{5,9},{9,5},{6,10},{10,6},{7,11},{11,7},{20,24},{24,20... | collective-permute-start | bytes 5160968 | tf_op jit(solution)/shard_map/ppermute | solution.py:260
  50.3 74.2 %collective-permute-start.5 = (bf16[64,13440]{1,0:T(8,128)(2,1)}, bf16[64,13440]{1,0:T(8,128)(2,1)S(1)}, u32[]{:S(2)}, u32[]{:S(2)}) collective-permute-start(bf16[64,13440]{1,0:T(8,128)(2,1)} %get-tuple-element.23.refs_3_), channel_id=1, source_target_pairs={{0,4},{4,0},{8,12},{12,8},{1,5},{5,1},{9,13},{13,9},{2,6},{6,2},{1... | collective-permute-start | bytes 5160968 | tf_op jit(solution)/shard_map/ppermute | solution.py:261
  87.5 6.7 %copy-start.4 = (bf16[64,13440]{1,0:T(8,128)(2,1)S(1)}, bf16[64,13440]{1,0:T(8,128)(2,1)}, u32[]{:S(2)}) copy-start(bf16[64,13440]{1,0:T(8,128)(2,1)} %copy-done.3) | copy-start | bytes 5160964
  91.9 40.1 %collective-permute-start.4 = (bf16[64,13440]{1,0:T(8,128)(2,1)S(1)}, bf16[64,13440]{1,0:T(8,128)(2,1)S(1)}, u32[]{:S(2)}, u32[]{:S(2)}) collective-permute-start(bf16[64,13440]{1,0:T(8,128)(2,1)S(1)} %get-tuple-element.24), channel_id=1, source_target_pairs={{4,8},{8,4},{5,9},{9,5},{6,10},{10,6},{7,11},{11,7},{20,24},{24,20... | collective-permute-start | bytes 5160968 | tf_op jit(solution)/shard_map/ppermute | solution.py:260
  100.3 61.7 %collective-permute-start.9 = (bf16[64,13440]{1,0:T(8,128)(2,1)}, bf16[64,13440]{1,0:T(8,128)(2,1)S(1)}, u32[]{:S(2)}, u32[]{:S(2)}) collective-permute-start(bf16[64,13440]{1,0:T(8,128)(2,1)} %get-tuple-element.26.refs_3_), channel_id=1, source_target_pairs={{0,4},{4,0},{8,12},{12,8},{1,5},{5,1},{9,13},{13,9},{2,6},{6,2},{1... | collective-permute-start | bytes 5160968 | tf_op jit(solution)/shard_map/ppermute | solution.py:261
  114.3 47.8 %collective-permute-start.11 = (bf16[64,13440]{1,0:T(8,128)(2,1)S(1)}, bf16[64,13440]{1,0:T(8,128)(2,1)S(1)}, u32[]{:S(2)}, u32[]{:S(2)}) collective-permute-start(bf16[64,13440]{1,0:T(8,128)(2,1)S(1)} %get-tuple-element.31), channel_id=1, source_target_pairs={{4,8},{8,4},{5,9},{9,5},{6,10},{10,6},{7,11},{11,7},{20,24},{24,20... | collective-permute-start | bytes 5160968 | tf_op jit(solution)/shard_map/ppermute | solution.py:260
  115.1 77.5 %collective-permute-start.10 = (bf16[64,13440]{1,0:T(8,128)(2,1)S(1)}, bf16[64,13440]{1,0:T(8,128)(2,1)S(1)}, u32[]{:S(2)}, u32[]{:S(2)}) collective-permute-start(bf16[64,13440]{1,0:T(8,128)(2,1)S(1)} %get-tuple-element.27.refs_3_), channel_id=1, source_target_pairs={{0,4},{4,0},{8,12},{12,8},{1,5},{5,1},{9,13},{13,9},{2,6},{6,2},{1... | collective-permute-start | bytes 5160968 | tf_op jit(solution)/shard_map/ppermute | solution.py:261
  133.4 63.1 %collective-permute-start.13 = (bf16[64,9984]{1,0:T(8,128)(2,1)S(1)}, bf16[64,9984]{1,0:T(8,128)(2,1)S(1)}, u32[]{:S(2)}, u32[]{:S(2)}) collective-permute-start(bf16[64,9984]{1,0:T(8,128)(2,1)S(1)} %get-tuple-element.32), channel_id=1, source_target_pairs={{4,8},{8,4},{5,9},{9,5},{6,10},{10,6},{7,11},{11,7},{20,24},{24,20... | collective-permute-start | bytes 3833864 | tf_op jit(solution)/shard_map/ppermute | solution.py:260
  134.1 85.9 %collective-permute-start.12 = (bf16[64,9984]{1,0:T(8,128)(2,1)S(1)}, bf16[64,9984]{1,0:T(8,128)(2,1)S(1)}, u32[]{:S(2)}, u32[]{:S(2)}) collective-permute-start(bf16[64,9984]{1,0:T(8,128)(2,1)S(1)} %get-tuple-element.28.refs_3_), channel_id=1, source_target_pairs={{0,4},{4,0},{8,12},{12,8},{1,5},{5,1},{9,13},{13,9},{2,6},{6,2},{1... | collective-permute-start | bytes 3833864 | tf_op jit(solution)/shard_map/ppermute | solution.py:261
  161.9 67.6 %collective-permute-start.7 = (bf16[64,3456]{1,0:T(8,128)(2,1)S(1)}, bf16[64,3456]{1,0:T(8,128)(2,1)S(1)}, u32[]{:S(2)}, u32[]{:S(2)}) collective-permute-start(bf16[64,3456]{1,0:T(8,128)(2,1)S(1)} %get-tuple-element.29), channel_id=1, source_target_pairs={{0,4},{4,0},{8,12},{12,8},{1,5},{5,1},{9,13},{13,9},{2,6},{6,2},{1... | collective-permute-start | bytes 1327112 | tf_op jit(solution)/shard_map/ppermute | solution.py:261
  162.1 67.4 %collective-permute-start.8 = (bf16[64,3456]{1,0:T(8,128)(2,1)S(1)}, bf16[64,3456]{1,0:T(8,128)(2,1)S(1)}, u32[]{:S(2)}, u32[]{:S(2)}) collective-permute-start(bf16[64,3456]{1,0:T(8,128)(2,1)S(1)} %get-tuple-element.30), channel_id=1, source_target_pairs={{4,8},{8,4},{5,9},{9,5},{6,10},{10,6},{7,11},{11,7},{20,24},{24,20... | collective-permute-start | bytes 1327112 | tf_op jit(solution)/shard_map/ppermute | solution.py:260
  196.5 33.0 %copy-start.7 = (f32[2,96]{1,0:T(2,128)S(1)}, f32[2,96]{1,0:T(2,128)}, u32[]{:S(2)}) copy-start(f32[2,96]{1,0:T(2,128)} %refs_11_.1) | copy-start | bytes 2308
  231.3 3.3 %collective-permute-start.14 = (f32[64,512]{1,0:T(8,128)S(1)}, f32[64,512]{1,0:T(8,128)S(1)}, u32[]{:S(2)}, u32[]{:S(2)}) collective-permute-start(f32[64,512]{1,0:T(8,128)S(1)} %get-tuple-element.34), channel_id=1, source_target_pairs={{0,1},{1,0},{2,3},{3,2},{4,5},{5,4},{6,7},{7,6},{8,9},{9,8},{10,11... | collective-permute-start | bytes 393224 | tf_op jit(solution)/shard_map/ppermute | solution.py:373
  232.9 5.1 %collective-permute-start.15 = (f32[64,512]{1,0:T(8,128)S(1)}, f32[64,512]{1,0:T(8,128)S(1)}, u32[]{:S(2)}, u32[]{:S(2)}) collective-permute-start(f32[64,512]{1,0:T(8,128)S(1)} %get-tuple-element.35), channel_id=1, source_target_pairs={{0,2},{1,3},{2,0},{3,1},{4,6},{5,7},{6,4},{7,5},{8,10},{9,11},{10,... | collective-permute-start | bytes 393224 | tf_op jit(solution)/shard_map/ppermute | solution.py:373
  233.2 7.8 %collective-permute-start.16 = (f32[64,512]{1,0:T(8,128)S(1)}, f32[64,512]{1,0:T(8,128)S(1)}, u32[]{:S(2)}, u32[]{:S(2)}) collective-permute-start(f32[64,512]{1,0:T(8,128)S(1)} %get-tuple-element.36), channel_id=1, source_target_pairs={{0,3},{1,2},{2,1},{3,0},{4,7},{5,6},{6,5},{7,4},{8,11},{9,10},{10,... | collective-permute-start | bytes 393224 | tf_op jit(solution)/shard_map/ppermute | solution.py:373
  241.2 10.2 %collective-permute-start.17 = (f32[64,512]{1,0:T(8,128)S(1)}, f32[64,512]{1,0:T(8,128)S(1)}, u32[]{:S(2)}, u32[]{:S(2)}) collective-permute-start(f32[64,512]{1,0:T(8,128)S(1)} %broadcast_select_fusion), channel_id=1, source_target_pairs={{0,0},{1,4},{2,8},{3,12},{4,1},{5,5},{6,9},{7,13},{8,2},{9,6},{10,... | collective-permute-start | bytes 393224 | tf_op jit(solution)/shard_map/ppermute | solution.py:379
  251.4 4.3 %collective-permute-start.18 = (f32[64,256]{1,0:T(8,128)S(1)}, f32[64,256]{1,0:T(8,128)S(1)}, u32[]{:S(2)}, u32[]{:S(2)}) collective-permute-start(f32[64,256]{1,0:T(8,128)S(1)} %get-tuple-element.42), channel_id=1, source_target_pairs={{0,1},{1,0},{2,3},{3,2},{4,5},{5,4},{6,7},{7,6},{8,9},{9,8},{10,11... | collective-permute-start | bytes 196616 | tf_op jit(solution)/shard_map/ppermute | solution.py:382
  254.3 3.0 %collective-permute-start.20 = (f32[64]{0:T(128)S(1)}, f32[64]{0:T(128)S(1)}, u32[]{:S(2)}, u32[]{:S(2)}) collective-permute-start(f32[64]{0:T(128)S(1)} %get-tuple-element.37), channel_id=1, source_target_pairs={{0,3},{1,2},{2,1},{3,0},{4,7},{5,6},{6,5},{7,4},{8,11},{9,10},{10,... | collective-permute-start | bytes 776 | tf_op jit(solution)/shard_map/ppermute | solution.py:382
  254.4 3.0 %collective-permute-start.19 = (f32[64]{0:T(128)S(1)}, f32[64]{0:T(128)S(1)}, u32[]{:S(2)}, u32[]{:S(2)}) collective-permute-start(f32[64]{0:T(128)S(1)} %get-tuple-element.37), channel_id=1, source_target_pairs={{0,2},{1,3},{2,0},{3,1},{4,6},{5,7},{6,4},{7,5},{8,10},{9,11},{10,... | collective-permute-start | bytes 776 | tf_op jit(solution)/shard_map/ppermute | solution.py:382
  (7 other events, 30.7 us)

commit v11 on v8

--- a/solution.py
+++ b/solution.py
@@ -200,11 +200,12 @@
             @pl.when(step == count - 1)
             def _():
                 weight = jnp.sum(profile_ref[...])
-                lane = lax.broadcasted_iota(jnp.int32, (frames, LANES), 1)
+                lane = lax.broadcasted_iota(jnp.int32, (frames, width), 1)
                 for turn, out in enumerate(outs):
-                    out[...] = acc[k ^ turn]
-                    middle = slice(LANES, 2 * LANES)
-                    out[:, middle] = jnp.where(lane == FREE - 1 - LANES, weight, acc[k ^ turn, :, middle])
+                    value = acc[k ^ turn]
+                    moved = pltpu.roll(value, width // 2 + nrows, axis=1)
+                    out[:frames, :] = jnp.where(lane < nrows, value, moved)[:, :2 * nrows]
+                    out[frames:, :] = jnp.full((8, 2 * nrows), weight, jnp.float32)
 
     def base(array):
         return 0 if array.shape[1] <= count * tile + rest_width else start
@@ -230,8 +231,9 @@
     else:
         in_specs.append(pl.BlockSpec(profile.shape, lambda i, s: (0, 0)))
         operands.append(profile)
-        out_shape = [jax.ShapeDtypeStruct(sums_shape[1:], jnp.float32)] * blocks
-        out_specs = [pl.BlockSpec(sums_shape[1:], lambda i, s: (0, 0))] * blocks
+        message = (frames + 8, 2 * nrows)
+        out_shape = [jax.ShapeDtypeStruct(message, jnp.float32)] * blocks
+        out_specs = [pl.BlockSpec(message, lambda i, s: (0, 0))] * blocks
         scratch = [pltpu.VMEM(sums_shape, jnp.float32)]
     return pl.pallas_call(
         kernel,
@@ -371,16 +373,20 @@
     for turn in range(1, owners):
         summed += lax.ppermute(messages[turn], SITES, [(i, i ^ turn) for i in range(owners)])
     half = WIDTH // 2
-    frame_sum = jnp.sum(summed[:, :nrows], axis=1) + jnp.sum(summed[:, half:half + nrows], axis=1)
-    lane = jnp.arange(half)
-    mine, extra = (jnp.where(lane[None, :] == FREE, frame_sum[:, None], x) for x in (summed[:, :half], summed[:, half:]))
+    weights, summed = summed[frames:frames + 1], summed[:frames]
+    frame_sum = jnp.sum(summed, axis=1)
+    lane = jnp.arange(half)[None, :]
+    skip = 2 * nrows - half
+    mine = jnp.where(lane == FREE - 1, weights[:, :half], summed[:, :half])
+    mine = jnp.where(lane == FREE, frame_sum[:, None], mine)
+    extra = jnp.where(lane == 0, frame_sum[:, None], summed[:, skip:])
     def flip(turn):
         return [(a * owners + b, b * owners + (a ^ turn)) for a in range(wide) for b in range(owners)]
 
     mine, extra = lax.ppermute(mine, ALL, flip(0)), lax.ppermute(extra, ALL, flip(1))
-    total = mine[:, FREE] + extra[:, FREE] + lax.ppermute(frame_sum, ALL, flip(2)) + lax.ppermute(frame_sum, ALL, flip(3))
+    total = mine[:, FREE] + extra[:, 0] + lax.ppermute(frame_sum, ALL, flip(2)) + lax.ppermute(frame_sum, ALL, flip(3))
     weight_sum = mine[:, FREE - 1]
-    charges = (mine + extra)[:, :nrows].reshape(frames, panels, rows).transpose(1, 2, 0)
+    charges = (mine[:, :nrows] + extra[:, nrows - skip:]).reshape(frames, panels, rows).transpose(1, 2, 0)
     return finish(charges, total, weight_sum, profile)
 
 

time: 256 us -> 255 us (level)
  no operation moved by 1% of the time
where the time goes in v11:
time: 255 us; the launch traced here: 252 us
  waiting for transfers between devices  109 us (43%)
  starting transfers between devices  79.1 us (31%)
  Pallas kernels  47.6 us (19%)
  local copies, waits for them, and re-layouts  11.7 us (5%)
  other arithmetic  4.11 us (2%)
    ppermute x7, waiting for transfers between devices, send(): lax.ppermute(pair[0], 'wide', outer)  101 us
    ppermute x7, starting transfers between devices, send(): lax.ppermute(pair[0], 'wide', outer)  57.8 us
    pallas_call x7, Pallas kernels, absorb(): pl.pallas_call(kernel, grid_spec=pltpu.PrefetchScalarGridSpec(num_scalar_...  31 us
    pallas_call x5, Pallas kernels, route(): pl.pallas_call(kernel, grid_spec=pltpu.PrefetchScalarGridSpec(num_scalar_...  13.1 us
    unnamed x20, local copies, waits for them, and re-layouts  10.7 us
    ppermute x7, starting transfers between devices, send(): lax.ppermute(pair[1], 'wide', inner)  7.57 us
    ppermute x3, waiting for transfers between devices, line_plan(): lax.ppermute(messages[turn], SITES, [(i, i ^ turn) for i in range(owners)])  5.45 us
    ppermute x1, starting transfers between devices, line_plan(): lax.ppermute(mine, ALL, flip(0))  5.32 us
  transfers between devices with their start and end apart: 21, of which 10 were waited for; matrix products, arithmetic and copies ran while one was open for 0% of the time, Pallas kernels for 18%

profile of v11, /device:TPU:3, one launch (start us, length us, event | category | flops | bytes accessed | tf_op | source)
XLA Modules:
  0.0 251.8 jit_solution(13911039864962429495)
XLA Ops:
  9.4 3.5 %shard_map.55 = (bf16[64,13440]{1,0:T(8,128)(2,1)}, bf16[64,13312]{1,0:T(8,128)(2,1)S(1)}) custom-call(bf16[64,40000]{1,0:T(8,128)(2,1)S(1)} %copy-done.2, s32[1,40000]{1,0:T(1,128)S(1)} %reshape.31.labels_b.labels_c.labels_rest, bf16[64,40000]{1,0:T(8,128)(2,1)S(1)} %copy-done.2, s32[1,40000]{1,0:T(1,128)S(1)} %reshape.31.labels_b.labels_c.labels_rest, ...), custom_call_target="tpu_custom_call" | custom-call | flops 1000 | bytes 1000 | tf_op jit(solution)/shard_map/pallas_call | solution.py:96
  13.0 2.6 %collective-permute-start.1 = (bf16[64,13440]{1,0:T(8,128)(2,1)}, bf16[64,13440]{1,0:T(8,128)(2,1)}, u32[]{:S(2)}, u32[]{:S(2)}) collective-permute-start(bf16[64,13440]{1,0:T(8,128)(2,1)} %get-tuple-element.21.refs_3_.refs_6_), channel_id=1, source_target_pairs={{0,4},{4,0},{8,12},{12,8},{1,5},{5,1},{9,13},{13,9},{2,6},{6,2},{1... | collective-permute-start | bytes 5160968 | tf_op jit(solution)/shard_map/ppermute | solution.py:262
  17.5 24.7 %collective-permute-done.3.refs_2_.refs_0_ = bf16[64,13440]{1,0:T(8,128)(2,1)} collective-permute-done((bf16[64,13440]{1,0:T(8,128)(2,1)S(1)}, bf16[64,13440]{1,0:T(8,128)(2,1)}, u32[]{:S(2)}, u32[]{:S(2)}) %collective-permute-start.3) | collective-permute-done | bytes 1720352 | tf_op jit(solution)/shard_map/ppermute | solution.py:262
  42.2 4.3 %shard_map.56 = (bf16[64,13440]{1,0:T(8,128)(2,1)}, bf16[64,13440]{1,0:T(8,128)(2,1)}) custom-call(s32[2]{0:T(128)S(1)} %pad_add_fusion.place_ref, bf16[64,13312]{1,0:T(8,128)(2,1)S(1)} %get-tuple-element.22.refs_0_.refs_2_.refs_4_, bf16[64,13440]{1,0:T(8,128)(2,1)} %collective-permute-done.2.refs_1_, bf16[64,13440]{1,0:T(8,128)(2,1)} %collective-permute-done.3.refs_2_.refs_0_), custom_call_target="tpu_custom_call" | custom-call | flops 1000 | bytes 1000 | tf_op jit(solution)/shard_map/pallas_call | solution.py:145
  47.3 7.7 %collective-permute-start.5 = (bf16[64,13440]{1,0:T(8,128)(2,1)}, bf16[64,13440]{1,0:T(8,128)(2,1)S(1)}, u32[]{:S(2)}, u32[]{:S(2)}) collective-permute-start(bf16[64,13440]{1,0:T(8,128)(2,1)} %get-tuple-element.23.refs_3_), channel_id=1, source_target_pairs={{0,4},{4,0},{8,12},{12,8},{1,5},{5,1},{9,13},{13,9},{2,6},{6,2},{1... | collective-permute-start | bytes 5160968 | tf_op jit(solution)/shard_map/ppermute | solution.py:262
  55.0 24.1 %collective-permute-done.1.refs_2_.refs_0_.refs_7_ = bf16[64,13440]{1,0:T(8,128)(2,1)} collective-permute-done((bf16[64,13440]{1,0:T(8,128)(2,1)}, bf16[64,13440]{1,0:T(8,128)(2,1)}, u32[]{:S(2)}, u32[]{:S(2)}) %collective-permute-start.1) | collective-permute-done | bytes 1720352 | tf_op jit(solution)/shard_map/ppermute | solution.py:262
  79.1 5.4 %copy-done = bf16[2,96,40000]{2,1,0:T(8,128)(2,1)S(1)} copy-done((bf16[2,96,40000]{2,1,0:T(8,128)(2,1)S(1)}, bf16[2,96,40000]{2,1,0:T(8,128)(2,1)}, u32[]{:S(2)}) %copy-start) | copy-done | bytes 15360024
  84.5 4.4 %shard_map.57 = (bf16[64,13440]{1,0:T(8,128)(2,1)}, bf16[64,13440]{1,0:T(8,128)(2,1)S(1)}) custom-call(s32[2]{0:T(128)S(1)} %pad_add_fusion.place_ref, bf16[192,40000]{1,0:T(8,128)(2,1)S(1)} %bitcast.11, bf16[64,13440]{1,0:T(8,128)(2,1)} %collective-permute-done.refs_1_.refs_8_, bf16[64,13440]{1,0:T(8,128)(2,1)} %collective-permute-done.1.refs_2_.refs_0_.refs_7_, ...), custom_call_target="tpu_custom_call" | custom-call | flops 1000 | bytes 1000 | tf_op jit(solution)/shard_map/pallas_call | solution.py:145
  91.2 6.0 %shard_map.58.refs_4_ = f32[4,64,512]{2,1,0:T(8,128)S(1)} custom-call(s32[2]{0:T(128)S(1)} %pad_add_fusion.place_ref, bf16[64,13440]{1,0:T(8,128)(2,1)} %collective-permute-done.3.refs_2_.refs_0_, bf16[64,13440]{1,0:T(8,128)(2,1)} %collective-permute-done.2.refs_1_, bf16[192,40000]{1,0:T(8,128)(2,1)S(1)} %bitcast.12, bf16[64,13440]{1,0:T(8,128)(2,1)S(1)} %copy-done.4), custom_call_target="tpu_custom_call" | custom-call | flops 1000 | bytes 1000 | tf_op jit(solution)/shard_map/pallas_call | solution.py:238
  97.2 9.9 %collective-permute-start.9 = (bf16[64,13440]{1,0:T(8,128)(2,1)}, bf16[64,13440]{1,0:T(8,128)(2,1)S(1)}, u32[]{:S(2)}, u32[]{:S(2)}) collective-permute-start(bf16[64,13440]{1,0:T(8,128)(2,1)} %get-tuple-element.26.refs_3_), channel_id=1, source_target_pairs={{0,4},{4,0},{8,12},{12,8},{1,5},{5,1},{9,13},{13,9},{2,6},{6,2},{1... | collective-permute-start | bytes 5160968 | tf_op jit(solution)/shard_map/ppermute | solution.py:262
  107.1 6.4 %shard_map.59.refs_4_.refs_5_ = f32[4,64,512]{2,1,0:T(8,128)S(1)} custom-call(s32[2]{0:T(128)S(1)} %pad_add_fusion.place_ref, bf16[64,13440]{1,0:T(8,128)(2,1)} %collective-permute-done.1.refs_2_.refs_0_.refs_7_, bf16[64,13440]{1,0:T(8,128)(2,1)} %collective-permute-done.refs_1_.refs_8_, bf16[192,40000]{1,0:T(8,128)(2,1)S(1)} %bitcast.13, ...), custom_call_target="tpu_custom_call" | custom-call | flops 1000 | bytes 1000 | tf_op jit(solution)/shard_map/pallas_call | solution.py:238
  116.1 9.5 %collective-permute-start.10 = (bf16[64,13440]{1,0:T(8,128)(2,1)S(1)}, bf16[64,13440]{1,0:T(8,128)(2,1)S(1)}, u32[]{:S(2)}, u32[]{:S(2)}) collective-permute-start(bf16[64,13440]{1,0:T(8,128)(2,1)S(1)} %get-tuple-element.27.refs_3_), channel_id=1, source_target_pairs={{0,4},{4,0},{8,12},{12,8},{1,5},{5,1},{9,13},{13,9},{2,6},{6,2},{1... | collective-permute-start | bytes 5160968 | tf_op jit(solution)/shard_map/ppermute | solution.py:262
  127.1 6.0 %shard_map.61.refs_4_.refs_3_ = f32[4,64,512]{2,1,0:T(8,128)S(1)} custom-call(s32[2]{0:T(128)S(1)} %pad_add_fusion.place_ref, bf16[64,13440]{1,0:T(8,128)(2,1)S(1)} %collective-permute-done.5.refs_0_.refs_2_, bf16[64,13440]{1,0:T(8,128)(2,1)S(1)} %copy-done.6, bf16[192,40000]{1,0:T(8,128)(2,1)S(1)} %bitcast.16, bf16[192,40000]{1,0:T(8,128)(2,1)S(1)} %bitcast.17, ...), custom_call_target="tpu_custom_call" | custom-call | flops 1000 | bytes 1000 | tf_op jit(solution)/shard_map/pallas_call | solution.py:238
  135.2 26.6 %collective-permute-start.12 = (bf16[64,9984]{1,0:T(8,128)(2,1)S(1)}, bf16[64,9984]{1,0:T(8,128)(2,1)S(1)}, u32[]{:S(2)}, u32[]{:S(2)}) collective-permute-start(bf16[64,9984]{1,0:T(8,128)(2,1)S(1)} %get-tuple-element.28.refs_3_), channel_id=1, source_target_pairs={{0,4},{4,0},{8,12},{12,8},{1,5},{5,1},{9,13},{13,9},{2,6},{6,2},{1... | collective-permute-start | bytes 3833864 | tf_op jit(solution)/shard_map/ppermute | solution.py:262
  163.9 3.9 %shard_map.64.refs_5_ = f32[4,64,512]{2,1,0:T(8,128)S(1)} custom-call(s32[2]{0:T(128)S(1)} %pad_add_fusion.place_ref, bf16[64,13440]{1,0:T(8,128)(2,1)S(1)} %collective-permute-done.9.refs_0_.refs_5_.refs_3_, bf16[64,13440]{1,0:T(8,128)(2,1)S(1)} %collective-permute-done.4.refs_1_.refs_6_, bf16[192,40000]{1,0:T(8,128)(2,1)S(1)} %bitcast.20, ...), custom_call_target="tpu_custom_call" | custom-call | flops 1000 | bytes 1000 | tf_op jit(solution)/shard_map/pallas_call | solution.py:238
  167.7 21.9 %collective-permute-done.10.refs_0_.refs_5_ = bf16[64,13440]{1,0:T(8,128)(2,1)S(1)} collective-permute-done((bf16[64,13440]{1,0:T(8,128)(2,1)S(1)}, bf16[64,13440]{1,0:T(8,128)(2,1)S(1)}, u32[]{:S(2)}, u32[]{:S(2)}) %collective-permute-start.10) | collective-permute-done | bytes 1720352 | tf_op jit(solution)/shard_map/ppermute | solution.py:262
  189.6 3.8 %shard_map.65.refs_7_ = f32[4,64,512]{2,1,0:T(8,128)S(1)} custom-call(s32[2]{0:T(128)S(1)} %pad_add_fusion.place_ref, bf16[64,13440]{1,0:T(8,128)(2,1)S(1)} %collective-permute-done.10.refs_0_.refs_5_, bf16[64,13440]{1,0:T(8,128)(2,1)S(1)} %collective-permute-done.11.refs_1_.refs_6_, bf16[192,40000]{1,0:T(8,128)(2,1)S(1)} %bitcast.22, ...), custom_call_target="tpu_custom_call" | custom-call | flops 1000 | bytes 1000 | tf_op jit(solution)/shard_map/pallas_call | solution.py:238
  193.4 23.5 %collective-permute-done.12.refs_0_ = bf16[64,9984]{1,0:T(8,128)(2,1)S(1)} collective-permute-done((bf16[64,9984]{1,0:T(8,128)(2,1)S(1)}, bf16[64,9984]{1,0:T(8,128)(2,1)S(1)}, u32[]{:S(2)}, u32[]{:S(2)}) %collective-permute-start.12) | collective-permute-done | bytes 1277984 | tf_op jit(solution)/shard_map/ppermute | solution.py:262
  217.0 3.1 %shard_map.66.refs_7_ = f32[4,64,512]{2,1,0:T(8,128)S(1)} custom-call(s32[2]{0:T(128)S(1)} %pad_add_fusion.place_ref, bf16[64,9984]{1,0:T(8,128)(2,1)S(1)} %collective-permute-done.12.refs_0_, bf16[64,9984]{1,0:T(8,128)(2,1)S(1)} %collective-permute-done.13.refs_1_, bf16[192,40000]{1,0:T(8,128)(2,1)S(1)} %bitcast.23, ...), custom_call_target="tpu_custom_call" | custom-call | flops 1000 | bytes 1000 | tf_op jit(solution)/shard_map/pallas_call | solution.py:238
  220.1 6.4 %collective-permute-done.7.refs_0_.refs_9_ = bf16[64,3456]{1,0:T(8,128)(2,1)S(1)} collective-permute-done((bf16[64,3456]{1,0:T(8,128)(2,1)S(1)}, bf16[64,3456]{1,0:T(8,128)(2,1)S(1)}, u32[]{:S(2)}, u32[]{:S(2)}) %collective-permute-start.7) | collective-permute-done | bytes 442400 | tf_op jit(solution)/shard_map/ppermute | solution.py:262
  231.6 2.9 %collective-permute-done.15 = f32[72,384]{1,0:T(8,128)S(1)} collective-permute-done((f32[72,384]{1,0:T(8,128)S(1)}, f32[72,384]{1,0:T(8,128)S(1)}, u32[]{:S(2)}, u32[]{:S(2)}) %collective-permute-start.15) | collective-permute-done | bytes 110624 | tf_op jit(solution)/shard_map/ppermute | solution.py:374
  234.6 2.5 %collective-permute-done.16 = f32[72,384]{1,0:T(8,128)S(1)} collective-permute-done((f32[72,384]{1,0:T(8,128)S(1)}, f32[72,384]{1,0:T(8,128)S(1)}, u32[]{:S(2)}, u32[]{:S(2)}) %collective-permute-start.16) | collective-permute-done | bytes 110624 | tf_op jit(solution)/shard_map/ppermute | solution.py:374
  237.3 5.3 %collective-permute-start.17 = (f32[64,256]{1,0:T(8,128)S(1)}, f32[64,256]{1,0:T(8,128)S(1)}, u32[]{:S(2)}, u32[]{:S(2)}) collective-permute-start(f32[64,256]{1,0:T(8,128)S(1)} %get-tuple-element.39), channel_id=1, source_target_pairs={{0,0},{1,4},{2,8},{3,12},{4,1},{5,5},{6,9},{7,13},{8,2},{9,6},{10,... | collective-permute-start | bytes 196616 | tf_op jit(solution)/shard_map/ppermute | solution.py:386
  242.6 4.5 %collective-permute-start.18 = (f32[64,256]{1,0:T(8,128)S(1)}, f32[64,256]{1,0:T(8,128)S(1)}, u32[]{:S(2)}, u32[]{:S(2)}) collective-permute-start(f32[64,256]{1,0:T(8,128)S(1)} %get-tuple-element.40), channel_id=1, source_target_pairs={{0,1},{1,5},{2,9},{3,13},{4,0},{5,4},{6,8},{7,12},{8,3},{9,7},{10,... | collective-permute-start | bytes 196616 | tf_op jit(solution)/shard_map/ppermute | solution.py:386
  (67 shorter events, 32.6 us)
Async XLA Ops:
  3.6 9.4 %copy-start.3 = (bf16[64,13440]{1,0:T(8,128)(2,1)}, bf16[64,13440]{1,0:T(8,128)(2,1)S(1)}, u32[]{:S(2)}) copy-start(bf16[64,13440]{1,0:T(8,128)(2,1)S(1)} %add_convert_fusion.token_ref.refs_3_) | copy-start | bytes 5160964
  3.6 38.6 %collective-permute-start.3 = (bf16[64,13440]{1,0:T(8,128)(2,1)S(1)}, bf16[64,13440]{1,0:T(8,128)(2,1)}, u32[]{:S(2)}, u32[]{:S(2)}) collective-permute-start(bf16[64,13440]{1,0:T(8,128)(2,1)S(1)} %add_convert_fusion.token_ref.refs_3_), channel_id=1, source_target_pairs={{0,4},{4,0},{8,12},{12,8},{1,5},{5,1},{9,13},{13,9},{2,6},{6,2},{1... | collective-permute-start | bytes 5160968 | tf_op jit(solution)/shard_map/ppermute | solution.py:262
  5.0 37.2 %collective-permute-start.2 = (bf16[64,13440]{1,0:T(8,128)(2,1)S(1)}, bf16[64,13440]{1,0:T(8,128)(2,1)}, u32[]{:S(2)}, u32[]{:S(2)}) collective-permute-start(bf16[64,13440]{1,0:T(8,128)(2,1)S(1)} %add_convert_fusion.token_ref.refs_3_), channel_id=1, source_target_pairs={{4,8},{8,4},{5,9},{9,5},{6,10},{10,6},{7,11},{11,7},{20,24},{24,20... | collective-permute-start | bytes 5160968 | tf_op jit(solution)/shard_map/ppermute | solution.py:262
  13.0 66.1 %collective-permute-start.1 = (bf16[64,13440]{1,0:T(8,128)(2,1)}, bf16[64,13440]{1,0:T(8,128)(2,1)}, u32[]{:S(2)}, u32[]{:S(2)}) collective-permute-start(bf16[64,13440]{1,0:T(8,128)(2,1)} %get-tuple-element.21.refs_3_.refs_6_), channel_id=1, source_target_pairs={{0,4},{4,0},{8,12},{12,8},{1,5},{5,1},{9,13},{13,9},{2,6},{6,2},{1... | collective-permute-start | bytes 5160968 | tf_op jit(solution)/shard_map/ppermute | solution.py:262
  15.6 63.5 %collective-permute-start = (bf16[64,13440]{1,0:T(8,128)(2,1)}, bf16[64,13440]{1,0:T(8,128)(2,1)}, u32[]{:S(2)}, u32[]{:S(2)}) collective-permute-start(bf16[64,13440]{1,0:T(8,128)(2,1)} %get-tuple-element.21.refs_3_.refs_6_), channel_id=1, source_target_pairs={{4,8},{8,4},{5,9},{9,5},{6,10},{10,6},{7,11},{11,7},{20,24},{24,20... | collective-permute-start | bytes 5160968 | tf_op jit(solution)/shard_map/ppermute | solution.py:262
  46.6 66.9 %collective-permute-start.6 = (bf16[64,13440]{1,0:T(8,128)(2,1)}, bf16[64,13440]{1,0:T(8,128)(2,1)S(1)}, u32[]{:S(2)}, u32[]{:S(2)}) collective-permute-start(bf16[64,13440]{1,0:T(8,128)(2,1)} %get-tuple-element.25), channel_id=1, source_target_pairs={{4,8},{8,4},{5,9},{9,5},{6,10},{10,6},{7,11},{11,7},{20,24},{24,20... | collective-permute-start | bytes 5160968 | tf_op jit(solution)/shard_map/ppermute | solution.py:262
  47.3 78.3 %collective-permute-start.5 = (bf16[64,13440]{1,0:T(8,128)(2,1)}, bf16[64,13440]{1,0:T(8,128)(2,1)S(1)}, u32[]{:S(2)}, u32[]{:S(2)}) collective-permute-start(bf16[64,13440]{1,0:T(8,128)(2,1)} %get-tuple-element.23.refs_3_), channel_id=1, source_target_pairs={{0,4},{4,0},{8,12},{12,8},{1,5},{5,1},{9,13},{13,9},{2,6},{6,2},{1... | collective-permute-start | bytes 5160968 | tf_op jit(solution)/shard_map/ppermute | solution.py:262
  84.5 6.7 %copy-start.4 = (bf16[64,13440]{1,0:T(8,128)(2,1)S(1)}, bf16[64,13440]{1,0:T(8,128)(2,1)}, u32[]{:S(2)}) copy-start(bf16[64,13440]{1,0:T(8,128)(2,1)} %copy-done.3) | copy-start | bytes 5160964
  88.9 44.2 %collective-permute-start.4 = (bf16[64,13440]{1,0:T(8,128)(2,1)S(1)}, bf16[64,13440]{1,0:T(8,128)(2,1)S(1)}, u32[]{:S(2)}, u32[]{:S(2)}) collective-permute-start(bf16[64,13440]{1,0:T(8,128)(2,1)S(1)} %get-tuple-element.24), channel_id=1, source_target_pairs={{4,8},{8,4},{5,9},{9,5},{6,10},{10,6},{7,11},{11,7},{20,24},{24,20... | collective-permute-start | bytes 5160968 | tf_op jit(solution)/shard_map/ppermute | solution.py:262
  97.2 65.7 %collective-permute-start.9 = (bf16[64,13440]{1,0:T(8,128)(2,1)}, bf16[64,13440]{1,0:T(8,128)(2,1)S(1)}, u32[]{:S(2)}, u32[]{:S(2)}) collective-permute-start(bf16[64,13440]{1,0:T(8,128)(2,1)} %get-tuple-element.26.refs_3_), channel_id=1, source_target_pairs={{0,4},{4,0},{8,12},{12,8},{1,5},{5,1},{9,13},{13,9},{2,6},{6,2},{1... | collective-permute-start | bytes 5160968 | tf_op jit(solution)/shard_map/ppermute | solution.py:262
  115.3 47.8 %collective-permute-start.11 = (bf16[64,13440]{1,0:T(8,128)(2,1)S(1)}, bf16[64,13440]{1,0:T(8,128)(2,1)S(1)}, u32[]{:S(2)}, u32[]{:S(2)}) collective-permute-start(bf16[64,13440]{1,0:T(8,128)(2,1)S(1)} %get-tuple-element.31), channel_id=1, source_target_pairs={{4,8},{8,4},{5,9},{9,5},{6,10},{10,6},{7,11},{11,7},{20,24},{24,20... | collective-permute-start | bytes 5160968 | tf_op jit(solution)/shard_map/ppermute | solution.py:262
  116.1 73.5 %collective-permute-start.10 = (bf16[64,13440]{1,0:T(8,128)(2,1)S(1)}, bf16[64,13440]{1,0:T(8,128)(2,1)S(1)}, u32[]{:S(2)}, u32[]{:S(2)}) collective-permute-start(bf16[64,13440]{1,0:T(8,128)(2,1)S(1)} %get-tuple-element.27.refs_3_), channel_id=1, source_target_pairs={{0,4},{4,0},{8,12},{12,8},{1,5},{5,1},{9,13},{13,9},{2,6},{6,2},{1... | collective-permute-start | bytes 5160968 | tf_op jit(solution)/shard_map/ppermute | solution.py:262
  134.4 59.0 %collective-permute-start.13 = (bf16[64,9984]{1,0:T(8,128)(2,1)S(1)}, bf16[64,9984]{1,0:T(8,128)(2,1)S(1)}, u32[]{:S(2)}, u32[]{:S(2)}) collective-permute-start(bf16[64,9984]{1,0:T(8,128)(2,1)S(1)} %get-tuple-element.32), channel_id=1, source_target_pairs={{4,8},{8,4},{5,9},{9,5},{6,10},{10,6},{7,11},{11,7},{20,24},{24,20... | collective-permute-start | bytes 3833864 | tf_op jit(solution)/shard_map/ppermute | solution.py:262
  135.2 81.8 %collective-permute-start.12 = (bf16[64,9984]{1,0:T(8,128)(2,1)S(1)}, bf16[64,9984]{1,0:T(8,128)(2,1)S(1)}, u32[]{:S(2)}, u32[]{:S(2)}) collective-permute-start(bf16[64,9984]{1,0:T(8,128)(2,1)S(1)} %get-tuple-element.28.refs_3_), channel_id=1, source_target_pairs={{0,4},{4,0},{8,12},{12,8},{1,5},{5,1},{9,13},{13,9},{2,6},{6,2},{1... | collective-permute-start | bytes 3833864 | tf_op jit(solution)/shard_map/ppermute | solution.py:262
  163.0 63.5 %collective-permute-start.7 = (bf16[64,3456]{1,0:T(8,128)(2,1)S(1)}, bf16[64,3456]{1,0:T(8,128)(2,1)S(1)}, u32[]{:S(2)}, u32[]{:S(2)}) collective-permute-start(bf16[64,3456]{1,0:T(8,128)(2,1)S(1)} %get-tuple-element.29), channel_id=1, source_target_pairs={{0,4},{4,0},{8,12},{12,8},{1,5},{5,1},{9,13},{13,9},{2,6},{6,2},{1... | collective-permute-start | bytes 1327112 | tf_op jit(solution)/shard_map/ppermute | solution.py:262
  163.2 63.3 %collective-permute-start.8 = (bf16[64,3456]{1,0:T(8,128)(2,1)S(1)}, bf16[64,3456]{1,0:T(8,128)(2,1)S(1)}, u32[]{:S(2)}, u32[]{:S(2)}) collective-permute-start(bf16[64,3456]{1,0:T(8,128)(2,1)S(1)} %get-tuple-element.30), channel_id=1, source_target_pairs={{4,8},{8,4},{5,9},{9,5},{6,10},{10,6},{7,11},{11,7},{20,24},{24,20... | collective-permute-start | bytes 1327112 | tf_op jit(solution)/shard_map/ppermute | solution.py:262
  193.4 33.0 %copy-start.7 = (f32[2,96]{1,0:T(2,128)S(1)}, f32[2,96]{1,0:T(2,128)}, u32[]{:S(2)}) copy-start(f32[2,96]{1,0:T(2,128)} %refs_11_.1) | copy-start | bytes 2308
  228.3 3.3 %collective-permute-start.14 = (f32[72,384]{1,0:T(8,128)S(1)}, f32[72,384]{1,0:T(8,128)S(1)}, u32[]{:S(2)}, u32[]{:S(2)}) collective-permute-start(f32[72,384]{1,0:T(8,128)S(1)} %get-tuple-element.34), channel_id=1, source_target_pairs={{0,1},{1,0},{2,3},{3,2},{4,5},{5,4},{6,7},{7,6},{8,9},{9,8},{10,11... | collective-permute-start | bytes 331784 | tf_op jit(solution)/shard_map/ppermute | solution.py:374
  229.9 4.6 %collective-permute-start.15 = (f32[72,384]{1,0:T(8,128)S(1)}, f32[72,384]{1,0:T(8,128)S(1)}, u32[]{:S(2)}, u32[]{:S(2)}) collective-permute-start(f32[72,384]{1,0:T(8,128)S(1)} %get-tuple-element.35), channel_id=1, source_target_pairs={{0,2},{1,3},{2,0},{3,1},{4,6},{5,7},{6,4},{7,5},{8,10},{9,11},{10,... | collective-permute-start | bytes 331784 | tf_op jit(solution)/shard_map/ppermute | solution.py:374
  230.0 7.1 %collective-permute-start.16 = (f32[72,384]{1,0:T(8,128)S(1)}, f32[72,384]{1,0:T(8,128)S(1)}, u32[]{:S(2)}, u32[]{:S(2)}) collective-permute-start(f32[72,384]{1,0:T(8,128)S(1)} %get-tuple-element.36), channel_id=1, source_target_pairs={{0,3},{1,2},{2,1},{3,0},{4,7},{5,6},{6,5},{7,4},{8,11},{9,10},{10,... | collective-permute-start | bytes 331784 | tf_op jit(solution)/shard_map/ppermute | solution.py:374
  237.3 10.4 %collective-permute-start.17 = (f32[64,256]{1,0:T(8,128)S(1)}, f32[64,256]{1,0:T(8,128)S(1)}, u32[]{:S(2)}, u32[]{:S(2)}) collective-permute-start(f32[64,256]{1,0:T(8,128)S(1)} %get-tuple-element.39), channel_id=1, source_target_pairs={{0,0},{1,4},{2,8},{3,12},{4,1},{5,5},{6,9},{7,13},{8,2},{9,6},{10,... | collective-permute-start | bytes 196616 | tf_op jit(solution)/shard_map/ppermute | solution.py:386
  242.6 7.0 %collective-permute-start.18 = (f32[64,256]{1,0:T(8,128)S(1)}, f32[64,256]{1,0:T(8,128)S(1)}, u32[]{:S(2)}, u32[]{:S(2)}) collective-permute-start(f32[64,256]{1,0:T(8,128)S(1)} %get-tuple-element.40), channel_id=1, source_target_pairs={{0,1},{1,5},{2,9},{3,13},{4,0},{5,4},{6,8},{7,12},{8,3},{9,7},{10,... | collective-permute-start | bytes 196616 | tf_op jit(solution)/shard_map/ppermute | solution.py:386
  247.2 3.0 %collective-permute-start.20 = (f32[64]{0:T(128)S(1)}, f32[64]{0:T(128)S(1)}, u32[]{:S(2)}, u32[]{:S(2)}) collective-permute-start(f32[64]{0:T(128)S(1)} %slice_reduce_fusion), channel_id=1, source_target_pairs={{0,3},{1,7},{2,11},{3,15},{4,2},{5,6},{6,10},{7,14},{8,1},{9,5},{1... | collective-permute-start | bytes 776 | tf_op jit(solution)/shard_map/ppermute | solution.py:387
  247.2 3.9 %collective-permute-start.19 = (f32[64]{0:T(128)S(1)}, f32[64]{0:T(128)S(1)}, u32[]{:S(2)}, u32[]{:S(2)}) collective-permute-start(f32[64]{0:T(128)S(1)} %slice_reduce_fusion), channel_id=1, source_target_pairs={{0,2},{1,6},{2,10},{3,14},{4,3},{5,7},{6,11},{7,15},{8,0},{9,4},{1... | collective-permute-start | bytes 776 | tf_op jit(solution)/shard_map/ppermute | solution.py:387
  (7 other events, 28.1 us)

commit v12 on v11

--- a/solution.py
+++ b/solution.py
@@ -259,7 +259,8 @@
     inner = [(1, 2), (2, 1)]
 
     def send(pair):
-        return lax.ppermute(pair[0], "wide", outer), lax.ppermute(pair[1], "wide", inner)
+        y = lax.ppermute(pair[1], "wide", inner)
+        return lax.ppermute(pair[0], "wide", outer), y
 
     def routed(sources, to_outer, to_inner, width, tokens, start=0):
         sources = [s if isinstance(s, tuple) else (s, 0, 0) for s in sources]
@@ -341,8 +342,8 @@
             add(z, 3 * LANES, both[:frames])
             add(3 - z, 3 * LANES, both[frames:])
 
-    r3, sent = routed([own_c, r1[1], r1[0]], (0, 1), 2, long, [])
-    r4, sent = routed([spare(0), r2[1], r2[0]], (0, 1), 2, long, [sent])
+    r3, sent = routed([own_c, r1[0], r1[1]], (0, 2), 1, long, [])
+    r4, sent = routed([spare(0), r2[0], r2[1]], (0, 2), 1, long, [sent])
     sums = absorb(
         place, third, dict(both("", r1), slab=(slab, always, at(0)), own=(own_a, always, at(0))), work1, sums_shape, None)
     sums = absorb(

time: 255 us -> 256 us (level)
  waiting for transfers between devices: 109 us -> 120 us
  starting transfers between devices: 79.1 us -> 69.9 us
    ppermute x14, waiting for transfers between devices: 101 us -> 112 us  [the longest x7 112 us: send(): return (lax.ppermute(pair[0], 'wide', outer), y)]
    ppermute x14, starting transfers between devices: 65.4 us -> 57.3 us  [the longest x7 49.7 us: send(): return (lax.ppermute(pair[0], 'wide', outer), y)]
  transfers between devices with their start and end apart: 21 -> 21, of which waited for: 10 -> 8; matrix products, arithmetic and copies ran while one was open for 0% -> 0% of each run, Pallas kernels for 18% -> 18%
where the time goes in v12:
time: 256 us; the launch traced here: 254 us
  waiting for transfers between devices  120 us (47%)
  starting transfers between devices  69.9 us (27%)
  Pallas kernels  47.6 us (19%)
  local copies, waits for them, and re-layouts  11.7 us (5%)
  other arithmetic  4.1 us (2%)
    ppermute x7, waiting for transfers between devices, send(): return (lax.ppermute(pair[0], 'wide', outer), y)  112 us
    ppermute x7, starting transfers between devices, send(): return (lax.ppermute(pair[0], 'wide', outer), y)  49.7 us
    pallas_call x7, Pallas kernels, absorb(): pl.pallas_call(kernel, grid_spec=pltpu.PrefetchScalarGridSpec(num_scalar_...  31 us
    pallas_call x5, Pallas kernels, route(): pl.pallas_call(kernel, grid_spec=pltpu.PrefetchScalarGridSpec(num_scalar_...  13.1 us
    unnamed x20, local copies, waits for them, and re-layouts  10.7 us
    ppermute x7, starting transfers between devices, send(): y = lax.ppermute(pair[1], 'wide', inner)  7.68 us
    ppermute x3, waiting for transfers between devices, line_plan(): lax.ppermute(messages[turn], SITES, [(i, i ^ turn) for i in range(owners)])  5.45 us
  transfers between devices with their start and end apart: 21, of which 8 were waited for; matrix products, arithmetic and copies ran while one was open for 0% of the time, Pallas kernels for 18%

profile of v12, /device:TPU:3, one launch (start us, length us, event | category | flops | bytes accessed | tf_op | source)
XLA Modules:
  0.0 253.7 jit_solution(7019548128520474190)
XLA Ops:
  5.6 2.6 %collective-permute-start.2 = (bf16[64,13440]{1,0:T(8,128)(2,1)S(1)}, bf16[64,13440]{1,0:T(8,128)(2,1)}, u32[]{:S(2)}, u32[]{:S(2)}) collective-permute-start(bf16[64,13440]{1,0:T(8,128)(2,1)S(1)} %add_convert_fusion.token_ref.refs_3_), channel_id=1, source_target_pairs={{0,4},{4,0},{8,12},{12,8},{1,5},{5,1},{9,13},{13,9},{2,6},{6,2},{1... | collective-permute-start | bytes 5160968 | tf_op jit(solution)/shard_map/ppermute | solution.py:263
  10.8 3.5 %shard_map.55 = (bf16[64,13440]{1,0:T(8,128)(2,1)}, bf16[64,13312]{1,0:T(8,128)(2,1)S(1)}) custom-call(bf16[64,40000]{1,0:T(8,128)(2,1)S(1)} %copy-done.2, s32[1,40000]{1,0:T(1,128)S(1)} %reshape.31.labels_b.labels_c.labels_rest, bf16[64,40000]{1,0:T(8,128)(2,1)S(1)} %copy-done.2, s32[1,40000]{1,0:T(1,128)S(1)} %reshape.31.labels_b.labels_c.labels_rest, ...), custom_call_target="tpu_custom_call" | custom-call | flops 1000 | bytes 1000 | tf_op jit(solution)/shard_map/pallas_call | solution.py:96
  17.6 27.6 %collective-permute-done.2.refs_1_.refs_0_ = bf16[64,13440]{1,0:T(8,128)(2,1)} collective-permute-done((bf16[64,13440]{1,0:T(8,128)(2,1)S(1)}, bf16[64,13440]{1,0:T(8,128)(2,1)}, u32[]{:S(2)}, u32[]{:S(2)}) %collective-permute-start.2) | collective-permute-done | bytes 1720352 | tf_op jit(solution)/shard_map/ppermute | solution.py:263
  45.3 4.3 %shard_map.56 = (bf16[64,13440]{1,0:T(8,128)(2,1)}, bf16[64,13440]{1,0:T(8,128)(2,1)}) custom-call(s32[2]{0:T(128)S(1)} %pad_add_fusion.place_ref, bf16[64,13312]{1,0:T(8,128)(2,1)S(1)} %get-tuple-element.22.refs_0_.refs_2_.refs_4_, bf16[64,13440]{1,0:T(8,128)(2,1)} %collective-permute-done.2.refs_1_.refs_0_, ...), custom_call_target="tpu_custom_call" | custom-call | flops 1000 | bytes 1000 | tf_op jit(solution)/shard_map/pallas_call | solution.py:145
  50.4 3.6 %collective-permute-start.5 = (bf16[64,13440]{1,0:T(8,128)(2,1)}, bf16[64,13440]{1,0:T(8,128)(2,1)S(1)}, u32[]{:S(2)}, u32[]{:S(2)}) collective-permute-start(bf16[64,13440]{1,0:T(8,128)(2,1)} %get-tuple-element.23.refs_3_), channel_id=1, source_target_pairs={{0,4},{4,0},{8,12},{12,8},{1,5},{5,1},{9,13},{13,9},{2,6},{6,2},{1... | collective-permute-start | bytes 5160968 | tf_op jit(solution)/shard_map/ppermute | solution.py:263
  54.0 28.2 %collective-permute-done.refs_1_.refs_0_.refs_7_ = bf16[64,13440]{1,0:T(8,128)(2,1)} collective-permute-done((bf16[64,13440]{1,0:T(8,128)(2,1)}, bf16[64,13440]{1,0:T(8,128)(2,1)}, u32[]{:S(2)}, u32[]{:S(2)}) %collective-permute-start) | collective-permute-done | bytes 1720352 | tf_op jit(solution)/shard_map/ppermute | solution.py:263
  82.1 5.4 %copy-done = bf16[2,96,40000]{2,1,0:T(8,128)(2,1)S(1)} copy-done((bf16[2,96,40000]{2,1,0:T(8,128)(2,1)S(1)}, bf16[2,96,40000]{2,1,0:T(8,128)(2,1)}, u32[]{:S(2)}) %copy-start) | copy-done | bytes 15360024
  87.5 4.4 %shard_map.57 = (bf16[64,13440]{1,0:T(8,128)(2,1)}, bf16[64,13440]{1,0:T(8,128)(2,1)S(1)}) custom-call(s32[2]{0:T(128)S(1)} %pad_add_fusion.place_ref, bf16[192,40000]{1,0:T(8,128)(2,1)S(1)} %bitcast.11, bf16[64,13440]{1,0:T(8,128)(2,1)} %collective-permute-done.refs_1_.refs_0_.refs_7_, bf16[64,13440]{1,0:T(8,128)(2,1)} %collective-permute-done.1.refs_2_.refs_1_.refs_8_, ...), custom_call_target="tpu_custom_call" | custom-call | flops 1000 | bytes 1000 | tf_op jit(solution)/shard_map/pallas_call | solution.py:145
  94.2 6.0 %shard_map.58.refs_4_ = f32[4,64,512]{2,1,0:T(8,128)S(1)} custom-call(s32[2]{0:T(128)S(1)} %pad_add_fusion.place_ref, bf16[64,13440]{1,0:T(8,128)(2,1)} %collective-permute-done.2.refs_1_.refs_0_, bf16[64,13440]{1,0:T(8,128)(2,1)} %collective-permute-done.3.refs_2_.refs_1_, bf16[192,40000]{1,0:T(8,128)(2,1)S(1)} %bitcast.12, bf16[64,13440]{1,0:T(8,128)(2,1)S(1)} %copy-done.4), custom_call_target="tpu_custom_call" | custom-call | flops 1000 | bytes 1000 | tf_op jit(solution)/shard_map/pallas_call | solution.py:238
  100.3 5.8 %collective-permute-start.9 = (bf16[64,13440]{1,0:T(8,128)(2,1)}, bf16[64,13440]{1,0:T(8,128)(2,1)S(1)}, u32[]{:S(2)}, u32[]{:S(2)}) collective-permute-start(bf16[64,13440]{1,0:T(8,128)(2,1)} %get-tuple-element.26.refs_3_), channel_id=1, source_target_pairs={{0,4},{4,0},{8,12},{12,8},{1,5},{5,1},{9,13},{13,9},{2,6},{6,2},{1... | collective-permute-start | bytes 5160968 | tf_op jit(solution)/shard_map/ppermute | solution.py:263
  106.1 6.4 %shard_map.59.refs_4_.refs_5_ = f32[4,64,512]{2,1,0:T(8,128)S(1)} custom-call(s32[2]{0:T(128)S(1)} %pad_add_fusion.place_ref, bf16[64,13440]{1,0:T(8,128)(2,1)} %collective-permute-done.refs_1_.refs_0_.refs_7_, bf16[64,13440]{1,0:T(8,128)(2,1)} %collective-permute-done.1.refs_2_.refs_1_.refs_8_, bf16[192,40000]{1,0:T(8,128)(2,1)S(1)} %bitcast.13, ...), custom_call_target="tpu_custom_call" | custom-call | flops 1000 | bytes 1000 | tf_op jit(solution)/shard_map/pallas_call | solution.py:238
  115.1 9.5 %collective-permute-start.10 = (bf16[64,13440]{1,0:T(8,128)(2,1)S(1)}, bf16[64,13440]{1,0:T(8,128)(2,1)S(1)}, u32[]{:S(2)}, u32[]{:S(2)}) collective-permute-start(bf16[64,13440]{1,0:T(8,128)(2,1)S(1)} %get-tuple-element.27.refs_3_), channel_id=1, source_target_pairs={{0,4},{4,0},{8,12},{12,8},{1,5},{5,1},{9,13},{13,9},{2,6},{6,2},{1... | collective-permute-start | bytes 5160968 | tf_op jit(solution)/shard_map/ppermute | solution.py:263
  126.0 6.0 %shard_map.61.refs_4_.refs_3_ = f32[4,64,512]{2,1,0:T(8,128)S(1)} custom-call(s32[2]{0:T(128)S(1)} %pad_add_fusion.place_ref, bf16[64,13440]{1,0:T(8,128)(2,1)S(1)} %collective-permute-done.5.refs_0_.refs_2_, bf16[64,13440]{1,0:T(8,128)(2,1)S(1)} %copy-done.6, bf16[192,40000]{1,0:T(8,128)(2,1)S(1)} %bitcast.16, bf16[192,40000]{1,0:T(8,128)(2,1)S(1)} %bitcast.17, ...), custom_call_target="tpu_custom_call" | custom-call | flops 1000 | bytes 1000 | tf_op jit(solution)/shard_map/pallas_call | solution.py:238
  134.1 26.6 %collective-permute-start.12 = (bf16[64,9984]{1,0:T(8,128)(2,1)S(1)}, bf16[64,9984]{1,0:T(8,128)(2,1)S(1)}, u32[]{:S(2)}, u32[]{:S(2)}) collective-permute-start(bf16[64,9984]{1,0:T(8,128)(2,1)S(1)} %get-tuple-element.28.refs_3_), channel_id=1, source_target_pairs={{0,4},{4,0},{8,12},{12,8},{1,5},{5,1},{9,13},{13,9},{2,6},{6,2},{1... | collective-permute-start | bytes 3833864 | tf_op jit(solution)/shard_map/ppermute | solution.py:263
  162.8 3.8 %shard_map.64.refs_5_ = f32[4,64,512]{2,1,0:T(8,128)S(1)} custom-call(s32[2]{0:T(128)S(1)} %pad_add_fusion.place_ref, bf16[64,13440]{1,0:T(8,128)(2,1)S(1)} %collective-permute-done.9.refs_0_.refs_5_.refs_3_, bf16[64,13440]{1,0:T(8,128)(2,1)S(1)} %collective-permute-done.4.refs_1_.refs_6_, bf16[192,40000]{1,0:T(8,128)(2,1)S(1)} %bitcast.20, ...), custom_call_target="tpu_custom_call" | custom-call | flops 1000 | bytes 1000 | tf_op jit(solution)/shard_map/pallas_call | solution.py:238
  166.7 25.9 %collective-permute-done.10.refs_0_.refs_5_ = bf16[64,13440]{1,0:T(8,128)(2,1)S(1)} collective-permute-done((bf16[64,13440]{1,0:T(8,128)(2,1)S(1)}, bf16[64,13440]{1,0:T(8,128)(2,1)S(1)}, u32[]{:S(2)}, u32[]{:S(2)}) %collective-permute-start.10) | collective-permute-done | bytes 1720352 | tf_op jit(solution)/shard_map/ppermute | solution.py:263
  192.6 3.8 %shard_map.65.refs_7_ = f32[4,64,512]{2,1,0:T(8,128)S(1)} custom-call(s32[2]{0:T(128)S(1)} %pad_add_fusion.place_ref, bf16[64,13440]{1,0:T(8,128)(2,1)S(1)} %collective-permute-done.10.refs_0_.refs_5_, bf16[64,13440]{1,0:T(8,128)(2,1)S(1)} %collective-permute-done.11.refs_1_.refs_6_, bf16[192,40000]{1,0:T(8,128)(2,1)S(1)} %bitcast.22, ...), custom_call_target="tpu_custom_call" | custom-call | flops 1000 | bytes 1000 | tf_op jit(solution)/shard_map/pallas_call | solution.py:238
  196.5 23.5 %collective-permute-done.12.refs_0_ = bf16[64,9984]{1,0:T(8,128)(2,1)S(1)} collective-permute-done((bf16[64,9984]{1,0:T(8,128)(2,1)S(1)}, bf16[64,9984]{1,0:T(8,128)(2,1)S(1)}, u32[]{:S(2)}, u32[]{:S(2)}) %collective-permute-start.12) | collective-permute-done | bytes 1277984 | tf_op jit(solution)/shard_map/ppermute | solution.py:263
  220.0 3.1 %shard_map.66.refs_7_ = f32[4,64,512]{2,1,0:T(8,128)S(1)} custom-call(s32[2]{0:T(128)S(1)} %pad_add_fusion.place_ref, bf16[64,9984]{1,0:T(8,128)(2,1)S(1)} %collective-permute-done.12.refs_0_, bf16[64,9984]{1,0:T(8,128)(2,1)S(1)} %collective-permute-done.13.refs_1_, bf16[192,40000]{1,0:T(8,128)(2,1)S(1)} %bitcast.23, ...), custom_call_target="tpu_custom_call" | custom-call | flops 1000 | bytes 1000 | tf_op jit(solution)/shard_map/pallas_call | solution.py:238
  223.1 6.4 %collective-permute-done.7.refs_0_.refs_9_ = bf16[64,3456]{1,0:T(8,128)(2,1)S(1)} collective-permute-done((bf16[64,3456]{1,0:T(8,128)(2,1)S(1)}, bf16[64,3456]{1,0:T(8,128)(2,1)S(1)}, u32[]{:S(2)}, u32[]{:S(2)}) %collective-permute-start.7) | collective-permute-done | bytes 442400 | tf_op jit(solution)/shard_map/ppermute | solution.py:263
  234.7 2.9 %collective-permute-done.15 = f32[72,384]{1,0:T(8,128)S(1)} collective-permute-done((f32[72,384]{1,0:T(8,128)S(1)}, f32[72,384]{1,0:T(8,128)S(1)}, u32[]{:S(2)}, u32[]{:S(2)}) %collective-permute-start.15) | collective-permute-done | bytes 110624 | tf_op jit(solution)/shard_map/ppermute | solution.py:375
  240.4 4.2 %collective-permute-start.17 = (f32[64,256]{1,0:T(8,128)S(1)}, f32[64,256]{1,0:T(8,128)S(1)}, u32[]{:S(2)}, u32[]{:S(2)}) collective-permute-start(f32[64,256]{1,0:T(8,128)S(1)} %get-tuple-element.39), channel_id=1, source_target_pairs={{0,0},{1,4},{2,8},{3,12},{4,1},{5,5},{6,9},{7,13},{8,2},{9,6},{10,... | collective-permute-start | bytes 196616 | tf_op jit(solution)/shard_map/ppermute | solution.py:387
  244.5 2.8 %collective-permute-start.18 = (f32[64,256]{1,0:T(8,128)S(1)}, f32[64,256]{1,0:T(8,128)S(1)}, u32[]{:S(2)}, u32[]{:S(2)}) collective-permute-start(f32[64,256]{1,0:T(8,128)S(1)} %get-tuple-element.40), channel_id=1, source_target_pairs={{0,1},{1,5},{2,9},{3,13},{4,0},{5,4},{6,8},{7,12},{8,3},{9,7},{10,... | collective-permute-start | bytes 196616 | tf_op jit(solution)/shard_map/ppermute | solution.py:387
  249.6 2.9 %collective-permute-done.18 = f32[64,256]{1,0:T(8,128)S(1)} collective-permute-done((f32[64,256]{1,0:T(8,128)S(1)}, f32[64,256]{1,0:T(8,128)S(1)}, u32[]{:S(2)}, u32[]{:S(2)}) %collective-permute-start.18) | collective-permute-done | bytes 65568 | tf_op jit(solution)/shard_map/ppermute | solution.py:387
  (67 shorter events, 34.0 us)
Async XLA Ops:
  3.6 10.7 %copy-start.3 = (bf16[64,13440]{1,0:T(8,128)(2,1)}, bf16[64,13440]{1,0:T(8,128)(2,1)S(1)}, u32[]{:S(2)}) copy-start(bf16[64,13440]{1,0:T(8,128)(2,1)S(1)} %add_convert_fusion.token_ref.refs_3_) | copy-start | bytes 5160964
  3.6 14.0 %collective-permute-start.3 = (bf16[64,13440]{1,0:T(8,128)(2,1)S(1)}, bf16[64,13440]{1,0:T(8,128)(2,1)}, u32[]{:S(2)}, u32[]{:S(2)}) collective-permute-start(bf16[64,13440]{1,0:T(8,128)(2,1)S(1)} %add_convert_fusion.token_ref.refs_3_), channel_id=1, source_target_pairs={{4,8},{8,4},{5,9},{9,5},{6,10},{10,6},{7,11},{11,7},{20,24},{24,20... | collective-permute-start | bytes 5160968 | tf_op jit(solution)/shard_map/ppermute | solution.py:262
  5.6 39.7 %collective-permute-start.2 = (bf16[64,13440]{1,0:T(8,128)(2,1)S(1)}, bf16[64,13440]{1,0:T(8,128)(2,1)}, u32[]{:S(2)}, u32[]{:S(2)}) collective-permute-start(bf16[64,13440]{1,0:T(8,128)(2,1)S(1)} %add_convert_fusion.token_ref.refs_3_), channel_id=1, source_target_pairs={{0,4},{4,0},{8,12},{12,8},{1,5},{5,1},{9,13},{13,9},{2,6},{6,2},{1... | collective-permute-start | bytes 5160968 | tf_op jit(solution)/shard_map/ppermute | solution.py:263
  14.3 39.6 %collective-permute-start.1 = (bf16[64,13440]{1,0:T(8,128)(2,1)}, bf16[64,13440]{1,0:T(8,128)(2,1)}, u32[]{:S(2)}, u32[]{:S(2)}) collective-permute-start(bf16[64,13440]{1,0:T(8,128)(2,1)} %get-tuple-element.21.refs_3_.refs_6_), channel_id=1, source_target_pairs={{4,8},{8,4},{5,9},{9,5},{6,10},{10,6},{7,11},{11,7},{20,24},{24,20... | collective-permute-start | bytes 5160968 | tf_op jit(solution)/shard_map/ppermute | solution.py:262
  16.2 65.9 %collective-permute-start = (bf16[64,13440]{1,0:T(8,128)(2,1)}, bf16[64,13440]{1,0:T(8,128)(2,1)}, u32[]{:S(2)}, u32[]{:S(2)}) collective-permute-start(bf16[64,13440]{1,0:T(8,128)(2,1)} %get-tuple-element.21.refs_3_.refs_6_), channel_id=1, source_target_pairs={{0,4},{4,0},{8,12},{12,8},{1,5},{5,1},{9,13},{13,9},{2,6},{6,2},{1... | collective-permute-start | bytes 5160968 | tf_op jit(solution)/shard_map/ppermute | solution.py:263
  49.6 62.8 %collective-permute-start.6 = (bf16[64,13440]{1,0:T(8,128)(2,1)}, bf16[64,13440]{1,0:T(8,128)(2,1)S(1)}, u32[]{:S(2)}, u32[]{:S(2)}) collective-permute-start(bf16[64,13440]{1,0:T(8,128)(2,1)} %get-tuple-element.25), channel_id=1, source_target_pairs={{4,8},{8,4},{5,9},{9,5},{6,10},{10,6},{7,11},{11,7},{20,24},{24,20... | collective-permute-start | bytes 5160968 | tf_op jit(solution)/shard_map/ppermute | solution.py:262
  50.4 74.2 %collective-permute-start.5 = (bf16[64,13440]{1,0:T(8,128)(2,1)}, bf16[64,13440]{1,0:T(8,128)(2,1)S(1)}, u32[]{:S(2)}, u32[]{:S(2)}) collective-permute-start(bf16[64,13440]{1,0:T(8,128)(2,1)} %get-tuple-element.23.refs_3_), channel_id=1, source_target_pairs={{0,4},{4,0},{8,12},{12,8},{1,5},{5,1},{9,13},{13,9},{2,6},{6,2},{1... | collective-permute-start | bytes 5160968 | tf_op jit(solution)/shard_map/ppermute | solution.py:263
  87.5 6.7 %copy-start.4 = (bf16[64,13440]{1,0:T(8,128)(2,1)S(1)}, bf16[64,13440]{1,0:T(8,128)(2,1)}, u32[]{:S(2)}) copy-start(bf16[64,13440]{1,0:T(8,128)(2,1)} %copy-done.3) | copy-start | bytes 5160964
  91.9 40.1 %collective-permute-start.4 = (bf16[64,13440]{1,0:T(8,128)(2,1)S(1)}, bf16[64,13440]{1,0:T(8,128)(2,1)S(1)}, u32[]{:S(2)}, u32[]{:S(2)}) collective-permute-start(bf16[64,13440]{1,0:T(8,128)(2,1)S(1)} %get-tuple-element.24), channel_id=1, source_target_pairs={{4,8},{8,4},{5,9},{9,5},{6,10},{10,6},{7,11},{11,7},{20,24},{24,20... | collective-permute-start | bytes 5160968 | tf_op jit(solution)/shard_map/ppermute | solution.py:262
  100.3 61.7 %collective-permute-start.9 = (bf16[64,13440]{1,0:T(8,128)(2,1)}, bf16[64,13440]{1,0:T(8,128)(2,1)S(1)}, u32[]{:S(2)}, u32[]{:S(2)}) collective-permute-start(bf16[64,13440]{1,0:T(8,128)(2,1)} %get-tuple-element.26.refs_3_), channel_id=1, source_target_pairs={{0,4},{4,0},{8,12},{12,8},{1,5},{5,1},{9,13},{13,9},{2,6},{6,2},{1... | collective-permute-start | bytes 5160968 | tf_op jit(solution)/shard_map/ppermute | solution.py:263
  114.3 47.8 %collective-permute-start.11 = (bf16[64,13440]{1,0:T(8,128)(2,1)S(1)}, bf16[64,13440]{1,0:T(8,128)(2,1)S(1)}, u32[]{:S(2)}, u32[]{:S(2)}) collective-permute-start(bf16[64,13440]{1,0:T(8,128)(2,1)S(1)} %get-tuple-element.31), channel_id=1, source_target_pairs={{4,8},{8,4},{5,9},{9,5},{6,10},{10,6},{7,11},{11,7},{20,24},{24,20... | collective-permute-start | bytes 5160968 | tf_op jit(solution)/shard_map/ppermute | solution.py:262
  115.1 77.5 %collective-permute-start.10 = (bf16[64,13440]{1,0:T(8,128)(2,1)S(1)}, bf16[64,13440]{1,0:T(8,128)(2,1)S(1)}, u32[]{:S(2)}, u32[]{:S(2)}) collective-permute-start(bf16[64,13440]{1,0:T(8,128)(2,1)S(1)} %get-tuple-element.27.refs_3_), channel_id=1, source_target_pairs={{0,4},{4,0},{8,12},{12,8},{1,5},{5,1},{9,13},{13,9},{2,6},{6,2},{1... | collective-permute-start | bytes 5160968 | tf_op jit(solution)/shard_map/ppermute | solution.py:263
  133.4 63.1 %collective-permute-start.13 = (bf16[64,9984]{1,0:T(8,128)(2,1)S(1)}, bf16[64,9984]{1,0:T(8,128)(2,1)S(1)}, u32[]{:S(2)}, u32[]{:S(2)}) collective-permute-start(bf16[64,9984]{1,0:T(8,128)(2,1)S(1)} %get-tuple-element.32), channel_id=1, source_target_pairs={{4,8},{8,4},{5,9},{9,5},{6,10},{10,6},{7,11},{11,7},{20,24},{24,20... | collective-permute-start | bytes 3833864 | tf_op jit(solution)/shard_map/ppermute | solution.py:262
  134.1 85.9 %collective-permute-start.12 = (bf16[64,9984]{1,0:T(8,128)(2,1)S(1)}, bf16[64,9984]{1,0:T(8,128)(2,1)S(1)}, u32[]{:S(2)}, u32[]{:S(2)}) collective-permute-start(bf16[64,9984]{1,0:T(8,128)(2,1)S(1)} %get-tuple-element.28.refs_3_), channel_id=1, source_target_pairs={{0,4},{4,0},{8,12},{12,8},{1,5},{5,1},{9,13},{13,9},{2,6},{6,2},{1... | collective-permute-start | bytes 3833864 | tf_op jit(solution)/shard_map/ppermute | solution.py:263
  161.9 67.6 %collective-permute-start.7 = (bf16[64,3456]{1,0:T(8,128)(2,1)S(1)}, bf16[64,3456]{1,0:T(8,128)(2,1)S(1)}, u32[]{:S(2)}, u32[]{:S(2)}) collective-permute-start(bf16[64,3456]{1,0:T(8,128)(2,1)S(1)} %get-tuple-element.29), channel_id=1, source_target_pairs={{0,4},{4,0},{8,12},{12,8},{1,5},{5,1},{9,13},{13,9},{2,6},{6,2},{1... | collective-permute-start | bytes 1327112 | tf_op jit(solution)/shard_map/ppermute | solution.py:263
  162.1 67.4 %collective-permute-start.8 = (bf16[64,3456]{1,0:T(8,128)(2,1)S(1)}, bf16[64,3456]{1,0:T(8,128)(2,1)S(1)}, u32[]{:S(2)}, u32[]{:S(2)}) collective-permute-start(bf16[64,3456]{1,0:T(8,128)(2,1)S(1)} %get-tuple-element.30), channel_id=1, source_target_pairs={{4,8},{8,4},{5,9},{9,5},{6,10},{10,6},{7,11},{11,7},{20,24},{24,20... | collective-permute-start | bytes 1327112 | tf_op jit(solution)/shard_map/ppermute | solution.py:262
  196.5 33.0 %copy-start.7 = (f32[2,96]{1,0:T(2,128)S(1)}, f32[2,96]{1,0:T(2,128)}, u32[]{:S(2)}) copy-start(f32[2,96]{1,0:T(2,128)} %refs_11_.1) | copy-start | bytes 2308
  231.4 3.3 %collective-permute-start.14 = (f32[72,384]{1,0:T(8,128)S(1)}, f32[72,384]{1,0:T(8,128)S(1)}, u32[]{:S(2)}, u32[]{:S(2)}) collective-permute-start(f32[72,384]{1,0:T(8,128)S(1)} %get-tuple-element.34), channel_id=1, source_target_pairs={{0,1},{1,0},{2,3},{3,2},{4,5},{5,4},{6,7},{7,6},{8,9},{9,8},{10,11... | collective-permute-start | bytes 331784 | tf_op jit(solution)/shard_map/ppermute | solution.py:375
  233.0 4.6 %collective-permute-start.15 = (f32[72,384]{1,0:T(8,128)S(1)}, f32[72,384]{1,0:T(8,128)S(1)}, u32[]{:S(2)}, u32[]{:S(2)}) collective-permute-start(f32[72,384]{1,0:T(8,128)S(1)} %get-tuple-element.35), channel_id=1, source_target_pairs={{0,2},{1,3},{2,0},{3,1},{4,6},{5,7},{6,4},{7,5},{8,10},{9,11},{10,... | collective-permute-start | bytes 331784 | tf_op jit(solution)/shard_map/ppermute | solution.py:375
  233.2 6.9 %collective-permute-start.16 = (f32[72,384]{1,0:T(8,128)S(1)}, f32[72,384]{1,0:T(8,128)S(1)}, u32[]{:S(2)}, u32[]{:S(2)}) collective-permute-start(f32[72,384]{1,0:T(8,128)S(1)} %get-tuple-element.36), channel_id=1, source_target_pairs={{0,3},{1,2},{2,1},{3,0},{4,7},{5,6},{6,5},{7,4},{8,11},{9,10},{10,... | collective-permute-start | bytes 331784 | tf_op jit(solution)/shard_map/ppermute | solution.py:375
  240.4 9.2 %collective-permute-start.17 = (f32[64,256]{1,0:T(8,128)S(1)}, f32[64,256]{1,0:T(8,128)S(1)}, u32[]{:S(2)}, u32[]{:S(2)}) collective-permute-start(f32[64,256]{1,0:T(8,128)S(1)} %get-tuple-element.39), channel_id=1, source_target_pairs={{0,0},{1,4},{2,8},{3,12},{4,1},{5,5},{6,9},{7,13},{8,2},{9,6},{10,... | collective-permute-start | bytes 196616 | tf_op jit(solution)/shard_map/ppermute | solution.py:387
  244.5 8.0 %collective-permute-start.18 = (f32[64,256]{1,0:T(8,128)S(1)}, f32[64,256]{1,0:T(8,128)S(1)}, u32[]{:S(2)}, u32[]{:S(2)}) collective-permute-start(f32[64,256]{1,0:T(8,128)S(1)} %get-tuple-element.40), channel_id=1, source_target_pairs={{0,1},{1,5},{2,9},{3,13},{4,0},{5,4},{6,8},{7,12},{8,3},{9,7},{10,... | collective-permute-start | bytes 196616 | tf_op jit(solution)/shard_map/ppermute | solution.py:387
  247.4 5.6 %collective-permute-start.20 = (f32[64]{0:T(128)S(1)}, f32[64]{0:T(128)S(1)}, u32[]{:S(2)}, u32[]{:S(2)}) collective-permute-start(f32[64]{0:T(128)S(1)} %slice_reduce_fusion), channel_id=1, source_target_pairs={{0,3},{1,7},{2,11},{3,15},{4,2},{5,6},{6,10},{7,14},{8,1},{9,5},{1... | collective-permute-start | bytes 776 | tf_op jit(solution)/shard_map/ppermute | solution.py:388
  247.4 5.6 %collective-permute-start.19 = (f32[64]{0:T(128)S(1)}, f32[64]{0:T(128)S(1)}, u32[]{:S(2)}, u32[]{:S(2)}) collective-permute-start(f32[64]{0:T(128)S(1)} %slice_reduce_fusion), channel_id=1, source_target_pairs={{0,2},{1,6},{2,10},{3,14},{4,3},{5,7},{6,11},{7,15},{8,0},{9,4},{1... | collective-permute-start | bytes 776 | tf_op jit(solution)/shard_map/ppermute | solution.py:388
  (7 other events, 30.7 us)

commit v13 on v11

--- a/solution.py
+++ b/solution.py
@@ -37,7 +37,7 @@
 
 
 LANES = 128
-STEPS = 4
+STEPS = 8
 ROWS = 64
 WIDTH = 4 * LANES
 FREE = LANES * 2 - 1

time: 255 us -> 261 us (1.024)
  Pallas kernels: 47.6 us -> 62.3 us
  waiting for transfers between devices: 109 us -> 98.9 us
    ppermute x7, waiting for transfers between devices: 101 us -> 90.1 us  [send(): lax.ppermute(pair[0], 'wide', outer)]
    pallas_call x7, Pallas kernels: 31 us -> 39.9 us  [absorb(): pl.pallas_call(kernel, grid_spec=pltpu.PrefetchScalarGridSpec(num_scalar_...]
    pallas_call x5, Pallas kernels: 13.1 us -> 18.3 us  [route(): pl.pallas_call(kernel, grid_spec=pltpu.PrefetchScalarGridSpec(num_scalar_...]
    ppermute x1, starting transfers between devices: 4.52 us -> 9.12 us  [line_plan(): lax.ppermute(extra, ALL, flip(1))]
    ppermute x7, starting transfers between devices: 57.8 us -> 54.8 us  [send(): lax.ppermute(pair[0], 'wide', outer)]
    unnamed x20 -> x16, local copies, waits for them, and re-layouts: 10.7 us -> 9.31 us
  transfers between devices with their start and end apart: 21 -> 21, of which waited for: 10 -> 9; matrix products, arithmetic and copies ran while one was open for 0% -> 0% of each run, Pallas kernels for 18% -> 24%
where the time goes in v13:
time: 261 us; the launch traced here: 257 us
  waiting for transfers between devices  98.9 us (38%)
  starting transfers between devices  80.9 us (31%)
  Pallas kernels  62.3 us (24%)
  local copies, waits for them, and re-layouts  10.3 us (4%)
  other arithmetic  4.11 us (2%)
    ppermute x7, waiting for transfers between devices, send(): lax.ppermute(pair[0], 'wide', outer)  90.1 us
    ppermute x7, starting transfers between devices, send(): lax.ppermute(pair[0], 'wide', outer)  54.8 us
    pallas_call x7, Pallas kernels, absorb(): pl.pallas_call(kernel, grid_spec=pltpu.PrefetchScalarGridSpec(num_scalar_...  39.9 us
    pallas_call x5, Pallas kernels, route(): pl.pallas_call(kernel, grid_spec=pltpu.PrefetchScalarGridSpec(num_scalar_...  18.3 us
    unnamed x16, local copies, waits for them, and re-layouts  9.31 us
    ppermute x1, starting transfers between devices, line_plan(): lax.ppermute(extra, ALL, flip(1))  9.12 us
    ppermute x7, starting transfers between devices, send(): lax.ppermute(pair[1], 'wide', inner)  7.45 us
    ppermute x3, waiting for transfers between devices, line_plan(): lax.ppermute(messages[turn], SITES, [(i, i ^ turn) for i in range(owners)])  5.45 us
  transfers between devices with their start and end apart: 21, of which 9 were waited for; matrix products, arithmetic and copies ran while one was open for 0% of the time, Pallas kernels for 24%

profile of v13, /device:TPU:3, one launch (start us, length us, event | category | flops | bytes accessed | tf_op | source)
XLA Modules:
  0.0 256.8 jit_solution(6661161026312319467)
XLA Ops:
  9.4 4.2 %shard_map.55 = (bf16[64,13440]{1,0:T(8,128)(2,1)}, bf16[64,13312]{1,0:T(8,128)(2,1)S(1)}) custom-call(bf16[64,40000]{1,0:T(8,128)(2,1)S(1)} %copy-done.2, s32[1,40000]{1,0:T(1,128)S(1)} %reshape.31.labels_b.labels_c.labels_rest, bf16[64,40000]{1,0:T(8,128)(2,1)S(1)} %copy-done.2, s32[1,40000]{1,0:T(1,128)S(1)} %reshape.31.labels_b.labels_c.labels_rest, ...), custom_call_target="tpu_custom_call" | custom-call | flops 1000 | bytes 1000 | tf_op jit(solution)/shard_map/pallas_call | solution.py:96
  13.6 2.6 %collective-permute-start.1 = (bf16[64,13440]{1,0:T(8,128)(2,1)}, bf16[64,13440]{1,0:T(8,128)(2,1)}, u32[]{:S(2)}, u32[]{:S(2)}) collective-permute-start(bf16[64,13440]{1,0:T(8,128)(2,1)} %get-tuple-element.21.refs_3_.refs_6_), channel_id=1, source_target_pairs={{0,4},{4,0},{8,12},{12,8},{1,5},{5,1},{9,13},{13,9},{2,6},{6,2},{1... | collective-permute-start | bytes 5160968 | tf_op jit(solution)/shard_map/ppermute | solution.py:262
  18.1 24.1 %collective-permute-done.3.refs_2_.refs_0_ = bf16[64,13440]{1,0:T(8,128)(2,1)} collective-permute-done((bf16[64,13440]{1,0:T(8,128)(2,1)S(1)}, bf16[64,13440]{1,0:T(8,128)(2,1)}, u32[]{:S(2)}, u32[]{:S(2)}) %collective-permute-start.3) | collective-permute-done | bytes 1720352 | tf_op jit(solution)/shard_map/ppermute | solution.py:262
  42.2 5.4 %shard_map.56 = (bf16[64,13440]{1,0:T(8,128)(2,1)}, bf16[64,13440]{1,0:T(8,128)(2,1)}) custom-call(s32[2]{0:T(128)S(1)} %pad_add_fusion.place_ref, bf16[64,13312]{1,0:T(8,128)(2,1)S(1)} %get-tuple-element.22.refs_0_.refs_2_.refs_4_, bf16[64,13440]{1,0:T(8,128)(2,1)} %collective-permute-done.2.refs_1_, bf16[64,13440]{1,0:T(8,128)(2,1)} %collective-permute-done.3.refs_2_.refs_0_), custom_call_target="tpu_custom_call" | custom-call | flops 1000 | bytes 1000 | tf_op jit(solution)/shard_map/pallas_call | solution.py:145
  48.4 8.5 %collective-permute-start.5 = (bf16[64,13440]{1,0:T(8,128)(2,1)}, bf16[64,13440]{1,0:T(8,128)(2,1)}, u32[]{:S(2)}, u32[]{:S(2)}) collective-permute-start(bf16[64,13440]{1,0:T(8,128)(2,1)} %get-tuple-element.23.refs_3_), channel_id=1, source_target_pairs={{0,4},{4,0},{8,12},{12,8},{1,5},{5,1},{9,13},{13,9},{2,6},{6,2},{1... | collective-permute-start | bytes 5160968 | tf_op jit(solution)/shard_map/ppermute | solution.py:262
  56.9 22.2 %collective-permute-done.1.refs_2_.refs_0_.refs_7_ = bf16[64,13440]{1,0:T(8,128)(2,1)} collective-permute-done((bf16[64,13440]{1,0:T(8,128)(2,1)}, bf16[64,13440]{1,0:T(8,128)(2,1)}, u32[]{:S(2)}, u32[]{:S(2)}) %collective-permute-start.1) | collective-permute-done | bytes 1720352 | tf_op jit(solution)/shard_map/ppermute | solution.py:262
  79.1 5.4 %copy-done = bf16[2,96,40000]{2,1,0:T(8,128)(2,1)S(1)} copy-done((bf16[2,96,40000]{2,1,0:T(8,128)(2,1)S(1)}, bf16[2,96,40000]{2,1,0:T(8,128)(2,1)}, u32[]{:S(2)}) %copy-start) | copy-done | bytes 15360024
  84.4 5.7 %shard_map.57 = (bf16[64,13440]{1,0:T(8,128)(2,1)}, bf16[64,13440]{1,0:T(8,128)(2,1)S(1)}) custom-call(s32[2]{0:T(128)S(1)} %pad_add_fusion.place_ref, bf16[192,40000]{1,0:T(8,128)(2,1)S(1)} %bitcast.11, bf16[64,13440]{1,0:T(8,128)(2,1)} %collective-permute-done.refs_1_.refs_8_, bf16[64,13440]{1,0:T(8,128)(2,1)} %collective-permute-done.1.refs_2_.refs_0_.refs_7_, ...), custom_call_target="tpu_custom_call" | custom-call | flops 1000 | bytes 1000 | tf_op jit(solution)/shard_map/pallas_call | solution.py:145
  90.9 7.6 %shard_map.58.refs_4_ = f32[4,64,512]{2,1,0:T(8,128)S(1)} custom-call(s32[2]{0:T(128)S(1)} %pad_add_fusion.place_ref, bf16[64,13440]{1,0:T(8,128)(2,1)} %collective-permute-done.3.refs_2_.refs_0_, bf16[64,13440]{1,0:T(8,128)(2,1)} %collective-permute-done.2.refs_1_, bf16[192,40000]{1,0:T(8,128)(2,1)S(1)} %bitcast.12, ...), custom_call_target="tpu_custom_call" | custom-call | flops 1000 | bytes 1000 | tf_op jit(solution)/shard_map/pallas_call | solution.py:238
  98.5 12.1 %collective-permute-start.9 = (bf16[64,13440]{1,0:T(8,128)(2,1)}, bf16[64,13440]{1,0:T(8,128)(2,1)S(1)}, u32[]{:S(2)}, u32[]{:S(2)}) collective-permute-start(bf16[64,13440]{1,0:T(8,128)(2,1)} %get-tuple-element.26.refs_3_), channel_id=1, source_target_pairs={{0,4},{4,0},{8,12},{12,8},{1,5},{5,1},{9,13},{13,9},{2,6},{6,2},{1... | collective-permute-start | bytes 5160968 | tf_op jit(solution)/shard_map/ppermute | solution.py:262
  110.7 8.4 %shard_map.59.refs_4_.refs_5_ = f32[4,64,512]{2,1,0:T(8,128)S(1)} custom-call(s32[2]{0:T(128)S(1)} %pad_add_fusion.place_ref, bf16[64,13440]{1,0:T(8,128)(2,1)} %collective-permute-done.1.refs_2_.refs_0_.refs_7_, bf16[64,13440]{1,0:T(8,128)(2,1)} %collective-permute-done.refs_1_.refs_8_, bf16[192,40000]{1,0:T(8,128)(2,1)S(1)} %bitcast.13, ...), custom_call_target="tpu_custom_call" | custom-call | flops 1000 | bytes 1000 | tf_op jit(solution)/shard_map/pallas_call | solution.py:238
  122.5 4.5 %collective-permute-start.10 = (bf16[64,13440]{1,0:T(8,128)(2,1)S(1)}, bf16[64,13440]{1,0:T(8,128)(2,1)S(1)}, u32[]{:S(2)}, u32[]{:S(2)}) collective-permute-start(bf16[64,13440]{1,0:T(8,128)(2,1)S(1)} %get-tuple-element.27.refs_3_), channel_id=1, source_target_pairs={{0,4},{4,0},{8,12},{12,8},{1,5},{5,1},{9,13},{13,9},{2,6},{6,2},{1... | collective-permute-start | bytes 5160968 | tf_op jit(solution)/shard_map/ppermute | solution.py:262
  128.4 7.8 %shard_map.61.refs_4_.refs_3_ = f32[4,64,512]{2,1,0:T(8,128)S(1)} custom-call(s32[2]{0:T(128)S(1)} %pad_add_fusion.place_ref, bf16[64,13440]{1,0:T(8,128)(2,1)} %collective-permute-done.5.refs_0_.refs_2_, bf16[64,13440]{1,0:T(8,128)(2,1)S(1)} %copy-done.4, bf16[192,40000]{1,0:T(8,128)(2,1)S(1)} %bitcast.16, bf16[192,40000]{1,0:T(8,128)(2,1)S(1)} %bitcast.17, ...), custom_call_target="tpu_custom_call" | custom-call | flops 1000 | bytes 1000 | tf_op jit(solution)/shard_map/pallas_call | solution.py:238
  136.3 2.7 %shard_map.62 = (bf16[64,11648]{1,0:T(8,128)(2,1)S(1)}, bf16[64,11648]{1,0:T(8,128)(2,1)S(1)}) custom-call(s32[2]{0:T(128)S(1)} %pad_add_fusion.place_ref, bf16[192,40000]{1,0:T(8,128)(2,1)S(1)} %bitcast.18, bf16[64,13440]{1,0:T(8,128)(2,1)S(1)} %collective-permute-done.4.refs_1_.refs_6_, bf16[64,13440]{1,0:T(8,128)(2,1)} %collective-permute-done.5.refs_0_.refs_2_, ...), custom_call_target="tpu_custom_call" | custom-call | flops 1000 | bytes 1000 | tf_op jit(solution)/shard_map/pallas_call | solution.py:145
  139.7 25.6 %collective-permute-start.12 = (bf16[64,11648]{1,0:T(8,128)(2,1)S(1)}, bf16[64,11648]{1,0:T(8,128)(2,1)S(1)}, u32[]{:S(2)}, u32[]{:S(2)}) collective-permute-start(bf16[64,11648]{1,0:T(8,128)(2,1)S(1)} %get-tuple-element.28.refs_3_), channel_id=1, source_target_pairs={{0,4},{4,0},{8,12},{12,8},{1,5},{5,1},{9,13},{13,9},{2,6},{6,2},{1... | collective-permute-start | bytes 4472840 | tf_op jit(solution)/shard_map/ppermute | solution.py:262
  168.0 5.0 %shard_map.64.refs_5_ = f32[4,64,512]{2,1,0:T(8,128)S(1)} custom-call(s32[2]{0:T(128)S(1)} %pad_add_fusion.place_ref, bf16[64,13440]{1,0:T(8,128)(2,1)S(1)} %collective-permute-done.9.refs_0_.refs_5_.refs_3_, bf16[64,13440]{1,0:T(8,128)(2,1)S(1)} %collective-permute-done.4.refs_1_.refs_6_, bf16[192,40000]{1,0:T(8,128)(2,1)S(1)} %bitcast.20, ...), custom_call_target="tpu_custom_call" | custom-call | flops 1000 | bytes 1000 | tf_op jit(solution)/shard_map/pallas_call | solution.py:238
  173.1 16.5 %collective-permute-done.10.refs_0_.refs_5_ = bf16[64,13440]{1,0:T(8,128)(2,1)S(1)} collective-permute-done((bf16[64,13440]{1,0:T(8,128)(2,1)S(1)}, bf16[64,13440]{1,0:T(8,128)(2,1)S(1)}, u32[]{:S(2)}, u32[]{:S(2)}) %collective-permute-start.10) | collective-permute-done | bytes 1720352 | tf_op jit(solution)/shard_map/ppermute | solution.py:262
  189.6 5.0 %shard_map.65.refs_7_ = f32[4,64,512]{2,1,0:T(8,128)S(1)} custom-call(s32[2]{0:T(128)S(1)} %pad_add_fusion.place_ref, bf16[64,13440]{1,0:T(8,128)(2,1)S(1)} %collective-permute-done.10.refs_0_.refs_5_, bf16[64,13440]{1,0:T(8,128)(2,1)S(1)} %collective-permute-done.11.refs_1_.refs_6_, bf16[192,40000]{1,0:T(8,128)(2,1)S(1)} %bitcast.22, ...), custom_call_target="tpu_custom_call" | custom-call | flops 1000 | bytes 1000 | tf_op jit(solution)/shard_map/pallas_call | solution.py:238
  194.6 26.9 %collective-permute-done.12.refs_0_ = bf16[64,11648]{1,0:T(8,128)(2,1)S(1)} collective-permute-done((bf16[64,11648]{1,0:T(8,128)(2,1)S(1)}, bf16[64,11648]{1,0:T(8,128)(2,1)S(1)}, u32[]{:S(2)}, u32[]{:S(2)}) %collective-permute-start.12) | collective-permute-done | bytes 1490976 | tf_op jit(solution)/shard_map/ppermute | solution.py:262
  221.5 4.4 %shard_map.66.refs_7_ = f32[4,64,512]{2,1,0:T(8,128)S(1)} custom-call(s32[2]{0:T(128)S(1)} %pad_add_fusion.place_ref, bf16[64,11648]{1,0:T(8,128)(2,1)S(1)} %collective-permute-done.12.refs_0_, bf16[64,11648]{1,0:T(8,128)(2,1)S(1)} %collective-permute-done.13.refs_1_, bf16[192,40000]{1,0:T(8,128)(2,1)S(1)} %bitcast.23, ...), custom_call_target="tpu_custom_call" | custom-call | flops 1000 | bytes 1000 | tf_op jit(solution)/shard_map/pallas_call | solution.py:238
  232.0 2.9 %collective-permute-done.15 = f32[72,384]{1,0:T(8,128)S(1)} collective-permute-done((f32[72,384]{1,0:T(8,128)S(1)}, f32[72,384]{1,0:T(8,128)S(1)}, u32[]{:S(2)}, u32[]{:S(2)}) %collective-permute-start.15) | collective-permute-done | bytes 110624 | tf_op jit(solution)/shard_map/ppermute | solution.py:374
  237.7 5.3 %collective-permute-start.17 = (f32[64,256]{1,0:T(8,128)S(1)}, f32[64,256]{1,0:T(8,128)S(1)}, u32[]{:S(2)}, u32[]{:S(2)}) collective-permute-start(f32[64,256]{1,0:T(8,128)S(1)} %get-tuple-element.39), channel_id=1, source_target_pairs={{0,0},{1,4},{2,8},{3,12},{4,1},{5,5},{6,9},{7,13},{8,2},{9,6},{10,... | collective-permute-start | bytes 196616 | tf_op jit(solution)/shard_map/ppermute | solution.py:386
  243.0 9.1 %collective-permute-start.18 = (f32[64,256]{1,0:T(8,128)S(1)}, f32[64,256]{1,0:T(8,128)S(1)}, u32[]{:S(2)}, u32[]{:S(2)}) collective-permute-start(f32[64,256]{1,0:T(8,128)S(1)} %get-tuple-element.40), channel_id=1, source_target_pairs={{0,1},{1,5},{2,9},{3,13},{4,0},{5,4},{6,8},{7,12},{8,3},{9,7},{10,... | collective-permute-start | bytes 196616 | tf_op jit(solution)/shard_map/ppermute | solution.py:386
  252.3 2.8 %collective-permute-done.18 = f32[64,256]{1,0:T(8,128)S(1)} collective-permute-done((f32[64,256]{1,0:T(8,128)S(1)}, f32[64,256]{1,0:T(8,128)S(1)}, u32[]{:S(2)}, u32[]{:S(2)}) %collective-permute-start.18) | collective-permute-done | bytes 65568 | tf_op jit(solution)/shard_map/ppermute | solution.py:386
  (63 shorter events, 31.8 us)
Async XLA Ops:
  1.6 5.4 %copy-start.6 = (f32[64,2]{0,1:T(2,128)S(1)}, f32[64,2]{0,1:T(2,128)}, u32[]{:S(2)}) copy-start(f32[64,2]{0,1:T(2,128)} %param.7) | copy-start | bytes 1540
  3.6 38.6 %collective-permute-start.3 = (bf16[64,13440]{1,0:T(8,128)(2,1)S(1)}, bf16[64,13440]{1,0:T(8,128)(2,1)}, u32[]{:S(2)}, u32[]{:S(2)}) collective-permute-start(bf16[64,13440]{1,0:T(8,128)(2,1)S(1)} %add_convert_fusion.token_ref.refs_3_), channel_id=1, source_target_pairs={{0,4},{4,0},{8,12},{12,8},{1,5},{5,1},{9,13},{13,9},{2,6},{6,2},{1... | collective-permute-start | bytes 5160968 | tf_op jit(solution)/shard_map/ppermute | solution.py:262
  5.0 37.2 %collective-permute-start.2 = (bf16[64,13440]{1,0:T(8,128)(2,1)S(1)}, bf16[64,13440]{1,0:T(8,128)(2,1)}, u32[]{:S(2)}, u32[]{:S(2)}) collective-permute-start(bf16[64,13440]{1,0:T(8,128)(2,1)S(1)} %add_convert_fusion.token_ref.refs_3_), channel_id=1, source_target_pairs={{4,8},{8,4},{5,9},{9,5},{6,10},{10,6},{7,11},{11,7},{20,24},{24,20... | collective-permute-start | bytes 5160968 | tf_op jit(solution)/shard_map/ppermute | solution.py:262
  13.6 65.5 %collective-permute-start.1 = (bf16[64,13440]{1,0:T(8,128)(2,1)}, bf16[64,13440]{1,0:T(8,128)(2,1)}, u32[]{:S(2)}, u32[]{:S(2)}) collective-permute-start(bf16[64,13440]{1,0:T(8,128)(2,1)} %get-tuple-element.21.refs_3_.refs_6_), channel_id=1, source_target_pairs={{0,4},{4,0},{8,12},{12,8},{1,5},{5,1},{9,13},{13,9},{2,6},{6,2},{1... | collective-permute-start | bytes 5160968 | tf_op jit(solution)/shard_map/ppermute | solution.py:262
  16.2 62.9 %collective-permute-start = (bf16[64,13440]{1,0:T(8,128)(2,1)}, bf16[64,13440]{1,0:T(8,128)(2,1)}, u32[]{:S(2)}, u32[]{:S(2)}) collective-permute-start(bf16[64,13440]{1,0:T(8,128)(2,1)} %get-tuple-element.21.refs_3_.refs_6_), channel_id=1, source_target_pairs={{4,8},{8,4},{5,9},{9,5},{6,10},{10,6},{7,11},{11,7},{20,24},{24,20... | collective-permute-start | bytes 5160968 | tf_op jit(solution)/shard_map/ppermute | solution.py:262
  47.7 71.4 %collective-permute-start.6 = (bf16[64,13440]{1,0:T(8,128)(2,1)}, bf16[64,13440]{1,0:T(8,128)(2,1)S(1)}, u32[]{:S(2)}, u32[]{:S(2)}) collective-permute-start(bf16[64,13440]{1,0:T(8,128)(2,1)} %get-tuple-element.25), channel_id=1, source_target_pairs={{4,8},{8,4},{5,9},{9,5},{6,10},{10,6},{7,11},{11,7},{20,24},{24,20... | collective-permute-start | bytes 5160968 | tf_op jit(solution)/shard_map/ppermute | solution.py:262
  48.4 78.6 %collective-permute-start.5 = (bf16[64,13440]{1,0:T(8,128)(2,1)}, bf16[64,13440]{1,0:T(8,128)(2,1)}, u32[]{:S(2)}, u32[]{:S(2)}) collective-permute-start(bf16[64,13440]{1,0:T(8,128)(2,1)} %get-tuple-element.23.refs_3_), channel_id=1, source_target_pairs={{0,4},{4,0},{8,12},{12,8},{1,5},{5,1},{9,13},{13,9},{2,6},{6,2},{1... | collective-permute-start | bytes 5160968 | tf_op jit(solution)/shard_map/ppermute | solution.py:262
  84.4 6.4 %copy-start.1 = (bf16[2,96,40000]{2,1,0:T(8,128)(2,1)S(1)}, bf16[2,96,40000]{2,1,0:T(8,128)(2,1)}, u32[]{:S(2)}) copy-start(bf16[2,96,40000]{2,1,0:T(8,128)(2,1)} %param.5) | copy-start | bytes 46080004
  90.1 46.1 %collective-permute-start.4 = (bf16[64,13440]{1,0:T(8,128)(2,1)S(1)}, bf16[64,13440]{1,0:T(8,128)(2,1)S(1)}, u32[]{:S(2)}, u32[]{:S(2)}) collective-permute-start(bf16[64,13440]{1,0:T(8,128)(2,1)S(1)} %get-tuple-element.24), channel_id=1, source_target_pairs={{4,8},{8,4},{5,9},{9,5},{6,10},{10,6},{7,11},{11,7},{20,24},{24,20... | collective-permute-start | bytes 5160968 | tf_op jit(solution)/shard_map/ppermute | solution.py:262
  98.5 68.7 %collective-permute-start.9 = (bf16[64,13440]{1,0:T(8,128)(2,1)}, bf16[64,13440]{1,0:T(8,128)(2,1)S(1)}, u32[]{:S(2)}, u32[]{:S(2)}) collective-permute-start(bf16[64,13440]{1,0:T(8,128)(2,1)} %get-tuple-element.26.refs_3_), channel_id=1, source_target_pairs={{0,4},{4,0},{8,12},{12,8},{1,5},{5,1},{9,13},{13,9},{2,6},{6,2},{1... | collective-permute-start | bytes 5160968 | tf_op jit(solution)/shard_map/ppermute | solution.py:262
  121.7 45.7 %collective-permute-start.11 = (bf16[64,13440]{1,0:T(8,128)(2,1)S(1)}, bf16[64,13440]{1,0:T(8,128)(2,1)S(1)}, u32[]{:S(2)}, u32[]{:S(2)}) collective-permute-start(bf16[64,13440]{1,0:T(8,128)(2,1)S(1)} %get-tuple-element.31), channel_id=1, source_target_pairs={{4,8},{8,4},{5,9},{9,5},{6,10},{10,6},{7,11},{11,7},{20,24},{24,20... | collective-permute-start | bytes 5160968 | tf_op jit(solution)/shard_map/ppermute | solution.py:262
  122.5 67.1 %collective-permute-start.10 = (bf16[64,13440]{1,0:T(8,128)(2,1)S(1)}, bf16[64,13440]{1,0:T(8,128)(2,1)S(1)}, u32[]{:S(2)}, u32[]{:S(2)}) collective-permute-start(bf16[64,13440]{1,0:T(8,128)(2,1)S(1)} %get-tuple-element.27.refs_3_), channel_id=1, source_target_pairs={{0,4},{4,0},{8,12},{12,8},{1,5},{5,1},{9,13},{13,9},{2,6},{6,2},{1... | collective-permute-start | bytes 5160968 | tf_op jit(solution)/shard_map/ppermute | solution.py:262
  138.9 55.7 %collective-permute-start.13 = (bf16[64,11648]{1,0:T(8,128)(2,1)S(1)}, bf16[64,11648]{1,0:T(8,128)(2,1)S(1)}, u32[]{:S(2)}, u32[]{:S(2)}) collective-permute-start(bf16[64,11648]{1,0:T(8,128)(2,1)S(1)} %get-tuple-element.32), channel_id=1, source_target_pairs={{4,8},{8,4},{5,9},{9,5},{6,10},{10,6},{7,11},{11,7},{20,24},{24,20... | collective-permute-start | bytes 4472840 | tf_op jit(solution)/shard_map/ppermute | solution.py:262
  139.7 81.8 %collective-permute-start.12 = (bf16[64,11648]{1,0:T(8,128)(2,1)S(1)}, bf16[64,11648]{1,0:T(8,128)(2,1)S(1)}, u32[]{:S(2)}, u32[]{:S(2)}) collective-permute-start(bf16[64,11648]{1,0:T(8,128)(2,1)S(1)} %get-tuple-element.28.refs_3_), channel_id=1, source_target_pairs={{0,4},{4,0},{8,12},{12,8},{1,5},{5,1},{9,13},{13,9},{2,6},{6,2},{1... | collective-permute-start | bytes 4472840 | tf_op jit(solution)/shard_map/ppermute | solution.py:262
  167.2 59.2 %collective-permute-start.7 = (bf16[64,1792]{1,0:T(8,128)(2,1)S(1)}, bf16[64,1792]{1,0:T(8,128)(2,1)S(1)}, u32[]{:S(2)}, u32[]{:S(2)}) collective-permute-start(bf16[64,1792]{1,0:T(8,128)(2,1)S(1)} %get-tuple-element.29), channel_id=1, source_target_pairs={{0,4},{4,0},{8,12},{12,8},{1,5},{5,1},{9,13},{13,9},{2,6},{6,2},{1... | collective-permute-start | bytes 688136 | tf_op jit(solution)/shard_map/ppermute | solution.py:262
  167.4 59.1 %collective-permute-start.8 = (bf16[64,1792]{1,0:T(8,128)(2,1)S(1)}, bf16[64,1792]{1,0:T(8,128)(2,1)S(1)}, u32[]{:S(2)}, u32[]{:S(2)}) collective-permute-start(bf16[64,1792]{1,0:T(8,128)(2,1)S(1)} %get-tuple-element.30), channel_id=1, source_target_pairs={{4,8},{8,4},{5,9},{9,5},{6,10},{10,6},{7,11},{11,7},{20,24},{24,20... | collective-permute-start | bytes 688136 | tf_op jit(solution)/shard_map/ppermute | solution.py:262
  194.6 31.8 %copy-start.5 = (f32[2,96]{1,0:T(2,128)S(1)}, f32[2,96]{1,0:T(2,128)}, u32[]{:S(2)}) copy-start(f32[2,96]{1,0:T(2,128)} %refs_11_.1) | copy-start | bytes 2308
  228.0 4.0 %collective-permute-start.14 = (f32[72,384]{1,0:T(8,128)S(1)}, f32[72,384]{1,0:T(8,128)S(1)}, u32[]{:S(2)}, u32[]{:S(2)}) collective-permute-start(f32[72,384]{1,0:T(8,128)S(1)} %get-tuple-element.34), channel_id=1, source_target_pairs={{0,1},{1,0},{2,3},{3,2},{4,5},{5,4},{6,7},{7,6},{8,9},{9,8},{10,11... | collective-permute-start | bytes 331784 | tf_op jit(solution)/shard_map/ppermute | solution.py:374
  230.3 4.6 %collective-permute-start.15 = (f32[72,384]{1,0:T(8,128)S(1)}, f32[72,384]{1,0:T(8,128)S(1)}, u32[]{:S(2)}, u32[]{:S(2)}) collective-permute-start(f32[72,384]{1,0:T(8,128)S(1)} %get-tuple-element.35), channel_id=1, source_target_pairs={{0,2},{1,3},{2,0},{3,1},{4,6},{5,7},{6,4},{7,5},{8,10},{9,11},{10,... | collective-permute-start | bytes 331784 | tf_op jit(solution)/shard_map/ppermute | solution.py:374
  230.3 7.2 %collective-permute-start.16 = (f32[72,384]{1,0:T(8,128)S(1)}, f32[72,384]{1,0:T(8,128)S(1)}, u32[]{:S(2)}, u32[]{:S(2)}) collective-permute-start(f32[72,384]{1,0:T(8,128)S(1)} %get-tuple-element.36), channel_id=1, source_target_pairs={{0,3},{1,2},{2,1},{3,0},{4,7},{5,6},{6,5},{7,4},{8,11},{9,10},{10,... | collective-permute-start | bytes 331784 | tf_op jit(solution)/shard_map/ppermute | solution.py:374
  237.7 14.6 %collective-permute-start.17 = (f32[64,256]{1,0:T(8,128)S(1)}, f32[64,256]{1,0:T(8,128)S(1)}, u32[]{:S(2)}, u32[]{:S(2)}) collective-permute-start(f32[64,256]{1,0:T(8,128)S(1)} %get-tuple-element.39), channel_id=1, source_target_pairs={{0,0},{1,4},{2,8},{3,12},{4,1},{5,5},{6,9},{7,13},{8,2},{9,6},{10,... | collective-permute-start | bytes 196616 | tf_op jit(solution)/shard_map/ppermute | solution.py:386
  243.0 12.1 %collective-permute-start.18 = (f32[64,256]{1,0:T(8,128)S(1)}, f32[64,256]{1,0:T(8,128)S(1)}, u32[]{:S(2)}, u32[]{:S(2)}) collective-permute-start(f32[64,256]{1,0:T(8,128)S(1)} %get-tuple-element.40), channel_id=1, source_target_pairs={{0,1},{1,5},{2,9},{3,13},{4,0},{5,4},{6,8},{7,12},{8,3},{9,7},{10,... | collective-permute-start | bytes 196616 | tf_op jit(solution)/shard_map/ppermute | solution.py:386
  252.2 3.4 %collective-permute-start.20 = (f32[64]{0:T(128)S(1)}, f32[64]{0:T(128)S(1)}, u32[]{:S(2)}, u32[]{:S(2)}) collective-permute-start(f32[64]{0:T(128)S(1)} %slice_reduce_fusion), channel_id=1, source_target_pairs={{0,3},{1,7},{2,11},{3,15},{4,2},{5,6},{6,10},{7,14},{8,1},{9,5},{1... | collective-permute-start | bytes 776 | tf_op jit(solution)/shard_map/ppermute | solution.py:387
  252.2 3.9 %collective-permute-start.19 = (f32[64]{0:T(128)S(1)}, f32[64]{0:T(128)S(1)}, u32[]{:S(2)}, u32[]{:S(2)}) collective-permute-start(f32[64]{0:T(128)S(1)} %slice_reduce_fusion), channel_id=1, source_target_pairs={{0,2},{1,6},{2,10},{3,14},{4,3},{5,7},{6,11},{7,15},{8,0},{9,4},{1... | collective-permute-start | bytes 776 | tf_op jit(solution)/shard_map/ppermute | solution.py:387
  (5 other events, 17.1 us)
